TPU v7x, 32 devices: a whole 2x2x4 slice. The times are simulated.
32 devices in a mesh: group: 2 (over x), row: 4 (over y, core), tilt: 4 (over z).
Axes of the slice: x: 2, y: 2, z: 4, core: 2. Of those that a mesh axis runs over, the one named last changes fastest.
Arguments:
- projections: bfloat16 [8, 256, 2048], P(('group', 'tilt'), 'row'), parts along dimension 0, may hold values from -6 to 6
- tilt_angle: float32 [8], P('group'), parts along dimension 0, may hold values from -1.05 to 1.05
- band_start: int32 [8, 4, 4], P('group'), parts along dimension 0, may hold values from 0 to 1792
- defocus: int32 [8, 4], P('group'), parts along dimension 0, may hold values from 60 to 239
Outputs:
- volume: bfloat16 [128, 256, 512], P(('group', 'tilt'), 'row'), parts along dimension 0
There are 2 independent parts, one for each index of `group`. A program takes and returns all parts, laid end to end along the dimension named above; each array names one. Nothing has to cross between parts.
All inputs are finite; a program needn't handle non-finite values.
Results may differ from a plain program's by a relative error of at most 0.0061.
Values may be sent and summed in bfloat16 or wider, within the bound.
No kernel may reach another device: no remote copies, remote signals or barrier semaphores. Data moves between devices by JAX's collectives and lax.ppermute only.
A program may use at most 128 MiB of HBM per device.

v0:
```python
import functools
import math

import jax
import jax.numpy as jnp
import numpy as np
from jax import lax
from jax.experimental import pallas as pl
from jax.experimental.pallas import tpu as pltpu
from jax.sharding import PartitionSpec as P

SLAB = 16
XBW = 128
BAND = 256
XBLK = 4
SLICES = 64
RADIX = 8
WINDOW = BAND + 128


def column_blocks(columns):
    size = columns // RADIX
    return [(0, size), (size, size)] + [(2 * size * j, 2 * size) for j in (1, 2, 3)]


def packed_frequencies(columns):
    size = columns // RADIX
    half = size // 2
    parts = [RADIX * np.arange(half + 1), RADIX * np.arange(1, half)]
    parts += [RADIX * np.arange(half) + 4] * 2
    for j in (1, 2, 3):
        parts += [RADIX * np.arange(size) + j] * 2
    freq = np.concatenate(parts)
    count = np.where((freq == 0) | (freq == columns // 2), 1.0, 2.0)
    return np.minimum(freq, columns - freq), count


def column_tables(columns):
    size = columns // RADIX
    half = size // 2
    u = np.arange(size)[:, None]

    def angles(freq):
        return 2.0 * np.pi * ((u * freq[None, :]) % columns) / columns

    k0, s0 = RADIX * np.arange(half + 1), RADIX * np.arange(1, half)
    k4 = RADIX * np.arange(half) + 4
    m0 = np.concatenate([np.cos(angles(k0)), -np.sin(angles(s0))], 1)
    m4 = np.concatenate([np.cos(angles(k4)), -np.sin(angles(k4))], 1)
    forward, backward = [np.concatenate([m0, m4])], [np.concatenate([m0.T, m4.T])]
    for j in (1, 2, 3):
        t = angles(RADIX * np.arange(size) + j)
        m = np.block([[np.cos(t), -np.sin(t)], [np.sin(t), np.cos(t)]])
        forward.append(m)
        backward.append(m.T)
    forward, backward = np.concatenate(forward, 1), np.concatenate(backward, 1)
    high = forward.astype(jnp.bfloat16)
    low = (forward - high.astype(np.float64)).astype(jnp.bfloat16)
    return high, low, backward.astype(jnp.bfloat16)


def row_table(full_rows):
    half = full_rows // 2
    y = np.arange(full_rows)[:, None]
    freq = np.concatenate([np.arange(half + 1), np.arange(1, half)])
    angle = 2.0 * np.pi * (y * freq[None, :] % full_rows) / full_rows
    waves = np.where(np.arange(full_rows)[None, :] <= half, np.cos(angle), np.sin(angle))
    return waves, freq, np.where((freq == 0) | (freq == half), 1.0, 2.0)


def table_slices(columns):
    size = columns // RADIX
    places = column_blocks(columns)
    out = [(places[0], slice(0, size), slice(0, size)), (places[1], slice(size, 2 * size), slice(0, size))]
    for i, place in enumerate(places[2:]):
        first = size + 2 * size * i
        out.append((place, slice(0, 2 * size), slice(first, first + 2 * size)))
    return out


def filter_kernel(slots, row_blocks, meta, a_ref, gain_ref, high_ref, low_ref, back_ref, *refs):
    block_refs = refs[:row_blocks]
    out_refs = refs[row_blocks : row_blocks + slots]
    zhi, zlo, spec, turned = refs[row_blocks + slots :]
    rows, columns = block_refs[0].shape
    size = columns // RADIX
    full_rows = rows * row_blocks
    row_index = meta[0]
    root = math.sqrt(0.5)

    for distance in range(row_blocks):
        source = block_refs[distance]
        first_row = (row_index ^ distance) * rows

        def butterfly(step, carry):
            here = pl.ds(pl.multiple_of(step * 16, 16), 16)
            there = pl.ds(pl.multiple_of(first_row + step * 16, 16), 16)
            x = [source[here, m * size : (m + 1) * size].astype(jnp.float32) for m in range(8)]
            p0, p1, p2, p3 = (x[m] + x[m + 4] for m in range(4))
            q0, q1, q2, q3 = (x[m] - x[m + 4] for m in range(4))
            e, f = p0 + p2, p1 + p3
            g, h = root * (q1 - q3), root * (q1 + q3)
            z = [e + f, e - f, q0 + g, -q2 - h, p0 - p2, p3 - p1, q0 - g, q2 - h]
            for i in range(8):
                top = z[i].astype(jnp.bfloat16)
                zhi[there, i * size : (i + 1) * size] = top
                zlo[there, i * size : (i + 1) * size] = (z[i] - top.astype(jnp.float32)).astype(jnp.bfloat16)
            return carry

        lax.fori_loop(0, rows // 16, butterfly, 0)

    chunk = min(full_rows, 256)
    tables = table_slices(columns)
    for (first, width), table_rows, table_columns in tables:
        high, low = high_ref[table_rows, table_columns], low_ref[table_rows, table_columns]
        for c in range(full_rows // chunk):
            here = slice(c * chunk, (c + 1) * chunk)
            top, rest = zhi[here, first : first + width], zlo[here, first : first + width]
            total = jnp.dot(top, high, preferred_element_type=jnp.float32)
            total += jnp.dot(top, low, preferred_element_type=jnp.float32)
            total += jnp.dot(rest, high, preferred_element_type=jnp.float32)
            spec[here, first : first + width] = total.astype(jnp.bfloat16)

    row_filter = a_ref[...]
    for (first, width), table_rows, table_columns in tables:
        there = slice(first, first + width)
        y = jnp.dot(row_filter, spec[:, there], preferred_element_type=jnp.float32)
        filtered = [
            (y[slot * rows : (slot + 1) * rows] * gain_ref[slot : slot + 1, there]).astype(jnp.bfloat16)
            for slot in range(slots)
        ]
        turned[:, there] = jnp.dot(
            jnp.concatenate(filtered, 0), back_ref[table_rows, table_columns], preferred_element_type=jnp.float32
        )

    def inverse_butterfly(step, carry):
        here = pl.ds(pl.multiple_of(step * 16, 16), 16)
        z0, z4, r1, i1, r2, i2, r3, i3 = (turned[here, i * size : (i + 1) * size] for i in range(8))
        e, f = z0 + z4, z0 - z4
        a, b = r1 + r3, r1 - r3
        c, d = i1 + i3, i1 - i3
        even0, even2 = e + r2, e - r2
        odd1, odd3 = f - i2, f + i2
        g, h = root * (b - c), root * (b + c)
        out = [even0 + a, odd1 + g, even2 - d, odd3 - h, even0 - a, odd1 - g, even2 + d, odd3 + h]
        for m in range(8):
            turned[here, m * size : (m + 1) * size] = out[m]
        return carry

    lax.fori_loop(0, slots * rows // 16, inverse_butterfly, 0)

    for slot in range(slots):
        for block in range(XBLK):
            start = meta[1 + slot * XBLK + block]
            base = pl.multiple_of(jnp.minimum((start // 128) * 128, columns - WINDOW), 128)
            window = turned[slot * rows : (slot + 1) * rows, pl.ds(base, WINDOW)]
            shift = base - start
            shift = jnp.where(shift < 0, shift + WINDOW, shift)
            out_refs[slot][block] = pltpu.roll(window, shift, 1)[:, :BAND].astype(jnp.bfloat16)


def filtered_patches(meta, row_filters, gains, tables, blocks):
    slots, row_blocks = gains.shape[0], len(blocks)
    rows, columns = blocks[0].shape
    full_rows = rows * row_blocks
    vmem = pl.BlockSpec(memory_space=pltpu.VMEM)
    flops = 2 * columns * (3 * full_rows * columns // 4 + slots * rows * (full_rows + columns // 4))
    return pl.pallas_call(
        functools.partial(filter_kernel, slots, row_blocks),
        out_shape=[jax.ShapeDtypeStruct((XBLK, rows, BAND), jnp.bfloat16)] * slots,
        in_specs=[pl.BlockSpec(memory_space=pltpu.SMEM)] + [vmem] * (5 + row_blocks),
        out_specs=[vmem] * slots,
        scratch_shapes=[
            pltpu.VMEM((full_rows, columns), jnp.bfloat16),
            pltpu.VMEM((full_rows, columns), jnp.bfloat16),
            pltpu.VMEM((full_rows, columns), jnp.bfloat16),
            pltpu.VMEM((slots * rows, columns), jnp.float32),
        ],
        compiler_params=pltpu.CompilerParams(vmem_limit_bytes=40 * 2**20),
        cost_estimate=pl.CostEstimate(flops=flops, bytes_accessed=10 * 2**20, transcendentals=0),
        name="filter",
    )(meta, row_filters, gains, *tables, *blocks)


def interpolate_kernel(slots, factor, weights_ref, *refs):
    patch_refs, out_ref = refs[:slots], refs[slots]
    blocks, rows, taps = patch_refs[0].shape
    total = jnp.zeros((blocks * rows, weights_ref.shape[2]), jnp.float32)
    for slot in range(slots):
        total += jnp.dot(
            patch_refs[slot][...].reshape(blocks * rows, taps), weights_ref[slot], preferred_element_type=jnp.float32
        )
    for c in range(out_ref.shape[0]):
        for block in range(blocks):
            out_ref[c, :, block * XBW : (block + 1) * XBW] = (
                factor * total[block * rows : (block + 1) * rows, c * XBW : (c + 1) * XBW]
            ).astype(jnp.bfloat16)


def interpolated(weights, patches, factor):
    slots, taps, width = weights.shape
    blocks, rows, _ = patches[0].shape
    slices = width // XBW
    step = math.gcd(slices, 4)
    return pl.pallas_call(
        functools.partial(interpolate_kernel, slots, factor),
        grid=(slices // step,),
        out_shape=jax.ShapeDtypeStruct((slices, rows, blocks * XBW), jnp.bfloat16),
        in_specs=[pl.BlockSpec((slots, taps, step * XBW), lambda i: (0, 0, i))]
        + [pl.BlockSpec((blocks, rows, taps), lambda i: (0, 0, 0))] * slots,
        out_specs=pl.BlockSpec((step, rows, blocks * XBW), lambda i: (i, 0, 0)),
        compiler_params=pltpu.CompilerParams(vmem_limit_bytes=24 * 2**20),
        cost_estimate=pl.CostEstimate(
            flops=2 * blocks * rows * slots * taps * width, bytes_accessed=6 * 2**20, transcendentals=0
        ),
        name="interpolate",
    )(weights, *patches)


def exchange(array, axis, distance):
    count = lax.axis_size(axis)
    return lax.ppermute(array, axis, [(i, i ^ distance) for i in range(count)])


def per_device(projections, tilt_angle, band_start, defocus):
    _, rows, columns = projections.shape
    row_devices, tilt_devices = lax.axis_size("row"), lax.axis_size("tilt")
    full_rows = rows * row_devices
    row_index, tilt_index = lax.axis_index("row"), lax.axis_index("tilt")
    image = projections[0]

    blocks = {0: image}
    bit = row_devices // 2
    while bit:
        blocks.update({d ^ bit: exchange(block, "row", bit) for d, block in blocks.items()})
        bit //= 2

    slices_owned = SLICES // tilt_devices
    distances = jnp.arange(tilt_devices, dtype=jnp.int32)
    owners = tilt_index ^ distances
    slabs = owners * slices_owned // SLAB
    own_defocus = jnp.take(lax.dynamic_index_in_dim(defocus, tilt_index, 0, keepdims=False), slabs)
    own_starts = jnp.take(lax.dynamic_index_in_dim(band_start, tilt_index, 0, keepdims=False), slabs, axis=0)
    meta = jnp.concatenate([row_index[None].astype(jnp.int32), own_starts.reshape(-1)])

    row_waves, row_fold, row_count = row_table(full_rows)
    row_fold = jnp.asarray(row_fold, jnp.int32)
    row_cycles = row_fold * row_fold * own_defocus[:, None] // (full_rows * full_rows)
    row_sign = (1 - 2 * (row_cycles % 2)).astype(jnp.float32) * jnp.asarray(row_count / full_rows, jnp.float32)
    row_waves = jnp.asarray(row_waves, jnp.float32)
    own_waves = lax.dynamic_slice_in_dim(row_waves, row_index * rows, rows, 0)
    row_filters = lax.dot_general(
        (row_sign[:, None, :] * own_waves[None]).reshape(tilt_devices * rows, full_rows),
        row_waves,
        (((1,), (1,)), ((), ())),
        precision=lax.Precision.HIGHEST,
    ).astype(jnp.bfloat16)
    column_fold, count = packed_frequencies(columns)
    ramp = jnp.asarray(count * (column_fold + 0.5) / (0.5 * columns) / columns, jnp.float32)
    column_fold = jnp.asarray(column_fold, jnp.int32)
    column_cycles = column_fold * column_fold * own_defocus[:, None] // (columns * columns)
    gains = (1 - 2 * (column_cycles % 2)).astype(jnp.float32) * ramp

    tables = [jnp.asarray(t) for t in column_tables(columns)]
    sent = filtered_patches(meta, row_filters, gains, tables, [blocks[d] for d in range(row_devices)])
    patches = [sent[0]] + [exchange(sent[d], "tilt", d) for d in range(1, tilt_devices)]

    angles = jnp.take(tilt_angle, owners)
    local_first = tilt_index * slices_owned % SLAB
    offsets = (local_first + jnp.arange(slices_owned, dtype=jnp.int32)).astype(jnp.float32) - 0.5 * (SLAB - 1)
    column = jnp.arange(XBW, dtype=jnp.float32)
    centre = (
        0.5 * XBW
        + column[None, None, :] * jnp.cos(angles)[:, None, None]
        + offsets[None, :, None] * jnp.sin(angles)[:, None, None]
    ).reshape(tilt_devices, 1, slices_owned * XBW)
    tap = jnp.arange(BAND, dtype=jnp.float32)[None, :, None]
    weights = jnp.maximum(0.0, 1.0 - jnp.abs(tap - centre)).astype(jnp.bfloat16)
    return interpolated(weights, patches, 1.0 / math.sqrt(tilt_devices))


def solution(mesh):
    in_specs = (
        P(("group", "tilt"), "row", None),
        P("group"),
        P("group", None, None),
        P("group", None),
    )
    out_specs = P(("group", "tilt"), "row", None)
    return jax.shard_map(
        per_device, mesh=mesh, in_specs=in_specs, out_specs=out_specs, check_vma=False
    )
```

profile of v0, /device:TPU:0, one launch (start us, length us, event | category | flops | bytes accessed | tf_op | source)
XLA Modules:
  0.0 38.8 jit_solution(17781676306843652504)
XLA Ops:
  0.0 3.0 %collective-permute-start.1 = (bf16[64,2048]{1,0:T(8,128)(2,1)}, bf16[64,2048]{1,0:T(8,128)(2,1)S(1)}, u32[]{:S(2)}, u32[]{:S(2)}) collective-permute-start(bf16[64,2048]{1,0:T(8,128)(2,1)} %bitcast.18), channel_id=1, source_target_pairs={{0,8},{4,12},{8,0},{12,4},{1,9},{5,13},{9,1},{13,5},{2,10},{6,14},... | collective-permute-start | bytes 786440 | tf_op jit(solution)/shard_map/ppermute | solution.py:222
  3.0 0.7 %fusion.16 = s32[4]{0:T(128)S(1)} fusion(s32[4,4]{1,0:T(4,128)} %param.15, s32[]{:T(128)S(6)} %select_n.140), kind=kLoop, calls=%fused_computation.66 | loop fusion | bytes 36 | tf_op jit(solution)/shard_map/jit(dynamic_index_in_dim)/squeeze | solution.py:242
  3.7 1.3 %gather_fusion = f32[4]{0:T(128)S(1)} fusion(f32[4]{0:T(128)} %param.13, s32[1024]{0:T(1024)S(1)} %pad_clamp_fusion.1), kind=kCustom, calls=%fused_computation | custom fusion | bytes 48 | tf_op jit(solution)/shard_map/jit(_take)/gather | solution.py:268
  5.2 0.6 %gather_fusion.2 = s32[4]{0:T(128)S(1)} fusion(s32[4]{0:T(128)S(1)} %fusion.16, s32[1024]{0:T(1024)S(1)} %pad_clamp_fusion), kind=kCustom, calls=%fused_computation.2 | custom fusion | bytes 48 | tf_op jit(solution)/shard_map/jit(_take)/gather | solution.py:242
  5.9 0.6 %gather_fusion.1 = s32[4,4]{1,0:T(4,128)S(1)} fusion(s32[4,4]{1,0:T(4,128)S(1)} %dynamic-slice_bitcast_fusion, s32[1024]{0:T(1024)S(1)} %pad_clamp_fusion), kind=kCustom, calls=%fused_computation.1 | custom fusion | bytes 144 | tf_op jit(solution)/shard_map/jit(_take)/gather | solution.py:243
  6.6 0.8 %fusion.13 = f32[4,256]{1,0:T(4,128)S(1)} fusion(f32[256]{0:T(256)} %constant.162.clone, s32[4]{0:T(128)S(1)} %broadcast_select_fusion.1, s32[256]{0:T(256)} %constant.170), kind=kLoop, calls=%fused_computation.41 | loop fusion | flops 31744 | bytes 6160 | tf_op jit(solution)/shard_map/mul | solution.py:249
  7.4 0.9 %fusion.5.gain_ref = f32[4,2048]{1,0:T(4,128)S(1)} fusion(f32[2048]{0:T(1024)} %constant.164.clone, s32[4]{0:T(128)S(1)} %broadcast_select_fusion.1, s32[2048]{0:T(1024)} %constant.171), kind=kLoop, calls=%fused_computation.21 | loop fusion | flops 253952 | bytes 49168 | tf_op jit(solution)/shard_map/mul | solution.py:262
  8.3 0.9 %constant_dynamic-slice_fusion = f32[64,256]{1,0:T(8,128)S(1)} fusion(f32[256,256]{1,0:T(8,128)} %constant.163.clone, s32[]{:T(128)S(6)} %select_n.148), kind=kLoop, calls=%fused_computation.64 | loop fusion | bytes 131076 | tf_op jit(solution)/shard_map/dynamic_slice | solution.py:251
  9.2 0.1 select_n.144
  9.3 0.2 collective-permute-done.1.refs_2_
  9.5 0.4 collective-permute-start.2
  9.9 1.4 %convolution_convert_fusion.a_ref = bf16[256,256]{1,0:T(8,128)(2,1)S(1)} fusion(f32[256,256]{1,0:T(8,128)S(1)} %bitcast.21, f32[256,256]{1,0:T(8,128)} %constant.163.clone), kind=kOutput, calls=%fused_computation.4 | convolution fusion | flops 201392128 | bytes 655360 | tf_op jit(solution)/shard_map/dot_general | solution.py:252
  11.3 0.9 %copy-done.1 = bf16[1,64,2048]{2,1,0:T(8,128)(2,1)S(1)} copy-done((bf16[1,64,2048]{2,1,0:T(8,128)(2,1)S(1)}, bf16[1,64,2048]{2,1,0:T(8,128)(2,1)}, u32[]{:S(2)}) %copy-start.1) | copy-done | bytes 262168
  12.3 1.5 %copy-done.2 = bf16[512,1792]{1,0:T(8,128)(2,1)S(1)} copy-done((bf16[512,1792]{1,0:T(8,128)(2,1)S(1)}, bf16[512,1792]{1,0:T(8,128)(2,1)}, u32[]{:S(2)}) %copy-start.2) | copy-done | bytes 1835032
  13.8 1.5 %copy-done.3 = bf16[512,1792]{1,0:T(8,128)(2,1)S(1)} copy-done((bf16[512,1792]{1,0:T(8,128)(2,1)S(1)}, bf16[512,1792]{1,0:T(8,128)(2,1)}, u32[]{:S(2)}) %copy-start.3) | copy-done | bytes 1835032
  15.3 1.5 %copy-done.4 = bf16[512,1792]{1,0:T(8,128)(2,1)S(1)} copy-done((bf16[512,1792]{1,0:T(8,128)(2,1)S(1)}, bf16[512,1792]{1,0:T(8,128)(2,1)}, u32[]{:S(2)}) %copy-start.4) | copy-done | bytes 1835032
  16.8 4.4 %filter.1 = (bf16[4,64,256]{2,1,0:T(8,128)(2,1)S(1)}, bf16[4,64,256]{2,1,0:T(8,128)(2,1)S(1)}, bf16[4,64,256]{2,1,0:T(8,128)(2,1)S(1)}, bf16[4,64,256]{2,1,0:T(8,128)(2,1)S(1)}) custom-call(s32[17]{0:T(128)S(1)} %pad_add_fusion.meta, bf16[256,256]{1,0:T(8,128)(2,1)S(1)} %convolution_convert_fusion.a_ref, f32[4,2048]{1,0:T(4,128)S(1)} %fusion.5.gain_ref, ...), custom_call_target="tpu_custom_call" | custom-call | flops 2415919104 | bytes 10485760 | tf_op jit(solution)/shard_map/filter/pallas_call | solution.py:168
  21.2 1.7 %collective-permute-start.3 = (bf16[4,64,256]{2,1,0:T(8,128)(2,1)S(1)}, bf16[4,64,256]{2,1,0:T(8,128)(2,1)S(1)}, u32[]{:S(2)}, u32[]{:S(2)}) collective-permute-start(bf16[4,64,256]{2,1,0:T(8,128)(2,1)S(1)} %get-tuple-element.10), channel_id=1, source_target_pairs={{0,1},{1,0},{2,3},{3,2},{4,5},{5,4},{6,7},{7,6},{8,9},{9,8},{10,11... | collective-permute-start | bytes 393224 | tf_op jit(solution)/shard_map/ppermute | solution.py:222
  22.9 2.6 %collective-permute-start.4 = (bf16[4,64,256]{2,1,0:T(8,128)(2,1)S(1)}, bf16[4,64,256]{2,1,0:T(8,128)(2,1)S(1)}, u32[]{:S(2)}, u32[]{:S(2)}) collective-permute-start(bf16[4,64,256]{2,1,0:T(8,128)(2,1)S(1)} %get-tuple-element.11), channel_id=1, source_target_pairs={{0,2},{1,3},{2,0},{3,1},{4,6},{5,7},{6,4},{7,5},{8,10},{9,11},{10,... | collective-permute-start | bytes 393224 | tf_op jit(solution)/shard_map/ppermute | solution.py:222
  25.5 0.2 collective-permute-start.5
  25.7 1.3 %maximum_convert_fusion.weights_ref = bf16[4,256,2048]{2,1,0:T(8,128)(2,1)S(1)} fusion(f32[4,2048]{1,0:T(4,128)S(1)} %bitcast.22), kind=kLoop, calls=%fused_computation.3 | loop fusion | flops 10485760 | bytes 4227072 | tf_op jit(solution)/shard_map/convert_element_type | solution.py:278
  27.0 2.0 %collective-permute-done.3.refs_1_ = bf16[4,64,256]{2,1,0:T(8,128)(2,1)S(1)} collective-permute-done((bf16[4,64,256]{2,1,0:T(8,128)(2,1)S(1)}, bf16[4,64,256]{2,1,0:T(8,128)(2,1)S(1)}, u32[]{:S(2)}, u32[]{:S(2)}) %collective-permute-start.3) | collective-permute-done | bytes 131104 | tf_op jit(solution)/shard_map/ppermute | solution.py:222
  29.0 6.8 %collective-permute-done.4.refs_2_ = bf16[4,64,256]{2,1,0:T(8,128)(2,1)S(1)} collective-permute-done((bf16[4,64,256]{2,1,0:T(8,128)(2,1)S(1)}, bf16[4,64,256]{2,1,0:T(8,128)(2,1)S(1)}, u32[]{:S(2)}, u32[]{:S(2)}) %collective-permute-start.4) | collective-permute-done | bytes 131104 | tf_op jit(solution)/shard_map/ppermute | solution.py:222
  35.8 3.0 %interpolate.1 = bf16[16,64,512]{2,1,0:T(8,128)(2,1)} custom-call(bf16[4,256,2048]{2,1,0:T(8,128)(2,1)S(1)} %maximum_convert_fusion.weights_ref, bf16[4,64,256]{2,1,0:T(8,128)(2,1)S(1)} %get-tuple-element.9.refs_0_, bf16[4,64,256]{2,1,0:T(8,128)(2,1)S(1)} %collective-permute-done.3.refs_1_, bf16[4,64,256]{2,1,0:T(8,128)(2,1)S(1)} %collective-permute-done.4.refs_2_, ...), custom_call_target="tpu_custom_call" | custom-call | flops 1073741824 | bytes 6291456 | tf_op jit(solution)/shard_map/interpolate/pallas_call | solution.py:205
  (26 shorter events, 0.6 us)
Async XLA Ops:
  0.0 3.7 %copy-start = (s32[4,4,4]{2,1,0:T(4,128)S(1)}, s32[4,4,4]{2,1,0:T(4,128)}, u32[]{:S(2)}) copy-start(s32[4,4,4]{2,1,0:T(4,128)} %param.14) | copy-start | bytes 772
  0.0 9.5 %collective-permute-start.1 = (bf16[64,2048]{1,0:T(8,128)(2,1)}, bf16[64,2048]{1,0:T(8,128)(2,1)S(1)}, u32[]{:S(2)}, u32[]{:S(2)}) collective-permute-start(bf16[64,2048]{1,0:T(8,128)(2,1)} %bitcast.18), channel_id=1, source_target_pairs={{0,8},{4,12},{8,0},{12,4},{1,9},{5,13},{9,1},{13,5},{2,10},{6,14},... | collective-permute-start | bytes 786440 | tf_op jit(solution)/shard_map/ppermute | solution.py:222
  3.0 8.3 %collective-permute-start = (bf16[64,2048]{1,0:T(8,128)(2,1)}, bf16[64,2048]{1,0:T(8,128)(2,1)S(1)}, u32[]{:S(2)}, u32[]{:S(2)}) collective-permute-start(bf16[64,2048]{1,0:T(8,128)(2,1)} %bitcast.19), channel_id=1, source_target_pairs={{0,4},{4,0},{8,12},{12,8},{1,5},{5,1},{9,13},{13,9},{2,6},{6,2},{1... | collective-permute-start | bytes 786440 | tf_op jit(solution)/shard_map/ppermute | solution.py:222
  9.5 1.8 %collective-permute-start.2 = (bf16[64,2048]{1,0:T(8,128)(2,1)S(1)}, bf16[64,2048]{1,0:T(8,128)(2,1)S(1)}, u32[]{:S(2)}, u32[]{:S(2)}) collective-permute-start(bf16[64,2048]{1,0:T(8,128)(2,1)S(1)} %collective-permute-done.1.refs_2_), channel_id=1, source_target_pairs={{0,4},{4,0},{8,12},{12,8},{1,5},{5,1},{9,13},{13,9},{2,6},{6,2},{1... | collective-permute-start | bytes 786440 | tf_op jit(solution)/shard_map/ppermute | solution.py:222
  11.3 1.0 %copy-start.1 = (bf16[1,64,2048]{2,1,0:T(8,128)(2,1)S(1)}, bf16[1,64,2048]{2,1,0:T(8,128)(2,1)}, u32[]{:S(2)}) copy-start(bf16[1,64,2048]{2,1,0:T(8,128)(2,1)} %param.12) | copy-start | bytes 786436
  12.3 1.5 %copy-start.2 = (bf16[512,1792]{1,0:T(8,128)(2,1)S(1)}, bf16[512,1792]{1,0:T(8,128)(2,1)}, u32[]{:S(2)}) copy-start(bf16[512,1792]{1,0:T(8,128)(2,1)} %constant.168.clone.back_ref) | copy-start | bytes 5505028
  13.8 1.5 %copy-start.3 = (bf16[512,1792]{1,0:T(8,128)(2,1)S(1)}, bf16[512,1792]{1,0:T(8,128)(2,1)}, u32[]{:S(2)}) copy-start(bf16[512,1792]{1,0:T(8,128)(2,1)} %constant.167.clone.low_ref) | copy-start | bytes 5505028
  15.3 1.5 %copy-start.4 = (bf16[512,1792]{1,0:T(8,128)(2,1)S(1)}, bf16[512,1792]{1,0:T(8,128)(2,1)}, u32[]{:S(2)}) copy-start(bf16[512,1792]{1,0:T(8,128)(2,1)} %constant.166.clone.high_ref) | copy-start | bytes 5505028
  21.2 7.8 %collective-permute-start.3 = (bf16[4,64,256]{2,1,0:T(8,128)(2,1)S(1)}, bf16[4,64,256]{2,1,0:T(8,128)(2,1)S(1)}, u32[]{:S(2)}, u32[]{:S(2)}) collective-permute-start(bf16[4,64,256]{2,1,0:T(8,128)(2,1)S(1)} %get-tuple-element.10), channel_id=1, source_target_pairs={{0,1},{1,0},{2,3},{3,2},{4,5},{5,4},{6,7},{7,6},{8,9},{9,8},{10,11... | collective-permute-start | bytes 393224 | tf_op jit(solution)/shard_map/ppermute | solution.py:222
  22.9 12.9 %collective-permute-start.4 = (bf16[4,64,256]{2,1,0:T(8,128)(2,1)S(1)}, bf16[4,64,256]{2,1,0:T(8,128)(2,1)S(1)}, u32[]{:S(2)}, u32[]{:S(2)}) collective-permute-start(bf16[4,64,256]{2,1,0:T(8,128)(2,1)S(1)} %get-tuple-element.11), channel_id=1, source_target_pairs={{0,2},{1,3},{2,0},{3,1},{4,6},{5,7},{6,4},{7,5},{8,10},{9,11},{10,... | collective-permute-start | bytes 393224 | tf_op jit(solution)/shard_map/ppermute | solution.py:222
  25.5 10.3 %collective-permute-start.5 = (bf16[4,64,256]{2,1,0:T(8,128)(2,1)S(1)}, bf16[4,64,256]{2,1,0:T(8,128)(2,1)S(1)}, u32[]{:S(2)}, u32[]{:S(2)}) collective-permute-start(bf16[4,64,256]{2,1,0:T(8,128)(2,1)S(1)} %get-tuple-element.12), channel_id=1, source_target_pairs={{0,3},{1,2},{2,1},{3,0},{4,7},{5,6},{6,5},{7,4},{8,11},{9,10},{10,... | collective-permute-start | bytes 393224 | tf_op jit(solution)/shard_map/ppermute | solution.py:222
where the time goes:
time: 39.2 us; the launch traced here: 38.8 us
  local copies, waits for them, and re-layouts  9.63 us (25%)
  waiting for transfers between devices  9.02 us (23%)
  starting transfers between devices  7.78 us (20%)
  Pallas kernels  7.45 us (19%)
  other arithmetic  3.47 us (9%)
  matrix products  1.36 us (3%)
    ppermute x6, waiting for transfers between devices, exchange(): return lax.ppermute(array, axis, [(i, i ^ distance) for i in range(count)])  9.02 us
    ppermute x6, starting transfers between devices, exchange(): return lax.ppermute(array, axis, [(i, i ^ distance) for i in range(count)])  7.78 us
    unnamed x11, local copies, waits for them, and re-layouts  5.46 us
    pallas_call x1, Pallas kernels, filtered_patches(): pl.pallas_call(functools.partial(filter_kernel, slots, row_blocks), out_s...  4.44 us
    pallas_call x1, Pallas kernels, interpolated(): pl.pallas_call(functools.partial(interpolate_kernel, slots, factor), grid...  3.01 us
    dot_general x1, matrix products, per_device(): lax.dot_general((row_sign[:, None, :] * own_waves[None]).reshape(tilt_dev...  1.36 us
    convert_element_type x1, other arithmetic, per_device(): weights = jnp.maximum(0.0, 1.0 - jnp.abs(tap - centre)).astype(jnp.bfloat16)  1.34 us
    gather x1, local copies, waits for them, and re-layouts, per_device(): angles = jnp.take(tilt_angle, owners)  1.3 us
  transfers between devices with their start and end apart: 6, of which 3 were waited for; matrix products, arithmetic and copies ran while one was open for 23% of the time, Pallas kernels for 0%

commit v1 on v0

--- a/solution.py
+++ b/solution.py
@@ -79,18 +79,17 @@
 
 
 def filter_kernel(slots, row_blocks, meta, a_ref, gain_ref, high_ref, low_ref, back_ref, *refs):
-    block_refs = refs[:row_blocks]
-    out_refs = refs[row_blocks : row_blocks + slots]
-    zhi, zlo, spec, turned = refs[row_blocks + slots :]
-    rows, columns = block_refs[0].shape
+    block_refs = refs[0]
+    out_refs = refs[1 : 1 + slots]
+    zhi, zlo, spec, turned = refs[1 + slots :]
+    _, rows, columns = block_refs.shape
     size = columns // RADIX
     full_rows = rows * row_blocks
-    row_index = meta[0]
     root = math.sqrt(0.5)
 
     for distance in range(row_blocks):
-        source = block_refs[distance]
-        first_row = (row_index ^ distance) * rows
+        source = block_refs.at[distance]
+        first_row = distance * rows
 
         def butterfly(step, carry):
             here = pl.ds(pl.multiple_of(step * 16, 16), 16)
@@ -160,15 +159,15 @@
 
 
 def filtered_patches(meta, row_filters, gains, tables, blocks):
-    slots, row_blocks = gains.shape[0], len(blocks)
-    rows, columns = blocks[0].shape
+    slots = gains.shape[0]
+    row_blocks, rows, columns = blocks.shape
     full_rows = rows * row_blocks
     vmem = pl.BlockSpec(memory_space=pltpu.VMEM)
     flops = 2 * columns * (3 * full_rows * columns // 4 + slots * rows * (full_rows + columns // 4))
     return pl.pallas_call(
         functools.partial(filter_kernel, slots, row_blocks),
         out_shape=[jax.ShapeDtypeStruct((XBLK, rows, BAND), jnp.bfloat16)] * slots,
-        in_specs=[pl.BlockSpec(memory_space=pltpu.SMEM)] + [vmem] * (5 + row_blocks),
+        in_specs=[pl.BlockSpec(memory_space=pltpu.SMEM)] + [vmem] * 6,
         out_specs=[vmem] * slots,
         scratch_shapes=[
             pltpu.VMEM((full_rows, columns), jnp.bfloat16),
@@ -179,7 +178,7 @@
         compiler_params=pltpu.CompilerParams(vmem_limit_bytes=40 * 2**20),
         cost_estimate=pl.CostEstimate(flops=flops, bytes_accessed=10 * 2**20, transcendentals=0),
         name="filter",
-    )(meta, row_filters, gains, *tables, *blocks)
+    )(meta, row_filters, gains, *tables, blocks)
 
 
 def interpolate_kernel(slots, factor, weights_ref, *refs):
@@ -229,11 +228,7 @@
     row_index, tilt_index = lax.axis_index("row"), lax.axis_index("tilt")
     image = projections[0]
 
-    blocks = {0: image}
-    bit = row_devices // 2
-    while bit:
-        blocks.update({d ^ bit: exchange(block, "row", bit) for d, block in blocks.items()})
-        bit //= 2
+    blocks = lax.all_gather(image, "row")
 
     slices_owned = SLICES // tilt_devices
     distances = jnp.arange(tilt_devices, dtype=jnp.int32)
@@ -262,8 +257,10 @@
     gains = (1 - 2 * (column_cycles % 2)).astype(jnp.float32) * ramp
 
     tables = [jnp.asarray(t) for t in column_tables(columns)]
-    sent = filtered_patches(meta, row_filters, gains, tables, [blocks[d] for d in range(row_devices)])
-    patches = [sent[0]] + [exchange(sent[d], "tilt", d) for d in range(1, tilt_devices)]
+    sent = filtered_patches(meta, row_filters, gains, tables, blocks)
+    patches = [sent[0]] + [None] * (tilt_devices - 1)
+    for d in sorted(range(1, tilt_devices), key=lambda d: -(d & -d)):
+        patches[d] = exchange(sent[d], "tilt", d)
 
     angles = jnp.take(tilt_angle, owners)
     local_first = tilt_index * slices_owned % SLAB

time: 39.2 us -> 63.3 us (1.61)
  waiting for transfers between devices: 9.02 us -> 22.7 us
  between operations: 0.11 us -> 13.5 us
  starting transfers between devices: 7.78 us -> 4.45 us
    all_gather x0 -> x1, waiting for transfers between devices: none -> 13.3 us  [per_device(): blocks = lax.all_gather(image, 'row')]
    ppermute x6 -> x3, starting transfers between devices: 7.78 us -> 4.45 us  [exchange(): return lax.ppermute(array, axis, [(i, i ^ distance) for i in range(count)])]
    unnamed x0 -> x1, waiting for transfers between devices: none -> 0.71 us
    ppermute x6 -> x3, waiting for transfers between devices: 9.02 us -> 8.64 us  [exchange(): return lax.ppermute(array, axis, [(i, i ^ distance) for i in range(count)])]
  transfers between devices with their start and end apart: 6 -> 4, of which waited for: 3 -> 3; matrix products, arithmetic and copies ran while one was open for 23% -> 14% of each run, Pallas kernels for 0% -> 0%
where the time goes in v1:
time: 63.3 us; the launch traced here: 62.8 us
  waiting for transfers between devices  22.7 us (36%)
  between operations  13.5 us (21%)
  local copies, waits for them, and re-layouts  9.9 us (16%)
  Pallas kernels  7.45 us (12%)
  starting transfers between devices  4.45 us (7%)
  other arithmetic  3.49 us (6%)
  matrix products  1.36 us (2%)
    all_gather x1, waiting for transfers between devices, per_device(): blocks = lax.all_gather(image, 'row')  13.3 us
    ppermute x3, waiting for transfers between devices, exchange(): return lax.ppermute(array, axis, [(i, i ^ distance) for i in range(count)])  8.64 us
    unnamed x11, local copies, waits for them, and re-layouts  5.74 us
    ppermute x3, starting transfers between devices, exchange(): return lax.ppermute(array, axis, [(i, i ^ distance) for i in range(count)])  4.45 us
    pallas_call x1, Pallas kernels, filtered_patches(): pl.pallas_call(functools.partial(filter_kernel, slots, row_blocks), out_s...  4.44 us
    pallas_call x1, Pallas kernels, interpolated(): pl.pallas_call(functools.partial(interpolate_kernel, slots, factor), grid...  3 us
    dot_general x1, matrix products, per_device(): lax.dot_general((row_sign[:, None, :] * own_waves[None]).reshape(tilt_dev...  1.36 us
    convert_element_type x1, other arithmetic, per_device(): weights = jnp.maximum(0.0, 1.0 - jnp.abs(tap - centre)).astype(jnp.bfloat16)  1.34 us
  transfers between devices with their start and end apart: 4, of which 3 were waited for; matrix products, arithmetic and copies ran while one was open for 14% of the time, Pallas kernels for 0%

profile of v1, /device:TPU:0, one launch (start us, length us, event | category | flops | bytes accessed | tf_op | source)
XLA Modules:
  0.0 62.8 jit_solution(3250502343557315693)
XLA Ops:
  6.5 0.7 %all-gather.2.cloned.1.call-update = ((bf16[1,64,2048]{2,1,0:T(8,128)(2,1)}), bf16[4,64,2048]{2,1,0:T(8,128)(2,1)}) async-update(((), (), s32[]{:S(2)}) %all-gather.2.cloned.1.call-start, bf16[1,64,2048]{2,1,0:T(8,128)(2,1)} %param.12) | async-update | bytes 1572888
  7.3 0.7 %fusion.16 = s32[4]{0:T(128)S(1)} fusion(s32[4,4]{1,0:T(4,128)} %param.15, s32[]{:T(128)S(6)} %select_n.140), kind=kLoop, calls=%fused_computation.66 | loop fusion | bytes 36 | tf_op jit(solution)/shard_map/jit(dynamic_index_in_dim)/squeeze | solution.py:237
  8.0 1.3 %gather_fusion = f32[4]{0:T(128)S(1)} fusion(f32[4]{0:T(128)} %param.13, s32[1024]{0:T(1024)S(1)} %pad_clamp_fusion.1), kind=kCustom, calls=%fused_computation | custom fusion | bytes 48 | tf_op jit(solution)/shard_map/jit(_take)/gather | solution.py:265
  9.5 0.6 %gather_fusion.2 = s32[4]{0:T(128)S(1)} fusion(s32[4]{0:T(128)S(1)} %fusion.16, s32[1024]{0:T(1024)S(1)} %pad_clamp_fusion), kind=kCustom, calls=%fused_computation.2 | custom fusion | bytes 48 | tf_op jit(solution)/shard_map/jit(_take)/gather | solution.py:237
  10.2 0.6 gather_fusion.1
  10.8 0.1 select_n.144
  11.0 0.1 pad_add_fusion.meta
  11.1 0.8 %constant_dynamic-slice_fusion = f32[64,256]{1,0:T(8,128)S(1)} fusion(f32[256,256]{1,0:T(8,128)} %constant.163.clone, s32[]{:T(128)S(6)} %select_n.148), kind=kLoop, calls=%fused_computation.64 | loop fusion | bytes 131076 | tf_op jit(solution)/shard_map/dynamic_slice | solution.py:246
  12.0 0.8 %fusion.13 = f32[4,256]{1,0:T(4,128)S(1)} fusion(f32[256]{0:T(256)} %constant.162.clone, s32[4]{0:T(128)S(1)} %broadcast_select_fusion.1, s32[256]{0:T(256)} %constant.170), kind=kLoop, calls=%fused_computation.41 | loop fusion | flops 31744 | bytes 6160 | tf_op jit(solution)/shard_map/mul | solution.py:244
  12.8 1.4 %convolution_convert_fusion.a_ref = bf16[256,256]{1,0:T(8,128)(2,1)S(1)} fusion(f32[256,256]{1,0:T(8,128)S(1)} %bitcast.17, f32[256,256]{1,0:T(8,128)} %constant.163.clone), kind=kOutput, calls=%fused_computation.4 | convolution fusion | flops 201392128 | bytes 655360 | tf_op jit(solution)/shard_map/dot_general | solution.py:247
  14.2 0.9 %fusion.5.gain_ref = f32[4,2048]{1,0:T(4,128)S(1)} fusion(f32[2048]{0:T(1024)} %constant.164.clone, s32[4]{0:T(128)S(1)} %broadcast_select_fusion.1, s32[2048]{0:T(1024)} %constant.171), kind=kLoop, calls=%fused_computation.21 | loop fusion | flops 253952 | bytes 49168 | tf_op jit(solution)/shard_map/mul | solution.py:257
  15.0 13.3 %all-gather.2.cloned.1.call-done.refs_0_ = bf16[4,64,2048]{2,1,0:T(8,128)(2,1)} async-done(((bf16[1,64,2048]{2,1,0:T(8,128)(2,1)}), bf16[4,64,2048]{2,1,0:T(8,128)(2,1)}) %all-gather.2.cloned.1.call-update) | async-done | bytes 1048592 | tf_op jit(solution)/shard_map/all_gather | solution.py:231
  28.4 1.2 %copy-done.1 = bf16[4,64,2048]{2,1,0:T(8,128)(2,1)S(1)} copy-done((bf16[4,64,2048]{2,1,0:T(8,128)(2,1)S(1)}, bf16[4,64,2048]{2,1,0:T(8,128)(2,1)}, u32[]{:S(2)}) %copy-start.1) | copy-done | bytes 1048600
  29.6 1.5 %copy-done.2 = bf16[512,1792]{1,0:T(8,128)(2,1)S(1)} copy-done((bf16[512,1792]{1,0:T(8,128)(2,1)S(1)}, bf16[512,1792]{1,0:T(8,128)(2,1)}, u32[]{:S(2)}) %copy-start.2) | copy-done | bytes 1835032
  31.1 1.5 %copy-done.3 = bf16[512,1792]{1,0:T(8,128)(2,1)S(1)} copy-done((bf16[512,1792]{1,0:T(8,128)(2,1)S(1)}, bf16[512,1792]{1,0:T(8,128)(2,1)}, u32[]{:S(2)}) %copy-start.3) | copy-done | bytes 1835032
  32.6 1.5 %copy-done.4 = bf16[512,1792]{1,0:T(8,128)(2,1)S(1)} copy-done((bf16[512,1792]{1,0:T(8,128)(2,1)S(1)}, bf16[512,1792]{1,0:T(8,128)(2,1)}, u32[]{:S(2)}) %copy-start.4) | copy-done | bytes 1835032
  34.1 4.4 %filter.1 = (bf16[4,64,256]{2,1,0:T(8,128)(2,1)S(1)}, bf16[4,64,256]{2,1,0:T(8,128)(2,1)S(1)}, bf16[4,64,256]{2,1,0:T(8,128)(2,1)S(1)}, bf16[4,64,256]{2,1,0:T(8,128)(2,1)S(1)}) custom-call(s32[17]{0:T(128)S(1)} %pad_add_fusion.meta, bf16[256,256]{1,0:T(8,128)(2,1)S(1)} %convolution_convert_fusion.a_ref, f32[4,2048]{1,0:T(4,128)S(1)} %fusion.5.gain_ref, ...), custom_call_target="tpu_custom_call" | custom-call | flops 2415919104 | bytes 10485760 | tf_op jit(solution)/shard_map/filter/pallas_call | solution.py:167
  38.6 1.6 %collective-permute-start = (bf16[4,64,256]{2,1,0:T(8,128)(2,1)S(1)}, bf16[4,64,256]{2,1,0:T(8,128)(2,1)S(1)}, u32[]{:S(2)}, u32[]{:S(2)}) collective-permute-start(bf16[4,64,256]{2,1,0:T(8,128)(2,1)S(1)} %get-tuple-element.10), channel_id=1, source_target_pairs={{0,1},{1,0},{2,3},{3,2},{4,5},{5,4},{6,7},{7,6},{8,9},{9,8},{10,11... | collective-permute-start | bytes 393224 | tf_op jit(solution)/shard_map/ppermute | solution.py:221
  40.1 2.4 %collective-permute-start.1 = (bf16[4,64,256]{2,1,0:T(8,128)(2,1)S(1)}, bf16[4,64,256]{2,1,0:T(8,128)(2,1)S(1)}, u32[]{:S(2)}, u32[]{:S(2)}) collective-permute-start(bf16[4,64,256]{2,1,0:T(8,128)(2,1)S(1)} %get-tuple-element.11), channel_id=1, source_target_pairs={{0,2},{1,3},{2,0},{3,1},{4,6},{5,7},{6,4},{7,5},{8,10},{9,11},{10,... | collective-permute-start | bytes 393224 | tf_op jit(solution)/shard_map/ppermute | solution.py:221
  42.5 0.5 collective-permute-start.2
  43.0 1.3 %maximum_convert_fusion.weights_ref = bf16[4,256,2048]{2,1,0:T(8,128)(2,1)S(1)} fusion(f32[4,2048]{1,0:T(4,128)S(1)} %bitcast.18), kind=kLoop, calls=%fused_computation.3 | loop fusion | flops 10485760 | bytes 4227072 | tf_op jit(solution)/shard_map/convert_element_type | solution.py:275
  44.4 2.0 %collective-permute-done.refs_1_ = bf16[4,64,256]{2,1,0:T(8,128)(2,1)S(1)} collective-permute-done((bf16[4,64,256]{2,1,0:T(8,128)(2,1)S(1)}, bf16[4,64,256]{2,1,0:T(8,128)(2,1)S(1)}, u32[]{:S(2)}, u32[]{:S(2)}) %collective-permute-start) | collective-permute-done | bytes 131104 | tf_op jit(solution)/shard_map/ppermute | solution.py:221
  46.3 6.7 %collective-permute-done.1.refs_2_ = bf16[4,64,256]{2,1,0:T(8,128)(2,1)S(1)} collective-permute-done((bf16[4,64,256]{2,1,0:T(8,128)(2,1)S(1)}, bf16[4,64,256]{2,1,0:T(8,128)(2,1)S(1)}, u32[]{:S(2)}, u32[]{:S(2)}) %collective-permute-start.1) | collective-permute-done | bytes 131104 | tf_op jit(solution)/shard_map/ppermute | solution.py:221
  53.0 3.0 %interpolate.1 = bf16[16,64,512]{2,1,0:T(8,128)(2,1)} custom-call(bf16[4,256,2048]{2,1,0:T(8,128)(2,1)S(1)} %maximum_convert_fusion.weights_ref, bf16[4,64,256]{2,1,0:T(8,128)(2,1)S(1)} %get-tuple-element.9.refs_0_, bf16[4,64,256]{2,1,0:T(8,128)(2,1)S(1)} %collective-permute-done.refs_1_, bf16[4,64,256]{2,1,0:T(8,128)(2,1)S(1)} %collective-permute-done.1.refs_2_, ...), custom_call_target="tpu_custom_call" | custom-call | flops 1073741824 | bytes 6291456 | tf_op jit(solution)/shard_map/interpolate/pallas_call | solution.py:204
  (23 shorter events, 0.5 us)
Async XLA Ops:
  6.5 1.5 %copy-start = (s32[4,4,4]{2,1,0:T(4,128)S(1)}, s32[4,4,4]{2,1,0:T(4,128)}, u32[]{:S(2)}) copy-start(s32[4,4,4]{2,1,0:T(4,128)} %param.14) | copy-start | bytes 772
  6.5 21.8 %all-gather.2.cloned.1.call-start = ((), (), s32[]{:S(2)}) async-start(), calls=%async_computation | async-start | bytes 1310720 | tf_op jit(solution)/shard_map/all_gather | solution.py:231
  28.4 1.2 %copy-start.1 = (bf16[4,64,2048]{2,1,0:T(8,128)(2,1)S(1)}, bf16[4,64,2048]{2,1,0:T(8,128)(2,1)}, u32[]{:S(2)}) copy-start(bf16[4,64,2048]{2,1,0:T(8,128)(2,1)} %all-gather.2.cloned.1.call-done.refs_0_) | copy-start | bytes 3145732
  29.6 1.5 %copy-start.2 = (bf16[512,1792]{1,0:T(8,128)(2,1)S(1)}, bf16[512,1792]{1,0:T(8,128)(2,1)}, u32[]{:S(2)}) copy-start(bf16[512,1792]{1,0:T(8,128)(2,1)} %constant.168.clone.back_ref) | copy-start | bytes 5505028
  31.1 1.5 %copy-start.3 = (bf16[512,1792]{1,0:T(8,128)(2,1)S(1)}, bf16[512,1792]{1,0:T(8,128)(2,1)}, u32[]{:S(2)}) copy-start(bf16[512,1792]{1,0:T(8,128)(2,1)} %constant.167.clone.low_ref) | copy-start | bytes 5505028
  32.6 1.5 %copy-start.4 = (bf16[512,1792]{1,0:T(8,128)(2,1)S(1)}, bf16[512,1792]{1,0:T(8,128)(2,1)}, u32[]{:S(2)}) copy-start(bf16[512,1792]{1,0:T(8,128)(2,1)} %constant.166.clone.high_ref) | copy-start | bytes 5505028
  38.6 7.8 %collective-permute-start = (bf16[4,64,256]{2,1,0:T(8,128)(2,1)S(1)}, bf16[4,64,256]{2,1,0:T(8,128)(2,1)S(1)}, u32[]{:S(2)}, u32[]{:S(2)}) collective-permute-start(bf16[4,64,256]{2,1,0:T(8,128)(2,1)S(1)} %get-tuple-element.10), channel_id=1, source_target_pairs={{0,1},{1,0},{2,3},{3,2},{4,5},{5,4},{6,7},{7,6},{8,9},{9,8},{10,11... | collective-permute-start | bytes 393224 | tf_op jit(solution)/shard_map/ppermute | solution.py:221
  40.1 12.9 %collective-permute-start.1 = (bf16[4,64,256]{2,1,0:T(8,128)(2,1)S(1)}, bf16[4,64,256]{2,1,0:T(8,128)(2,1)S(1)}, u32[]{:S(2)}, u32[]{:S(2)}) collective-permute-start(bf16[4,64,256]{2,1,0:T(8,128)(2,1)S(1)} %get-tuple-element.11), channel_id=1, source_target_pairs={{0,2},{1,3},{2,0},{3,1},{4,6},{5,7},{6,4},{7,5},{8,10},{9,11},{10,... | collective-permute-start | bytes 393224 | tf_op jit(solution)/shard_map/ppermute | solution.py:221
  42.5 10.5 %collective-permute-start.2 = (bf16[4,64,256]{2,1,0:T(8,128)(2,1)S(1)}, bf16[4,64,256]{2,1,0:T(8,128)(2,1)S(1)}, u32[]{:S(2)}, u32[]{:S(2)}) collective-permute-start(bf16[4,64,256]{2,1,0:T(8,128)(2,1)S(1)} %get-tuple-element.12), channel_id=1, source_target_pairs={{0,3},{1,2},{2,1},{3,0},{4,7},{5,6},{6,5},{7,4},{8,11},{9,10},{10,... | collective-permute-start | bytes 393224 | tf_op jit(solution)/shard_map/ppermute | solution.py:221
Sparse Core Ops, SparseCore 0:
  8.9 19.4 all-gather.1

commit v2 on v1

v2 whole, which is shorter than its diff:
```python
import functools
import math

import jax
import jax.numpy as jnp
import numpy as np
from jax import lax
from jax.experimental import pallas as pl
from jax.experimental.pallas import tpu as pltpu
from jax.sharding import PartitionSpec as P

SLAB = 16
XBW = 128
BAND = 256
XBLK = 4
SLICES = 64
RADIX = 8
WINDOW = BAND + 128
ROOT = math.sqrt(0.5)


def column_tables(columns):
    size = columns // RADIX
    half = size // 2
    u = np.arange(size)[:, None]

    def angles(freq):
        return 2.0 * np.pi * ((u * freq[None, :]) % columns) / columns

    k0, s0 = RADIX * np.arange(half + 1), RADIX * np.arange(1, half)
    k4 = RADIX * np.arange(half) + 4
    m0 = np.concatenate([np.cos(angles(k0)), -np.sin(angles(s0))], 1)
    m4 = np.concatenate([np.cos(angles(k4)), -np.sin(angles(k4))], 1)
    full = angles(RADIX * np.arange(size))
    waves = np.concatenate([np.cos(full), np.sin(full)], 1)
    ends = np.concatenate([m0, m4], 1)

    def split(table):
        high = table.astype(jnp.bfloat16)
        return high, (table - high.astype(np.float64)).astype(jnp.bfloat16)

    matrices = np.stack([*split(ends), *split(waves), np.concatenate([m0.T, m4.T], 1).astype(jnp.bfloat16)])
    freq = [np.concatenate([k0, s0]), np.concatenate([k4, k4])]
    turns = []
    for j in (1, 2, 3):
        freq += [RADIX * np.arange(size) + j] * 2
        angle = 2.0 * np.pi * np.arange(size) * j / columns
        turns += [np.cos(angle), np.sin(angle)]
    freq = np.stack(freq)
    count = np.where((freq == 0) | (freq == columns // 2), 1.0, 2.0)
    fold = np.minimum(freq, columns - freq)
    ramp = count * (fold + 0.5) / (0.5 * columns) / columns
    lines = np.concatenate([ramp, np.stack(turns + [np.zeros(size)] * 2)]).astype(np.float32)
    return matrices, lines, (fold * fold).astype(np.int32)


def row_tables(full_rows):
    half = full_rows // 2
    y = np.arange(full_rows)[:, None]
    freq = np.concatenate([np.arange(half + 1), np.arange(1, half)])
    angle = 2.0 * np.pi * (y * freq[None, :] % full_rows) / full_rows
    waves = np.where(np.arange(full_rows)[None, :] <= half, np.cos(angle), np.sin(angle))
    count = np.where((freq == 0) | (freq == half), 1.0, 2.0) / full_rows
    return waves.astype(np.float32), (freq * freq).astype(np.int32)[None], count.astype(np.float32)[None]


def flip_sign(squares, defocus, length):
    cycles = lax.div(squares * defocus, jnp.int32(length * length))
    return (1 - 2 * (cycles & 1)).astype(jnp.float32)


def column_kernel(slots, slices_owned, defocus, starts, image_ref, matrix_ref, lines_ref, squares_ref, *refs):
    out_refs = refs[:slots]
    image, matrix, zhi, zlo, ends, waves, turned, image_sem, matrix_sem = refs[slots:]
    rows, columns = image.shape
    size = columns // RADIX
    copies = [pltpu.make_async_copy(image_ref, image, image_sem)]
    copies += [pltpu.make_async_copy(matrix_ref.at[i], matrix.at[i], matrix_sem.at[i]) for i in range(5)]
    for copy in copies:
        copy.start()
    tilt = lax.axis_index("tilt")
    turns = [lines_ref[8 + i : 9 + i, :] for i in range(6)]
    copies[0].wait()

    def butterfly(step, carry):
        here = pl.ds(pl.multiple_of(step * 16, 16), 16)
        x = [image[here, m * size : (m + 1) * size].astype(jnp.float32) for m in range(8)]
        p0, p1, p2, p3 = (x[m] + x[m + 4] for m in range(4))
        q0, q1, q2, q3 = (x[m] - x[m + 4] for m in range(4))
        e, f = p0 + p2, p1 + p3
        g, h = ROOT * (q1 - q3), ROOT * (q1 + q3)
        z = [e + f, e - f]
        for j, (real, imag) in enumerate([(q0 + g, -q2 - h), (p0 - p2, p3 - p1), (q0 - g, q2 - h)]):
            c, s = turns[2 * j], turns[2 * j + 1]
            z += [real * c + imag * s, imag * c - real * s]
        for i in range(8):
            top = z[i].astype(jnp.bfloat16)
            zhi[i, here, :] = top
            zlo[i, here, :] = (z[i] - top.astype(jnp.float32)).astype(jnp.bfloat16)
        return carry

    lax.fori_loop(0, rows // 16, butterfly, 0)
    for copy in copies[1:5]:
        copy.wait()

    def product(first, count, table, here):
        top = zhi[first : first + count].reshape(count * rows, size)
        rest = zlo[first : first + count].reshape(count * rows, size)
        total = jnp.dot(top, matrix[table, :, here], preferred_element_type=jnp.float32)
        total += jnp.dot(top, matrix[table + 1, :, here], preferred_element_type=jnp.float32)
        return total + jnp.dot(rest, matrix[table, :, here], preferred_element_type=jnp.float32)

    spectrum = [product(0, 1, 0, slice(0, size)), product(1, 1, 0, slice(size, 2 * size))]
    mixed = product(2, 6, 2, slice(None))
    for j in range(3):
        real, imag = mixed[2 * j * rows : (2 * j + 1) * rows], mixed[(2 * j + 1) * rows : (2 * j + 2) * rows]
        spectrum += [real[:, :size] + imag[:, size:], imag[:, :size] - real[:, size:]]

    slabs = [(tilt ^ slot) * slices_owned // SLAB for slot in range(slots)]
    gains = [
        flip_sign(squares_ref[...], defocus[tilt, slabs[slot]], columns) * lines_ref[:8, :] for slot in range(slots)
    ]
    filtered = [
        jnp.concatenate(
            [(spectrum[i] * gains[slot][i : i + 1, :]).astype(jnp.bfloat16) for slot in range(slots)], 0
        )
        for i in range(8)
    ]
    copies[5].wait()
    for i in range(2):
        ends[i] = jnp.dot(filtered[i], matrix[4, :, i * size : (i + 1) * size], preferred_element_type=jnp.float32)
    for i in range(6):
        waves[i] = jnp.dot(filtered[2 + i], matrix[2], preferred_element_type=jnp.float32)

    def inverse_butterfly(step, carry):
        here = pl.ds(pl.multiple_of(step * 8, 8), 8)
        r, s = [], []
        for j in range(3):
            c, d = turns[2 * j], turns[2 * j + 1]
            real = waves[2 * j, here, :size] - waves[2 * j + 1, here, size:]
            imag = waves[2 * j, here, size:] + waves[2 * j + 1, here, :size]
            r.append(real * c - imag * d)
            s.append(real * d + imag * c)
        e, f = ends[0, here, :] + ends[1, here, :], ends[0, here, :] - ends[1, here, :]
        a, b, c, d = r[0] + r[2], r[0] - r[2], s[0] + s[2], s[0] - s[2]
        even0, even2, odd1, odd3 = e + r[1], e - r[1], f - s[1], f + s[1]
        g, h = ROOT * (b - c), ROOT * (b + c)
        out = [even0 + a, odd1 + g, even2 - d, odd3 - h, even0 - a, odd1 - g, even2 + d, odd3 + h]
        for m in range(8):
            turned[here, m * size : (m + 1) * size] = out[m]
        return carry

    lax.fori_loop(0, slots * rows // 8, inverse_butterfly, 0)

    for slot in range(slots):
        for block in range(XBLK):
            start = starts[tilt, slabs[slot], block]
            base = pl.multiple_of(jnp.minimum((start // 128) * 128, columns - WINDOW), 128)
            window = turned[slot * rows : (slot + 1) * rows, pl.ds(base, WINDOW)]
            shift = base - start
            shift = jnp.where(shift < 0, shift + WINDOW, shift)
            out_refs[slot][:, block * BAND : (block + 1) * BAND] = pltpu.roll(window, shift, 1)[:, :BAND].astype(
                jnp.bfloat16
            )


def column_filtered(slots, slices_owned, defocus, starts, image):
    rows, columns = image.shape
    size = columns // RADIX
    matrices, lines, squares = column_tables(columns)
    smem, vmem = pl.BlockSpec(memory_space=pltpu.SMEM), pl.BlockSpec(memory_space=pltpu.VMEM)
    away = pl.BlockSpec(memory_space=pl.ANY)
    return pl.pallas_call(
        functools.partial(column_kernel, slots, slices_owned),
        out_shape=[jax.ShapeDtypeStruct((rows, XBLK * BAND), jnp.bfloat16)] * slots,
        in_specs=[smem, smem, away, away, vmem, vmem],
        out_specs=[vmem] * slots,
        scratch_shapes=[
            pltpu.VMEM((rows, columns), jnp.bfloat16),
            pltpu.VMEM(matrices.shape, jnp.bfloat16),
            pltpu.VMEM((8, rows, size), jnp.bfloat16),
            pltpu.VMEM((8, rows, size), jnp.bfloat16),
            pltpu.VMEM((2, slots * rows, size), jnp.float32),
            pltpu.VMEM((6, slots * rows, 2 * size), jnp.float32),
            pltpu.VMEM((slots * rows, columns), jnp.float32),
            pltpu.SemaphoreType.DMA,
            pltpu.SemaphoreType.DMA((5,)),
        ],
        compiler_params=pltpu.CompilerParams(vmem_limit_bytes=40 * 2**20),
        cost_estimate=pl.CostEstimate(flops=2 * rows * columns * 2048 * 2, bytes_accessed=4 * 2**20, transcendentals=0),
        name="column_filter",
    )(defocus, starts, image, jnp.asarray(matrices), jnp.asarray(lines), jnp.asarray(squares))


def prepare_kernel(slots, slices_owned, defocus, cosines, sines, waves, squares, count, rows_ref, weights_ref, mine, order):
    tilt, row = lax.axis_index("tilt"), lax.axis_index("row")
    slab, local_first = tilt * slices_owned // SLAB, tilt * slices_owned % SLAB
    full_rows = waves.shape[0]
    rows = rows_ref.shape[0] // slots
    own = waves[pl.ds(pl.multiple_of(row * rows, rows), rows), :]
    for slot in range(slots):
        sign = flip_sign(squares[...], defocus[tilt ^ slot, slab], full_rows)
        mine[slot * rows : (slot + 1) * rows, :] = own * (sign * count[...])
    for block in range(full_rows // rows):
        order[block * rows : (block + 1) * rows, :] = waves[pl.ds(pl.multiple_of((row ^ block) * rows, rows), rows), :]
    rows_ref[...] = lax.dot_general(
        mine[...],
        order[...],
        (((1,), (1,)), ((), ())),
        precision=lax.Precision.HIGHEST,
        preferred_element_type=jnp.float32,
    ).astype(jnp.bfloat16)

    column = lax.broadcasted_iota(jnp.int32, (1, XBW), 1).astype(jnp.float32)
    tap = lax.broadcasted_iota(jnp.int32, (BAND, XBW), 0).astype(jnp.float32)
    for slot in range(slots):
        cosine, sine = cosines[tilt ^ slot], sines[tilt ^ slot]

        def one_slice(c, carry):
            offset = (local_first + c).astype(jnp.float32) - 0.5 * (SLAB - 1)
            centre = 0.5 * XBW + column * cosine + offset * sine
            there = pl.ds(pl.multiple_of(c * XBW, XBW), XBW)
            weights_ref[slot, :, there] = jnp.maximum(0.0, 1.0 - jnp.abs(tap - centre)).astype(jnp.bfloat16)
            return carry

        lax.fori_loop(0, slices_owned, one_slice, 0)


def prepared(slots, slices_owned, rows, full_rows, defocus, tilt_angle):
    smem, vmem = pl.BlockSpec(memory_space=pltpu.SMEM), pl.BlockSpec(memory_space=pltpu.VMEM)
    tables = [jnp.asarray(t) for t in row_tables(full_rows)]
    return pl.pallas_call(
        functools.partial(prepare_kernel, slots, slices_owned),
        out_shape=[
            jax.ShapeDtypeStruct((slots * rows, full_rows), jnp.bfloat16),
            jax.ShapeDtypeStruct((slots, BAND, slices_owned * XBW), jnp.bfloat16),
        ],
        in_specs=[smem] * 3 + [vmem] * 3,
        out_specs=[vmem] * 2,
        scratch_shapes=[
            pltpu.VMEM((slots * rows, full_rows), jnp.float32),
            pltpu.VMEM((full_rows, full_rows), jnp.float32),
        ],
        compiler_params=pltpu.CompilerParams(vmem_limit_bytes=32 * 2**20),
        cost_estimate=pl.CostEstimate(flops=2**30, bytes_accessed=6 * 2**20, transcendentals=0),
        name="prepare",
    )(defocus, jnp.cos(tilt_angle), jnp.sin(tilt_angle), *tables)


def interpolate_kernel(slots, row_devices, factor, rows_ref, weights_ref, *refs):
    patch_refs = refs[: slots * row_devices]
    out_ref, out, sems = refs[slots * row_devices :]
    rows = patch_refs[0].shape[0]
    slices = out.shape[0]
    corrected = []
    for slot in range(slots):
        patches = jnp.concatenate([patch_refs[slot * row_devices + r][...] for r in range(row_devices)], 0)
        image = jnp.dot(rows_ref[slot * rows : (slot + 1) * rows, :], patches, preferred_element_type=jnp.float32)
        image = image.astype(jnp.bfloat16)
        corrected.append(
            jnp.concatenate([image[:, block * BAND : (block + 1) * BAND] for block in range(XBLK)], 0)
        )
    step = math.gcd(slices, 4)
    copies = []
    for group in range(slices // step):
        here = slice(group * step * XBW, (group + 1) * step * XBW)
        total = jnp.dot(corrected[0], weights_ref[0, :, here], preferred_element_type=jnp.float32)
        for slot in range(1, slots):
            total += jnp.dot(corrected[slot], weights_ref[slot, :, here], preferred_element_type=jnp.float32)
        for c in range(step):
            for block in range(XBLK):
                out[group * step + c, :, block * XBW : (block + 1) * XBW] = (
                    factor * total[block * rows : (block + 1) * rows, c * XBW : (c + 1) * XBW]
                ).astype(jnp.bfloat16)
        part = pl.ds(group * step, step)
        copies.append(pltpu.make_async_copy(out.at[part], out_ref.at[part], sems.at[group]))
        copies[-1].start()
    for copy in copies:
        copy.wait()


def interpolated(row_filters, weights, patches, factor):
    slots, _, width = weights.shape
    row_devices = len(patches[0])
    rows = patches[0][0].shape[0]
    shape = (width // XBW, rows, XBLK * XBW)
    vmem = pl.BlockSpec(memory_space=pltpu.VMEM)
    return pl.pallas_call(
        functools.partial(interpolate_kernel, slots, row_devices, factor),
        out_shape=jax.ShapeDtypeStruct(shape, jnp.bfloat16),
        in_specs=[vmem] * (2 + slots * row_devices),
        out_specs=pl.BlockSpec(memory_space=pl.ANY),
        scratch_shapes=[
            pltpu.VMEM(shape, jnp.bfloat16),
            pltpu.SemaphoreType.DMA((shape[0] // math.gcd(shape[0], 4),)),
        ],
        compiler_params=pltpu.CompilerParams(vmem_limit_bytes=32 * 2**20),
        cost_estimate=pl.CostEstimate(
            flops=2 * slots * BAND * width * XBLK * rows, bytes_accessed=6 * 2**20, transcendentals=0
        ),
        name="interpolate",
    )(row_filters, weights, *[block for slot in patches for block in slot])


def exchange(array, axis, distance):
    count = lax.axis_size(axis)
    return lax.ppermute(array, axis, [(i, i ^ distance) for i in range(count)])


def gather_rows(array):
    blocks = {0: array}
    bit = lax.axis_size("row") // 2
    while bit:
        blocks.update({d ^ bit: exchange(block, "row", bit) for d, block in blocks.items()})
        bit //= 2
    return [blocks[d] for d in sorted(blocks)]


def per_device(projections, tilt_angle, band_start, defocus):
    _, rows, _ = projections.shape
    row_devices, tilt_devices = lax.axis_size("row"), lax.axis_size("tilt")
    slices_owned = SLICES // tilt_devices
    sent = column_filtered(tilt_devices, slices_owned, defocus, band_start, projections[0])
    arrived = {0: sent[0]}
    for d in sorted(range(1, tilt_devices), reverse=True):
        arrived[d] = exchange(sent[d], "tilt", d)
    patches = [gather_rows(arrived[d]) for d in range(tilt_devices)]
    row_filters, weights = prepared(tilt_devices, slices_owned, rows, rows * row_devices, defocus, tilt_angle)
    return interpolated(row_filters, weights, patches, 1.0 / math.sqrt(tilt_devices))


def solution(mesh):
    in_specs = (
        P(("group", "tilt"), "row", None),
        P("group"),
        P("group", None, None),
        P("group", None),
    )
    out_specs = P(("group", "tilt"), "row", None)
    return jax.shard_map(
        per_device, mesh=mesh, in_specs=in_specs, out_specs=out_specs, check_vma=False
    )
```

time: 63.3 us -> 43 us (0.68)
  between operations: 13.5 us -> 0.09 us
  waiting for transfers between devices: 22.7 us -> 12.3 us
  starting transfers between devices: 4.45 us -> 12.4 us
  other arithmetic: 3.49 us -> 0 us
  Pallas kernels: 7.45 us -> 8.95 us
  matrix products: 1.36 us -> 0 us
  local copies, waits for them, and re-layouts: 9.9 us -> 8.73 us
    all_gather x1 -> x0, waiting for transfers between devices: 13.3 us -> none  [per_device(): blocks = lax.all_gather(image, 'row')]
    ppermute x3 -> x15, starting transfers between devices: 4.45 us -> 12.4 us  [exchange(): return lax.ppermute(array, axis, [(i, i ^ distance) for i in range(count)])]
    ppermute x3 -> x15, waiting for transfers between devices: 8.64 us -> 12.3 us  [exchange(): return lax.ppermute(array, axis, [(i, i ^ distance) for i in range(count)])]
    gather x3 -> x0, local copies, waits for them, and re-layouts: 2.5 us -> none  [the longest x1 1.3 us: per_device(): angles = jnp.take(tilt_angle, owners)]
    unnamed x11 -> x20, local copies, waits for them, and re-layouts: 5.74 us -> 8.04 us
    mul x4 -> x0, other arithmetic: 1.74 us -> none  [the longest x1 0.86 us: per_device(): gains = (1 - 2 * (column_cycles % 2)).astype(jnp.float32) * ramp]
    pallas_call x2 -> x3, Pallas kernels: 7.45 us -> 8.95 us  [the longest x1 3.73 us: column_filtered(): pl.pallas_call(functools.partial(column_kernel, slots, slices_owned), out...]
    dot_general x1 -> x0, matrix products: 1.36 us -> none  [per_device(): lax.dot_general((row_sign[:, None, :] * own_waves[None]).reshape(tilt_dev...]
  transfers between devices with their start and end apart: 4 -> 15, of which waited for: 3 -> 4; matrix products, arithmetic and copies ran while one was open for 14% -> 2% of each run, Pallas kernels for 0% -> 7%
where the time goes in v2:
time: 43 us; the launch traced here: 42.5 us
  starting transfers between devices  12.4 us (29%)
  waiting for transfers between devices  12.3 us (29%)
  Pallas kernels  8.95 us (21%)
  local copies, waits for them, and re-layouts  8.73 us (20%)
    ppermute x15, starting transfers between devices, exchange(): return lax.ppermute(array, axis, [(i, i ^ distance) for i in range(count)])  12.4 us
    ppermute x15, waiting for transfers between devices, exchange(): return lax.ppermute(array, axis, [(i, i ^ distance) for i in range(count)])  12.3 us
    unnamed x20, local copies, waits for them, and re-layouts  8.04 us
    pallas_call x1, Pallas kernels, column_filtered(): pl.pallas_call(functools.partial(column_kernel, slots, slices_owned), out...  3.73 us
    pallas_call x1, Pallas kernels, prepared(): pl.pallas_call(functools.partial(prepare_kernel, slots, slices_owned), ou...  2.84 us
    pallas_call x1, Pallas kernels, interpolated(): pl.pallas_call(functools.partial(interpolate_kernel, slots, row_devices,...  2.38 us
  transfers between devices with their start and end apart: 15, of which 4 were waited for; matrix products, arithmetic and copies ran while one was open for 2% of the time, Pallas kernels for 7%

profile of v2, /device:TPU:0, one launch (start us, length us, event | category | flops | bytes accessed | tf_op | source)
XLA Modules:
  0.0 42.5 jit_solution(14806077003645256879)
XLA Ops:
  0.0 0.9 %copy-done = bf16[1,64,2048]{2,1,0:T(8,128)(2,1)S(1)} copy-done((bf16[1,64,2048]{2,1,0:T(8,128)(2,1)S(1)}, bf16[1,64,2048]{2,1,0:T(8,128)(2,1)}, u32[]{:S(2)}) %copy-start) | copy-done | bytes 262168
  1.0 0.7 %copy-done.1 = s32[4,4,4]{2,1,0:T(4,128)S(1)} copy-done((s32[4,4,4]{2,1,0:T(4,128)S(1)}, s32[4,4,4]{2,1,0:T(4,128)}, u32[]{:S(2)}) %copy-start.1) | copy-done | bytes 280
  1.7 0.7 %copy-done.2 = s32[4,4]{1,0:T(4,128)S(1)} copy-done((s32[4,4]{1,0:T(4,128)S(1)}, s32[4,4]{1,0:T(4,128)}, u32[]{:S(2)}) %copy-start.2) | copy-done | bytes 88
  2.3 1.3 %copy-done.4 = bf16[5,256,512]{2,1,0:T(8,128)(2,1)S(1)} copy-done((bf16[5,256,512]{2,1,0:T(8,128)(2,1)S(1)}, bf16[5,256,512]{2,1,0:T(8,128)(2,1)}, u32[]{:S(2)}) %copy-start.4) | copy-done | bytes 1310744
  3.6 0.7 %copy-done.6 = f32[16,256]{1,0:T(8,128)S(1)} copy-done((f32[16,256]{1,0:T(8,128)S(1)}, f32[16,256]{1,0:T(8,128)}, u32[]{:S(2)}) %copy-start.6) | copy-done | bytes 16408
  4.4 0.7 %copy-done.7 = s32[8,256]{1,0:T(8,128)S(1)} copy-done((s32[8,256]{1,0:T(8,128)S(1)}, s32[8,256]{1,0:T(8,128)}, u32[]{:S(2)}) %copy-start.7) | copy-done | bytes 8216
  5.1 3.7 %column_filter.1 = (bf16[64,1024]{1,0:T(8,128)(2,1)S(1)}, bf16[64,1024]{1,0:T(8,128)(2,1)S(1)}, bf16[64,1024]{1,0:T(8,128)(2,1)S(1)}, bf16[64,1024]{1,0:T(8,128)(2,1)S(1)}) custom-call(s32[4,4]{1,0:T(4,128)S(1)} %copy-done.2, s32[4,4,4]{2,1,0:T(4,128)S(1)} %copy-done.1, bf16[64,2048]{1,0:T(8,128)(2,1)S(1)} %bitcast.1, bf16[5,256,512]{2,1,0:T(8,128)(2,1)S(1)} %copy-done.4, ...), custom_call_target="tpu_custom_call" | custom-call | flops 1073741824 | bytes 4194304 | tf_op jit(solution)/shard_map/column_filter/pallas_call | solution.py:173
  8.8 3.1 %collective-permute-start.3 = (bf16[64,1024]{1,0:T(8,128)(2,1)S(1)}, bf16[64,1024]{1,0:T(8,128)(2,1)S(1)}, u32[]{:S(2)}, u32[]{:S(2)}) collective-permute-start(bf16[64,1024]{1,0:T(8,128)(2,1)S(1)} %get-tuple-element.14), channel_id=1, source_target_pairs={{0,1},{1,0},{2,3},{3,2},{4,5},{5,4},{6,7},{7,6},{8,9},{9,8},{10,11... | collective-permute-start | bytes 393224 | tf_op jit(solution)/shard_map/ppermute | solution.py:307
  11.9 2.6 %collective-permute-start.7 = (bf16[64,1024]{1,0:T(8,128)(2,1)S(1)}, bf16[64,1024]{1,0:T(8,128)(2,1)S(1)}, u32[]{:S(2)}, u32[]{:S(2)}) collective-permute-start(bf16[64,1024]{1,0:T(8,128)(2,1)S(1)} %get-tuple-element.15), channel_id=1, source_target_pairs={{0,2},{1,3},{2,0},{3,1},{4,6},{5,7},{6,4},{7,5},{8,10},{9,11},{10,... | collective-permute-start | bytes 393224 | tf_op jit(solution)/shard_map/ppermute | solution.py:307
  14.5 1.7 %collective-permute-start.1 = (bf16[64,1024]{1,0:T(8,128)(2,1)S(1)}, bf16[64,1024]{1,0:T(8,128)(2,1)S(1)}, u32[]{:S(2)}, u32[]{:S(2)}) collective-permute-start(bf16[64,1024]{1,0:T(8,128)(2,1)S(1)} %get-tuple-element.13.refs_0_), channel_id=1, source_target_pairs={{0,8},{4,12},{8,0},{12,4},{1,9},{5,13},{9,1},{13,5},{2,10},{6,14},... | collective-permute-start | bytes 393224 | tf_op jit(solution)/shard_map/ppermute | solution.py:307
  16.2 0.7 %collective-permute-done.3.refs_4_ = bf16[64,1024]{1,0:T(8,128)(2,1)S(1)} collective-permute-done((bf16[64,1024]{1,0:T(8,128)(2,1)S(1)}, bf16[64,1024]{1,0:T(8,128)(2,1)S(1)}, u32[]{:S(2)}, u32[]{:S(2)}) %collective-permute-start.3) | collective-permute-done | bytes 131104 | tf_op jit(solution)/shard_map/ppermute | solution.py:307
  16.9 1.7 %collective-permute-start.5 = (bf16[64,1024]{1,0:T(8,128)(2,1)S(1)}, bf16[64,1024]{1,0:T(8,128)(2,1)S(1)}, u32[]{:S(2)}, u32[]{:S(2)}) collective-permute-start(bf16[64,1024]{1,0:T(8,128)(2,1)S(1)} %collective-permute-done.3.refs_4_), channel_id=1, source_target_pairs={{0,8},{4,12},{8,0},{12,4},{1,9},{5,13},{9,1},{13,5},{2,10},{6,14},... | collective-permute-start | bytes 393224 | tf_op jit(solution)/shard_map/ppermute | solution.py:307
  18.7 6.2 %collective-permute-done.7.refs_8_ = bf16[64,1024]{1,0:T(8,128)(2,1)S(1)} collective-permute-done((bf16[64,1024]{1,0:T(8,128)(2,1)S(1)}, bf16[64,1024]{1,0:T(8,128)(2,1)S(1)}, u32[]{:S(2)}, u32[]{:S(2)}) %collective-permute-start.7) | collective-permute-done | bytes 131104 | tf_op jit(solution)/shard_map/ppermute | solution.py:307
  24.8 1.5 %collective-permute-start.9 = (bf16[64,1024]{1,0:T(8,128)(2,1)S(1)}, bf16[64,1024]{1,0:T(8,128)(2,1)S(1)}, u32[]{:S(2)}, u32[]{:S(2)}) collective-permute-start(bf16[64,1024]{1,0:T(8,128)(2,1)S(1)} %collective-permute-done.7.refs_8_), channel_id=1, source_target_pairs={{0,8},{4,12},{8,0},{12,4},{1,9},{5,13},{9,1},{13,5},{2,10},{6,14},... | collective-permute-start | bytes 393224 | tf_op jit(solution)/shard_map/ppermute | solution.py:307
  26.6 0.5 %collective-permute-start.13 = (bf16[64,1024]{1,0:T(8,128)(2,1)S(1)}, bf16[64,1024]{1,0:T(8,128)(2,1)S(1)}, u32[]{:S(2)}, u32[]{:S(2)}) collective-permute-start(bf16[64,1024]{1,0:T(8,128)(2,1)S(1)} %collective-permute-done.11.refs_12_), channel_id=1, source_target_pairs={{0,8},{4,12},{8,0},{12,4},{1,9},{5,13},{9,1},{13,5},{2,10},{6,14},... | collective-permute-start | bytes 393224 | tf_op jit(solution)/shard_map/ppermute | solution.py:307
  27.6 3.5 %collective-permute-done.9.refs_10_ = bf16[64,1024]{1,0:T(8,128)(2,1)S(1)} collective-permute-done((bf16[64,1024]{1,0:T(8,128)(2,1)S(1)}, bf16[64,1024]{1,0:T(8,128)(2,1)S(1)}, u32[]{:S(2)}, u32[]{:S(2)}) %collective-permute-start.9) | collective-permute-done | bytes 131104 | tf_op jit(solution)/shard_map/ppermute | solution.py:307
  31.6 1.9 %collective-permute-done.13.refs_14_ = bf16[64,1024]{1,0:T(8,128)(2,1)S(1)} collective-permute-done((bf16[64,1024]{1,0:T(8,128)(2,1)S(1)}, bf16[64,1024]{1,0:T(8,128)(2,1)S(1)}, u32[]{:S(2)}, u32[]{:S(2)}) %collective-permute-start.13) | collective-permute-done | bytes 131104 | tf_op jit(solution)/shard_map/ppermute | solution.py:307
  33.5 0.7 %fusion = (f32[4]{0:T(128)S(1)}, f32[4]{0:T(128)S(1)}) fusion(f32[4]{0:T(128)} %param.11), kind=kLoop, calls=%fused_computation | loop fusion | bytes 48 | tf_op jit(solution)/shard_map/sin | solution.py:247
  34.3 0.7 %copy-done.3 = s32[4,4]{1,0:T(4,128)S(1)} copy-done((s32[4,4]{1,0:T(4,128)S(1)}, s32[4,4]{1,0:T(4,128)}, u32[]{:S(2)}) %copy-start.3) | copy-done | bytes 88
  34.9 0.9 %copy-done.5 = f32[256,256]{1,0:T(8,128)S(1)} copy-done((f32[256,256]{1,0:T(8,128)S(1)}, f32[256,256]{1,0:T(8,128)}, u32[]{:S(2)}) %copy-start.5) | copy-done | bytes 262168
  35.9 0.7 %copy-done.8 = f32[1,256]{1,0:T(1,128)S(1)} copy-done((f32[1,256]{1,0:T(1,128)S(1)}, f32[1,256]{1,0:T(1,128)}, u32[]{:S(2)}) %copy-start.8) | copy-done | bytes 1048
  36.6 0.7 %copy-done.9 = s32[1,256]{1,0:T(1,128)S(1)} copy-done((s32[1,256]{1,0:T(1,128)S(1)}, s32[1,256]{1,0:T(1,128)}, u32[]{:S(2)}) %copy-start.9) | copy-done | bytes 1048
  37.2 2.8 %prepare.1 = (bf16[256,256]{1,0:T(8,128)(2,1)S(1)}, bf16[4,256,2048]{2,1,0:T(8,128)(2,1)S(1)}) custom-call(s32[4,4]{1,0:T(4,128)S(1)} %copy-done.3, f32[4]{0:T(128)S(1)} %get-tuple-element.18.cosines, f32[4]{0:T(128)S(1)} %get-tuple-element.17.sines, f32[256,256]{1,0:T(8,128)S(1)} %copy-done.5, s32[1,256]{1,0:T(1,128)S(1)} %copy-done.9, f32[1,256]{1,0:T(1,128)S(1)} %copy-done.8), custom_call_target="tpu_custom_call" | custom-call | flops 1073741824 | bytes 6291456 | tf_op jit(solution)/shard_map/prepare/pallas_call | solution.py:232
  40.1 2.4 %interpolate.1 = bf16[16,64,512]{2,1,0:T(8,128)(2,1)} custom-call(bf16[256,256]{1,0:T(8,128)(2,1)S(1)} %get-tuple-element.11.rows_ref, bf16[4,256,2048]{2,1,0:T(8,128)(2,1)S(1)} %get-tuple-element.12.weights_ref, bf16[64,1024]{1,0:T(8,128)(2,1)S(1)} %get-tuple-element.13.refs_0_, bf16[64,1024]{1,0:T(8,128)(2,1)S(1)} %collective-permute-done.refs_1_, ...), custom_call_target="tpu_custom_call" | custom-call | flops 1073741824 | bytes 6291456 | tf_op jit(solution)/shard_map/interpolate/pallas_call | solution.py:288
  (30 shorter events, 1.3 us)
Async XLA Ops:
  0.0 0.9 %copy-start = (bf16[1,64,2048]{2,1,0:T(8,128)(2,1)S(1)}, bf16[1,64,2048]{2,1,0:T(8,128)(2,1)}, u32[]{:S(2)}) copy-start(bf16[1,64,2048]{2,1,0:T(8,128)(2,1)} %param.10) | copy-start | bytes 786436
  1.0 0.7 %copy-start.1 = (s32[4,4,4]{2,1,0:T(4,128)S(1)}, s32[4,4,4]{2,1,0:T(4,128)}, u32[]{:S(2)}) copy-start(s32[4,4,4]{2,1,0:T(4,128)} %starts.1) | copy-start | bytes 772
  1.6 0.7 %copy-start.2 = (s32[4,4]{1,0:T(4,128)S(1)}, s32[4,4]{1,0:T(4,128)}, u32[]{:S(2)}) copy-start(s32[4,4]{1,0:T(4,128)} %defocus.3) | copy-start | bytes 196
  2.3 1.3 %copy-start.4 = (bf16[5,256,512]{2,1,0:T(8,128)(2,1)S(1)}, bf16[5,256,512]{2,1,0:T(8,128)(2,1)}, u32[]{:S(2)}) copy-start(bf16[5,256,512]{2,1,0:T(8,128)(2,1)} %constant.12.clone.matrix_ref) | copy-start | bytes 3932164
  3.6 0.7 %copy-start.6 = (f32[16,256]{1,0:T(8,128)S(1)}, f32[16,256]{1,0:T(8,128)}, u32[]{:S(2)}) copy-start(f32[16,256]{1,0:T(8,128)} %constant.13.clone.lines_ref) | copy-start | bytes 49156
  4.4 0.7 %copy-start.7 = (s32[8,256]{1,0:T(8,128)S(1)}, s32[8,256]{1,0:T(8,128)}, u32[]{:S(2)}) copy-start(s32[8,256]{1,0:T(8,128)} %constant.14.clone.squares_ref) | copy-start | bytes 24580
  8.8 8.1 %collective-permute-start.3 = (bf16[64,1024]{1,0:T(8,128)(2,1)S(1)}, bf16[64,1024]{1,0:T(8,128)(2,1)S(1)}, u32[]{:S(2)}, u32[]{:S(2)}) collective-permute-start(bf16[64,1024]{1,0:T(8,128)(2,1)S(1)} %get-tuple-element.14), channel_id=1, source_target_pairs={{0,1},{1,0},{2,3},{3,2},{4,5},{5,4},{6,7},{7,6},{8,9},{9,8},{10,11... | collective-permute-start | bytes 393224 | tf_op jit(solution)/shard_map/ppermute | solution.py:307
  11.9 12.9 %collective-permute-start.7 = (bf16[64,1024]{1,0:T(8,128)(2,1)S(1)}, bf16[64,1024]{1,0:T(8,128)(2,1)S(1)}, u32[]{:S(2)}, u32[]{:S(2)}) collective-permute-start(bf16[64,1024]{1,0:T(8,128)(2,1)S(1)} %get-tuple-element.15), channel_id=1, source_target_pairs={{0,2},{1,3},{2,0},{3,1},{4,6},{5,7},{6,4},{7,5},{8,10},{9,11},{10,... | collective-permute-start | bytes 393224 | tf_op jit(solution)/shard_map/ppermute | solution.py:307
  14.5 10.3 %collective-permute-start.11 = (bf16[64,1024]{1,0:T(8,128)(2,1)S(1)}, bf16[64,1024]{1,0:T(8,128)(2,1)S(1)}, u32[]{:S(2)}, u32[]{:S(2)}) collective-permute-start(bf16[64,1024]{1,0:T(8,128)(2,1)S(1)} %get-tuple-element.16), channel_id=1, source_target_pairs={{0,3},{1,2},{2,1},{3,0},{4,7},{5,6},{6,5},{7,4},{8,11},{9,10},{10,... | collective-permute-start | bytes 393224 | tf_op jit(solution)/shard_map/ppermute | solution.py:307
  14.5 11.9 %collective-permute-start.1 = (bf16[64,1024]{1,0:T(8,128)(2,1)S(1)}, bf16[64,1024]{1,0:T(8,128)(2,1)S(1)}, u32[]{:S(2)}, u32[]{:S(2)}) collective-permute-start(bf16[64,1024]{1,0:T(8,128)(2,1)S(1)} %get-tuple-element.13.refs_0_), channel_id=1, source_target_pairs={{0,8},{4,12},{8,0},{12,4},{1,9},{5,13},{9,1},{13,5},{2,10},{6,14},... | collective-permute-start | bytes 393224 | tf_op jit(solution)/shard_map/ppermute | solution.py:307
  16.2 10.3 %collective-permute-start = (bf16[64,1024]{1,0:T(8,128)(2,1)S(1)}, bf16[64,1024]{1,0:T(8,128)(2,1)S(1)}, u32[]{:S(2)}, u32[]{:S(2)}) collective-permute-start(bf16[64,1024]{1,0:T(8,128)(2,1)S(1)} %get-tuple-element.13.refs_0_), channel_id=1, source_target_pairs={{0,4},{4,0},{8,12},{12,8},{1,5},{5,1},{9,13},{13,9},{2,6},{6,2},{1... | collective-permute-start | bytes 393224 | tf_op jit(solution)/shard_map/ppermute | solution.py:307
  16.9 10.2 %collective-permute-start.5 = (bf16[64,1024]{1,0:T(8,128)(2,1)S(1)}, bf16[64,1024]{1,0:T(8,128)(2,1)S(1)}, u32[]{:S(2)}, u32[]{:S(2)}) collective-permute-start(bf16[64,1024]{1,0:T(8,128)(2,1)S(1)} %collective-permute-done.3.refs_4_), channel_id=1, source_target_pairs={{0,8},{4,12},{8,0},{12,4},{1,9},{5,13},{9,1},{13,5},{2,10},{6,14},... | collective-permute-start | bytes 393224 | tf_op jit(solution)/shard_map/ppermute | solution.py:307
  24.8 2.3 %collective-permute-start.4 = (bf16[64,1024]{1,0:T(8,128)(2,1)S(1)}, bf16[64,1024]{1,0:T(8,128)(2,1)S(1)}, u32[]{:S(2)}, u32[]{:S(2)}) collective-permute-start(bf16[64,1024]{1,0:T(8,128)(2,1)S(1)} %collective-permute-done.3.refs_4_), channel_id=1, source_target_pairs={{0,4},{4,0},{8,12},{12,8},{1,5},{5,1},{9,13},{13,9},{2,6},{6,2},{1... | collective-permute-start | bytes 393224 | tf_op jit(solution)/shard_map/ppermute | solution.py:307
  24.8 6.3 %collective-permute-start.9 = (bf16[64,1024]{1,0:T(8,128)(2,1)S(1)}, bf16[64,1024]{1,0:T(8,128)(2,1)S(1)}, u32[]{:S(2)}, u32[]{:S(2)}) collective-permute-start(bf16[64,1024]{1,0:T(8,128)(2,1)S(1)} %collective-permute-done.7.refs_8_), channel_id=1, source_target_pairs={{0,8},{4,12},{8,0},{12,4},{1,9},{5,13},{9,1},{13,5},{2,10},{6,14},... | collective-permute-start | bytes 393224 | tf_op jit(solution)/shard_map/ppermute | solution.py:307
  26.3 4.8 %collective-permute-start.8 = (bf16[64,1024]{1,0:T(8,128)(2,1)S(1)}, bf16[64,1024]{1,0:T(8,128)(2,1)S(1)}, u32[]{:S(2)}, u32[]{:S(2)}) collective-permute-start(bf16[64,1024]{1,0:T(8,128)(2,1)S(1)} %collective-permute-done.7.refs_8_), channel_id=1, source_target_pairs={{0,4},{4,0},{8,12},{12,8},{1,5},{5,1},{9,13},{13,9},{2,6},{6,2},{1... | collective-permute-start | bytes 393224 | tf_op jit(solution)/shard_map/ppermute | solution.py:307
  26.6 7.0 %collective-permute-start.13 = (bf16[64,1024]{1,0:T(8,128)(2,1)S(1)}, bf16[64,1024]{1,0:T(8,128)(2,1)S(1)}, u32[]{:S(2)}, u32[]{:S(2)}) collective-permute-start(bf16[64,1024]{1,0:T(8,128)(2,1)S(1)} %collective-permute-done.11.refs_12_), channel_id=1, source_target_pairs={{0,8},{4,12},{8,0},{12,4},{1,9},{5,13},{9,1},{13,5},{2,10},{6,14},... | collective-permute-start | bytes 393224 | tf_op jit(solution)/shard_map/ppermute | solution.py:307
  27.1 13.0 %collective-permute-start.12 = (bf16[64,1024]{1,0:T(8,128)(2,1)S(1)}, bf16[64,1024]{1,0:T(8,128)(2,1)S(1)}, u32[]{:S(2)}, u32[]{:S(2)}) collective-permute-start(bf16[64,1024]{1,0:T(8,128)(2,1)S(1)} %collective-permute-done.11.refs_12_), channel_id=1, source_target_pairs={{0,4},{4,0},{8,12},{12,8},{1,5},{5,1},{9,13},{13,9},{2,6},{6,2},{1... | collective-permute-start | bytes 393224 | tf_op jit(solution)/shard_map/ppermute | solution.py:307
  27.1 13.0 %collective-permute-start.2 = (bf16[64,1024]{1,0:T(8,128)(2,1)S(1)}, bf16[64,1024]{1,0:T(8,128)(2,1)S(1)}, u32[]{:S(2)}, u32[]{:S(2)}) collective-permute-start(bf16[64,1024]{1,0:T(8,128)(2,1)S(1)} %collective-permute-done.1.refs_2_), channel_id=1, source_target_pairs={{0,4},{4,0},{8,12},{12,8},{1,5},{5,1},{9,13},{13,9},{2,6},{6,2},{1... | collective-permute-start | bytes 393224 | tf_op jit(solution)/shard_map/ppermute | solution.py:307
  31.1 9.0 %collective-permute-start.6 = (bf16[64,1024]{1,0:T(8,128)(2,1)S(1)}, bf16[64,1024]{1,0:T(8,128)(2,1)S(1)}, u32[]{:S(2)}, u32[]{:S(2)}) collective-permute-start(bf16[64,1024]{1,0:T(8,128)(2,1)S(1)} %collective-permute-done.5.refs_6_), channel_id=1, source_target_pairs={{0,4},{4,0},{8,12},{12,8},{1,5},{5,1},{9,13},{13,9},{2,6},{6,2},{1... | collective-permute-start | bytes 393224 | tf_op jit(solution)/shard_map/ppermute | solution.py:307
  31.1 9.0 %collective-permute-start.10 = (bf16[64,1024]{1,0:T(8,128)(2,1)S(1)}, bf16[64,1024]{1,0:T(8,128)(2,1)S(1)}, u32[]{:S(2)}, u32[]{:S(2)}) collective-permute-start(bf16[64,1024]{1,0:T(8,128)(2,1)S(1)} %collective-permute-done.9.refs_10_), channel_id=1, source_target_pairs={{0,4},{4,0},{8,12},{12,8},{1,5},{5,1},{9,13},{13,9},{2,6},{6,2},{1... | collective-permute-start | bytes 393224 | tf_op jit(solution)/shard_map/ppermute | solution.py:307
  33.5 6.6 %collective-permute-start.14 = (bf16[64,1024]{1,0:T(8,128)(2,1)S(1)}, bf16[64,1024]{1,0:T(8,128)(2,1)S(1)}, u32[]{:S(2)}, u32[]{:S(2)}) collective-permute-start(bf16[64,1024]{1,0:T(8,128)(2,1)S(1)} %collective-permute-done.13.refs_14_), channel_id=1, source_target_pairs={{0,4},{4,0},{8,12},{12,8},{1,5},{5,1},{9,13},{13,9},{2,6},{6,2},{1... | collective-permute-start | bytes 393224 | tf_op jit(solution)/shard_map/ppermute | solution.py:307
  34.2 0.7 %copy-start.3 = (s32[4,4]{1,0:T(4,128)S(1)}, s32[4,4]{1,0:T(4,128)}, u32[]{:S(2)}) copy-start(s32[4,4]{1,0:T(4,128)} %defocus.3) | copy-start | bytes 196
  34.9 0.9 %copy-start.5 = (f32[256,256]{1,0:T(8,128)S(1)}, f32[256,256]{1,0:T(8,128)}, u32[]{:S(2)}) copy-start(f32[256,256]{1,0:T(8,128)} %constant.15.clone.waves) | copy-start | bytes 786436
  36.6 0.7 %copy-start.9 = (s32[1,256]{1,0:T(1,128)S(1)}, s32[1,256]{1,0:T(1,128)}, u32[]{:S(2)}) copy-start(s32[1,256]{1,0:T(1,128)} %constant.16.clone.squares) | copy-start | bytes 3076
  (1 other events, 0.7 us)

commit v3 on v2

--- a/solution.py
+++ b/solution.py
@@ -15,7 +15,11 @@
 XBLK = 4
 SLICES = 64
 RADIX = 8
-WINDOW = BAND + 128
+MAIN = 128
+REST = 32
+REACH = MAIN + REST
+PACKED = XBLK * REACH
+WINDOW = 384
 ROOT = math.sqrt(0.5)
 
 
@@ -50,8 +54,8 @@
     count = np.where((freq == 0) | (freq == columns // 2), 1.0, 2.0)
     fold = np.minimum(freq, columns - freq)
     ramp = count * (fold + 0.5) / (0.5 * columns) / columns
-    lines = np.concatenate([ramp, np.stack(turns + [np.zeros(size)] * 2)]).astype(np.float32)
-    return matrices, lines, (fold * fold).astype(np.int32)
+    lines = np.concatenate([ramp, fold * fold, np.stack(turns + [np.zeros(size)] * 2)])
+    return matrices, lines.astype(np.float32)
 
 
 def row_tables(full_rows):
@@ -61,26 +65,35 @@
     angle = 2.0 * np.pi * (y * freq[None, :] % full_rows) / full_rows
     waves = np.where(np.arange(full_rows)[None, :] <= half, np.cos(angle), np.sin(angle))
     count = np.where((freq == 0) | (freq == half), 1.0, 2.0) / full_rows
-    return waves.astype(np.float32), (freq * freq).astype(np.int32)[None], count.astype(np.float32)[None]
+    return np.concatenate([waves, count[None], (freq * freq)[None], np.zeros((6, full_rows))]).astype(np.float32)
 
 
 def flip_sign(squares, defocus, length):
-    cycles = lax.div(squares * defocus, jnp.int32(length * length))
+    cycles = lax.div(squares.astype(jnp.int32) * defocus, jnp.int32(length * length))
     return (1 - 2 * (cycles & 1)).astype(jnp.float32)
 
 
-def column_kernel(slots, slices_owned, defocus, starts, image_ref, matrix_ref, lines_ref, squares_ref, *refs):
+def fetched(sources, targets, sems):
+    copies = [pltpu.make_async_copy(s, t, sems.at[i]) for i, (s, t) in enumerate(zip(sources, targets))]
+    for copy in copies:
+        copy.start()
+    return copies
+
+
+def column_kernel(slots, slices_owned, image_ref, lines_ref, matrix_ref, defocus_ref, starts_ref, first_ref, *refs):
     out_refs = refs[:slots]
-    image, matrix, zhi, zlo, ends, waves, turned, image_sem, matrix_sem = refs[slots:]
+    image, lines, matrix, defocus, starts, first_tap, zhi, zlo, ends, waves, turned, sems = refs[slots:]
     rows, columns = image.shape
     size = columns // RADIX
-    copies = [pltpu.make_async_copy(image_ref, image, image_sem)]
-    copies += [pltpu.make_async_copy(matrix_ref.at[i], matrix.at[i], matrix_sem.at[i]) for i in range(5)]
-    for copy in copies:
-        copy.start()
+    copies = fetched(
+        [image_ref, lines_ref] + [matrix_ref.at[i] for i in range(5)] + [defocus_ref, starts_ref, first_ref],
+        [image, lines] + [matrix.at[i] for i in range(5)] + [defocus, starts, first_tap],
+        sems,
+    )
     tilt = lax.axis_index("tilt")
-    turns = [lines_ref[8 + i : 9 + i, :] for i in range(6)]
     copies[0].wait()
+    copies[1].wait()
+    turns = [lines[16 + i : 17 + i, :] for i in range(6)]
 
     def butterfly(step, carry):
         here = pl.ds(pl.multiple_of(step * 16, 16), 16)
@@ -100,7 +113,7 @@
         return carry
 
     lax.fori_loop(0, rows // 16, butterfly, 0)
-    for copy in copies[1:5]:
+    for copy in copies[2:6]:
         copy.wait()
 
     def product(first, count, table, here):
@@ -116,9 +129,11 @@
         real, imag = mixed[2 * j * rows : (2 * j + 1) * rows], mixed[(2 * j + 1) * rows : (2 * j + 2) * rows]
         spectrum += [real[:, :size] + imag[:, size:], imag[:, :size] - real[:, size:]]
 
+    for copy in copies[6:]:
+        copy.wait()
     slabs = [(tilt ^ slot) * slices_owned // SLAB for slot in range(slots)]
     gains = [
-        flip_sign(squares_ref[...], defocus[tilt, slabs[slot]], columns) * lines_ref[:8, :] for slot in range(slots)
+        flip_sign(lines[8:16, :], defocus[tilt, slabs[slot]], columns) * lines[:8, :] for slot in range(slots)
     ]
     filtered = [
         jnp.concatenate(
@@ -126,7 +141,6 @@
         )
         for i in range(8)
     ]
-    copies[5].wait()
     for i in range(2):
         ends[i] = jnp.dot(filtered[i], matrix[4, :, i * size : (i + 1) * size], preferred_element_type=jnp.float32)
     for i in range(6):
@@ -152,57 +166,69 @@
 
     lax.fori_loop(0, slots * rows // 8, inverse_butterfly, 0)
 
+    lane = lax.broadcasted_iota(jnp.int32, (rows, MAIN), 1) // REST
     for slot in range(slots):
+        rest = jnp.zeros((rows, MAIN), jnp.float32)
         for block in range(XBLK):
-            start = starts[tilt, slabs[slot], block]
+            start = starts[tilt, slabs[slot], block] + first_tap[tilt]
             base = pl.multiple_of(jnp.minimum((start // 128) * 128, columns - WINDOW), 128)
             window = turned[slot * rows : (slot + 1) * rows, pl.ds(base, WINDOW)]
             shift = base - start
-            shift = jnp.where(shift < 0, shift + WINDOW, shift)
-            out_refs[slot][:, block * BAND : (block + 1) * BAND] = pltpu.roll(window, shift, 1)[:, :BAND].astype(
-                jnp.bfloat16
-            )
-
-
-def column_filtered(slots, slices_owned, defocus, starts, image):
+            reach = pltpu.roll(window, jnp.where(shift < 0, shift + WINDOW, shift), 1)[:, : 2 * MAIN]
+            out_refs[slot][:, block * MAIN : (block + 1) * MAIN] = reach[:, :MAIN].astype(jnp.bfloat16)
+            last = reach[:, MAIN:]
+            rest = jnp.where(lane == block, pltpu.roll(last, block * REST, 1) if block else last, rest)
+        out_refs[slot][:, XBLK * MAIN :] = rest.astype(jnp.bfloat16)
+
+
+def column_filtered(slots, slices_owned, defocus, starts, first_tap, image):
     rows, columns = image.shape
     size = columns // RADIX
-    matrices, lines, squares = column_tables(columns)
-    smem, vmem = pl.BlockSpec(memory_space=pltpu.SMEM), pl.BlockSpec(memory_space=pltpu.VMEM)
-    away = pl.BlockSpec(memory_space=pl.ANY)
+    matrices, lines = column_tables(columns)
+    vmem, away = pl.BlockSpec(memory_space=pltpu.VMEM), pl.BlockSpec(memory_space=pl.ANY)
     return pl.pallas_call(
         functools.partial(column_kernel, slots, slices_owned),
-        out_shape=[jax.ShapeDtypeStruct((rows, XBLK * BAND), jnp.bfloat16)] * slots,
-        in_specs=[smem, smem, away, away, vmem, vmem],
+        out_shape=[jax.ShapeDtypeStruct((rows, PACKED), jnp.bfloat16)] * slots,
+        in_specs=[away] * 6,
         out_specs=[vmem] * slots,
         scratch_shapes=[
             pltpu.VMEM((rows, columns), jnp.bfloat16),
+            pltpu.VMEM(lines.shape, jnp.float32),
             pltpu.VMEM(matrices.shape, jnp.bfloat16),
+            pltpu.SMEM(defocus.shape, jnp.int32),
+            pltpu.SMEM(starts.shape, jnp.int32),
+            pltpu.SMEM(first_tap.shape, jnp.int32),
             pltpu.VMEM((8, rows, size), jnp.bfloat16),
             pltpu.VMEM((8, rows, size), jnp.bfloat16),
             pltpu.VMEM((2, slots * rows, size), jnp.float32),
             pltpu.VMEM((6, slots * rows, 2 * size), jnp.float32),
             pltpu.VMEM((slots * rows, columns), jnp.float32),
-            pltpu.SemaphoreType.DMA,
-            pltpu.SemaphoreType.DMA((5,)),
+            pltpu.SemaphoreType.DMA((10,)),
         ],
         compiler_params=pltpu.CompilerParams(vmem_limit_bytes=40 * 2**20),
         cost_estimate=pl.CostEstimate(flops=2 * rows * columns * 2048 * 2, bytes_accessed=4 * 2**20, transcendentals=0),
         name="column_filter",
-    )(defocus, starts, image, jnp.asarray(matrices), jnp.asarray(lines), jnp.asarray(squares))
-
-
-def prepare_kernel(slots, slices_owned, defocus, cosines, sines, waves, squares, count, rows_ref, weights_ref, mine, order):
+    )(image, jnp.asarray(lines), jnp.asarray(matrices), defocus, starts, first_tap)
+
+
+def prepare_kernel(slots, slices_owned, passed, table_ref, defocus_ref, first_ref, cosine_ref, sine_ref, *refs):
+    rows_ref, weights_ref = refs[passed : passed + 2]
+    table, defocus, first_tap, cosines, sines, mine, order, sems = refs[2 * passed + 2 :]
+    copies = fetched(
+        [table_ref, defocus_ref, first_ref, cosine_ref, sine_ref], [table, defocus, first_tap, cosines, sines], sems
+    )
     tilt, row = lax.axis_index("tilt"), lax.axis_index("row")
     slab, local_first = tilt * slices_owned // SLAB, tilt * slices_owned % SLAB
-    full_rows = waves.shape[0]
+    full_rows = table.shape[1]
     rows = rows_ref.shape[0] // slots
-    own = waves[pl.ds(pl.multiple_of(row * rows, rows), rows), :]
+    for copy in copies:
+        copy.wait()
+    own = table[pl.ds(pl.multiple_of(row * rows, rows), rows), :]
     for slot in range(slots):
-        sign = flip_sign(squares[...], defocus[tilt ^ slot, slab], full_rows)
-        mine[slot * rows : (slot + 1) * rows, :] = own * (sign * count[...])
+        sign = flip_sign(table[full_rows + 1 : full_rows + 2, :], defocus[tilt ^ slot, slab], full_rows)
+        mine[slot * rows : (slot + 1) * rows, :] = own * (sign * table[full_rows : full_rows + 1, :])
     for block in range(full_rows // rows):
-        order[block * rows : (block + 1) * rows, :] = waves[pl.ds(pl.multiple_of((row ^ block) * rows, rows), rows), :]
+        order[block * rows : (block + 1) * rows, :] = table[pl.ds(pl.multiple_of((row ^ block) * rows, rows), rows), :]
     rows_ref[...] = lax.dot_general(
         mine[...],
         order[...],
@@ -212,9 +238,11 @@
     ).astype(jnp.bfloat16)
 
     column = lax.broadcasted_iota(jnp.int32, (1, XBW), 1).astype(jnp.float32)
-    tap = lax.broadcasted_iota(jnp.int32, (BAND, XBW), 0).astype(jnp.float32)
+    place = lax.broadcasted_iota(jnp.int32, (2 * MAIN, XBW), 0)
+    place = jnp.where(place < MAIN, place, MAIN + place % REST)
     for slot in range(slots):
         cosine, sine = cosines[tilt ^ slot], sines[tilt ^ slot]
+        tap = (place + first_tap[tilt ^ slot]).astype(jnp.float32)
 
         def one_slice(c, carry):
             offset = (local_first + c).astype(jnp.float32) - 0.5 * (SLAB - 1)
@@ -226,25 +254,35 @@
         lax.fori_loop(0, slices_owned, one_slice, 0)
 
 
-def prepared(slots, slices_owned, rows, full_rows, defocus, tilt_angle):
-    smem, vmem = pl.BlockSpec(memory_space=pltpu.SMEM), pl.BlockSpec(memory_space=pltpu.VMEM)
-    tables = [jnp.asarray(t) for t in row_tables(full_rows)]
-    return pl.pallas_call(
-        functools.partial(prepare_kernel, slots, slices_owned),
+def prepared(slots, slices_owned, rows, full_rows, defocus, first_tap, cosines, sines, passed):
+    vmem, away = pl.BlockSpec(memory_space=pltpu.VMEM), pl.BlockSpec(memory_space=pl.ANY)
+    table = row_tables(full_rows)
+    count = len(passed)
+    out = pl.pallas_call(
+        functools.partial(prepare_kernel, slots, slices_owned, count),
         out_shape=[
             jax.ShapeDtypeStruct((slots * rows, full_rows), jnp.bfloat16),
-            jax.ShapeDtypeStruct((slots, BAND, slices_owned * XBW), jnp.bfloat16),
-        ],
-        in_specs=[smem] * 3 + [vmem] * 3,
-        out_specs=[vmem] * 2,
+            jax.ShapeDtypeStruct((slots, 2 * MAIN, slices_owned * XBW), jnp.bfloat16),
+        ]
+        + [jax.ShapeDtypeStruct(p.shape, p.dtype) for p in passed],
+        in_specs=[away] * (5 + count),
+        out_specs=[vmem] * 2 + [away] * count,
         scratch_shapes=[
+            pltpu.VMEM(table.shape, jnp.float32),
+            pltpu.SMEM(defocus.shape, jnp.int32),
+            pltpu.SMEM(first_tap.shape, jnp.int32),
+            pltpu.SMEM(cosines.shape, jnp.float32),
+            pltpu.SMEM(sines.shape, jnp.float32),
             pltpu.VMEM((slots * rows, full_rows), jnp.float32),
             pltpu.VMEM((full_rows, full_rows), jnp.float32),
+            pltpu.SemaphoreType.DMA((5,)),
         ],
+        input_output_aliases={5 + i: 2 + i for i in range(count)},
         compiler_params=pltpu.CompilerParams(vmem_limit_bytes=32 * 2**20),
         cost_estimate=pl.CostEstimate(flops=2**30, bytes_accessed=6 * 2**20, transcendentals=0),
         name="prepare",
-    )(defocus, jnp.cos(tilt_angle), jnp.sin(tilt_angle), *tables)
+    )(jnp.asarray(table), defocus, first_tap, cosines, sines, *passed)
+    return out[0], out[1], out[2:]
 
 
 def interpolate_kernel(slots, row_devices, factor, rows_ref, weights_ref, *refs):
@@ -252,14 +290,16 @@
     out_ref, out, sems = refs[slots * row_devices :]
     rows = patch_refs[0].shape[0]
     slices = out.shape[0]
+    lane = lax.broadcasted_iota(jnp.int32, (rows, MAIN), 1) // REST
     corrected = []
     for slot in range(slots):
         patches = jnp.concatenate([patch_refs[slot * row_devices + r][...] for r in range(row_devices)], 0)
         image = jnp.dot(rows_ref[slot * rows : (slot + 1) * rows, :], patches, preferred_element_type=jnp.float32)
-        image = image.astype(jnp.bfloat16)
-        corrected.append(
-            jnp.concatenate([image[:, block * BAND : (block + 1) * BAND] for block in range(XBLK)], 0)
+        main = jnp.concatenate([image[:, block * MAIN : (block + 1) * MAIN] for block in range(XBLK)], 0)
+        rest = jnp.concatenate(
+            [jnp.where(lane == block, image[:, XBLK * MAIN :], 0.0) for block in range(XBLK)], 0
         )
+        corrected.append(jnp.concatenate([main, rest], 1).astype(jnp.bfloat16))
     step = math.gcd(slices, 4)
     copies = []
     for group in range(slices // step):
@@ -296,7 +336,7 @@
         ],
         compiler_params=pltpu.CompilerParams(vmem_limit_bytes=32 * 2**20),
         cost_estimate=pl.CostEstimate(
-            flops=2 * slots * BAND * width * XBLK * rows, bytes_accessed=6 * 2**20, transcendentals=0
+            flops=2 * slots * 2 * MAIN * width * XBLK * rows, bytes_accessed=6 * 2**20, transcendentals=0
         ),
         name="interpolate",
     )(row_filters, weights, *[block for slot in patches for block in slot])
@@ -320,12 +360,19 @@
     _, rows, _ = projections.shape
     row_devices, tilt_devices = lax.axis_size("row"), lax.axis_size("tilt")
     slices_owned = SLICES // tilt_devices
-    sent = column_filtered(tilt_devices, slices_owned, defocus, band_start, projections[0])
-    arrived = {0: sent[0]}
-    for d in sorted(range(1, tilt_devices), reverse=True):
+    cosines, sines = jnp.cos(tilt_angle), jnp.sin(tilt_angle)
+    lowest = 0.5 * XBW + jnp.minimum((XBW - 1) * cosines, 0.0) - 0.5 * (SLAB - 1) * jnp.abs(sines)
+    first_tap = jnp.clip(jnp.floor(lowest).astype(jnp.int32) - 8, 0, BAND - REACH)
+    sent = column_filtered(tilt_devices, slices_owned, defocus, band_start, first_tap, projections[0])
+    last = tilt_devices - 1
+    arrived = {last: exchange(sent[last], "tilt", last)}
+    row_filters, weights, sent = prepared(
+        tilt_devices, slices_owned, rows, rows * row_devices, defocus, first_tap, cosines, sines, sent[:last]
+    )
+    for d in range(last - 1, 0, -1):
         arrived[d] = exchange(sent[d], "tilt", d)
+    arrived[0] = sent[0]
     patches = [gather_rows(arrived[d]) for d in range(tilt_devices)]
-    row_filters, weights = prepared(tilt_devices, slices_owned, rows, rows * row_devices, defocus, tilt_angle)
     return interpolated(row_filters, weights, patches, 1.0 / math.sqrt(tilt_devices))
 
 

time: 43 us -> 34.3 us (0.80)
  waiting for transfers between devices: 12.3 us -> 7.9 us
  local copies, waits for them, and re-layouts: 8.73 us -> 6.02 us
  starting transfers between devices: 12.4 us -> 10.9 us
    ppermute x15, waiting for transfers between devices: 12.3 us -> 7.9 us  [exchange(): return lax.ppermute(array, axis, [(i, i ^ distance) for i in range(count)])]
    unnamed x20 -> x12, local copies, waits for them, and re-layouts: 8.04 us -> 5.33 us
    ppermute x15, starting transfers between devices: 12.4 us -> 10.9 us  [exchange(): return lax.ppermute(array, axis, [(i, i ^ distance) for i in range(count)])]
    sin x1 -> x0, local copies, waits for them, and re-layouts: 0.69 us -> none  [prepared(): jnp.sin(tilt_angle)]
    cos x0 -> x1, local copies, waits for them, and re-layouts: none -> 0.69 us  [per_device(): cosines, sines = (jnp.cos(tilt_angle), jnp.sin(tilt_angle))]
  transfers between devices with their start and end apart: 15 -> 15, of which waited for: 4 -> 5; matrix products, arithmetic and copies ran while one was open for 2% -> 0% of each run, Pallas kernels for 7% -> 9%
where the time goes in v3:
time: 34.3 us; the launch traced here: 34 us
  starting transfers between devices  10.9 us (32%)
  Pallas kernels  9.04 us (26%)
  waiting for transfers between devices  7.9 us (23%)
  local copies, waits for them, and re-layouts  6.02 us (18%)
    ppermute x15, starting transfers between devices, exchange(): return lax.ppermute(array, axis, [(i, i ^ distance) for i in range(count)])  10.9 us
    ppermute x15, waiting for transfers between devices, exchange(): return lax.ppermute(array, axis, [(i, i ^ distance) for i in range(count)])  7.9 us
    unnamed x12, local copies, waits for them, and re-layouts  5.33 us
    pallas_call x1, Pallas kernels, column_filtered(): pl.pallas_call(functools.partial(column_kernel, slots, slices_owned), out...  3.72 us
    pallas_call x1, Pallas kernels, prepared(): pl.pallas_call(functools.partial(prepare_kernel, slots, slices_owned, cou...  3.11 us
    pallas_call x1, Pallas kernels, interpolated(): pl.pallas_call(functools.partial(interpolate_kernel, slots, row_devices,...  2.21 us
    cos x1, local copies, waits for them, and re-layouts, per_device(): cosines, sines = (jnp.cos(tilt_angle), jnp.sin(tilt_angle))  0.69 us
  transfers between devices with their start and end apart: 15, of which 5 were waited for; matrix products, arithmetic and copies ran while one was open for 0% of the time, Pallas kernels for 9%

profile of v3, /device:TPU:0, one launch (start us, length us, event | category | flops | bytes accessed | tf_op | source)
XLA Modules:
  0.0 34.0 jit_solution(10294493835752743899)
XLA Ops:
  0.0 0.7 %fusion = (f32[4]{0:T(128)S(1)}, f32[4]{0:T(128)S(1)}) fusion(f32[4]{0:T(128)} %param.8), kind=kLoop, calls=%fused_computation.1 | loop fusion | bytes 48 | tf_op jit(solution)/shard_map/cos | solution.py:363
  0.7 0.9 %copy-done = bf16[1,64,2048]{2,1,0:T(8,128)(2,1)S(1)} copy-done((bf16[1,64,2048]{2,1,0:T(8,128)(2,1)S(1)}, bf16[1,64,2048]{2,1,0:T(8,128)(2,1)}, u32[]{:S(2)}) %copy-start) | copy-done | bytes 262168
  1.7 0.7 %copy-done.1 = s32[4,4,4]{2,1,0:T(4,128)S(1)} copy-done((s32[4,4,4]{2,1,0:T(4,128)S(1)}, s32[4,4,4]{2,1,0:T(4,128)}, u32[]{:S(2)}) %copy-start.1) | copy-done | bytes 280
  2.4 0.7 %copy-done.2 = s32[4,4]{1,0:T(4,128)S(1)} copy-done((s32[4,4]{1,0:T(4,128)S(1)}, s32[4,4]{1,0:T(4,128)}, u32[]{:S(2)}) %copy-start.2) | copy-done | bytes 88
  3.0 1.3 %copy-done.3 = bf16[5,256,512]{2,1,0:T(8,128)(2,1)S(1)} copy-done((bf16[5,256,512]{2,1,0:T(8,128)(2,1)S(1)}, bf16[5,256,512]{2,1,0:T(8,128)(2,1)}, u32[]{:S(2)}) %copy-start.3) | copy-done | bytes 1310744
  4.4 0.7 %copy-done.5 = f32[24,256]{1,0:T(8,128)S(1)} copy-done((f32[24,256]{1,0:T(8,128)S(1)}, f32[24,256]{1,0:T(8,128)}, u32[]{:S(2)}) %copy-start.5) | copy-done | bytes 24600
  5.1 3.7 %column_filter.1 = (bf16[64,640]{1,0:T(8,128)(2,1)S(1)}, bf16[64,640]{1,0:T(8,128)(2,1)S(1)}, bf16[64,640]{1,0:T(8,128)(2,1)S(1)}, bf16[64,640]{1,0:T(8,128)(2,1)S(1)}) custom-call(bf16[64,2048]{1,0:T(8,128)(2,1)S(1)} %bitcast.1, f32[24,256]{1,0:T(8,128)S(1)} %copy-done.5, bf16[5,256,512]{2,1,0:T(8,128)(2,1)S(1)} %copy-done.3, s32[4,4]{1,0:T(4,128)S(1)} %copy-done.2, ...), custom_call_target="tpu_custom_call" | custom-call | flops 1073741824 | bytes 4194304 | tf_op jit(solution)/shard_map/column_filter/pallas_call | solution.py:189
  8.8 5.1 %collective-permute-start.11 = (bf16[64,640]{1,0:T(8,128)(2,1)S(1)}, bf16[64,640]{1,0:T(8,128)(2,1)S(1)}, u32[]{:S(2)}, u32[]{:S(2)}) collective-permute-start(bf16[64,640]{1,0:T(8,128)(2,1)S(1)} %get-tuple-element.22), channel_id=1, source_target_pairs={{0,3},{1,2},{2,1},{3,0},{4,7},{5,6},{6,5},{7,4},{8,11},{9,10},{10,... | collective-permute-start | bytes 245768 | tf_op jit(solution)/shard_map/ppermute | solution.py:347
  13.9 1.0 %copy-done.4 = f32[264,256]{1,0:T(8,128)S(1)} copy-done((f32[264,256]{1,0:T(8,128)S(1)}, f32[264,256]{1,0:T(8,128)}, u32[]{:S(2)}) %copy-start.4) | copy-done | bytes 270360
  14.9 3.1 %prepare.1 = (bf16[256,256]{1,0:T(8,128)(2,1)S(1)}, bf16[4,256,2048]{2,1,0:T(8,128)(2,1)S(1)}, bf16[64,640]{1,0:T(8,128)(2,1)S(1)}, bf16[64,640]{1,0:T(8,128)(2,1)S(1)}, bf16[64,640]{1,0:T(8,128)(2,1)S(1)}) custom-call(f32[264,256]{1,0:T(8,128)S(1)} %copy-done.4, s32[4,4]{1,0:T(4,128)S(1)} %copy-done.2, ...), custom_call_target="tpu_custom_call", output_to_operand_aliasing={{2}: (5, {}), {3}: (6, {}), {4}: (7, {})} | custom-call | flops 1073741824 | bytes 6291456 | tf_op jit(solution)/shard_map/prepare/pallas_call | solution.py:261
  18.1 0.6 %collective-permute-start.7 = (bf16[64,640]{1,0:T(8,128)(2,1)S(1)}, bf16[64,640]{1,0:T(8,128)(2,1)S(1)}, u32[]{:S(2)}, u32[]{:S(2)}) collective-permute-start(bf16[64,640]{1,0:T(8,128)(2,1)S(1)} %get-tuple-element.21), channel_id=1, source_target_pairs={{0,2},{1,3},{2,0},{3,1},{4,6},{5,7},{6,4},{7,5},{8,10},{9,11},{10,... | collective-permute-start | bytes 245768 | tf_op jit(solution)/shard_map/ppermute | solution.py:347
  18.7 1.7 %collective-permute-start.1 = (bf16[64,640]{1,0:T(8,128)(2,1)S(1)}, bf16[64,640]{1,0:T(8,128)(2,1)S(1)}, u32[]{:S(2)}, u32[]{:S(2)}) collective-permute-start(bf16[64,640]{1,0:T(8,128)(2,1)S(1)} %get-tuple-element.19.refs_0_), channel_id=1, source_target_pairs={{0,8},{4,12},{8,0},{12,4},{1,9},{5,13},{9,1},{13,5},{2,10},{6,14},... | collective-permute-start | bytes 245768 | tf_op jit(solution)/shard_map/ppermute | solution.py:347
  20.4 0.3 collective-permute-start.13
  20.7 2.3 %collective-permute-done.3.refs_4_ = bf16[64,640]{1,0:T(8,128)(2,1)S(1)} collective-permute-done((bf16[64,640]{1,0:T(8,128)(2,1)S(1)}, bf16[64,640]{1,0:T(8,128)(2,1)S(1)}, u32[]{:S(2)}, u32[]{:S(2)}) %collective-permute-start.3) | collective-permute-done | bytes 81952 | tf_op jit(solution)/shard_map/ppermute | solution.py:347
  23.0 1.1 %collective-permute-done.7.refs_8_ = bf16[64,640]{1,0:T(8,128)(2,1)S(1)} collective-permute-done((bf16[64,640]{1,0:T(8,128)(2,1)S(1)}, bf16[64,640]{1,0:T(8,128)(2,1)S(1)}, u32[]{:S(2)}, u32[]{:S(2)}) %collective-permute-start.7) | collective-permute-done | bytes 81952 | tf_op jit(solution)/shard_map/ppermute | solution.py:347
  24.1 1.5 %collective-permute-start.5 = (bf16[64,640]{1,0:T(8,128)(2,1)S(1)}, bf16[64,640]{1,0:T(8,128)(2,1)S(1)}, u32[]{:S(2)}, u32[]{:S(2)}) collective-permute-start(bf16[64,640]{1,0:T(8,128)(2,1)S(1)} %collective-permute-done.3.refs_4_), channel_id=1, source_target_pairs={{0,8},{4,12},{8,0},{12,4},{1,9},{5,13},{9,1},{13,5},{2,10},{6,14},... | collective-permute-start | bytes 245768 | tf_op jit(solution)/shard_map/ppermute | solution.py:347
  25.6 0.6 %collective-permute-start.9 = (bf16[64,640]{1,0:T(8,128)(2,1)S(1)}, bf16[64,640]{1,0:T(8,128)(2,1)S(1)}, u32[]{:S(2)}, u32[]{:S(2)}) collective-permute-start(bf16[64,640]{1,0:T(8,128)(2,1)S(1)} %collective-permute-done.7.refs_8_), channel_id=1, source_target_pairs={{0,8},{4,12},{8,0},{12,4},{1,9},{5,13},{9,1},{13,5},{2,10},{6,14},... | collective-permute-start | bytes 245768 | tf_op jit(solution)/shard_map/ppermute | solution.py:347
  26.2 0.2 collective-permute-start.8
  26.3 0.3 %collective-permute-start.2 = (bf16[64,640]{1,0:T(8,128)(2,1)S(1)}, bf16[64,640]{1,0:T(8,128)(2,1)S(1)}, u32[]{:S(2)}, u32[]{:S(2)}) collective-permute-start(bf16[64,640]{1,0:T(8,128)(2,1)S(1)} %collective-permute-done.1.refs_2_), channel_id=1, source_target_pairs={{0,4},{4,0},{8,12},{12,8},{1,5},{5,1},{9,13},{13,9},{2,6},{6,2},{1... | collective-permute-start | bytes 245768 | tf_op jit(solution)/shard_map/ppermute | solution.py:347
  26.7 1.8 %collective-permute-done.5.refs_6_ = bf16[64,640]{1,0:T(8,128)(2,1)S(1)} collective-permute-done((bf16[64,640]{1,0:T(8,128)(2,1)S(1)}, bf16[64,640]{1,0:T(8,128)(2,1)S(1)}, u32[]{:S(2)}, u32[]{:S(2)}) %collective-permute-start.5) | collective-permute-done | bytes 81952 | tf_op jit(solution)/shard_map/ppermute | solution.py:347
  28.5 0.5 %collective-permute-start.6 = (bf16[64,640]{1,0:T(8,128)(2,1)S(1)}, bf16[64,640]{1,0:T(8,128)(2,1)S(1)}, u32[]{:S(2)}, u32[]{:S(2)}) collective-permute-start(bf16[64,640]{1,0:T(8,128)(2,1)S(1)} %collective-permute-done.5.refs_6_), channel_id=1, source_target_pairs={{0,4},{4,0},{8,12},{12,8},{1,5},{5,1},{9,13},{13,9},{2,6},{6,2},{1... | collective-permute-start | bytes 245768 | tf_op jit(solution)/shard_map/ppermute | solution.py:347
  29.0 1.4 %collective-permute-done.9.refs_10_ = bf16[64,640]{1,0:T(8,128)(2,1)S(1)} collective-permute-done((bf16[64,640]{1,0:T(8,128)(2,1)S(1)}, bf16[64,640]{1,0:T(8,128)(2,1)S(1)}, u32[]{:S(2)}, u32[]{:S(2)}) %collective-permute-start.9) | collective-permute-done | bytes 81952 | tf_op jit(solution)/shard_map/ppermute | solution.py:347
  30.5 1.2 %collective-permute-done.10.refs_11_ = bf16[64,640]{1,0:T(8,128)(2,1)S(1)} collective-permute-done((bf16[64,640]{1,0:T(8,128)(2,1)S(1)}, bf16[64,640]{1,0:T(8,128)(2,1)S(1)}, u32[]{:S(2)}, u32[]{:S(2)}) %collective-permute-start.10) | collective-permute-done | bytes 81952 | tf_op jit(solution)/shard_map/ppermute | solution.py:347
  31.7 2.2 %interpolate.1 = bf16[16,64,512]{2,1,0:T(8,128)(2,1)} custom-call(bf16[256,256]{1,0:T(8,128)(2,1)S(1)} %get-tuple-element.17.rows_ref, bf16[4,256,2048]{2,1,0:T(8,128)(2,1)S(1)} %get-tuple-element.18.weights_ref, bf16[64,640]{1,0:T(8,128)(2,1)S(1)} %get-tuple-element.19.refs_0_, bf16[64,640]{1,0:T(8,128)(2,1)S(1)} %collective-permute-done.refs_1_, ...), custom_call_target="tpu_custom_call" | custom-call | flops 1073741824 | bytes 6291456 | tf_op jit(solution)/shard_map/interpolate/pallas_call | solution.py:328
  (23 shorter events, 0.1 us)
Async XLA Ops:
  0.7 1.0 %copy-start = (bf16[1,64,2048]{2,1,0:T(8,128)(2,1)S(1)}, bf16[1,64,2048]{2,1,0:T(8,128)(2,1)}, u32[]{:S(2)}) copy-start(bf16[1,64,2048]{2,1,0:T(8,128)(2,1)} %param.7) | copy-start | bytes 786436
  1.7 0.7 %copy-start.1 = (s32[4,4,4]{2,1,0:T(4,128)S(1)}, s32[4,4,4]{2,1,0:T(4,128)}, u32[]{:S(2)}) copy-start(s32[4,4,4]{2,1,0:T(4,128)} %starts_ref.1) | copy-start | bytes 772
  2.4 0.7 %copy-start.2 = (s32[4,4]{1,0:T(4,128)S(1)}, s32[4,4]{1,0:T(4,128)}, u32[]{:S(2)}) copy-start(s32[4,4]{1,0:T(4,128)} %defocus_ref.3) | copy-start | bytes 196
  3.0 1.3 %copy-start.3 = (bf16[5,256,512]{2,1,0:T(8,128)(2,1)S(1)}, bf16[5,256,512]{2,1,0:T(8,128)(2,1)}, u32[]{:S(2)}) copy-start(bf16[5,256,512]{2,1,0:T(8,128)(2,1)} %constant.22.clone.matrix_ref) | copy-start | bytes 3932164
  4.4 0.7 %copy-start.5 = (f32[24,256]{1,0:T(8,128)S(1)}, f32[24,256]{1,0:T(8,128)}, u32[]{:S(2)}) copy-start(f32[24,256]{1,0:T(8,128)} %constant.21.clone.lines_ref) | copy-start | bytes 73732
  8.8 11.6 %collective-permute-start.11 = (bf16[64,640]{1,0:T(8,128)(2,1)S(1)}, bf16[64,640]{1,0:T(8,128)(2,1)S(1)}, u32[]{:S(2)}, u32[]{:S(2)}) collective-permute-start(bf16[64,640]{1,0:T(8,128)(2,1)S(1)} %get-tuple-element.22), channel_id=1, source_target_pairs={{0,3},{1,2},{2,1},{3,0},{4,7},{5,6},{6,5},{7,4},{8,11},{9,10},{10,... | collective-permute-start | bytes 245768 | tf_op jit(solution)/shard_map/ppermute | solution.py:347
  13.9 1.0 %copy-start.4 = (f32[264,256]{1,0:T(8,128)S(1)}, f32[264,256]{1,0:T(8,128)}, u32[]{:S(2)}) copy-start(f32[264,256]{1,0:T(8,128)} %constant.23.clone.table_ref) | copy-start | bytes 811012
  18.0 5.0 %collective-permute-start.3 = (bf16[64,640]{1,0:T(8,128)(2,1)S(1)}, bf16[64,640]{1,0:T(8,128)(2,1)S(1)}, u32[]{:S(2)}, u32[]{:S(2)}) collective-permute-start(bf16[64,640]{1,0:T(8,128)(2,1)S(1)} %get-tuple-element.20), channel_id=1, source_target_pairs={{0,1},{1,0},{2,3},{3,2},{4,5},{5,4},{6,7},{7,6},{8,9},{9,8},{10,11... | collective-permute-start | bytes 245768 | tf_op jit(solution)/shard_map/ppermute | solution.py:347
  18.1 6.0 %collective-permute-start.7 = (bf16[64,640]{1,0:T(8,128)(2,1)S(1)}, bf16[64,640]{1,0:T(8,128)(2,1)S(1)}, u32[]{:S(2)}, u32[]{:S(2)}) collective-permute-start(bf16[64,640]{1,0:T(8,128)(2,1)S(1)} %get-tuple-element.21), channel_id=1, source_target_pairs={{0,2},{1,3},{2,0},{3,1},{4,6},{5,7},{6,4},{7,5},{8,10},{9,11},{10,... | collective-permute-start | bytes 245768 | tf_op jit(solution)/shard_map/ppermute | solution.py:347
  18.7 6.9 %collective-permute-start.1 = (bf16[64,640]{1,0:T(8,128)(2,1)S(1)}, bf16[64,640]{1,0:T(8,128)(2,1)S(1)}, u32[]{:S(2)}, u32[]{:S(2)}) collective-permute-start(bf16[64,640]{1,0:T(8,128)(2,1)S(1)} %get-tuple-element.19.refs_0_), channel_id=1, source_target_pairs={{0,8},{4,12},{8,0},{12,4},{1,9},{5,13},{9,1},{13,5},{2,10},{6,14},... | collective-permute-start | bytes 245768 | tf_op jit(solution)/shard_map/ppermute | solution.py:347
  20.4 5.2 %collective-permute-start = (bf16[64,640]{1,0:T(8,128)(2,1)S(1)}, bf16[64,640]{1,0:T(8,128)(2,1)S(1)}, u32[]{:S(2)}, u32[]{:S(2)}) collective-permute-start(bf16[64,640]{1,0:T(8,128)(2,1)S(1)} %get-tuple-element.19.refs_0_), channel_id=1, source_target_pairs={{0,4},{4,0},{8,12},{12,8},{1,5},{5,1},{9,13},{13,9},{2,6},{6,2},{1... | collective-permute-start | bytes 245768 | tf_op jit(solution)/shard_map/ppermute | solution.py:347
  20.4 5.8 %collective-permute-start.13 = (bf16[64,640]{1,0:T(8,128)(2,1)S(1)}, bf16[64,640]{1,0:T(8,128)(2,1)S(1)}, u32[]{:S(2)}, u32[]{:S(2)}) collective-permute-start(bf16[64,640]{1,0:T(8,128)(2,1)S(1)} %collective-permute-done.11.refs_12_), channel_id=1, source_target_pairs={{0,8},{4,12},{8,0},{12,4},{1,9},{5,13},{9,1},{13,5},{2,10},{6,14},... | collective-permute-start | bytes 245768 | tf_op jit(solution)/shard_map/ppermute | solution.py:347
  23.0 3.4 %collective-permute-start.12 = (bf16[64,640]{1,0:T(8,128)(2,1)S(1)}, bf16[64,640]{1,0:T(8,128)(2,1)S(1)}, u32[]{:S(2)}, u32[]{:S(2)}) collective-permute-start(bf16[64,640]{1,0:T(8,128)(2,1)S(1)} %collective-permute-done.11.refs_12_), channel_id=1, source_target_pairs={{0,4},{4,0},{8,12},{12,8},{1,5},{5,1},{9,13},{13,9},{2,6},{6,2},{1... | collective-permute-start | bytes 245768 | tf_op jit(solution)/shard_map/ppermute | solution.py:347
  24.1 4.4 %collective-permute-start.5 = (bf16[64,640]{1,0:T(8,128)(2,1)S(1)}, bf16[64,640]{1,0:T(8,128)(2,1)S(1)}, u32[]{:S(2)}, u32[]{:S(2)}) collective-permute-start(bf16[64,640]{1,0:T(8,128)(2,1)S(1)} %collective-permute-done.3.refs_4_), channel_id=1, source_target_pairs={{0,8},{4,12},{8,0},{12,4},{1,9},{5,13},{9,1},{13,5},{2,10},{6,14},... | collective-permute-start | bytes 245768 | tf_op jit(solution)/shard_map/ppermute | solution.py:347
  25.6 2.9 %collective-permute-start.4 = (bf16[64,640]{1,0:T(8,128)(2,1)S(1)}, bf16[64,640]{1,0:T(8,128)(2,1)S(1)}, u32[]{:S(2)}, u32[]{:S(2)}) collective-permute-start(bf16[64,640]{1,0:T(8,128)(2,1)S(1)} %collective-permute-done.3.refs_4_), channel_id=1, source_target_pairs={{0,4},{4,0},{8,12},{12,8},{1,5},{5,1},{9,13},{13,9},{2,6},{6,2},{1... | collective-permute-start | bytes 245768 | tf_op jit(solution)/shard_map/ppermute | solution.py:347
  25.6 4.9 %collective-permute-start.9 = (bf16[64,640]{1,0:T(8,128)(2,1)S(1)}, bf16[64,640]{1,0:T(8,128)(2,1)S(1)}, u32[]{:S(2)}, u32[]{:S(2)}) collective-permute-start(bf16[64,640]{1,0:T(8,128)(2,1)S(1)} %collective-permute-done.7.refs_8_), channel_id=1, source_target_pairs={{0,8},{4,12},{8,0},{12,4},{1,9},{5,13},{9,1},{13,5},{2,10},{6,14},... | collective-permute-start | bytes 245768 | tf_op jit(solution)/shard_map/ppermute | solution.py:347
  26.2 4.3 %collective-permute-start.8 = (bf16[64,640]{1,0:T(8,128)(2,1)S(1)}, bf16[64,640]{1,0:T(8,128)(2,1)S(1)}, u32[]{:S(2)}, u32[]{:S(2)}) collective-permute-start(bf16[64,640]{1,0:T(8,128)(2,1)S(1)} %collective-permute-done.7.refs_8_), channel_id=1, source_target_pairs={{0,4},{4,0},{8,12},{12,8},{1,5},{5,1},{9,13},{13,9},{2,6},{6,2},{1... | collective-permute-start | bytes 245768 | tf_op jit(solution)/shard_map/ppermute | solution.py:347
  26.3 4.1 %collective-permute-start.2 = (bf16[64,640]{1,0:T(8,128)(2,1)S(1)}, bf16[64,640]{1,0:T(8,128)(2,1)S(1)}, u32[]{:S(2)}, u32[]{:S(2)}) collective-permute-start(bf16[64,640]{1,0:T(8,128)(2,1)S(1)} %collective-permute-done.1.refs_2_), channel_id=1, source_target_pairs={{0,4},{4,0},{8,12},{12,8},{1,5},{5,1},{9,13},{13,9},{2,6},{6,2},{1... | collective-permute-start | bytes 245768 | tf_op jit(solution)/shard_map/ppermute | solution.py:347
  28.5 2.0 %collective-permute-start.14 = (bf16[64,640]{1,0:T(8,128)(2,1)S(1)}, bf16[64,640]{1,0:T(8,128)(2,1)S(1)}, u32[]{:S(2)}, u32[]{:S(2)}) collective-permute-start(bf16[64,640]{1,0:T(8,128)(2,1)S(1)} %collective-permute-done.13.refs_14_), channel_id=1, source_target_pairs={{0,4},{4,0},{8,12},{12,8},{1,5},{5,1},{9,13},{13,9},{2,6},{6,2},{1... | collective-permute-start | bytes 245768 | tf_op jit(solution)/shard_map/ppermute | solution.py:347
  28.5 2.0 %collective-permute-start.6 = (bf16[64,640]{1,0:T(8,128)(2,1)S(1)}, bf16[64,640]{1,0:T(8,128)(2,1)S(1)}, u32[]{:S(2)}, u32[]{:S(2)}) collective-permute-start(bf16[64,640]{1,0:T(8,128)(2,1)S(1)} %collective-permute-done.5.refs_6_), channel_id=1, source_target_pairs={{0,4},{4,0},{8,12},{12,8},{1,5},{5,1},{9,13},{13,9},{2,6},{6,2},{1... | collective-permute-start | bytes 245768 | tf_op jit(solution)/shard_map/ppermute | solution.py:347
  30.5 1.3 %collective-permute-start.10 = (bf16[64,640]{1,0:T(8,128)(2,1)S(1)}, bf16[64,640]{1,0:T(8,128)(2,1)S(1)}, u32[]{:S(2)}, u32[]{:S(2)}) collective-permute-start(bf16[64,640]{1,0:T(8,128)(2,1)S(1)} %collective-permute-done.9.refs_10_), channel_id=1, source_target_pairs={{0,4},{4,0},{8,12},{12,8},{1,5},{5,1},{9,13},{13,9},{2,6},{6,2},{1... | collective-permute-start | bytes 245768 | tf_op jit(solution)/shard_map/ppermute | solution.py:347

commit v4 on v3

--- a/solution.py
+++ b/solution.py
@@ -44,32 +44,25 @@
         return high, (table - high.astype(np.float64)).astype(jnp.bfloat16)
 
     matrices = np.stack([*split(ends), *split(waves), np.concatenate([m0.T, m4.T], 1).astype(jnp.bfloat16)])
-    freq = [np.concatenate([k0, s0]), np.concatenate([k4, k4])]
-    turns = []
-    for j in (1, 2, 3):
-        freq += [RADIX * np.arange(size) + j] * 2
-        angle = 2.0 * np.pi * np.arange(size) * j / columns
-        turns += [np.cos(angle), np.sin(angle)]
-    freq = np.stack(freq)
-    count = np.where((freq == 0) | (freq == columns // 2), 1.0, 2.0)
-    fold = np.minimum(freq, columns - freq)
-    ramp = count * (fold + 0.5) / (0.5 * columns) / columns
-    lines = np.concatenate([ramp, fold * fold, np.stack(turns + [np.zeros(size)] * 2)])
-    return matrices, lines.astype(np.float32)
-
-
-def row_tables(full_rows):
-    half = full_rows // 2
-    y = np.arange(full_rows)[:, None]
-    freq = np.concatenate([np.arange(half + 1), np.arange(1, half)])
-    angle = 2.0 * np.pi * (y * freq[None, :] % full_rows) / full_rows
-    waves = np.where(np.arange(full_rows)[None, :] <= half, np.cos(angle), np.sin(angle))
-    count = np.where((freq == 0) | (freq == half), 1.0, 2.0) / full_rows
-    return np.concatenate([waves, count[None], (freq * freq)[None], np.zeros((6, full_rows))]).astype(np.float32)
+    return matrices
+
+
+def column_lines(columns):
+    size = columns // RADIX
+    half = size // 2
+    line = lax.broadcasted_iota(jnp.int32, (8, size), 0)
+    u = lax.broadcasted_iota(jnp.int32, (8, size), 1)
+    freq = jnp.where(line == 0, RADIX * jnp.where(u <= half, u, u - half), RADIX * (u & (half - 1)) + 4)
+    freq = jnp.where(line < 2, freq, RADIX * u + line // 2)
+    fold = jnp.minimum(freq, columns - freq)
+    count = jnp.where((fold == 0) | (fold == columns // 2), 1.0, 2.0)
+    gain = count * (fold.astype(jnp.float32) + 0.5) * (2.0 / (columns * columns))
+    angle = (u * (line + 1)).astype(jnp.float32) * (2.0 * math.pi / columns)
+    return fold * fold, gain, jnp.cos(angle), jnp.sin(angle)
 
 
 def flip_sign(squares, defocus, length):
-    cycles = lax.div(squares.astype(jnp.int32) * defocus, jnp.int32(length * length))
+    cycles = lax.div(squares * defocus, jnp.int32(length * length))
     return (1 - 2 * (cycles & 1)).astype(jnp.float32)
 
 
@@ -80,20 +73,28 @@
     return copies
 
 
-def column_kernel(slots, slices_owned, image_ref, lines_ref, matrix_ref, defocus_ref, starts_ref, first_ref, *refs):
+def reach_of(angle):
+    line = jnp.full((8, XBW), angle, jnp.float32)
+    cosine, sine = jnp.cos(line), jnp.sin(line)
+    lowest = 0.5 * XBW + jnp.minimum((XBW - 1) * cosine, 0.0) - 0.5 * (SLAB - 1) * jnp.abs(sine)
+    first = jnp.clip(jnp.floor(lowest) - 8.0, 0.0, float(BAND - REACH))
+    return cosine[:1], sine[:1], jnp.max(first).astype(jnp.int32)
+
+
+def column_kernel(slots, slices_owned, image_ref, matrix_ref, angle_ref, defocus_ref, starts_ref, *refs):
     out_refs = refs[:slots]
-    image, lines, matrix, defocus, starts, first_tap, zhi, zlo, ends, waves, turned, sems = refs[slots:]
+    image, matrix, angles, defocus, starts, zhi, zlo, ends, waves, turned, out, sems, out_sems = refs[slots:]
     rows, columns = image.shape
     size = columns // RADIX
     copies = fetched(
-        [image_ref, lines_ref] + [matrix_ref.at[i] for i in range(5)] + [defocus_ref, starts_ref, first_ref],
-        [image, lines] + [matrix.at[i] for i in range(5)] + [defocus, starts, first_tap],
+        [image_ref, angle_ref, defocus_ref, starts_ref] + [matrix_ref.at[i] for i in range(5)],
+        [image, angles, defocus, starts] + [matrix.at[i] for i in range(5)],
         sems,
     )
     tilt = lax.axis_index("tilt")
+    squares, ramp, cosine_turns, sine_turns = column_lines(columns)
+    turns = [t[j : j + 1, :] for j in range(3) for t in (cosine_turns, sine_turns)]
     copies[0].wait()
-    copies[1].wait()
-    turns = [lines[16 + i : 17 + i, :] for i in range(6)]
 
     def butterfly(step, carry):
         here = pl.ds(pl.multiple_of(step * 16, 16), 16)
@@ -113,7 +114,7 @@
         return carry
 
     lax.fori_loop(0, rows // 16, butterfly, 0)
-    for copy in copies[2:6]:
+    for copy in copies[4:]:
         copy.wait()
 
     def product(first, count, table, here):
@@ -129,11 +130,11 @@
         real, imag = mixed[2 * j * rows : (2 * j + 1) * rows], mixed[(2 * j + 1) * rows : (2 * j + 2) * rows]
         spectrum += [real[:, :size] + imag[:, size:], imag[:, :size] - real[:, size:]]
 
-    for copy in copies[6:]:
+    for copy in copies[1:4]:
         copy.wait()
     slabs = [(tilt ^ slot) * slices_owned // SLAB for slot in range(slots)]
     gains = [
-        flip_sign(lines[8:16, :], defocus[tilt, slabs[slot]], columns) * lines[:8, :] for slot in range(slots)
+        flip_sign(squares, defocus[tilt, slab], columns) * ramp for slab in slabs
     ]
     filtered = [
         jnp.concatenate(
@@ -167,68 +168,85 @@
     lax.fori_loop(0, slots * rows // 8, inverse_butterfly, 0)
 
     lane = lax.broadcasted_iota(jnp.int32, (rows, MAIN), 1) // REST
-    for slot in range(slots):
+    _, _, first_tap = reach_of(angles[tilt])
+    sends = []
+    for slot in reversed(range(slots)):
         rest = jnp.zeros((rows, MAIN), jnp.float32)
         for block in range(XBLK):
-            start = starts[tilt, slabs[slot], block] + first_tap[tilt]
+            start = starts[tilt, slabs[slot], block] + first_tap
             base = pl.multiple_of(jnp.minimum((start // 128) * 128, columns - WINDOW), 128)
             window = turned[slot * rows : (slot + 1) * rows, pl.ds(base, WINDOW)]
             shift = base - start
             reach = pltpu.roll(window, jnp.where(shift < 0, shift + WINDOW, shift), 1)[:, : 2 * MAIN]
-            out_refs[slot][:, block * MAIN : (block + 1) * MAIN] = reach[:, :MAIN].astype(jnp.bfloat16)
+            out[slot, :, block * MAIN : (block + 1) * MAIN] = reach[:, :MAIN].astype(jnp.bfloat16)
             last = reach[:, MAIN:]
             rest = jnp.where(lane == block, pltpu.roll(last, block * REST, 1) if block else last, rest)
-        out_refs[slot][:, XBLK * MAIN :] = rest.astype(jnp.bfloat16)
-
-
-def column_filtered(slots, slices_owned, defocus, starts, first_tap, image):
+        out[slot, :, XBLK * MAIN :] = rest.astype(jnp.bfloat16)
+        sends.append(pltpu.make_async_copy(out.at[slot], out_refs[slot], out_sems.at[slot]))
+        sends[-1].start()
+    for copy in sends:
+        copy.wait()
+
+
+def column_filtered(slots, slices_owned, image, angles, defocus, starts):
     rows, columns = image.shape
     size = columns // RADIX
-    matrices, lines = column_tables(columns)
-    vmem, away = pl.BlockSpec(memory_space=pltpu.VMEM), pl.BlockSpec(memory_space=pl.ANY)
+    matrices = column_tables(columns)
+    away = pl.BlockSpec(memory_space=pl.ANY)
     return pl.pallas_call(
         functools.partial(column_kernel, slots, slices_owned),
         out_shape=[jax.ShapeDtypeStruct((rows, PACKED), jnp.bfloat16)] * slots,
-        in_specs=[away] * 6,
-        out_specs=[vmem] * slots,
+        in_specs=[away] * 5,
+        out_specs=[away] * slots,
         scratch_shapes=[
             pltpu.VMEM((rows, columns), jnp.bfloat16),
-            pltpu.VMEM(lines.shape, jnp.float32),
             pltpu.VMEM(matrices.shape, jnp.bfloat16),
+            pltpu.SMEM(angles.shape, jnp.float32),
             pltpu.SMEM(defocus.shape, jnp.int32),
             pltpu.SMEM(starts.shape, jnp.int32),
-            pltpu.SMEM(first_tap.shape, jnp.int32),
             pltpu.VMEM((8, rows, size), jnp.bfloat16),
             pltpu.VMEM((8, rows, size), jnp.bfloat16),
             pltpu.VMEM((2, slots * rows, size), jnp.float32),
             pltpu.VMEM((6, slots * rows, 2 * size), jnp.float32),
             pltpu.VMEM((slots * rows, columns), jnp.float32),
-            pltpu.SemaphoreType.DMA((10,)),
+            pltpu.VMEM((slots, rows, PACKED), jnp.bfloat16),
+            pltpu.SemaphoreType.DMA((9,)),
+            pltpu.SemaphoreType.DMA((slots,)),
         ],
-        compiler_params=pltpu.CompilerParams(vmem_limit_bytes=40 * 2**20),
+        compiler_params=pltpu.CompilerParams(vmem_limit_bytes=60 * 2**20),
         cost_estimate=pl.CostEstimate(flops=2 * rows * columns * 2048 * 2, bytes_accessed=4 * 2**20, transcendentals=0),
         name="column_filter",
-    )(image, jnp.asarray(lines), jnp.asarray(matrices), defocus, starts, first_tap)
-
-
-def prepare_kernel(slots, slices_owned, passed, table_ref, defocus_ref, first_ref, cosine_ref, sine_ref, *refs):
+    )(image, jnp.asarray(matrices), angles, defocus, starts)
+
+
+def prepare_kernel(slots, slices_owned, passed, angles, defocus, *refs):
     rows_ref, weights_ref = refs[passed : passed + 2]
-    table, defocus, first_tap, cosines, sines, mine, order, sems = refs[2 * passed + 2 :]
-    copies = fetched(
-        [table_ref, defocus_ref, first_ref, cosine_ref, sine_ref], [table, defocus, first_tap, cosines, sines], sems
-    )
+    waves, mine, order = refs[2 * passed + 2 :]
     tilt, row = lax.axis_index("tilt"), lax.axis_index("row")
     slab, local_first = tilt * slices_owned // SLAB, tilt * slices_owned % SLAB
-    full_rows = table.shape[1]
+    full_rows = waves.shape[0]
     rows = rows_ref.shape[0] // slots
-    for copy in copies:
-        copy.wait()
-    own = table[pl.ds(pl.multiple_of(row * rows, rows), rows), :]
+    half = full_rows // 2
+
+    def row_waves(block, carry):
+        here = pl.ds(pl.multiple_of(block * rows, rows), rows)
+        y = block * rows + lax.broadcasted_iota(jnp.int32, (rows, full_rows), 0)
+        column = lax.broadcasted_iota(jnp.int32, (rows, full_rows), 1)
+        freq = jnp.where(column <= half, column, column - half)
+        angle = ((y * freq) & (full_rows - 1)).astype(jnp.float32) * (2.0 * math.pi / full_rows)
+        waves[here, :] = jnp.where(column <= half, jnp.cos(angle), jnp.sin(angle))
+        return carry
+
+    lax.fori_loop(0, full_rows // rows, row_waves, 0)
+    own = waves[pl.ds(pl.multiple_of(row * rows, rows), rows), :]
+    column = lax.broadcasted_iota(jnp.int32, (8, full_rows), 1)
+    freq = jnp.where(column <= half, column, column - half)
+    count = jnp.where((freq == 0) | (freq == half), 1.0, 2.0) / full_rows
     for slot in range(slots):
-        sign = flip_sign(table[full_rows + 1 : full_rows + 2, :], defocus[tilt ^ slot, slab], full_rows)
-        mine[slot * rows : (slot + 1) * rows, :] = own * (sign * table[full_rows : full_rows + 1, :])
+        sign = flip_sign(freq * freq, defocus[tilt ^ slot, slab], full_rows)
+        mine[slot * rows : (slot + 1) * rows, :] = own * (sign * count)[:1]
     for block in range(full_rows // rows):
-        order[block * rows : (block + 1) * rows, :] = table[pl.ds(pl.multiple_of((row ^ block) * rows, rows), rows), :]
+        order[block * rows : (block + 1) * rows, :] = waves[pl.ds(pl.multiple_of((row ^ block) * rows, rows), rows), :]
     rows_ref[...] = lax.dot_general(
         mine[...],
         order[...],
@@ -239,10 +257,10 @@
 
     column = lax.broadcasted_iota(jnp.int32, (1, XBW), 1).astype(jnp.float32)
     place = lax.broadcasted_iota(jnp.int32, (2 * MAIN, XBW), 0)
-    place = jnp.where(place < MAIN, place, MAIN + place % REST)
+    place = jnp.where(place < MAIN, place, MAIN + place % REST).astype(jnp.float32)
     for slot in range(slots):
-        cosine, sine = cosines[tilt ^ slot], sines[tilt ^ slot]
-        tap = (place + first_tap[tilt ^ slot]).astype(jnp.float32)
+        cosine, sine, first_tap = reach_of(angles[tilt ^ slot])
+        tap = place + first_tap.astype(jnp.float32)
 
         def one_slice(c, carry):
             offset = (local_first + c).astype(jnp.float32) - 0.5 * (SLAB - 1)
@@ -254,9 +272,9 @@
         lax.fori_loop(0, slices_owned, one_slice, 0)
 
 
-def prepared(slots, slices_owned, rows, full_rows, defocus, first_tap, cosines, sines, passed):
-    vmem, away = pl.BlockSpec(memory_space=pltpu.VMEM), pl.BlockSpec(memory_space=pl.ANY)
-    table = row_tables(full_rows)
+def prepared(slots, slices_owned, rows, full_rows, angles, defocus, passed):
+    smem, vmem = pl.BlockSpec(memory_space=pltpu.SMEM), pl.BlockSpec(memory_space=pltpu.VMEM)
+    handed = pl.BlockSpec(memory_space=pl.ANY)
     count = len(passed)
     out = pl.pallas_call(
         functools.partial(prepare_kernel, slots, slices_owned, count),
@@ -265,23 +283,18 @@
             jax.ShapeDtypeStruct((slots, 2 * MAIN, slices_owned * XBW), jnp.bfloat16),
         ]
         + [jax.ShapeDtypeStruct(p.shape, p.dtype) for p in passed],
-        in_specs=[away] * (5 + count),
-        out_specs=[vmem] * 2 + [away] * count,
+        in_specs=[smem] * 2 + [handed] * count,
+        out_specs=[vmem] * 2 + [handed] * count,
         scratch_shapes=[
-            pltpu.VMEM(table.shape, jnp.float32),
-            pltpu.SMEM(defocus.shape, jnp.int32),
-            pltpu.SMEM(first_tap.shape, jnp.int32),
-            pltpu.SMEM(cosines.shape, jnp.float32),
-            pltpu.SMEM(sines.shape, jnp.float32),
+            pltpu.VMEM((full_rows, full_rows), jnp.float32),
             pltpu.VMEM((slots * rows, full_rows), jnp.float32),
             pltpu.VMEM((full_rows, full_rows), jnp.float32),
-            pltpu.SemaphoreType.DMA((5,)),
         ],
-        input_output_aliases={5 + i: 2 + i for i in range(count)},
+        input_output_aliases={2 + i: 2 + i for i in range(count)},
         compiler_params=pltpu.CompilerParams(vmem_limit_bytes=32 * 2**20),
         cost_estimate=pl.CostEstimate(flops=2**30, bytes_accessed=6 * 2**20, transcendentals=0),
         name="prepare",
-    )(jnp.asarray(table), defocus, first_tap, cosines, sines, *passed)
+    )(angles, defocus, *passed)
     return out[0], out[1], out[2:]
 
 
@@ -360,18 +373,14 @@
     _, rows, _ = projections.shape
     row_devices, tilt_devices = lax.axis_size("row"), lax.axis_size("tilt")
     slices_owned = SLICES // tilt_devices
-    cosines, sines = jnp.cos(tilt_angle), jnp.sin(tilt_angle)
-    lowest = 0.5 * XBW + jnp.minimum((XBW - 1) * cosines, 0.0) - 0.5 * (SLAB - 1) * jnp.abs(sines)
-    first_tap = jnp.clip(jnp.floor(lowest).astype(jnp.int32) - 8, 0, BAND - REACH)
-    sent = column_filtered(tilt_devices, slices_owned, defocus, band_start, first_tap, projections[0])
-    last = tilt_devices - 1
-    arrived = {last: exchange(sent[last], "tilt", last)}
-    row_filters, weights, sent = prepared(
-        tilt_devices, slices_owned, rows, rows * row_devices, defocus, first_tap, cosines, sines, sent[:last]
+    sent = column_filtered(tilt_devices, slices_owned, projections[0], tilt_angle, defocus, band_start)
+    arrived = {0: sent[0]}
+    for d in range(tilt_devices - 1, 1, -1):
+        arrived[d] = exchange(sent[d], "tilt", d)
+    row_filters, weights, (near,) = prepared(
+        tilt_devices, slices_owned, rows, rows * row_devices, tilt_angle, defocus, sent[1:2]
     )
-    for d in range(last - 1, 0, -1):
-        arrived[d] = exchange(sent[d], "tilt", d)
-    arrived[0] = sent[0]
+    arrived[1] = exchange(near, "tilt", 1)
     patches = [gather_rows(arrived[d]) for d in range(tilt_devices)]
     return interpolated(row_filters, weights, patches, 1.0 / math.sqrt(tilt_devices))
 

time: 34.3 us -> 32.1 us (0.936)
  local copies, waits for them, and re-layouts: 6.02 us -> 3.11 us
  Pallas kernels: 9.04 us -> 11.6 us
  waiting for transfers between devices: 7.9 us -> 6.12 us
    unnamed x12 -> x8, local copies, waits for them, and re-layouts: 5.33 us -> 3.11 us
    ppermute x15, waiting for transfers between devices: 7.9 us -> 6.12 us  [exchange(): return lax.ppermute(array, axis, [(i, i ^ distance) for i in range(count)])]
    pallas_call x1, Pallas kernels: 3.72 us -> 5.18 us  [column_filtered(): pl.pallas_call(functools.partial(column_kernel, slots, slices_owned), out...]
    pallas_call x1, Pallas kernels: 3.11 us -> 4.18 us  [prepared(): pl.pallas_call(functools.partial(prepare_kernel, slots, slices_owned, cou...]
    cos x1 -> x0, local copies, waits for them, and re-layouts: 0.69 us -> none  [per_device(): cosines, sines = (jnp.cos(tilt_angle), jnp.sin(tilt_angle))]
  transfers between devices with their start and end apart: 15 -> 15, of which waited for: 5 -> 5; matrix products, arithmetic and copies ran while one was open for 0% -> 0% of each run, Pallas kernels for 9% -> 13%
where the time goes in v4:
time: 32.1 us; the launch traced here: 31.9 us
  Pallas kernels  11.6 us (36%)
  starting transfers between devices  11 us (34%)
  waiting for transfers between devices  6.12 us (19%)
  local copies, waits for them, and re-layouts  3.11 us (10%)
    ppermute x15, starting transfers between devices, exchange(): return lax.ppermute(array, axis, [(i, i ^ distance) for i in range(count)])  11 us
    ppermute x15, waiting for transfers between devices, exchange(): return lax.ppermute(array, axis, [(i, i ^ distance) for i in range(count)])  6.12 us
    pallas_call x1, Pallas kernels, column_filtered(): pl.pallas_call(functools.partial(column_kernel, slots, slices_owned), out...  5.18 us
    pallas_call x1, Pallas kernels, prepared(): pl.pallas_call(functools.partial(prepare_kernel, slots, slices_owned, cou...  4.18 us
    unnamed x8, local copies, waits for them, and re-layouts  3.11 us
    pallas_call x1, Pallas kernels, interpolated(): pl.pallas_call(functools.partial(interpolate_kernel, slots, row_devices,...  2.22 us
  transfers between devices with their start and end apart: 15, of which 5 were waited for; matrix products, arithmetic and copies ran while one was open for 0% of the time, Pallas kernels for 13%

profile of v4, /device:TPU:0, one launch (start us, length us, event | category | flops | bytes accessed | tf_op | source)
XLA Modules:
  0.0 31.9 jit_solution(558202469469559720)
XLA Ops:
  0.0 5.2 %column_filter.1 = (bf16[64,640]{1,0:T(8,128)(2,1)}, bf16[64,640]{1,0:T(8,128)(2,1)}, bf16[64,640]{1,0:T(8,128)(2,1)}, bf16[64,640]{1,0:T(8,128)(2,1)}) custom-call(bf16[64,2048]{1,0:T(8,128)(2,1)} %bitcast.1, bf16[5,256,512]{2,1,0:T(8,128)(2,1)} %constant.2.clone.matrix_ref, f32[4]{0:T(128)} %angles.1, s32[4,4]{1,0:T(4,128)} %defocus.1, s32[4,4,4]{2,1,0:T(4,128)} %starts_ref.1), custom_call_target="tpu_custom_call" | custom-call | flops 1073741824 | bytes 4194304 | tf_op jit(solution)/shard_map/column_filter/pallas_call | solution.py:196
  5.2 3.0 %collective-permute-start.1 = (bf16[64,640]{1,0:T(8,128)(2,1)}, bf16[64,640]{1,0:T(8,128)(2,1)S(1)}, u32[]{:S(2)}, u32[]{:S(2)}) collective-permute-start(bf16[64,640]{1,0:T(8,128)(2,1)} %get-tuple-element.15.refs_0_), channel_id=1, source_target_pairs={{0,8},{4,12},{8,0},{12,4},{1,9},{5,13},{9,1},{13,5},{2,10},{6,14},... | collective-permute-start | bytes 245768 | tf_op jit(solution)/shard_map/ppermute | solution.py:360
  8.2 2.6 %collective-permute-start.7 = (bf16[64,640]{1,0:T(8,128)(2,1)}, bf16[64,640]{1,0:T(8,128)(2,1)S(1)}, u32[]{:S(2)}, u32[]{:S(2)}) collective-permute-start(bf16[64,640]{1,0:T(8,128)(2,1)} %get-tuple-element.17), channel_id=1, source_target_pairs={{0,2},{1,3},{2,0},{3,1},{4,6},{5,7},{6,4},{7,5},{8,10},{9,11},{10,... | collective-permute-start | bytes 245768 | tf_op jit(solution)/shard_map/ppermute | solution.py:360
  10.8 1.4 %collective-permute-start.11 = (bf16[64,640]{1,0:T(8,128)(2,1)}, bf16[64,640]{1,0:T(8,128)(2,1)S(1)}, u32[]{:S(2)}, u32[]{:S(2)}) collective-permute-start(bf16[64,640]{1,0:T(8,128)(2,1)} %get-tuple-element.18), channel_id=1, source_target_pairs={{0,3},{1,2},{2,1},{3,0},{4,7},{5,6},{6,5},{7,4},{8,11},{9,10},{10,... | collective-permute-start | bytes 245768 | tf_op jit(solution)/shard_map/ppermute | solution.py:360
  12.2 0.9 %copy-done.1 = bf16[64,640]{1,0:T(8,128)(2,1)S(1)} copy-done((bf16[64,640]{1,0:T(8,128)(2,1)S(1)}, bf16[64,640]{1,0:T(8,128)(2,1)}, u32[]{:S(2)}) %copy-start.1) | copy-done | bytes 81944
  13.0 0.7 %copy-done.2 = s32[4,4]{1,0:T(4,128)S(1)} copy-done((s32[4,4]{1,0:T(4,128)S(1)}, s32[4,4]{1,0:T(4,128)}, u32[]{:S(2)}) %copy-start.2) | copy-done | bytes 88
  13.7 0.7 %copy-done.3 = f32[4]{0:T(128)S(1)} copy-done((f32[4]{0:T(128)S(1)}, f32[4]{0:T(128)}, u32[]{:S(2)}) %copy-start.3) | copy-done | bytes 40
  14.4 4.2 %prepare.1 = (bf16[256,256]{1,0:T(8,128)(2,1)S(1)}, bf16[4,256,2048]{2,1,0:T(8,128)(2,1)S(1)}, bf16[64,640]{1,0:T(8,128)(2,1)S(1)}) custom-call(f32[4]{0:T(128)S(1)} %copy-done.3, s32[4,4]{1,0:T(4,128)S(1)} %copy-done.2, bf16[64,640]{1,0:T(8,128)(2,1)S(1)} %copy-done.1), custom_call_target="tpu_custom_call", output_to_operand_aliasing={{2}: (2, {})} | custom-call | flops 1073741824 | bytes 6291456 | tf_op jit(solution)/shard_map/prepare/pallas_call | solution.py:279
  18.6 0.3 collective-permute-start.3
  18.9 0.0 collective-permute-done.7.refs_8_
  18.9 0.5 %collective-permute-start.9 = (bf16[64,640]{1,0:T(8,128)(2,1)S(1)}, bf16[64,640]{1,0:T(8,128)(2,1)S(1)}, u32[]{:S(2)}, u32[]{:S(2)}) collective-permute-start(bf16[64,640]{1,0:T(8,128)(2,1)S(1)} %collective-permute-done.7.refs_8_), channel_id=1, source_target_pairs={{0,8},{4,12},{8,0},{12,4},{1,9},{5,13},{9,1},{13,5},{2,10},{6,14},... | collective-permute-start | bytes 245768 | tf_op jit(solution)/shard_map/ppermute | solution.py:360
  19.4 0.0 collective-permute-done.11.refs_12_
  19.4 1.6 %collective-permute-start.13 = (bf16[64,640]{1,0:T(8,128)(2,1)S(1)}, bf16[64,640]{1,0:T(8,128)(2,1)S(1)}, u32[]{:S(2)}, u32[]{:S(2)}) collective-permute-start(bf16[64,640]{1,0:T(8,128)(2,1)S(1)} %collective-permute-done.11.refs_12_), channel_id=1, source_target_pairs={{0,8},{4,12},{8,0},{12,4},{1,9},{5,13},{9,1},{13,5},{2,10},{6,14},... | collective-permute-start | bytes 245768 | tf_op jit(solution)/shard_map/ppermute | solution.py:360
  21.0 0.2 collective-permute-start.12
  21.1 1.9 %collective-permute-done.3.refs_4_ = bf16[64,640]{1,0:T(8,128)(2,1)S(1)} collective-permute-done((bf16[64,640]{1,0:T(8,128)(2,1)S(1)}, bf16[64,640]{1,0:T(8,128)(2,1)S(1)}, u32[]{:S(2)}, u32[]{:S(2)}) %collective-permute-start.3) | collective-permute-done | bytes 81952 | tf_op jit(solution)/shard_map/ppermute | solution.py:360
  23.1 0.5 %collective-permute-start.5 = (bf16[64,640]{1,0:T(8,128)(2,1)S(1)}, bf16[64,640]{1,0:T(8,128)(2,1)S(1)}, u32[]{:S(2)}, u32[]{:S(2)}) collective-permute-start(bf16[64,640]{1,0:T(8,128)(2,1)S(1)} %collective-permute-done.3.refs_4_), channel_id=1, source_target_pairs={{0,8},{4,12},{8,0},{12,4},{1,9},{5,13},{9,1},{13,5},{2,10},{6,14},... | collective-permute-start | bytes 245768 | tf_op jit(solution)/shard_map/ppermute | solution.py:360
  23.6 0.5 %collective-permute-done.9.refs_10_ = bf16[64,640]{1,0:T(8,128)(2,1)S(1)} collective-permute-done((bf16[64,640]{1,0:T(8,128)(2,1)S(1)}, bf16[64,640]{1,0:T(8,128)(2,1)S(1)}, u32[]{:S(2)}, u32[]{:S(2)}) %collective-permute-start.9) | collective-permute-done | bytes 81952 | tf_op jit(solution)/shard_map/ppermute | solution.py:360
  24.1 0.5 %collective-permute-start.2 = (bf16[64,640]{1,0:T(8,128)(2,1)S(1)}, bf16[64,640]{1,0:T(8,128)(2,1)S(1)}, u32[]{:S(2)}, u32[]{:S(2)}) collective-permute-start(bf16[64,640]{1,0:T(8,128)(2,1)S(1)} %collective-permute-done.1.refs_2_), channel_id=1, source_target_pairs={{0,4},{4,0},{8,12},{12,8},{1,5},{5,1},{9,13},{13,9},{2,6},{6,2},{1... | collective-permute-start | bytes 245768 | tf_op jit(solution)/shard_map/ppermute | solution.py:360
  24.6 0.9 %collective-permute-done.13.refs_14_ = bf16[64,640]{1,0:T(8,128)(2,1)S(1)} collective-permute-done((bf16[64,640]{1,0:T(8,128)(2,1)S(1)}, bf16[64,640]{1,0:T(8,128)(2,1)S(1)}, u32[]{:S(2)}, u32[]{:S(2)}) %collective-permute-start.13) | collective-permute-done | bytes 81952 | tf_op jit(solution)/shard_map/ppermute | solution.py:360
  25.6 0.5 %collective-permute-start.14 = (bf16[64,640]{1,0:T(8,128)(2,1)S(1)}, bf16[64,640]{1,0:T(8,128)(2,1)S(1)}, u32[]{:S(2)}, u32[]{:S(2)}) collective-permute-start(bf16[64,640]{1,0:T(8,128)(2,1)S(1)} %collective-permute-done.13.refs_14_), channel_id=1, source_target_pairs={{0,4},{4,0},{8,12},{12,8},{1,5},{5,1},{9,13},{13,9},{2,6},{6,2},{1... | collective-permute-start | bytes 245768 | tf_op jit(solution)/shard_map/ppermute | solution.py:360
  26.1 1.4 %collective-permute-done.5.refs_6_ = bf16[64,640]{1,0:T(8,128)(2,1)S(1)} collective-permute-done((bf16[64,640]{1,0:T(8,128)(2,1)S(1)}, bf16[64,640]{1,0:T(8,128)(2,1)S(1)}, u32[]{:S(2)}, u32[]{:S(2)}) %collective-permute-start.5) | collective-permute-done | bytes 81952 | tf_op jit(solution)/shard_map/ppermute | solution.py:360
  27.5 1.2 %collective-permute-done.6.refs_7_ = bf16[64,640]{1,0:T(8,128)(2,1)S(1)} collective-permute-done((bf16[64,640]{1,0:T(8,128)(2,1)S(1)}, bf16[64,640]{1,0:T(8,128)(2,1)S(1)}, u32[]{:S(2)}, u32[]{:S(2)}) %collective-permute-start.6) | collective-permute-done | bytes 81952 | tf_op jit(solution)/shard_map/ppermute | solution.py:360
  28.8 0.9 %copy-done = bf16[64,640]{1,0:T(8,128)(2,1)S(1)} copy-done((bf16[64,640]{1,0:T(8,128)(2,1)S(1)}, bf16[64,640]{1,0:T(8,128)(2,1)}, u32[]{:S(2)}) %copy-start) | copy-done | bytes 81944
  29.7 2.2 %interpolate.1 = bf16[16,64,512]{2,1,0:T(8,128)(2,1)} custom-call(bf16[256,256]{1,0:T(8,128)(2,1)S(1)} %get-tuple-element.13.rows_ref, bf16[4,256,2048]{2,1,0:T(8,128)(2,1)S(1)} %get-tuple-element.14.weights_ref, bf16[64,640]{1,0:T(8,128)(2,1)S(1)} %copy-done, bf16[64,640]{1,0:T(8,128)(2,1)S(1)} %collective-permute-done.refs_1_, ...), custom_call_target="tpu_custom_call" | custom-call | flops 1073741824 | bytes 6291456 | tf_op jit(solution)/shard_map/interpolate/pallas_call | solution.py:341
  (17 shorter events, 0.0 us)
Async XLA Ops:
  5.2 14.2 %collective-permute-start.1 = (bf16[64,640]{1,0:T(8,128)(2,1)}, bf16[64,640]{1,0:T(8,128)(2,1)S(1)}, u32[]{:S(2)}, u32[]{:S(2)}) collective-permute-start(bf16[64,640]{1,0:T(8,128)(2,1)} %get-tuple-element.15.refs_0_), channel_id=1, source_target_pairs={{0,8},{4,12},{8,0},{12,4},{1,9},{5,13},{9,1},{13,5},{2,10},{6,14},... | collective-permute-start | bytes 245768 | tf_op jit(solution)/shard_map/ppermute | solution.py:360
  8.2 12.7 %collective-permute-start = (bf16[64,640]{1,0:T(8,128)(2,1)}, bf16[64,640]{1,0:T(8,128)(2,1)S(1)}, u32[]{:S(2)}, u32[]{:S(2)}) collective-permute-start(bf16[64,640]{1,0:T(8,128)(2,1)} %get-tuple-element.15.refs_0_), channel_id=1, source_target_pairs={{0,4},{4,0},{8,12},{12,8},{1,5},{5,1},{9,13},{13,9},{2,6},{6,2},{1... | collective-permute-start | bytes 245768 | tf_op jit(solution)/shard_map/ppermute | solution.py:360
  8.2 10.6 %collective-permute-start.7 = (bf16[64,640]{1,0:T(8,128)(2,1)}, bf16[64,640]{1,0:T(8,128)(2,1)S(1)}, u32[]{:S(2)}, u32[]{:S(2)}) collective-permute-start(bf16[64,640]{1,0:T(8,128)(2,1)} %get-tuple-element.17), channel_id=1, source_target_pairs={{0,2},{1,3},{2,0},{3,1},{4,6},{5,7},{6,4},{7,5},{8,10},{9,11},{10,... | collective-permute-start | bytes 245768 | tf_op jit(solution)/shard_map/ppermute | solution.py:360
  10.8 8.6 %collective-permute-start.11 = (bf16[64,640]{1,0:T(8,128)(2,1)}, bf16[64,640]{1,0:T(8,128)(2,1)S(1)}, u32[]{:S(2)}, u32[]{:S(2)}) collective-permute-start(bf16[64,640]{1,0:T(8,128)(2,1)} %get-tuple-element.18), channel_id=1, source_target_pairs={{0,3},{1,2},{2,1},{3,0},{4,7},{5,6},{6,5},{7,4},{8,11},{9,10},{10,... | collective-permute-start | bytes 245768 | tf_op jit(solution)/shard_map/ppermute | solution.py:360
  12.2 0.9 %copy-start.1 = (bf16[64,640]{1,0:T(8,128)(2,1)S(1)}, bf16[64,640]{1,0:T(8,128)(2,1)}, u32[]{:S(2)}) copy-start(bf16[64,640]{1,0:T(8,128)(2,1)} %get-tuple-element.12.refs_0_) | copy-start | bytes 245764
  13.0 0.7 %copy-start.2 = (s32[4,4]{1,0:T(4,128)S(1)}, s32[4,4]{1,0:T(4,128)}, u32[]{:S(2)}) copy-start(s32[4,4]{1,0:T(4,128)} %defocus.1) | copy-start | bytes 196
  13.7 0.7 %copy-start.3 = (f32[4]{0:T(128)S(1)}, f32[4]{0:T(128)}, u32[]{:S(2)}) copy-start(f32[4]{0:T(128)} %angles.1) | copy-start | bytes 52
  18.6 4.5 %collective-permute-start.3 = (bf16[64,640]{1,0:T(8,128)(2,1)S(1)}, bf16[64,640]{1,0:T(8,128)(2,1)S(1)}, u32[]{:S(2)}, u32[]{:S(2)}) collective-permute-start(bf16[64,640]{1,0:T(8,128)(2,1)S(1)} %get-tuple-element.16), channel_id=1, source_target_pairs={{0,1},{1,0},{2,3},{3,2},{4,5},{5,4},{6,7},{7,6},{8,9},{9,8},{10,11... | collective-permute-start | bytes 245768 | tf_op jit(solution)/shard_map/ppermute | solution.py:360
  18.9 5.3 %collective-permute-start.9 = (bf16[64,640]{1,0:T(8,128)(2,1)S(1)}, bf16[64,640]{1,0:T(8,128)(2,1)S(1)}, u32[]{:S(2)}, u32[]{:S(2)}) collective-permute-start(bf16[64,640]{1,0:T(8,128)(2,1)S(1)} %collective-permute-done.7.refs_8_), channel_id=1, source_target_pairs={{0,8},{4,12},{8,0},{12,4},{1,9},{5,13},{9,1},{13,5},{2,10},{6,14},... | collective-permute-start | bytes 245768 | tf_op jit(solution)/shard_map/ppermute | solution.py:360
  19.4 4.8 %collective-permute-start.8 = (bf16[64,640]{1,0:T(8,128)(2,1)S(1)}, bf16[64,640]{1,0:T(8,128)(2,1)S(1)}, u32[]{:S(2)}, u32[]{:S(2)}) collective-permute-start(bf16[64,640]{1,0:T(8,128)(2,1)S(1)} %collective-permute-done.7.refs_8_), channel_id=1, source_target_pairs={{0,4},{4,0},{8,12},{12,8},{1,5},{5,1},{9,13},{13,9},{2,6},{6,2},{1... | collective-permute-start | bytes 245768 | tf_op jit(solution)/shard_map/ppermute | solution.py:360
  19.4 6.2 %collective-permute-start.13 = (bf16[64,640]{1,0:T(8,128)(2,1)S(1)}, bf16[64,640]{1,0:T(8,128)(2,1)S(1)}, u32[]{:S(2)}, u32[]{:S(2)}) collective-permute-start(bf16[64,640]{1,0:T(8,128)(2,1)S(1)} %collective-permute-done.11.refs_12_), channel_id=1, source_target_pairs={{0,8},{4,12},{8,0},{12,4},{1,9},{5,13},{9,1},{13,5},{2,10},{6,14},... | collective-permute-start | bytes 245768 | tf_op jit(solution)/shard_map/ppermute | solution.py:360
  21.0 4.6 %collective-permute-start.12 = (bf16[64,640]{1,0:T(8,128)(2,1)S(1)}, bf16[64,640]{1,0:T(8,128)(2,1)S(1)}, u32[]{:S(2)}, u32[]{:S(2)}) collective-permute-start(bf16[64,640]{1,0:T(8,128)(2,1)S(1)} %collective-permute-done.11.refs_12_), channel_id=1, source_target_pairs={{0,4},{4,0},{8,12},{12,8},{1,5},{5,1},{9,13},{13,9},{2,6},{6,2},{1... | collective-permute-start | bytes 245768 | tf_op jit(solution)/shard_map/ppermute | solution.py:360
  23.1 4.4 %collective-permute-start.5 = (bf16[64,640]{1,0:T(8,128)(2,1)S(1)}, bf16[64,640]{1,0:T(8,128)(2,1)S(1)}, u32[]{:S(2)}, u32[]{:S(2)}) collective-permute-start(bf16[64,640]{1,0:T(8,128)(2,1)S(1)} %collective-permute-done.3.refs_4_), channel_id=1, source_target_pairs={{0,8},{4,12},{8,0},{12,4},{1,9},{5,13},{9,1},{13,5},{2,10},{6,14},... | collective-permute-start | bytes 245768 | tf_op jit(solution)/shard_map/ppermute | solution.py:360
  24.1 3.4 %collective-permute-start.4 = (bf16[64,640]{1,0:T(8,128)(2,1)S(1)}, bf16[64,640]{1,0:T(8,128)(2,1)S(1)}, u32[]{:S(2)}, u32[]{:S(2)}) collective-permute-start(bf16[64,640]{1,0:T(8,128)(2,1)S(1)} %collective-permute-done.3.refs_4_), channel_id=1, source_target_pairs={{0,4},{4,0},{8,12},{12,8},{1,5},{5,1},{9,13},{13,9},{2,6},{6,2},{1... | collective-permute-start | bytes 245768 | tf_op jit(solution)/shard_map/ppermute | solution.py:360
  24.1 3.4 %collective-permute-start.2 = (bf16[64,640]{1,0:T(8,128)(2,1)S(1)}, bf16[64,640]{1,0:T(8,128)(2,1)S(1)}, u32[]{:S(2)}, u32[]{:S(2)}) collective-permute-start(bf16[64,640]{1,0:T(8,128)(2,1)S(1)} %collective-permute-done.1.refs_2_), channel_id=1, source_target_pairs={{0,4},{4,0},{8,12},{12,8},{1,5},{5,1},{9,13},{13,9},{2,6},{6,2},{1... | collective-permute-start | bytes 245768 | tf_op jit(solution)/shard_map/ppermute | solution.py:360
  25.6 1.9 %collective-permute-start.10 = (bf16[64,640]{1,0:T(8,128)(2,1)S(1)}, bf16[64,640]{1,0:T(8,128)(2,1)S(1)}, u32[]{:S(2)}, u32[]{:S(2)}) collective-permute-start(bf16[64,640]{1,0:T(8,128)(2,1)S(1)} %collective-permute-done.9.refs_10_), channel_id=1, source_target_pairs={{0,4},{4,0},{8,12},{12,8},{1,5},{5,1},{9,13},{13,9},{2,6},{6,2},{1... | collective-permute-start | bytes 245768 | tf_op jit(solution)/shard_map/ppermute | solution.py:360
  25.6 1.9 %collective-permute-start.14 = (bf16[64,640]{1,0:T(8,128)(2,1)S(1)}, bf16[64,640]{1,0:T(8,128)(2,1)S(1)}, u32[]{:S(2)}, u32[]{:S(2)}) collective-permute-start(bf16[64,640]{1,0:T(8,128)(2,1)S(1)} %collective-permute-done.13.refs_14_), channel_id=1, source_target_pairs={{0,4},{4,0},{8,12},{12,8},{1,5},{5,1},{9,13},{13,9},{2,6},{6,2},{1... | collective-permute-start | bytes 245768 | tf_op jit(solution)/shard_map/ppermute | solution.py:360
  27.5 1.3 %collective-permute-start.6 = (bf16[64,640]{1,0:T(8,128)(2,1)S(1)}, bf16[64,640]{1,0:T(8,128)(2,1)S(1)}, u32[]{:S(2)}, u32[]{:S(2)}) collective-permute-start(bf16[64,640]{1,0:T(8,128)(2,1)S(1)} %collective-permute-done.5.refs_6_), channel_id=1, source_target_pairs={{0,4},{4,0},{8,12},{12,8},{1,5},{5,1},{9,13},{13,9},{2,6},{6,2},{1... | collective-permute-start | bytes 245768 | tf_op jit(solution)/shard_map/ppermute | solution.py:360
  28.8 0.9 %copy-start = (bf16[64,640]{1,0:T(8,128)(2,1)S(1)}, bf16[64,640]{1,0:T(8,128)(2,1)}, u32[]{:S(2)}) copy-start(bf16[64,640]{1,0:T(8,128)(2,1)} %get-tuple-element.15.refs_0_) | copy-start | bytes 245764

commit v5 on v4

v5 whole, which is shorter than its diff:
```python
import functools
import math

import jax
import jax.numpy as jnp
import numpy as np
from jax import lax
from jax.experimental import pallas as pl
from jax.experimental.pallas import tpu as pltpu
from jax.sharding import PartitionSpec as P

SLAB = 16
XBW = 128
BAND = 256
XBLK = 4
SLICES = 64
RADIX = 8
MAIN = 128
REST = 32
REACH = MAIN + REST
PACKED = XBLK * REACH
WINDOW = 384
ROOT = math.sqrt(0.5)


def column_tables(columns):
    size = columns // RADIX
    half = size // 2
    u = np.arange(size)[:, None]

    def angles(freq):
        return 2.0 * np.pi * ((u * freq[None, :]) % columns) / columns

    k0, s0 = RADIX * np.arange(half + 1), RADIX * np.arange(1, half)
    k4 = RADIX * np.arange(half) + 4
    m0 = np.concatenate([np.cos(angles(k0)), -np.sin(angles(s0))], 1)
    m4 = np.concatenate([np.cos(angles(k4)), -np.sin(angles(k4))], 1)
    full = angles(RADIX * np.arange(size))
    waves = np.concatenate([np.cos(full), np.sin(full)], 1)
    ends = np.concatenate([m0, m4], 1)

    def split(table):
        high = table.astype(jnp.bfloat16)
        return high, (table - high.astype(np.float64)).astype(jnp.bfloat16)

    matrices = np.stack([*split(ends), *split(waves), np.concatenate([m0.T, m4.T], 1).astype(jnp.bfloat16)])
    return matrices


def column_lines(columns):
    size = columns // RADIX
    half = size // 2
    line = lax.broadcasted_iota(jnp.int32, (8, size), 0)
    u = lax.broadcasted_iota(jnp.int32, (8, size), 1)
    freq = jnp.where(line == 0, RADIX * jnp.where(u <= half, u, u - half), RADIX * (u & (half - 1)) + 4)
    freq = jnp.where(line < 2, freq, RADIX * u + line // 2)
    fold = jnp.minimum(freq, columns - freq)
    count = jnp.where((fold == 0) | (fold == columns // 2), 1.0, 2.0)
    gain = count * (fold.astype(jnp.float32) + 0.5) * (2.0 / (columns * columns))
    angle = (u * (line + 1)).astype(jnp.float32) * (2.0 * math.pi / columns)
    return fold * fold, gain, jnp.cos(angle), jnp.sin(angle)


def flip_sign(squares, defocus, length):
    cycles = lax.div(squares * defocus, jnp.int32(length * length))
    return (1 - 2 * (cycles & 1)).astype(jnp.float32)


def fetched(sources, targets, sems):
    copies = [pltpu.make_async_copy(s, t, sems.at[i]) for i, (s, t) in enumerate(zip(sources, targets))]
    for copy in copies:
        copy.start()
    return copies


def reach_of(angle):
    line = jnp.full((8, XBW), angle, jnp.float32)
    cosine, sine = jnp.cos(line), jnp.sin(line)
    lowest = 0.5 * XBW + jnp.minimum((XBW - 1) * cosine, 0.0) - 0.5 * (SLAB - 1) * jnp.abs(sine)
    first = jnp.clip(jnp.floor(lowest) - 8.0, 0.0, float(BAND - REACH))
    return cosine[:1], sine[:1], jnp.max(first).astype(jnp.int32)


def butterflies(image, turns, zhi, zlo):
    rows, columns = image.shape
    size = columns // RADIX

    def step(i, carry):
        here = pl.ds(pl.multiple_of(i * 16, 16), 16)
        x = [image[here, m * size : (m + 1) * size].astype(jnp.float32) for m in range(8)]
        p0, p1, p2, p3 = (x[m] + x[m + 4] for m in range(4))
        q0, q1, q2, q3 = (x[m] - x[m + 4] for m in range(4))
        e, f = p0 + p2, p1 + p3
        g, h = ROOT * (q1 - q3), ROOT * (q1 + q3)
        z = [e + f, e - f]
        for j, (real, imag) in enumerate([(q0 + g, -q2 - h), (p0 - p2, p3 - p1), (q0 - g, q2 - h)]):
            c, s = turns[2 * j], turns[2 * j + 1]
            z += [real * c + imag * s, imag * c - real * s]
        for line in range(8):
            top = z[line].astype(jnp.bfloat16)
            zhi[line, here, :] = top
            zlo[line, here, :] = (z[line] - top.astype(jnp.float32)).astype(jnp.bfloat16)
        return carry

    lax.fori_loop(0, rows // 16, step, 0)


def inverse_butterflies(ends, waves, turns, turned):
    rows, columns = turned.shape
    size = columns // RADIX

    def step(i, carry):
        here = pl.ds(pl.multiple_of(i * 8, 8), 8)
        r, s = [], []
        for j in range(3):
            c, d = turns[2 * j], turns[2 * j + 1]
            real = waves[2 * j, here, :size] - waves[2 * j + 1, here, size:]
            imag = waves[2 * j, here, size:] + waves[2 * j + 1, here, :size]
            r.append(real * c - imag * d)
            s.append(real * d + imag * c)
        e, f = ends[0, here, :] + ends[1, here, :], ends[0, here, :] - ends[1, here, :]
        a, b, c, d = r[0] + r[2], r[0] - r[2], s[0] + s[2], s[0] - s[2]
        even0, even2, odd1, odd3 = e + r[1], e - r[1], f - s[1], f + s[1]
        g, h = ROOT * (b - c), ROOT * (b + c)
        out = [even0 + a, odd1 + g, even2 - d, odd3 - h, even0 - a, odd1 - g, even2 + d, odd3 + h]
        for m in range(8):
            turned[here, m * size : (m + 1) * size] = out[m]
        return carry

    lax.fori_loop(0, rows // 8, step, 0)


def send_patches(slots, slices_owned, spectrum, wave_table, end_table, columns, facts, scratch, out_refs):
    squares, ramp, turns, angles, defocus, starts = facts
    ends, waves, turned, out, out_sems = scratch
    rows, size = spectrum[0].shape
    tilt = lax.axis_index("tilt")
    slabs = [(tilt ^ slot) * slices_owned // SLAB for slot in slots]
    gains = [flip_sign(squares, defocus[tilt, slab], columns) * ramp for slab in slabs]
    filtered = [
        jnp.concatenate([(spectrum[i] * gain[i : i + 1, :]).astype(jnp.bfloat16) for gain in gains], 0) for i in range(8)
    ]
    for i in range(2):
        ends[i] = jnp.dot(filtered[i], end_table[:, i * size : (i + 1) * size], preferred_element_type=jnp.float32)
    for i in range(6):
        waves[i] = jnp.dot(filtered[2 + i], wave_table[...], preferred_element_type=jnp.float32)
    inverse_butterflies(ends, waves, turns, turned)
    lane = lax.broadcasted_iota(jnp.int32, (rows, MAIN), 1) // REST
    _, _, first_tap = reach_of(angles[tilt])
    sends = []
    for i, slab in enumerate(slabs):
        rest = jnp.zeros((rows, MAIN), jnp.float32)
        for block in range(XBLK):
            start = starts[tilt, slab, block] + first_tap
            base = pl.multiple_of(jnp.minimum((start // 128) * 128, columns - WINDOW), 128)
            window = turned[i * rows : (i + 1) * rows, pl.ds(base, WINDOW)]
            shift = base - start
            reach = pltpu.roll(window, jnp.where(shift < 0, shift + WINDOW, shift), 1)[:, : 2 * MAIN]
            out[i, :, block * MAIN : (block + 1) * MAIN] = reach[:, :MAIN].astype(jnp.bfloat16)
            last = reach[:, MAIN:]
            rest = jnp.where(lane == block, pltpu.roll(last, block * REST, 1) if block else last, rest)
        out[i, :, XBLK * MAIN :] = rest.astype(jnp.bfloat16)
        sends.append(pltpu.make_async_copy(out.at[i], out_refs[i], out_sems.at[i]))
        sends[-1].start()
    return sends


def first_kernel(slots, slices_owned, image_ref, matrix_ref, angle_ref, defocus_ref, starts_ref, *refs):
    count = len(slots)
    out_refs, spectrum_ref = refs[:count], refs[count]
    image, matrix, angles, defocus, starts, zhi, zlo, held, *scratch, sems, held_sem = refs[count + 1 :]
    rows, columns = image.shape
    size = columns // RADIX
    copies = fetched(
        [image_ref, angle_ref, defocus_ref, starts_ref] + [matrix_ref.at[i] for i in range(5)],
        [image, angles, defocus, starts] + [matrix.at[i] for i in range(5)],
        sems,
    )
    squares, ramp, cosine_turns, sine_turns = column_lines(columns)
    turns = [t[j : j + 1, :] for j in range(3) for t in (cosine_turns, sine_turns)]
    copies[0].wait()
    butterflies(image, turns, zhi, zlo)
    for copy in copies[1:]:
        copy.wait()

    def product(first, lines, table, here):
        top = zhi[first : first + lines].reshape(lines * rows, size)
        rest = zlo[first : first + lines].reshape(lines * rows, size)
        total = jnp.dot(top, matrix[table, :, here], preferred_element_type=jnp.float32)
        total += jnp.dot(top, matrix[table + 1, :, here], preferred_element_type=jnp.float32)
        return total + jnp.dot(rest, matrix[table, :, here], preferred_element_type=jnp.float32)

    spectrum = [product(0, 1, 0, slice(0, size)), product(1, 1, 0, slice(size, 2 * size))]
    mixed = product(2, 6, 2, slice(None))
    for j in range(3):
        real, imag = mixed[2 * j * rows : (2 * j + 1) * rows], mixed[(2 * j + 1) * rows : (2 * j + 2) * rows]
        spectrum += [real[:, :size] + imag[:, size:], imag[:, :size] - real[:, size:]]
    for i in range(8):
        held[i] = spectrum[i]
    keep = pltpu.make_async_copy(held, spectrum_ref, held_sem)
    keep.start()
    facts = (squares, ramp, turns, angles, defocus, starts)
    sends = send_patches(
        slots, slices_owned, spectrum, matrix.at[2], matrix.at[4], columns, facts, scratch, out_refs
    )
    for copy in sends + [keep]:
        copy.wait()


def second_kernel(slots, slices_owned, spectrum_ref, matrix_ref, angle_ref, defocus_ref, starts_ref, *refs):
    count = len(slots)
    out_refs = refs[:count]
    held, matrix, angles, defocus, starts, *scratch, sems = refs[count:]
    columns = RADIX * held.shape[2]
    copies = fetched(
        [spectrum_ref, angle_ref, defocus_ref, starts_ref, matrix_ref.at[2], matrix_ref.at[4]],
        [held, angles, defocus, starts, matrix.at[0], matrix.at[1]],
        sems,
    )
    squares, ramp, cosine_turns, sine_turns = column_lines(columns)
    turns = [t[j : j + 1, :] for j in range(3) for t in (cosine_turns, sine_turns)]
    for copy in copies:
        copy.wait()
    facts = (squares, ramp, turns, angles, defocus, starts)
    sends = send_patches(
        slots, slices_owned, [held[i] for i in range(8)], matrix.at[0], matrix.at[1], columns, facts, scratch, out_refs
    )
    for copy in sends:
        copy.wait()


def column_filtered(slots, later, slices_owned, image, angles, defocus, starts):
    rows, columns = image.shape
    size = columns // RADIX
    matrices = jnp.asarray(column_tables(columns))
    away = pl.BlockSpec(memory_space=pl.ANY)
    spectrum = jax.ShapeDtypeStruct((8, rows, size), jnp.float32)
    patch = jax.ShapeDtypeStruct((rows, PACKED), jnp.bfloat16)
    small = [
        pltpu.SMEM(angles.shape, jnp.float32),
        pltpu.SMEM(defocus.shape, jnp.int32),
        pltpu.SMEM(starts.shape, jnp.int32),
    ]

    def buffers(count):
        return [
            pltpu.VMEM((2, count * rows, size), jnp.float32),
            pltpu.VMEM((6, count * rows, 2 * size), jnp.float32),
            pltpu.VMEM((count * rows, columns), jnp.float32),
            pltpu.VMEM((count, rows, PACKED), jnp.bfloat16),
            pltpu.SemaphoreType.DMA((count,)),
        ]

    def cost(products):
        return pl.CostEstimate(flops=2 * rows * size * size * products, bytes_accessed=3 * 2**20, transcendentals=0)

    params = pltpu.CompilerParams(vmem_limit_bytes=60 * 2**20)
    *first, held = pl.pallas_call(
        functools.partial(first_kernel, slots, slices_owned),
        out_shape=[patch] * len(slots) + [spectrum],
        in_specs=[away] * 5,
        out_specs=[away] * (len(slots) + 1),
        scratch_shapes=[
            pltpu.VMEM((rows, columns), jnp.bfloat16),
            pltpu.VMEM(matrices.shape, jnp.bfloat16),
            *small,
            pltpu.VMEM((8, rows, size), jnp.bfloat16),
            pltpu.VMEM((8, rows, size), jnp.bfloat16),
            pltpu.VMEM(spectrum.shape, jnp.float32),
            *buffers(len(slots)),
            pltpu.SemaphoreType.DMA((9,)),
            pltpu.SemaphoreType.DMA,
        ],
        compiler_params=params,
        cost_estimate=cost(42 + 14 * len(slots)),
        name="forward_and_first_slots",
    )(image, matrices, angles, defocus, starts)
    second = pl.pallas_call(
        functools.partial(second_kernel, later, slices_owned),
        out_shape=[patch] * len(later),
        in_specs=[away] * 5,
        out_specs=[away] * len(later),
        scratch_shapes=[
            pltpu.VMEM(spectrum.shape, jnp.float32),
            pltpu.VMEM((2,) + matrices.shape[1:], jnp.bfloat16),
            *small,
            *buffers(len(later)),
            pltpu.SemaphoreType.DMA((6,)),
        ],
        compiler_params=params,
        cost_estimate=cost(14 * len(later)),
        name="later_slots",
    )(held, matrices, angles, defocus, starts)
    return dict(zip(slots, first)) | dict(zip(later, second))


def after(array, *others):
    away = pl.BlockSpec(memory_space=pl.ANY)
    return pl.pallas_call(
        lambda *refs: None,
        out_shape=jax.ShapeDtypeStruct(array.shape, array.dtype),
        in_specs=[away] * (1 + len(others)),
        out_specs=away,
        input_output_aliases={0: 0},
        cost_estimate=pl.CostEstimate(flops=0, bytes_accessed=0, transcendentals=0),
        name="after",
    )(array, *others)


def prepare_kernel(slots, slices_owned, angles, defocus, rows_ref, weights_ref, waves, mine, order):
    tilt, row = lax.axis_index("tilt"), lax.axis_index("row")
    slab, local_first = tilt * slices_owned // SLAB, tilt * slices_owned % SLAB
    full_rows = waves.shape[0]
    rows = rows_ref.shape[0] // slots
    half = full_rows // 2

    def row_waves(block, carry):
        here = pl.ds(pl.multiple_of(block * rows, rows), rows)
        y = block * rows + lax.broadcasted_iota(jnp.int32, (rows, full_rows), 0)
        column = lax.broadcasted_iota(jnp.int32, (rows, full_rows), 1)
        freq = jnp.where(column <= half, column, column - half)
        angle = ((y * freq) & (full_rows - 1)).astype(jnp.float32) * (2.0 * math.pi / full_rows)
        waves[here, :] = jnp.cos(jnp.where(column <= half, angle, angle - 0.5 * math.pi))
        return carry

    lax.fori_loop(0, full_rows // rows, row_waves, 0)
    own = waves[pl.ds(pl.multiple_of(row * rows, rows), rows), :]
    column = lax.broadcasted_iota(jnp.int32, (8, full_rows), 1)
    freq = jnp.where(column <= half, column, column - half)
    count = jnp.where((freq == 0) | (freq == half), 1.0, 2.0) / full_rows
    for slot in range(slots):
        sign = flip_sign(freq * freq, defocus[tilt ^ slot, slab], full_rows)
        mine[slot * rows : (slot + 1) * rows, :] = own * (sign * count)[:1]
    for block in range(full_rows // rows):
        order[block * rows : (block + 1) * rows, :] = waves[pl.ds(pl.multiple_of((row ^ block) * rows, rows), rows), :]
    rows_ref[...] = lax.dot_general(
        mine[...],
        order[...],
        (((1,), (1,)), ((), ())),
        precision=lax.Precision.HIGHEST,
        preferred_element_type=jnp.float32,
    ).astype(jnp.bfloat16)

    column = lax.broadcasted_iota(jnp.int32, (1, XBW), 1).astype(jnp.float32)
    place = lax.broadcasted_iota(jnp.int32, (2 * MAIN, XBW), 0)
    place = jnp.where(place < MAIN, place, MAIN + place % REST).astype(jnp.float32)
    for slot in range(slots):
        cosine, sine, first_tap = reach_of(angles[tilt ^ slot])
        tap = place + first_tap.astype(jnp.float32)

        def one_slice(c, carry):
            offset = (local_first + c).astype(jnp.float32) - 0.5 * (SLAB - 1)
            centre = 0.5 * XBW + column * cosine + offset * sine
            there = pl.ds(pl.multiple_of(c * XBW, XBW), XBW)
            weights_ref[slot, :, there] = jnp.maximum(0.0, 1.0 - jnp.abs(tap - centre)).astype(jnp.bfloat16)
            return carry

        lax.fori_loop(0, slices_owned, one_slice, 0)


def prepared(slots, slices_owned, rows, full_rows, angles, defocus):
    smem, vmem = pl.BlockSpec(memory_space=pltpu.SMEM), pl.BlockSpec(memory_space=pltpu.VMEM)
    return pl.pallas_call(
        functools.partial(prepare_kernel, slots, slices_owned),
        out_shape=[
            jax.ShapeDtypeStruct((slots * rows, full_rows), jnp.bfloat16),
            jax.ShapeDtypeStruct((slots, 2 * MAIN, slices_owned * XBW), jnp.bfloat16),
        ],
        in_specs=[smem] * 2,
        out_specs=[vmem] * 2,
        scratch_shapes=[
            pltpu.VMEM((full_rows, full_rows), jnp.float32),
            pltpu.VMEM((slots * rows, full_rows), jnp.float32),
            pltpu.VMEM((full_rows, full_rows), jnp.float32),
        ],
        compiler_params=pltpu.CompilerParams(vmem_limit_bytes=32 * 2**20),
        cost_estimate=pl.CostEstimate(flops=2**31, bytes_accessed=6 * 2**20, transcendentals=0),
        name="prepare",
    )(angles, defocus)


def corrected_patches(slot, rows_ref, patch_refs):
    rows = patch_refs[0].shape[0]
    patches = jnp.concatenate([ref[...] for ref in patch_refs], 0)
    image = jnp.dot(rows_ref[slot * rows : (slot + 1) * rows, :], patches, preferred_element_type=jnp.float32)
    lane = lax.broadcasted_iota(jnp.int32, (rows, MAIN), 1) // REST
    main = jnp.concatenate([image[:, block * MAIN : (block + 1) * MAIN] for block in range(XBLK)], 0)
    rest = jnp.concatenate([jnp.where(lane == block, image[:, XBLK * MAIN :], 0.0) for block in range(XBLK)], 0)
    return jnp.concatenate([main, rest], 1).astype(jnp.bfloat16)


def sum_kernel(slots, row_devices, rows_ref, weights_ref, *refs):
    patch_refs, total_ref = refs[:-1], refs[-1]
    parts = [
        corrected_patches(slot, rows_ref, patch_refs[i * row_devices : (i + 1) * row_devices])
        for i, slot in enumerate(slots)
    ]
    step = 4 * XBW
    for first in range(0, total_ref.shape[1], step):
        here = slice(first, first + step)
        total = jnp.dot(parts[0], weights_ref[slots[0], :, here], preferred_element_type=jnp.float32)
        for part, slot in zip(parts[1:], slots[1:]):
            total += jnp.dot(part, weights_ref[slot, :, here], preferred_element_type=jnp.float32)
        total_ref[:, here] = total


def finish_kernel(factor, slots, row_devices, rows_ref, weights_ref, total_ref, *refs):
    patch_refs = refs[: len(slots) * row_devices]
    out_ref, out, sems = refs[len(slots) * row_devices :]
    rows = patch_refs[0].shape[0]
    parts = [
        corrected_patches(slot, rows_ref, patch_refs[i * row_devices : (i + 1) * row_devices])
        for i, slot in enumerate(slots)
    ]
    step = 4
    copies = []
    for group in range(out.shape[0] // step):
        here = slice(group * step * XBW, (group + 1) * step * XBW)
        total = total_ref[:, here]
        for part, slot in zip(parts, slots):
            total += jnp.dot(part, weights_ref[slot, :, here], preferred_element_type=jnp.float32)
        for c in range(step):
            for block in range(XBLK):
                out[group * step + c, :, block * XBW : (block + 1) * XBW] = (
                    factor * total[block * rows : (block + 1) * rows, c * XBW : (c + 1) * XBW]
                ).astype(jnp.bfloat16)
        part = pl.ds(group * step, step)
        copies.append(pltpu.make_async_copy(out.at[part], out_ref.at[part], sems.at[group]))
        copies[-1].start()
    for copy in copies:
        copy.wait()


def interpolation(kernel, slots, weights, row_filters, patches, totals, **call):
    _, _, width = weights.shape
    rows = patches[0][0].shape[0]
    vmem = pl.BlockSpec(memory_space=pltpu.VMEM)
    operands = [row_filters, weights, *totals, *(block for slot in slots for block in patches[slot])]
    flops = 4 * len(slots) * MAIN * width * XBLK * rows
    return pl.pallas_call(
        functools.partial(kernel, slots, len(patches[0])),
        in_specs=[vmem] * len(operands),
        compiler_params=pltpu.CompilerParams(vmem_limit_bytes=32 * 2**20),
        cost_estimate=pl.CostEstimate(flops=flops, bytes_accessed=3 * 2**20, transcendentals=0),
        **call,
    )(*operands)


def summed(row_filters, weights, patches, slots):
    return interpolation(
        sum_kernel,
        slots,
        weights,
        row_filters,
        patches,
        [],
        out_shape=jax.ShapeDtypeStruct((XBLK * patches[0][0].shape[0], weights.shape[2]), jnp.float32),
        out_specs=pl.BlockSpec(memory_space=pltpu.VMEM),
        name="sum_early_tilts",
    )


def finished(row_filters, weights, total, patches, slots, factor):
    shape = (weights.shape[2] // XBW, patches[0][0].shape[0], XBLK * XBW)
    return interpolation(
        functools.partial(finish_kernel, factor),
        slots,
        weights,
        row_filters,
        patches,
        [total],
        out_shape=jax.ShapeDtypeStruct(shape, jnp.bfloat16),
        out_specs=pl.BlockSpec(memory_space=pl.ANY),
        scratch_shapes=[pltpu.VMEM(shape, jnp.bfloat16), pltpu.SemaphoreType.DMA((shape[0] // 4,))],
        name="finish_volume",
    )


def exchange(array, axis, distance):
    count = lax.axis_size(axis)
    return lax.ppermute(array, axis, [(i, i ^ distance) for i in range(count)])


def gather_rows(array, awaited=()):
    blocks = {0: array}
    bit = lax.axis_size("row") // 2
    while bit:
        if bit == 1 and awaited:
            blocks = {d: after(block, *awaited) if d else block for d, block in blocks.items()}
        blocks.update({d ^ bit: exchange(block, "row", bit) for d, block in blocks.items()})
        bit //= 2
    return [blocks[d] for d in sorted(blocks)]


def per_device(projections, tilt_angle, band_start, defocus):
    _, rows, _ = projections.shape
    row_devices, tilt_devices = lax.axis_size("row"), lax.axis_size("tilt")
    slices_owned = SLICES // tilt_devices
    odd, even = list(range(tilt_devices - 1, 0, -2)), list(range(tilt_devices - 2, 0, -2))
    sent = column_filtered(odd, even + [0], slices_owned, projections[0], tilt_angle, defocus, band_start)
    arrived = {0: sent[0]} | {d: exchange(sent[d], "tilt", d) for d in odd}
    row_filters, weights = prepared(tilt_devices, slices_owned, rows, rows * row_devices, tilt_angle, defocus)
    patches = {0: gather_rows(arrived[0], (row_filters,))} | {d: gather_rows(arrived[d]) for d in odd}
    total = summed(row_filters, weights, patches, [0] + odd)
    for d in even:
        arrived[d] = exchange(after(sent[d], *(arrived[o] for o in odd)), "tilt", d)
        patches[d] = gather_rows(arrived[d], (total,))
    return finished(row_filters, weights, total, patches, even, 1.0 / math.sqrt(tilt_devices))


def solution(mesh):
    in_specs = (
        P(("group", "tilt"), "row", None),
        P("group"),
        P("group", None, None),
        P("group", None),
    )
    out_specs = P(("group", "tilt"), "row", None)
    return jax.shard_map(
        per_device, mesh=mesh, in_specs=in_specs, out_specs=out_specs, check_vma=False
    )
```

time: 32.1 us -> 40.8 us (1.27)
  local copies, waits for them, and re-layouts: 3.11 us -> 12.4 us
  waiting for transfers between devices: 6.12 us -> 2 us
  Pallas kernels: 11.6 us -> 13.8 us
  starting transfers between devices: 11 us -> 12.2 us
    unnamed x8 -> x38, local copies, waits for them, and re-layouts: 3.11 us -> 12.4 us
    ppermute x15, waiting for transfers between devices: 6.12 us -> 2 us  [exchange(): return lax.ppermute(array, axis, [(i, i ^ distance) for i in range(count)])]
    pallas_call x3 -> x8, Pallas kernels: 11.6 us -> 13.8 us  [the longest x1 4.15 us: prepared(): pl.pallas_call(functools.partial(prepare_kernel, slots, slices_owned), ou...]
    ppermute x15, starting transfers between devices: 11 us -> 12.2 us  [exchange(): return lax.ppermute(array, axis, [(i, i ^ distance) for i in range(count)])]
  transfers between devices with their start and end apart: 15 -> 15, of which waited for: 5 -> 4; matrix products, arithmetic and copies ran while one was open for 0% -> 0% of each run, Pallas kernels for 13% -> 21%
where the time goes in v5:
time: 40.8 us; the launch traced here: 40.5 us
  Pallas kernels  13.8 us (34%)
  local copies, waits for them, and re-layouts  12.4 us (30%)
  starting transfers between devices  12.2 us (30%)
  waiting for transfers between devices  2 us (5%)
    unnamed x38, local copies, waits for them, and re-layouts  12.4 us
    ppermute x15, starting transfers between devices, exchange(): return lax.ppermute(array, axis, [(i, i ^ distance) for i in range(count)])  12.2 us
    pallas_call x1, Pallas kernels, prepared(): pl.pallas_call(functools.partial(prepare_kernel, slots, slices_owned), ou...  4.15 us
    pallas_call x1, Pallas kernels, column_filtered(): pl.pallas_call(functools.partial(first_kernel, slots, slices_owned), out_...  4.08 us
    pallas_call x1, Pallas kernels, column_filtered(): pl.pallas_call(functools.partial(second_kernel, later, slices_owned), out...  2.99 us
    pallas_call x2, Pallas kernels, interpolation(): pl.pallas_call(functools.partial(kernel, slots, len(patches[0])), in_spec...  2.55 us
    ppermute x15, waiting for transfers between devices, exchange(): return lax.ppermute(array, axis, [(i, i ^ distance) for i in range(count)])  2 us
  transfers between devices with their start and end apart: 15, of which 4 were waited for; matrix products, arithmetic and copies ran while one was open for 0% of the time, Pallas kernels for 21%

profile of v5, /device:TPU:0, one launch (start us, length us, event | category | flops | bytes accessed | tf_op | source)
XLA Modules:
  0.0 40.5 jit_solution(259576574060749852)
XLA Ops:
  0.0 4.1 %forward_and_first_slots.1 = (bf16[64,640]{1,0:T(8,128)(2,1)}, bf16[64,640]{1,0:T(8,128)(2,1)}, f32[8,64,256]{2,1,0:T(8,128)}) custom-call(bf16[64,2048]{1,0:T(8,128)(2,1)} %bitcast.1, bf16[5,256,512]{2,1,0:T(8,128)(2,1)} %constant.2.clone.matrix_ref, f32[4]{0:T(128)} %angle_ref.3, s32[4,4]{1,0:T(4,128)} %defocus_ref.3, s32[4,4,4]{2,1,0:T(4,128)} %starts_ref.3), custom_call_target="tpu_custom_call" | custom-call | flops 587202560 | bytes 3145728 | tf_op jit(solution)/shard_map/forward_and_first_slots/pallas_call | solution.py:258
  4.1 5.1 %collective-permute-start.3 = (bf16[64,640]{1,0:T(8,128)(2,1)}, bf16[64,640]{1,0:T(8,128)(2,1)S(1)}, u32[]{:S(2)}, u32[]{:S(2)}) collective-permute-start(bf16[64,640]{1,0:T(8,128)(2,1)} %get-tuple-element.16), channel_id=1, source_target_pairs={{0,3},{1,2},{2,1},{3,0},{4,7},{5,6},{6,5},{7,4},{8,11},{9,10},{10,... | collective-permute-start | bytes 245768 | tf_op jit(solution)/shard_map/ppermute | solution.py:481
  9.2 3.0 %later_slots.1 = (bf16[64,640]{1,0:T(8,128)(2,1)}, bf16[64,640]{1,0:T(8,128)(2,1)}) custom-call(f32[8,64,256]{2,1,0:T(8,128)} %get-tuple-element.14.spectrum_ref, bf16[5,256,512]{2,1,0:T(8,128)(2,1)} %constant.2.clone.matrix_ref, f32[4]{0:T(128)} %angle_ref.3, s32[4,4]{1,0:T(4,128)} %defocus_ref.3, s32[4,4,4]{2,1,0:T(4,128)} %starts_ref.3), custom_call_target="tpu_custom_call" | custom-call | flops 234881024 | bytes 3145728 | tf_op jit(solution)/shard_map/later_slots/pallas_call | solution.py:278
  12.2 1.6 %collective-permute-start.1 = (bf16[64,640]{1,0:T(8,128)(2,1)}, bf16[64,640]{1,0:T(8,128)(2,1)S(1)}, u32[]{:S(2)}, u32[]{:S(2)}) collective-permute-start(bf16[64,640]{1,0:T(8,128)(2,1)} %get-tuple-element.15.refs_0_), channel_id=1, source_target_pairs={{0,8},{4,12},{8,0},{12,4},{1,9},{5,13},{9,1},{13,5},{2,10},{6,14},... | collective-permute-start | bytes 245768 | tf_op jit(solution)/shard_map/ppermute | solution.py:481
  13.9 0.5 %copy-done.10 = bf16[64,640]{1,0:T(8,128)(2,1)} copy-done((bf16[64,640]{1,0:T(8,128)(2,1)}, bf16[64,640]{1,0:T(8,128)(2,1)S(1)}, u32[]{:S(2)}) %copy-start.10) | copy-done | bytes 81944
  14.5 0.8 %collective-permute-start.11 = (bf16[64,640]{1,0:T(8,128)(2,1)}, bf16[64,640]{1,0:T(8,128)(2,1)S(1)}, u32[]{:S(2)}, u32[]{:S(2)}) collective-permute-start(bf16[64,640]{1,0:T(8,128)(2,1)} %after.4), channel_id=1, source_target_pairs={{0,2},{1,3},{2,0},{3,1},{4,6},{5,7},{6,4},{7,5},{8,10},{9,11},{10,... | collective-permute-start | bytes 245768 | tf_op jit(solution)/shard_map/ppermute | solution.py:481
  15.3 1.0 %collective-permute-start.5 = (bf16[64,640]{1,0:T(8,128)(2,1)}, bf16[64,640]{1,0:T(8,128)(2,1)S(1)}, u32[]{:S(2)}, u32[]{:S(2)}) collective-permute-start(bf16[64,640]{1,0:T(8,128)(2,1)} %copy-done.10), channel_id=1, source_target_pairs={{0,8},{4,12},{8,0},{12,4},{1,9},{5,13},{9,1},{13,5},{2,10},{6,14},... | collective-permute-start | bytes 245768 | tf_op jit(solution)/shard_map/ppermute | solution.py:481
  16.3 0.6 %collective-permute-done.1.refs_0_ = bf16[64,640]{1,0:T(8,128)(2,1)S(1)} collective-permute-done((bf16[64,640]{1,0:T(8,128)(2,1)}, bf16[64,640]{1,0:T(8,128)(2,1)S(1)}, u32[]{:S(2)}, u32[]{:S(2)}) %collective-permute-start.1) | collective-permute-done | bytes 81952 | tf_op jit(solution)/shard_map/ppermute | solution.py:481
  16.9 1.5 %collective-permute-start.9 = (bf16[64,640]{1,0:T(8,128)(2,1)}, bf16[64,640]{1,0:T(8,128)(2,1)S(1)}, u32[]{:S(2)}, u32[]{:S(2)}) collective-permute-start(bf16[64,640]{1,0:T(8,128)(2,1)} %copy-done.12), channel_id=1, source_target_pairs={{0,8},{4,12},{8,0},{12,4},{1,9},{5,13},{9,1},{13,5},{2,10},{6,14},... | collective-permute-start | bytes 245768 | tf_op jit(solution)/shard_map/ppermute | solution.py:481
  18.5 4.2 %prepare.1 = (bf16[256,256]{1,0:T(8,128)(2,1)S(1)}, bf16[4,256,2048]{2,1,0:T(8,128)(2,1)S(1)}) custom-call(f32[4]{0:T(128)S(1)} %copy-done.18, s32[4,4]{1,0:T(4,128)S(1)} %copy-done.17), custom_call_target="tpu_custom_call" | custom-call | flops 2147483648 | bytes 6291456 | tf_op jit(solution)/shard_map/prepare/pallas_call | solution.py:363
  22.6 2.0 %copy-done.2 = bf16[4,256,2048]{2,1,0:T(8,128)(2,1)} copy-done((bf16[4,256,2048]{2,1,0:T(8,128)(2,1)}, bf16[4,256,2048]{2,1,0:T(8,128)(2,1)S(1)}, u32[]{:S(2)}) %copy-start.2) | copy-done | bytes 4194328
  24.6 0.7 %copy-done.5 = bf16[256,256]{1,0:T(8,128)(2,1)} copy-done((bf16[256,256]{1,0:T(8,128)(2,1)}, bf16[256,256]{1,0:T(8,128)(2,1)S(1)}, u32[]{:S(2)}) %copy-start.5) | copy-done | bytes 131096
  25.3 0.5 %collective-permute-start.8 = (bf16[64,640]{1,0:T(8,128)(2,1)S(1)}, bf16[64,640]{1,0:T(8,128)(2,1)S(1)}, u32[]{:S(2)}, u32[]{:S(2)}) collective-permute-start(bf16[64,640]{1,0:T(8,128)(2,1)S(1)} %copy-done.13), channel_id=1, source_target_pairs={{0,4},{4,0},{8,12},{12,8},{1,5},{5,1},{9,13},{13,9},{2,6},{6,2},{1... | collective-permute-start | bytes 245768 | tf_op jit(solution)/shard_map/ppermute | solution.py:481
  26.3 0.5 %collective-permute-start.13 = (bf16[64,640]{1,0:T(8,128)(2,1)S(1)}, bf16[64,640]{1,0:T(8,128)(2,1)S(1)}, u32[]{:S(2)}, u32[]{:S(2)}) collective-permute-start(bf16[64,640]{1,0:T(8,128)(2,1)S(1)} %collective-permute-done.11.refs_0_), channel_id=1, source_target_pairs={{0,8},{4,12},{8,0},{12,4},{1,9},{5,13},{9,1},{13,5},{2,10},{6,14},... | collective-permute-start | bytes 245768 | tf_op jit(solution)/shard_map/ppermute | solution.py:481
  27.2 2.2 %copy-done.3 = bf16[4,256,2048]{2,1,0:T(8,128)(2,1)S(1)} copy-done((bf16[4,256,2048]{2,1,0:T(8,128)(2,1)S(1)}, bf16[4,256,2048]{2,1,0:T(8,128)(2,1)}, u32[]{:S(2)}) %copy-start.3) | copy-done | bytes 4194328
  29.4 0.9 %copy-done.6 = bf16[256,256]{1,0:T(8,128)(2,1)S(1)} copy-done((bf16[256,256]{1,0:T(8,128)(2,1)S(1)}, bf16[256,256]{1,0:T(8,128)(2,1)}, u32[]{:S(2)}) %copy-start.6) | copy-done | bytes 131096
  30.3 0.9 %copy-done.15 = bf16[64,640]{1,0:T(8,128)(2,1)S(1)} copy-done((bf16[64,640]{1,0:T(8,128)(2,1)S(1)}, bf16[64,640]{1,0:T(8,128)(2,1)}, u32[]{:S(2)}) %copy-start.15) | copy-done | bytes 81944
  31.2 1.2 %sum_early_tilts.1.refs_1_.total_ref = f32[256,2048]{1,0:T(8,128)S(1)} custom-call(bf16[256,256]{1,0:T(8,128)(2,1)S(1)} %copy-done.6, bf16[4,256,2048]{2,1,0:T(8,128)(2,1)S(1)} %copy-done.3, bf16[64,640]{1,0:T(8,128)(2,1)S(1)} %copy-done.16, bf16[64,640]{1,0:T(8,128)(2,1)S(1)} %collective-permute-done.refs_1_, bf16[64,640]{1,0:T(8,128)(2,1)S(1)} %copy-done.15, ...), custom_call_target="tpu_custom_call" | custom-call | flops 805306368 | bytes 3145728 | tf_op jit(solution)/shard_map/sum_early_tilts/pallas_call | solution.py:440
  32.4 1.4 %copy-done = f32[256,2048]{1,0:T(8,128)} copy-done((f32[256,2048]{1,0:T(8,128)}, f32[256,2048]{1,0:T(8,128)S(1)}, u32[]{:S(2)}) %copy-start) | copy-done | bytes 2097176
  33.8 0.6 %copy-done.8 = bf16[64,640]{1,0:T(8,128)(2,1)} copy-done((bf16[64,640]{1,0:T(8,128)(2,1)}, bf16[64,640]{1,0:T(8,128)(2,1)S(1)}, u32[]{:S(2)}) %copy-start.8) | copy-done | bytes 81944
  34.8 1.1 %collective-permute-done.14.refs_3_ = bf16[64,640]{1,0:T(8,128)(2,1)S(1)} collective-permute-done((bf16[64,640]{1,0:T(8,128)(2,1)}, bf16[64,640]{1,0:T(8,128)(2,1)S(1)}, u32[]{:S(2)}, u32[]{:S(2)}) %collective-permute-start.14) | collective-permute-done | bytes 81952 | tf_op jit(solution)/shard_map/ppermute | solution.py:481
  36.0 2.2 %copy-done.4 = bf16[4,256,2048]{2,1,0:T(8,128)(2,1)S(1)} copy-done((bf16[4,256,2048]{2,1,0:T(8,128)(2,1)S(1)}, bf16[4,256,2048]{2,1,0:T(8,128)(2,1)}, u32[]{:S(2)}) %copy-start.4) | copy-done | bytes 4194328
  38.2 0.9 %copy-done.9 = bf16[64,640]{1,0:T(8,128)(2,1)S(1)} copy-done((bf16[64,640]{1,0:T(8,128)(2,1)S(1)}, bf16[64,640]{1,0:T(8,128)(2,1)}, u32[]{:S(2)}) %copy-start.9) | copy-done | bytes 81944
  39.1 1.4 %finish_volume.1 = bf16[16,64,512]{2,1,0:T(8,128)(2,1)} custom-call(bf16[256,256]{1,0:T(8,128)(2,1)S(1)} %copy-done.7, bf16[4,256,2048]{2,1,0:T(8,128)(2,1)S(1)} %copy-done.4, f32[256,2048]{1,0:T(8,128)S(1)} %copy-done.1, bf16[64,640]{1,0:T(8,128)(2,1)S(1)} %collective-permute-done.11.refs_0_, bf16[64,640]{1,0:T(8,128)(2,1)S(1)} %collective-permute-done.12.refs_1_, ...), custom_call_target="tpu_custom_call" | custom-call | flops 268435456 | bytes 3145728 | tf_op jit(solution)/shard_map/finish_volume/pallas_call | solution.py:440
  (52 shorter events, 1.6 us)
Async XLA Ops:
  0.0 18.5 %copy-start.17 = (s32[4,4]{1,0:T(4,128)S(1)}, s32[4,4]{1,0:T(4,128)}, u32[]{:S(2)}) copy-start(s32[4,4]{1,0:T(4,128)} %defocus_ref.3) | copy-start | bytes 196
  0.0 18.5 %copy-start.18 = (f32[4]{0:T(128)S(1)}, f32[4]{0:T(128)}, u32[]{:S(2)}) copy-start(f32[4]{0:T(128)} %angle_ref.3) | copy-start | bytes 52
  4.1 9.7 %collective-permute-start.3 = (bf16[64,640]{1,0:T(8,128)(2,1)}, bf16[64,640]{1,0:T(8,128)(2,1)S(1)}, u32[]{:S(2)}, u32[]{:S(2)}) collective-permute-start(bf16[64,640]{1,0:T(8,128)(2,1)} %get-tuple-element.16), channel_id=1, source_target_pairs={{0,3},{1,2},{2,1},{3,0},{4,7},{5,6},{6,5},{7,4},{8,11},{9,10},{10,... | collective-permute-start | bytes 245768 | tf_op jit(solution)/shard_map/ppermute | solution.py:481
  9.2 4.7 %collective-permute-start.7 = (bf16[64,640]{1,0:T(8,128)(2,1)}, bf16[64,640]{1,0:T(8,128)(2,1)S(1)}, u32[]{:S(2)}, u32[]{:S(2)}) collective-permute-start(bf16[64,640]{1,0:T(8,128)(2,1)} %get-tuple-element.17), channel_id=1, source_target_pairs={{0,1},{1,0},{2,3},{3,2},{4,5},{5,4},{6,7},{7,6},{8,9},{9,8},{10,11... | collective-permute-start | bytes 245768 | tf_op jit(solution)/shard_map/ppermute | solution.py:481
  12.2 4.7 %collective-permute-start.1 = (bf16[64,640]{1,0:T(8,128)(2,1)}, bf16[64,640]{1,0:T(8,128)(2,1)S(1)}, u32[]{:S(2)}, u32[]{:S(2)}) collective-permute-start(bf16[64,640]{1,0:T(8,128)(2,1)} %get-tuple-element.15.refs_0_), channel_id=1, source_target_pairs={{0,8},{4,12},{8,0},{12,4},{1,9},{5,13},{9,1},{13,5},{2,10},{6,14},... | collective-permute-start | bytes 245768 | tf_op jit(solution)/shard_map/ppermute | solution.py:481
  13.8 11.5 %collective-permute-start = (bf16[64,640]{1,0:T(8,128)(2,1)}, bf16[64,640]{1,0:T(8,128)(2,1)S(1)}, u32[]{:S(2)}, u32[]{:S(2)}) collective-permute-start(bf16[64,640]{1,0:T(8,128)(2,1)} %get-tuple-element.15.refs_0_), channel_id=1, source_target_pairs={{0,4},{4,0},{8,12},{12,8},{1,5},{5,1},{9,13},{13,9},{2,6},{6,2},{1... | collective-permute-start | bytes 245768 | tf_op jit(solution)/shard_map/ppermute | solution.py:481
  14.5 10.7 %copy-start.13 = (bf16[64,640]{1,0:T(8,128)(2,1)S(1)}, bf16[64,640]{1,0:T(8,128)(2,1)}, u32[]{:S(2)}) copy-start(bf16[64,640]{1,0:T(8,128)(2,1)} %copy-done.12) | copy-start | bytes 245764
  14.5 12.7 %copy-start.11 = (bf16[64,640]{1,0:T(8,128)(2,1)S(1)}, bf16[64,640]{1,0:T(8,128)(2,1)}, u32[]{:S(2)}) copy-start(bf16[64,640]{1,0:T(8,128)(2,1)} %copy-done.10) | copy-start | bytes 245764
  14.5 12.7 %copy-start.16 = (bf16[64,640]{1,0:T(8,128)(2,1)S(1)}, bf16[64,640]{1,0:T(8,128)(2,1)}, u32[]{:S(2)}) copy-start(bf16[64,640]{1,0:T(8,128)(2,1)} %get-tuple-element.15.refs_0_) | copy-start | bytes 245764
  14.5 11.8 %collective-permute-start.11 = (bf16[64,640]{1,0:T(8,128)(2,1)}, bf16[64,640]{1,0:T(8,128)(2,1)S(1)}, u32[]{:S(2)}, u32[]{:S(2)}) collective-permute-start(bf16[64,640]{1,0:T(8,128)(2,1)} %after.4), channel_id=1, source_target_pairs={{0,2},{1,3},{2,0},{3,1},{4,6},{5,7},{6,4},{7,5},{8,10},{9,11},{10,... | collective-permute-start | bytes 245768 | tf_op jit(solution)/shard_map/ppermute | solution.py:481
  15.3 9.9 %collective-permute-start.5 = (bf16[64,640]{1,0:T(8,128)(2,1)}, bf16[64,640]{1,0:T(8,128)(2,1)S(1)}, u32[]{:S(2)}, u32[]{:S(2)}) collective-permute-start(bf16[64,640]{1,0:T(8,128)(2,1)} %copy-done.10), channel_id=1, source_target_pairs={{0,8},{4,12},{8,0},{12,4},{1,9},{5,13},{9,1},{13,5},{2,10},{6,14},... | collective-permute-start | bytes 245768 | tf_op jit(solution)/shard_map/ppermute | solution.py:481
  16.3 9.4 %collective-permute-start.4 = (bf16[64,640]{1,0:T(8,128)(2,1)}, bf16[64,640]{1,0:T(8,128)(2,1)S(1)}, u32[]{:S(2)}, u32[]{:S(2)}) collective-permute-start(bf16[64,640]{1,0:T(8,128)(2,1)} %copy-done.10), channel_id=1, source_target_pairs={{0,4},{4,0},{8,12},{12,8},{1,5},{5,1},{9,13},{13,9},{2,6},{6,2},{1... | collective-permute-start | bytes 245768 | tf_op jit(solution)/shard_map/ppermute | solution.py:481
  16.9 5.7 %copy-start.14 = (bf16[64,640]{1,0:T(8,128)(2,1)}, bf16[64,640]{1,0:T(8,128)(2,1)S(1)}, u32[]{:S(2)}) copy-start(bf16[64,640]{1,0:T(8,128)(2,1)S(1)} %collective-permute-done.1.refs_0_) | copy-start | bytes 245764
  16.9 8.9 %collective-permute-start.9 = (bf16[64,640]{1,0:T(8,128)(2,1)}, bf16[64,640]{1,0:T(8,128)(2,1)S(1)}, u32[]{:S(2)}, u32[]{:S(2)}) collective-permute-start(bf16[64,640]{1,0:T(8,128)(2,1)} %copy-done.12), channel_id=1, source_target_pairs={{0,8},{4,12},{8,0},{12,4},{1,9},{5,13},{9,1},{13,5},{2,10},{6,14},... | collective-permute-start | bytes 245768 | tf_op jit(solution)/shard_map/ppermute | solution.py:481
  25.3 1.8 %collective-permute-start.2 = (bf16[64,640]{1,0:T(8,128)(2,1)}, bf16[64,640]{1,0:T(8,128)(2,1)S(1)}, u32[]{:S(2)}, u32[]{:S(2)}) collective-permute-start(bf16[64,640]{1,0:T(8,128)(2,1)} %after.3.refs_2_), channel_id=1, source_target_pairs={{0,4},{4,0},{8,12},{12,8},{1,5},{5,1},{9,13},{13,9},{2,6},{6,2},{1... | collective-permute-start | bytes 245768 | tf_op jit(solution)/shard_map/ppermute | solution.py:481
  25.3 1.5 %collective-permute-start.8 = (bf16[64,640]{1,0:T(8,128)(2,1)S(1)}, bf16[64,640]{1,0:T(8,128)(2,1)S(1)}, u32[]{:S(2)}, u32[]{:S(2)}) collective-permute-start(bf16[64,640]{1,0:T(8,128)(2,1)S(1)} %copy-done.13), channel_id=1, source_target_pairs={{0,4},{4,0},{8,12},{12,8},{1,5},{5,1},{9,13},{13,9},{2,6},{6,2},{1... | collective-permute-start | bytes 245768 | tf_op jit(solution)/shard_map/ppermute | solution.py:481
  25.8 1.3 %collective-permute-start.6 = (bf16[64,640]{1,0:T(8,128)(2,1)S(1)}, bf16[64,640]{1,0:T(8,128)(2,1)S(1)}, u32[]{:S(2)}, u32[]{:S(2)}) collective-permute-start(bf16[64,640]{1,0:T(8,128)(2,1)S(1)} %collective-permute-done.5.refs_6_), channel_id=1, source_target_pairs={{0,4},{4,0},{8,12},{12,8},{1,5},{5,1},{9,13},{13,9},{2,6},{6,2},{1... | collective-permute-start | bytes 245768 | tf_op jit(solution)/shard_map/ppermute | solution.py:481
  25.9 1.4 %collective-permute-start.10 = (bf16[64,640]{1,0:T(8,128)(2,1)S(1)}, bf16[64,640]{1,0:T(8,128)(2,1)S(1)}, u32[]{:S(2)}, u32[]{:S(2)}) collective-permute-start(bf16[64,640]{1,0:T(8,128)(2,1)S(1)} %collective-permute-done.9.refs_10_), channel_id=1, source_target_pairs={{0,4},{4,0},{8,12},{12,8},{1,5},{5,1},{9,13},{13,9},{2,6},{6,2},{1... | collective-permute-start | bytes 245768 | tf_op jit(solution)/shard_map/ppermute | solution.py:481
  26.3 7.5 %collective-permute-start.13 = (bf16[64,640]{1,0:T(8,128)(2,1)S(1)}, bf16[64,640]{1,0:T(8,128)(2,1)S(1)}, u32[]{:S(2)}, u32[]{:S(2)}) collective-permute-start(bf16[64,640]{1,0:T(8,128)(2,1)S(1)} %collective-permute-done.11.refs_0_), channel_id=1, source_target_pairs={{0,8},{4,12},{8,0},{12,4},{1,9},{5,13},{9,1},{13,5},{2,10},{6,14},... | collective-permute-start | bytes 245768 | tf_op jit(solution)/shard_map/ppermute | solution.py:481
  26.8 8.0 %collective-permute-start.12 = (bf16[64,640]{1,0:T(8,128)(2,1)S(1)}, bf16[64,640]{1,0:T(8,128)(2,1)S(1)}, u32[]{:S(2)}, u32[]{:S(2)}) collective-permute-start(bf16[64,640]{1,0:T(8,128)(2,1)S(1)} %collective-permute-done.11.refs_0_), channel_id=1, source_target_pairs={{0,4},{4,0},{8,12},{12,8},{1,5},{5,1},{9,13},{13,9},{2,6},{6,2},{1... | collective-permute-start | bytes 245768 | tf_op jit(solution)/shard_map/ppermute | solution.py:481
  27.2 2.2 %copy-start.3 = (bf16[4,256,2048]{2,1,0:T(8,128)(2,1)S(1)}, bf16[4,256,2048]{2,1,0:T(8,128)(2,1)}, u32[]{:S(2)}) copy-start(bf16[4,256,2048]{2,1,0:T(8,128)(2,1)} %copy-done.2) | copy-start | bytes 12582916
  33.8 2.1 %copy-start.7 = (bf16[256,256]{1,0:T(8,128)(2,1)S(1)}, bf16[256,256]{1,0:T(8,128)(2,1)}, u32[]{:S(2)}) copy-start(bf16[256,256]{1,0:T(8,128)(2,1)} %copy-done.5) | copy-start | bytes 393220
  34.4 1.5 %collective-permute-start.14 = (bf16[64,640]{1,0:T(8,128)(2,1)}, bf16[64,640]{1,0:T(8,128)(2,1)S(1)}, u32[]{:S(2)}, u32[]{:S(2)}) collective-permute-start(bf16[64,640]{1,0:T(8,128)(2,1)} %after.5.refs_2_), channel_id=1, source_target_pairs={{0,4},{4,0},{8,12},{12,8},{1,5},{5,1},{9,13},{13,9},{2,6},{6,2},{1... | collective-permute-start | bytes 245768 | tf_op jit(solution)/shard_map/ppermute | solution.py:481
  36.0 2.2 %copy-start.4 = (bf16[4,256,2048]{2,1,0:T(8,128)(2,1)S(1)}, bf16[4,256,2048]{2,1,0:T(8,128)(2,1)}, u32[]{:S(2)}) copy-start(bf16[4,256,2048]{2,1,0:T(8,128)(2,1)} %copy-done.2) | copy-start | bytes 12582916
  (10 other events, 10.2 us)

commit v6 on v5

--- a/solution.py
+++ b/solution.py
@@ -302,6 +302,7 @@
         in_specs=[away] * (1 + len(others)),
         out_specs=away,
         input_output_aliases={0: 0},
+        compiler_params=pltpu.CompilerParams(vmem_limit_bytes=2**20),
         cost_estimate=pl.CostEstimate(flops=0, bytes_accessed=0, transcendentals=0),
         name="after",
     )(array, *others)

time: 40.8 us -> 31.6 us (0.77)
  local copies, waits for them, and re-layouts: 12.4 us -> 0.01 us
  waiting for transfers between devices: 2 us -> 5.49 us
    unnamed x38 -> x6, local copies, waits for them, and re-layouts: 12.4 us -> 0.01 us
    ppermute x15, waiting for transfers between devices: 2 us -> 5.49 us  [exchange(): return lax.ppermute(array, axis, [(i, i ^ distance) for i in range(count)])]
  transfers between devices with their start and end apart: 15 -> 15, of which waited for: 4 -> 6; matrix products, arithmetic and copies ran while one was open for 0% -> 0% of each run, Pallas kernels for 21% -> 26%
where the time goes in v6:
time: 31.6 us; the launch traced here: 31.4 us
  Pallas kernels  13.8 us (44%)
  starting transfers between devices  12.1 us (38%)
  waiting for transfers between devices  5.49 us (17%)
    ppermute x15, starting transfers between devices, exchange(): return lax.ppermute(array, axis, [(i, i ^ distance) for i in range(count)])  12.1 us
    ppermute x15, waiting for transfers between devices, exchange(): return lax.ppermute(array, axis, [(i, i ^ distance) for i in range(count)])  5.49 us
    pallas_call x1, Pallas kernels, prepared(): pl.pallas_call(functools.partial(prepare_kernel, slots, slices_owned), ou...  4.15 us
    pallas_call x1, Pallas kernels, column_filtered(): pl.pallas_call(functools.partial(first_kernel, slots, slices_owned), out_...  4.08 us
    pallas_call x1, Pallas kernels, column_filtered(): pl.pallas_call(functools.partial(second_kernel, later, slices_owned), out...  2.99 us
    pallas_call x2, Pallas kernels, interpolation(): pl.pallas_call(functools.partial(kernel, slots, len(patches[0])), in_spec...  2.55 us
  transfers between devices with their start and end apart: 15, of which 6 were waited for; matrix products, arithmetic and copies ran while one was open for 0% of the time, Pallas kernels for 26%

profile of v6, /device:TPU:0, one launch (start us, length us, event | category | flops | bytes accessed | tf_op | source)
XLA Modules:
  0.0 31.4 jit_solution(18165912846710791810)
XLA Ops:
  0.0 4.1 %forward_and_first_slots.1 = (bf16[64,640]{1,0:T(8,128)(2,1)}, bf16[64,640]{1,0:T(8,128)(2,1)}, f32[8,64,256]{2,1,0:T(8,128)}) custom-call(bf16[64,2048]{1,0:T(8,128)(2,1)} %bitcast.1, bf16[5,256,512]{2,1,0:T(8,128)(2,1)} %constant.2.clone.matrix_ref, f32[4]{0:T(128)} %angle_ref.3, s32[4,4]{1,0:T(4,128)} %defocus_ref.3, s32[4,4,4]{2,1,0:T(4,128)} %starts_ref.3), custom_call_target="tpu_custom_call" | custom-call | flops 587202560 | bytes 3145728 | tf_op jit(solution)/shard_map/forward_and_first_slots/pallas_call | solution.py:258
  4.1 5.1 %collective-permute-start.3 = (bf16[64,640]{1,0:T(8,128)(2,1)}, bf16[64,640]{1,0:T(8,128)(2,1)S(1)}, u32[]{:S(2)}, u32[]{:S(2)}) collective-permute-start(bf16[64,640]{1,0:T(8,128)(2,1)} %get-tuple-element.16), channel_id=1, source_target_pairs={{0,3},{1,2},{2,1},{3,0},{4,7},{5,6},{6,5},{7,4},{8,11},{9,10},{10,... | collective-permute-start | bytes 245768 | tf_op jit(solution)/shard_map/ppermute | solution.py:482
  9.2 3.0 %later_slots.1 = (bf16[64,640]{1,0:T(8,128)(2,1)}, bf16[64,640]{1,0:T(8,128)(2,1)}) custom-call(f32[8,64,256]{2,1,0:T(8,128)} %get-tuple-element.14.spectrum_ref, bf16[5,256,512]{2,1,0:T(8,128)(2,1)} %constant.2.clone.matrix_ref, f32[4]{0:T(128)} %angle_ref.3, s32[4,4]{1,0:T(4,128)} %defocus_ref.3, s32[4,4,4]{2,1,0:T(4,128)} %starts_ref.3), custom_call_target="tpu_custom_call" | custom-call | flops 234881024 | bytes 3145728 | tf_op jit(solution)/shard_map/later_slots/pallas_call | solution.py:278
  12.2 1.6 %collective-permute-start.1 = (bf16[64,640]{1,0:T(8,128)(2,1)}, bf16[64,640]{1,0:T(8,128)(2,1)S(1)}, u32[]{:S(2)}, u32[]{:S(2)}) collective-permute-start(bf16[64,640]{1,0:T(8,128)(2,1)} %get-tuple-element.15.refs_0_), channel_id=1, source_target_pairs={{0,8},{4,12},{8,0},{12,4},{1,9},{5,13},{9,1},{13,5},{2,10},{6,14},... | collective-permute-start | bytes 245768 | tf_op jit(solution)/shard_map/ppermute | solution.py:482
  13.8 0.1 collective-permute-done.7.refs_8_.refs_2_
  13.9 0.8 %collective-permute-start.11 = (bf16[64,640]{1,0:T(8,128)(2,1)}, bf16[64,640]{1,0:T(8,128)(2,1)S(1)}, u32[]{:S(2)}, u32[]{:S(2)}) collective-permute-start(bf16[64,640]{1,0:T(8,128)(2,1)} %after.4), channel_id=1, source_target_pairs={{0,2},{1,3},{2,0},{3,1},{4,6},{5,7},{6,4},{7,5},{8,10},{9,11},{10,... | collective-permute-start | bytes 245768 | tf_op jit(solution)/shard_map/ppermute | solution.py:482
  14.7 1.0 %collective-permute-start.5 = (bf16[64,640]{1,0:T(8,128)(2,1)S(1)}, bf16[64,640]{1,0:T(8,128)(2,1)S(1)}, u32[]{:S(2)}, u32[]{:S(2)}) collective-permute-start(bf16[64,640]{1,0:T(8,128)(2,1)S(1)} %collective-permute-done.3.refs_4_.refs_1_), channel_id=1, source_target_pairs={{0,8},{4,12},{8,0},{12,4},{1,9},{5,13},{9,1},{13,5},{2,10},{6,14},... | collective-permute-start | bytes 245768 | tf_op jit(solution)/shard_map/ppermute | solution.py:482
  15.7 1.2 %collective-permute-done.1.refs_0_ = bf16[64,640]{1,0:T(8,128)(2,1)S(1)} collective-permute-done((bf16[64,640]{1,0:T(8,128)(2,1)}, bf16[64,640]{1,0:T(8,128)(2,1)S(1)}, u32[]{:S(2)}, u32[]{:S(2)}) %collective-permute-start.1) | collective-permute-done | bytes 81952 | tf_op jit(solution)/shard_map/ppermute | solution.py:482
  16.9 2.1 %collective-permute-start.9 = (bf16[64,640]{1,0:T(8,128)(2,1)S(1)}, bf16[64,640]{1,0:T(8,128)(2,1)S(1)}, u32[]{:S(2)}, u32[]{:S(2)}) collective-permute-start(bf16[64,640]{1,0:T(8,128)(2,1)S(1)} %collective-permute-done.7.refs_8_.refs_2_), channel_id=1, source_target_pairs={{0,8},{4,12},{8,0},{12,4},{1,9},{5,13},{9,1},{13,5},{2,10},{6,14},... | collective-permute-start | bytes 245768 | tf_op jit(solution)/shard_map/ppermute | solution.py:482
  19.1 4.2 %prepare.1 = (bf16[256,256]{1,0:T(8,128)(2,1)S(1)}, bf16[4,256,2048]{2,1,0:T(8,128)(2,1)S(1)}) custom-call(f32[4]{0:T(128)S(1)} %copy-done.2, s32[4,4]{1,0:T(4,128)S(1)} %copy-done.1), custom_call_target="tpu_custom_call" | custom-call | flops 2147483648 | bytes 6291456 | tf_op jit(solution)/shard_map/prepare/pallas_call | solution.py:364
  23.2 0.0 collective-permute-done.refs_1_
  23.2 0.1 collective-permute-start.2
  23.3 0.5 %collective-permute-start.8 = (bf16[64,640]{1,0:T(8,128)(2,1)S(1)}, bf16[64,640]{1,0:T(8,128)(2,1)S(1)}, u32[]{:S(2)}, u32[]{:S(2)}) collective-permute-start(bf16[64,640]{1,0:T(8,128)(2,1)S(1)} %collective-permute-done.7.refs_8_.refs_2_), channel_id=1, source_target_pairs={{0,4},{4,0},{8,12},{12,8},{1,5},{5,1},{9,13},{13,9},{2,6},{6,2},{1... | collective-permute-start | bytes 245768 | tf_op jit(solution)/shard_map/ppermute | solution.py:482
  23.8 0.0 collective-permute-done.4.refs_5_
  23.8 0.1 collective-permute-start.6
  23.9 0.4 %collective-permute-start.10 = (bf16[64,640]{1,0:T(8,128)(2,1)S(1)}, bf16[64,640]{1,0:T(8,128)(2,1)S(1)}, u32[]{:S(2)}, u32[]{:S(2)}) collective-permute-start(bf16[64,640]{1,0:T(8,128)(2,1)S(1)} %collective-permute-done.9.refs_10_), channel_id=1, source_target_pairs={{0,4},{4,0},{8,12},{12,8},{1,5},{5,1},{9,13},{13,9},{2,6},{6,2},{1... | collective-permute-start | bytes 245768 | tf_op jit(solution)/shard_map/ppermute | solution.py:482
  24.3 0.0 collective-permute-start.13
  24.3 0.4 %collective-permute-done.8.refs_9_ = bf16[64,640]{1,0:T(8,128)(2,1)S(1)} collective-permute-done((bf16[64,640]{1,0:T(8,128)(2,1)S(1)}, bf16[64,640]{1,0:T(8,128)(2,1)S(1)}, u32[]{:S(2)}, u32[]{:S(2)}) %collective-permute-start.8) | collective-permute-done | bytes 81952 | tf_op jit(solution)/shard_map/ppermute | solution.py:482
  24.7 0.4 %collective-permute-start.12 = (bf16[64,640]{1,0:T(8,128)(2,1)S(1)}, bf16[64,640]{1,0:T(8,128)(2,1)S(1)}, u32[]{:S(2)}, u32[]{:S(2)}) collective-permute-start(bf16[64,640]{1,0:T(8,128)(2,1)S(1)} %collective-permute-done.11.refs_0_), channel_id=1, source_target_pairs={{0,4},{4,0},{8,12},{12,8},{1,5},{5,1},{9,13},{13,9},{2,6},{6,2},{1... | collective-permute-start | bytes 245768 | tf_op jit(solution)/shard_map/ppermute | solution.py:482
  25.1 0.2 collective-permute-done.10.refs_11_
  25.3 1.2 %sum_early_tilts.1.refs_1_.total_ref = f32[256,2048]{1,0:T(8,128)S(1)} custom-call(bf16[256,256]{1,0:T(8,128)(2,1)S(1)} %get-tuple-element.12.refs_1_.rows_ref, bf16[4,256,2048]{2,1,0:T(8,128)(2,1)S(1)} %get-tuple-element.13.weights_ref, bf16[64,640]{1,0:T(8,128)(2,1)S(1)} %copy-done, bf16[64,640]{1,0:T(8,128)(2,1)S(1)} %collective-permute-done.refs_1_, ...), custom_call_target="tpu_custom_call" | custom-call | flops 805306368 | bytes 3145728 | tf_op jit(solution)/shard_map/sum_early_tilts/pallas_call | solution.py:441
  26.4 2.3 %collective-permute-done.13.refs_0_ = bf16[64,640]{1,0:T(8,128)(2,1)S(1)} collective-permute-done((bf16[64,640]{1,0:T(8,128)(2,1)S(1)}, bf16[64,640]{1,0:T(8,128)(2,1)S(1)}, u32[]{:S(2)}, u32[]{:S(2)}) %collective-permute-start.13) | collective-permute-done | bytes 81952 | tf_op jit(solution)/shard_map/ppermute | solution.py:482
  28.8 1.3 %collective-permute-done.14.refs_3_ = bf16[64,640]{1,0:T(8,128)(2,1)S(1)} collective-permute-done((bf16[64,640]{1,0:T(8,128)(2,1)S(1)}, bf16[64,640]{1,0:T(8,128)(2,1)S(1)}, u32[]{:S(2)}, u32[]{:S(2)}) %collective-permute-start.14) | collective-permute-done | bytes 81952 | tf_op jit(solution)/shard_map/ppermute | solution.py:482
  30.1 1.4 %finish_volume.1 = bf16[16,64,512]{2,1,0:T(8,128)(2,1)} custom-call(bf16[256,256]{1,0:T(8,128)(2,1)S(1)} %get-tuple-element.12.refs_1_.rows_ref, bf16[4,256,2048]{2,1,0:T(8,128)(2,1)S(1)} %get-tuple-element.13.weights_ref, f32[256,2048]{1,0:T(8,128)S(1)} %sum_early_tilts.1.refs_1_.total_ref, bf16[64,640]{1,0:T(8,128)(2,1)S(1)} %collective-permute-done.11.refs_0_, ...), custom_call_target="tpu_custom_call" | custom-call | flops 268435456 | bytes 3145728 | tf_op jit(solution)/shard_map/finish_volume/pallas_call | solution.py:441
  (20 shorter events, 0.0 us)
Async XLA Ops:
  0.0 19.0 %copy-start.1 = (s32[4,4]{1,0:T(4,128)S(1)}, s32[4,4]{1,0:T(4,128)}, u32[]{:S(2)}) copy-start(s32[4,4]{1,0:T(4,128)} %defocus_ref.3) | copy-start | bytes 196
  0.0 19.0 %copy-start.2 = (f32[4]{0:T(128)S(1)}, f32[4]{0:T(128)}, u32[]{:S(2)}) copy-start(f32[4]{0:T(128)} %angle_ref.3) | copy-start | bytes 52
  4.1 9.7 %collective-permute-start.3 = (bf16[64,640]{1,0:T(8,128)(2,1)}, bf16[64,640]{1,0:T(8,128)(2,1)S(1)}, u32[]{:S(2)}, u32[]{:S(2)}) collective-permute-start(bf16[64,640]{1,0:T(8,128)(2,1)} %get-tuple-element.16), channel_id=1, source_target_pairs={{0,3},{1,2},{2,1},{3,0},{4,7},{5,6},{6,5},{7,4},{8,11},{9,10},{10,... | collective-permute-start | bytes 245768 | tf_op jit(solution)/shard_map/ppermute | solution.py:482
  9.2 4.7 %collective-permute-start.7 = (bf16[64,640]{1,0:T(8,128)(2,1)}, bf16[64,640]{1,0:T(8,128)(2,1)S(1)}, u32[]{:S(2)}, u32[]{:S(2)}) collective-permute-start(bf16[64,640]{1,0:T(8,128)(2,1)} %get-tuple-element.17), channel_id=1, source_target_pairs={{0,1},{1,0},{2,3},{3,2},{4,5},{5,4},{6,7},{7,6},{8,9},{9,8},{10,11... | collective-permute-start | bytes 245768 | tf_op jit(solution)/shard_map/ppermute | solution.py:482
  12.2 4.7 %collective-permute-start.1 = (bf16[64,640]{1,0:T(8,128)(2,1)}, bf16[64,640]{1,0:T(8,128)(2,1)S(1)}, u32[]{:S(2)}, u32[]{:S(2)}) collective-permute-start(bf16[64,640]{1,0:T(8,128)(2,1)} %get-tuple-element.15.refs_0_), channel_id=1, source_target_pairs={{0,8},{4,12},{8,0},{12,4},{1,9},{5,13},{9,1},{13,5},{2,10},{6,14},... | collective-permute-start | bytes 245768 | tf_op jit(solution)/shard_map/ppermute | solution.py:482
  13.8 9.4 %collective-permute-start = (bf16[64,640]{1,0:T(8,128)(2,1)}, bf16[64,640]{1,0:T(8,128)(2,1)S(1)}, u32[]{:S(2)}, u32[]{:S(2)}) collective-permute-start(bf16[64,640]{1,0:T(8,128)(2,1)} %get-tuple-element.15.refs_0_), channel_id=1, source_target_pairs={{0,4},{4,0},{8,12},{12,8},{1,5},{5,1},{9,13},{13,9},{2,6},{6,2},{1... | collective-permute-start | bytes 245768 | tf_op jit(solution)/shard_map/ppermute | solution.py:482
  13.9 11.4 %copy-start = (bf16[64,640]{1,0:T(8,128)(2,1)S(1)}, bf16[64,640]{1,0:T(8,128)(2,1)}, u32[]{:S(2)}) copy-start(bf16[64,640]{1,0:T(8,128)(2,1)} %get-tuple-element.15.refs_0_) | copy-start | bytes 245764
  13.9 10.4 %collective-permute-start.11 = (bf16[64,640]{1,0:T(8,128)(2,1)}, bf16[64,640]{1,0:T(8,128)(2,1)S(1)}, u32[]{:S(2)}, u32[]{:S(2)}) collective-permute-start(bf16[64,640]{1,0:T(8,128)(2,1)} %after.4), channel_id=1, source_target_pairs={{0,2},{1,3},{2,0},{3,1},{4,6},{5,7},{6,4},{7,5},{8,10},{9,11},{10,... | collective-permute-start | bytes 245768 | tf_op jit(solution)/shard_map/ppermute | solution.py:482
  14.7 8.6 %collective-permute-start.5 = (bf16[64,640]{1,0:T(8,128)(2,1)S(1)}, bf16[64,640]{1,0:T(8,128)(2,1)S(1)}, u32[]{:S(2)}, u32[]{:S(2)}) collective-permute-start(bf16[64,640]{1,0:T(8,128)(2,1)S(1)} %collective-permute-done.3.refs_4_.refs_1_), channel_id=1, source_target_pairs={{0,8},{4,12},{8,0},{12,4},{1,9},{5,13},{9,1},{13,5},{2,10},{6,14},... | collective-permute-start | bytes 245768 | tf_op jit(solution)/shard_map/ppermute | solution.py:482
  15.7 8.1 %collective-permute-start.4 = (bf16[64,640]{1,0:T(8,128)(2,1)S(1)}, bf16[64,640]{1,0:T(8,128)(2,1)S(1)}, u32[]{:S(2)}, u32[]{:S(2)}) collective-permute-start(bf16[64,640]{1,0:T(8,128)(2,1)S(1)} %collective-permute-done.3.refs_4_.refs_1_), channel_id=1, source_target_pairs={{0,4},{4,0},{8,12},{12,8},{1,5},{5,1},{9,13},{13,9},{2,6},{6,2},{1... | collective-permute-start | bytes 245768 | tf_op jit(solution)/shard_map/ppermute | solution.py:482
  16.9 7.0 %collective-permute-start.9 = (bf16[64,640]{1,0:T(8,128)(2,1)S(1)}, bf16[64,640]{1,0:T(8,128)(2,1)S(1)}, u32[]{:S(2)}, u32[]{:S(2)}) collective-permute-start(bf16[64,640]{1,0:T(8,128)(2,1)S(1)} %collective-permute-done.7.refs_8_.refs_2_), channel_id=1, source_target_pairs={{0,8},{4,12},{8,0},{12,4},{1,9},{5,13},{9,1},{13,5},{2,10},{6,14},... | collective-permute-start | bytes 245768 | tf_op jit(solution)/shard_map/ppermute | solution.py:482
  23.2 1.9 %collective-permute-start.2 = (bf16[64,640]{1,0:T(8,128)(2,1)S(1)}, bf16[64,640]{1,0:T(8,128)(2,1)S(1)}, u32[]{:S(2)}, u32[]{:S(2)}) collective-permute-start(bf16[64,640]{1,0:T(8,128)(2,1)S(1)} %after.3.refs_2_), channel_id=1, source_target_pairs={{0,4},{4,0},{8,12},{12,8},{1,5},{5,1},{9,13},{13,9},{2,6},{6,2},{1... | collective-permute-start | bytes 245768 | tf_op jit(solution)/shard_map/ppermute | solution.py:482
  23.3 1.4 %collective-permute-start.8 = (bf16[64,640]{1,0:T(8,128)(2,1)S(1)}, bf16[64,640]{1,0:T(8,128)(2,1)S(1)}, u32[]{:S(2)}, u32[]{:S(2)}) collective-permute-start(bf16[64,640]{1,0:T(8,128)(2,1)S(1)} %collective-permute-done.7.refs_8_.refs_2_), channel_id=1, source_target_pairs={{0,4},{4,0},{8,12},{12,8},{1,5},{5,1},{9,13},{13,9},{2,6},{6,2},{1... | collective-permute-start | bytes 245768 | tf_op jit(solution)/shard_map/ppermute | solution.py:482
  23.8 1.3 %collective-permute-start.6 = (bf16[64,640]{1,0:T(8,128)(2,1)S(1)}, bf16[64,640]{1,0:T(8,128)(2,1)S(1)}, u32[]{:S(2)}, u32[]{:S(2)}) collective-permute-start(bf16[64,640]{1,0:T(8,128)(2,1)S(1)} %collective-permute-done.5.refs_6_), channel_id=1, source_target_pairs={{0,4},{4,0},{8,12},{12,8},{1,5},{5,1},{9,13},{13,9},{2,6},{6,2},{1... | collective-permute-start | bytes 245768 | tf_op jit(solution)/shard_map/ppermute | solution.py:482
  23.9 1.3 %collective-permute-start.10 = (bf16[64,640]{1,0:T(8,128)(2,1)S(1)}, bf16[64,640]{1,0:T(8,128)(2,1)S(1)}, u32[]{:S(2)}, u32[]{:S(2)}) collective-permute-start(bf16[64,640]{1,0:T(8,128)(2,1)S(1)} %collective-permute-done.9.refs_10_), channel_id=1, source_target_pairs={{0,4},{4,0},{8,12},{12,8},{1,5},{5,1},{9,13},{13,9},{2,6},{6,2},{1... | collective-permute-start | bytes 245768 | tf_op jit(solution)/shard_map/ppermute | solution.py:482
  24.3 4.4 %collective-permute-start.13 = (bf16[64,640]{1,0:T(8,128)(2,1)S(1)}, bf16[64,640]{1,0:T(8,128)(2,1)S(1)}, u32[]{:S(2)}, u32[]{:S(2)}) collective-permute-start(bf16[64,640]{1,0:T(8,128)(2,1)S(1)} %collective-permute-done.11.refs_0_), channel_id=1, source_target_pairs={{0,8},{4,12},{8,0},{12,4},{1,9},{5,13},{9,1},{13,5},{2,10},{6,14},... | collective-permute-start | bytes 245768 | tf_op jit(solution)/shard_map/ppermute | solution.py:482
  24.7 4.0 %collective-permute-start.12 = (bf16[64,640]{1,0:T(8,128)(2,1)S(1)}, bf16[64,640]{1,0:T(8,128)(2,1)S(1)}, u32[]{:S(2)}, u32[]{:S(2)}) collective-permute-start(bf16[64,640]{1,0:T(8,128)(2,1)S(1)} %collective-permute-done.11.refs_0_), channel_id=1, source_target_pairs={{0,4},{4,0},{8,12},{12,8},{1,5},{5,1},{9,13},{13,9},{2,6},{6,2},{1... | collective-permute-start | bytes 245768 | tf_op jit(solution)/shard_map/ppermute | solution.py:482
  28.8 1.3 %collective-permute-start.14 = (bf16[64,640]{1,0:T(8,128)(2,1)S(1)}, bf16[64,640]{1,0:T(8,128)(2,1)S(1)}, u32[]{:S(2)}, u32[]{:S(2)}) collective-permute-start(bf16[64,640]{1,0:T(8,128)(2,1)S(1)} %after.5.refs_2_), channel_id=1, source_target_pairs={{0,4},{4,0},{8,12},{12,8},{1,5},{5,1},{9,13},{13,9},{2,6},{6,2},{1... | collective-permute-start | bytes 245768 | tf_op jit(solution)/shard_map/ppermute | solution.py:482

commit v7 on v6

--- a/solution.py
+++ b/solution.py
@@ -16,11 +16,15 @@
 SLICES = 64
 RADIX = 8
 MAIN = 128
-REST = 32
+REST = 16
 REACH = MAIN + REST
-PACKED = XBLK * REACH
 WINDOW = 384
 ROOT = math.sqrt(0.5)
+
+
+def split(table):
+    high = table.astype(jnp.bfloat16)
+    return high, (table - high.astype(np.float64)).astype(jnp.bfloat16)
 
 
 def column_tables(columns):
@@ -38,10 +42,6 @@
     full = angles(RADIX * np.arange(size))
     waves = np.concatenate([np.cos(full), np.sin(full)], 1)
     ends = np.concatenate([m0, m4], 1)
-
-    def split(table):
-        high = table.astype(jnp.bfloat16)
-        return high, (table - high.astype(np.float64)).astype(jnp.bfloat16)
 
     matrices = np.stack([*split(ends), *split(waves), np.concatenate([m0.T, m4.T], 1).astype(jnp.bfloat16)])
     return matrices
@@ -61,6 +61,18 @@
     return fold * fold, gain, jnp.cos(angle), jnp.sin(angle)
 
 
+def row_tables(full_rows):
+    half = full_rows // 2
+    column = np.arange(full_rows)
+    freq = np.where(column <= half, column, column - half)
+    angle = 2.0 * np.pi * (np.arange(full_rows)[:, None] * freq[None, :] % full_rows) / full_rows
+    return np.stack(split(np.where(column[None, :] <= half, np.cos(angle), np.sin(angle))))
+
+
+def packed_shape(rows):
+    return (2 * rows + rows // 4, 2 * MAIN)
+
+
 def flip_sign(squares, defocus, length):
     cycles = lax.div(squares * defocus, jnp.int32(length * length))
     return (1 - 2 * (cycles & 1)).astype(jnp.float32)
@@ -77,7 +89,7 @@
     line = jnp.full((8, XBW), angle, jnp.float32)
     cosine, sine = jnp.cos(line), jnp.sin(line)
     lowest = 0.5 * XBW + jnp.minimum((XBW - 1) * cosine, 0.0) - 0.5 * (SLAB - 1) * jnp.abs(sine)
-    first = jnp.clip(jnp.floor(lowest) - 8.0, 0.0, float(BAND - REACH))
+    first = jnp.clip(jnp.floor(lowest) - 4.0, 0.0, float(BAND - REACH))
     return cosine[:1], sine[:1], jnp.max(first).astype(jnp.int32)
 
 
@@ -156,10 +168,15 @@
             window = turned[i * rows : (i + 1) * rows, pl.ds(base, WINDOW)]
             shift = base - start
             reach = pltpu.roll(window, jnp.where(shift < 0, shift + WINDOW, shift), 1)[:, : 2 * MAIN]
-            out[i, :, block * MAIN : (block + 1) * MAIN] = reach[:, :MAIN].astype(jnp.bfloat16)
+            there = slice(block // 2 * rows, (block // 2 + 1) * rows), slice(block % 2 * MAIN, (block % 2 + 1) * MAIN)
+            out[i, *there] = reach[:, :MAIN].astype(jnp.bfloat16)
             last = reach[:, MAIN:]
             rest = jnp.where(lane == block, pltpu.roll(last, block * REST, 1) if block else last, rest)
-        out[i, :, XBLK * MAIN :] = rest.astype(jnp.bfloat16)
+        quarters = [rest[q * rows // 4 : (q + 1) * rows // 4] for q in range(4)]
+        for tile in range(2):
+            right = pltpu.roll(quarters[2 * tile + 1], XBLK * REST, 1)
+            both = jnp.where(lane[: rows // 4] < XBLK, quarters[2 * tile], right)
+            out[i, 2 * rows :, tile * MAIN : (tile + 1) * MAIN] = both.astype(jnp.bfloat16)
         sends.append(pltpu.make_async_copy(out.at[i], out_refs[i], out_sems.at[i]))
         sends[-1].start()
     return sends
@@ -235,7 +252,7 @@
     matrices = jnp.asarray(column_tables(columns))
     away = pl.BlockSpec(memory_space=pl.ANY)
     spectrum = jax.ShapeDtypeStruct((8, rows, size), jnp.float32)
-    patch = jax.ShapeDtypeStruct((rows, PACKED), jnp.bfloat16)
+    patch = jax.ShapeDtypeStruct(packed_shape(rows), jnp.bfloat16)
     small = [
         pltpu.SMEM(angles.shape, jnp.float32),
         pltpu.SMEM(defocus.shape, jnp.int32),
@@ -247,7 +264,7 @@
             pltpu.VMEM((2, count * rows, size), jnp.float32),
             pltpu.VMEM((6, count * rows, 2 * size), jnp.float32),
             pltpu.VMEM((count * rows, columns), jnp.float32),
-            pltpu.VMEM((count, rows, PACKED), jnp.bfloat16),
+            pltpu.VMEM((count, *packed_shape(rows)), jnp.bfloat16),
             pltpu.SemaphoreType.DMA((count,)),
         ]
 
@@ -308,55 +325,47 @@
     )(array, *others)
 
 
-def prepare_kernel(slots, slices_owned, angles, defocus, rows_ref, weights_ref, waves, mine, order):
+def prepare_kernel(slots, slices_owned, angles, defocus, waves, rows_ref, weights_ref, mine, order):
     tilt, row = lax.axis_index("tilt"), lax.axis_index("row")
     slab, local_first = tilt * slices_owned // SLAB, tilt * slices_owned % SLAB
-    full_rows = waves.shape[0]
+    full_rows = waves.shape[1]
     rows = rows_ref.shape[0] // slots
     half = full_rows // 2
-
-    def row_waves(block, carry):
-        here = pl.ds(pl.multiple_of(block * rows, rows), rows)
-        y = block * rows + lax.broadcasted_iota(jnp.int32, (rows, full_rows), 0)
-        column = lax.broadcasted_iota(jnp.int32, (rows, full_rows), 1)
-        freq = jnp.where(column <= half, column, column - half)
-        angle = ((y * freq) & (full_rows - 1)).astype(jnp.float32) * (2.0 * math.pi / full_rows)
-        waves[here, :] = jnp.cos(jnp.where(column <= half, angle, angle - 0.5 * math.pi))
-        return carry
-
-    lax.fori_loop(0, full_rows // rows, row_waves, 0)
-    own = waves[pl.ds(pl.multiple_of(row * rows, rows), rows), :]
     column = lax.broadcasted_iota(jnp.int32, (8, full_rows), 1)
     freq = jnp.where(column <= half, column, column - half)
     count = jnp.where((freq == 0) | (freq == half), 1.0, 2.0) / full_rows
-    for slot in range(slots):
-        sign = flip_sign(freq * freq, defocus[tilt ^ slot, slab], full_rows)
-        mine[slot * rows : (slot + 1) * rows, :] = own * (sign * count)[:1]
-    for block in range(full_rows // rows):
-        order[block * rows : (block + 1) * rows, :] = waves[pl.ds(pl.multiple_of((row ^ block) * rows, rows), rows), :]
-    rows_ref[...] = lax.dot_general(
-        mine[...],
-        order[...],
-        (((1,), (1,)), ((), ())),
-        precision=lax.Precision.HIGHEST,
-        preferred_element_type=jnp.float32,
-    ).astype(jnp.bfloat16)
-
-    column = lax.broadcasted_iota(jnp.int32, (1, XBW), 1).astype(jnp.float32)
-    place = lax.broadcasted_iota(jnp.int32, (2 * MAIN, XBW), 0)
-    place = jnp.where(place < MAIN, place, MAIN + place % REST).astype(jnp.float32)
+    scales = [(flip_sign(freq * freq, defocus[tilt ^ slot, slab], full_rows) * count)[:1] for slot in range(slots)]
+    for part in range(2):
+        for block in range(full_rows // rows):
+            there = pl.ds(pl.multiple_of((row ^ block) * rows, rows), rows)
+            order[part, block * rows : (block + 1) * rows, :] = waves[part, there, :]
+        own = order[part, :rows, :].astype(jnp.float32)
+        for slot in range(slots):
+            mine[part, slot * rows : (slot + 1) * rows, :] = (own * scales[slot]).astype(jnp.bfloat16)
+
+    def product(left, right):
+        over = (((1,), (1,)), ((), ()))
+        return lax.dot_general(mine[left], order[right], over, preferred_element_type=jnp.float32)
+
+    rows_ref[...] = (product(0, 0) + product(0, 1) + product(1, 0)).astype(jnp.bfloat16)
+
+    place = lax.broadcasted_iota(jnp.int32, (REACH, XBW), 0).astype(jnp.float32)
+    across = lax.broadcasted_iota(jnp.int32, (1, XBW), 1).astype(jnp.float32)
     for slot in range(slots):
         cosine, sine, first_tap = reach_of(angles[tilt ^ slot])
         tap = place + first_tap.astype(jnp.float32)
 
         def one_slice(c, carry):
             offset = (local_first + c).astype(jnp.float32) - 0.5 * (SLAB - 1)
-            centre = 0.5 * XBW + column * cosine + offset * sine
+            centre = 0.5 * XBW + across * cosine + offset * sine
             there = pl.ds(pl.multiple_of(c * XBW, XBW), XBW)
-            weights_ref[slot, :, there] = jnp.maximum(0.0, 1.0 - jnp.abs(tap - centre)).astype(jnp.bfloat16)
+            weights = jnp.maximum(0.0, 1.0 - jnp.abs(tap - centre)).astype(jnp.bfloat16)
+            weights_ref[slot, :REACH, there] = weights
+            for block in range(1, XBLK):
+                weights_ref[slot, MAIN + block * REST : MAIN + (block + 1) * REST, there] = weights[MAIN:]
             return carry
 
-        lax.fori_loop(0, slices_owned, one_slice, 0)
+        lax.fori_loop(0, slices_owned, one_slice, 0, unroll=2)
 
 
 def prepared(slots, slices_owned, rows, full_rows, angles, defocus):
@@ -365,29 +374,39 @@
         functools.partial(prepare_kernel, slots, slices_owned),
         out_shape=[
             jax.ShapeDtypeStruct((slots * rows, full_rows), jnp.bfloat16),
-            jax.ShapeDtypeStruct((slots, 2 * MAIN, slices_owned * XBW), jnp.bfloat16),
+            jax.ShapeDtypeStruct((slots, MAIN + XBLK * REST, slices_owned * XBW), jnp.bfloat16),
         ],
-        in_specs=[smem] * 2,
+        in_specs=[smem] * 2 + [vmem],
         out_specs=[vmem] * 2,
         scratch_shapes=[
-            pltpu.VMEM((full_rows, full_rows), jnp.float32),
-            pltpu.VMEM((slots * rows, full_rows), jnp.float32),
-            pltpu.VMEM((full_rows, full_rows), jnp.float32),
+            pltpu.VMEM((2, slots * rows, full_rows), jnp.bfloat16),
+            pltpu.VMEM((2, full_rows, full_rows), jnp.bfloat16),
         ],
         compiler_params=pltpu.CompilerParams(vmem_limit_bytes=32 * 2**20),
         cost_estimate=pl.CostEstimate(flops=2**31, bytes_accessed=6 * 2**20, transcendentals=0),
         name="prepare",
-    )(angles, defocus)
+    )(angles, defocus, jnp.asarray(row_tables(full_rows)))
+
+
+def unpacked(packed):
+    rows = 4 * packed.shape[0] // 9
+    rest = packed[2 * rows :].astype(jnp.float32)
+    quarters = []
+    for tile in range(2):
+        both = rest[:, tile * MAIN : (tile + 1) * MAIN]
+        quarters += [both, pltpu.roll(both, MAIN - XBLK * REST, 1)]
+    rest = jnp.concatenate(quarters, 0).astype(jnp.bfloat16)
+    return jnp.concatenate([packed[:rows], packed[rows : 2 * rows], rest], 1)
 
 
 def corrected_patches(slot, rows_ref, patch_refs):
-    rows = patch_refs[0].shape[0]
-    patches = jnp.concatenate([ref[...] for ref in patch_refs], 0)
+    patches = jnp.concatenate([unpacked(ref[...]) for ref in patch_refs], 0)
+    rows = patches.shape[0] // len(patch_refs)
     image = jnp.dot(rows_ref[slot * rows : (slot + 1) * rows, :], patches, preferred_element_type=jnp.float32)
     lane = lax.broadcasted_iota(jnp.int32, (rows, MAIN), 1) // REST
     main = jnp.concatenate([image[:, block * MAIN : (block + 1) * MAIN] for block in range(XBLK)], 0)
     rest = jnp.concatenate([jnp.where(lane == block, image[:, XBLK * MAIN :], 0.0) for block in range(XBLK)], 0)
-    return jnp.concatenate([main, rest], 1).astype(jnp.bfloat16)
+    return jnp.concatenate([main, rest[:, : XBLK * REST]], 1).astype(jnp.bfloat16)
 
 
 def sum_kernel(slots, row_devices, rows_ref, weights_ref, *refs):
@@ -408,7 +427,7 @@
 def finish_kernel(factor, slots, row_devices, rows_ref, weights_ref, total_ref, *refs):
     patch_refs = refs[: len(slots) * row_devices]
     out_ref, out, sems = refs[len(slots) * row_devices :]
-    rows = patch_refs[0].shape[0]
+    rows = total_ref.shape[0] // XBLK
     parts = [
         corrected_patches(slot, rows_ref, patch_refs[i * row_devices : (i + 1) * row_devices])
         for i, slot in enumerate(slots)
@@ -433,11 +452,11 @@
 
 
 def interpolation(kernel, slots, weights, row_filters, patches, totals, **call):
-    _, _, width = weights.shape
-    rows = patches[0][0].shape[0]
+    _, taps, width = weights.shape
+    rows = row_filters.shape[0] // weights.shape[0]
     vmem = pl.BlockSpec(memory_space=pltpu.VMEM)
     operands = [row_filters, weights, *totals, *(block for slot in slots for block in patches[slot])]
-    flops = 4 * len(slots) * MAIN * width * XBLK * rows
+    flops = 2 * len(slots) * taps * width * XBLK * rows
     return pl.pallas_call(
         functools.partial(kernel, slots, len(patches[0])),
         in_specs=[vmem] * len(operands),
@@ -455,14 +474,14 @@
         row_filters,
         patches,
         [],
-        out_shape=jax.ShapeDtypeStruct((XBLK * patches[0][0].shape[0], weights.shape[2]), jnp.float32),
+        out_shape=jax.ShapeDtypeStruct((XBLK * row_filters.shape[0] // weights.shape[0], weights.shape[2]), jnp.float32),
         out_specs=pl.BlockSpec(memory_space=pltpu.VMEM),
         name="sum_early_tilts",
     )
 
 
 def finished(row_filters, weights, total, patches, slots, factor):
-    shape = (weights.shape[2] // XBW, patches[0][0].shape[0], XBLK * XBW)
+    shape = (weights.shape[2] // XBW, row_filters.shape[0] // weights.shape[0], XBLK * XBW)
     return interpolation(
         functools.partial(finish_kernel, factor),
         slots,
@@ -504,7 +523,7 @@
     patches = {0: gather_rows(arrived[0], (row_filters,))} | {d: gather_rows(arrived[d]) for d in odd}
     total = summed(row_filters, weights, patches, [0] + odd)
     for d in even:
-        arrived[d] = exchange(after(sent[d], *(arrived[o] for o in odd)), "tilt", d)
+        arrived[d] = exchange(after(sent[d], arrived[1]), "tilt", d)
         patches[d] = gather_rows(arrived[d], (total,))
     return finished(row_filters, weights, total, patches, even, 1.0 / math.sqrt(tilt_devices))
 

time: 31.6 us -> 29.4 us (0.930)
  Pallas kernels: 13.8 us -> 12.3 us
  waiting for transfers between devices: 5.49 us -> 4.1 us
  local copies, waits for them, and re-layouts: 0.01 us -> 0.9 us
  starting transfers between devices: 12.1 us -> 11.7 us
    pallas_call x1, Pallas kernels: 4.15 us -> 2.52 us  [prepared(): pl.pallas_call(functools.partial(prepare_kernel, slots, slices_owned), ou...]
    ppermute x15, waiting for transfers between devices: 5.49 us -> 4.1 us  [exchange(): return lax.ppermute(array, axis, [(i, i ^ distance) for i in range(count)])]
    unnamed x6 -> x10, local copies, waits for them, and re-layouts: 0.01 us -> 0.9 us
    ppermute x15, starting transfers between devices: 12.1 us -> 11.7 us  [exchange(): return lax.ppermute(array, axis, [(i, i ^ distance) for i in range(count)])]
  transfers between devices with their start and end apart: 15 -> 15, of which waited for: 6 -> 3; matrix products, arithmetic and copies ran while one was open for 0% -> 0% of each run, Pallas kernels for 26% -> 23%
where the time goes in v7:
time: 29.4 us; the launch traced here: 29.2 us
  Pallas kernels  12.3 us (42%)
  starting transfers between devices  11.7 us (40%)
  waiting for transfers between devices  4.1 us (14%)
  local copies, waits for them, and re-layouts  0.9 us (3%)
    ppermute x15, starting transfers between devices, exchange(): return lax.ppermute(array, axis, [(i, i ^ distance) for i in range(count)])  11.7 us
    pallas_call x1, Pallas kernels, column_filtered(): pl.pallas_call(functools.partial(first_kernel, slots, slices_owned), out_...  4.15 us
    ppermute x15, waiting for transfers between devices, exchange(): return lax.ppermute(array, axis, [(i, i ^ distance) for i in range(count)])  4.1 us
    pallas_call x1, Pallas kernels, column_filtered(): pl.pallas_call(functools.partial(second_kernel, later, slices_owned), out...  3.05 us
    pallas_call x2, Pallas kernels, interpolation(): pl.pallas_call(functools.partial(kernel, slots, len(patches[0])), in_spec...  2.6 us
    pallas_call x1, Pallas kernels, prepared(): pl.pallas_call(functools.partial(prepare_kernel, slots, slices_owned), ou...  2.52 us
    unnamed x10, local copies, waits for them, and re-layouts  0.9 us
  transfers between devices with their start and end apart: 15, of which 3 were waited for; matrix products, arithmetic and copies ran while one was open for 0% of the time, Pallas kernels for 23%

profile of v7, /device:TPU:0, one launch (start us, length us, event | category | flops | bytes accessed | tf_op | source)
XLA Modules:
  0.0 29.2 jit_solution(13170300456430067303)
XLA Ops:
  0.0 4.2 %forward_and_first_slots.1 = (bf16[144,256]{1,0:T(8,128)(2,1)}, bf16[144,256]{1,0:T(8,128)(2,1)}, f32[8,64,256]{2,1,0:T(8,128)}) custom-call(bf16[64,2048]{1,0:T(8,128)(2,1)} %bitcast.1, bf16[5,256,512]{2,1,0:T(8,128)(2,1)} %constant.4.clone.matrix_ref, f32[4]{0:T(128)} %angle_ref.3, s32[4,4]{1,0:T(4,128)} %defocus_ref.3, s32[4,4,4]{2,1,0:T(4,128)} %starts_ref.3), custom_call_target="tpu_custom_call" | custom-call | flops 587202560 | bytes 3145728 | tf_op jit(solution)/shard_map/forward_and_first_slots/pallas_call | solution.py:275
  4.2 5.1 %collective-permute-start.3 = (bf16[144,256]{1,0:T(8,128)(2,1)}, bf16[144,256]{1,0:T(8,128)(2,1)S(1)}, u32[]{:S(2)}, u32[]{:S(2)}) collective-permute-start(bf16[144,256]{1,0:T(8,128)(2,1)} %get-tuple-element.16), channel_id=1, source_target_pairs={{0,3},{1,2},{2,1},{3,0},{4,7},{5,6},{6,5},{7,4},{8,11},{9,10},{10,... | collective-permute-start | bytes 221192 | tf_op jit(solution)/shard_map/ppermute | solution.py:501
  9.3 0.0 collective-permute-start.7
  9.3 3.0 %later_slots.1 = (bf16[144,256]{1,0:T(8,128)(2,1)}, bf16[144,256]{1,0:T(8,128)(2,1)}) custom-call(f32[8,64,256]{2,1,0:T(8,128)} %get-tuple-element.14.spectrum_ref, bf16[5,256,512]{2,1,0:T(8,128)(2,1)} %constant.4.clone.matrix_ref, f32[4]{0:T(128)} %angle_ref.3, s32[4,4]{1,0:T(4,128)} %defocus_ref.3, s32[4,4,4]{2,1,0:T(4,128)} %starts_ref.3), custom_call_target="tpu_custom_call" | custom-call | flops 234881024 | bytes 3145728 | tf_op jit(solution)/shard_map/later_slots/pallas_call | solution.py:295
  12.3 1.6 %collective-permute-start.1 = (bf16[144,256]{1,0:T(8,128)(2,1)}, bf16[144,256]{1,0:T(8,128)(2,1)S(1)}, u32[]{:S(2)}, u32[]{:S(2)}) collective-permute-start(bf16[144,256]{1,0:T(8,128)(2,1)} %get-tuple-element.15.refs_0_), channel_id=1, source_target_pairs={{0,8},{4,12},{8,0},{12,4},{1,9},{5,13},{9,1},{13,5},{2,10},{6,14},... | collective-permute-start | bytes 221192 | tf_op jit(solution)/shard_map/ppermute | solution.py:501
  13.9 0.0 collective-permute-done.7.refs_8_.refs_1_
  13.9 0.9 %copy-done = bf16[144,256]{1,0:T(8,128)(2,1)S(1)} copy-done((bf16[144,256]{1,0:T(8,128)(2,1)S(1)}, bf16[144,256]{1,0:T(8,128)(2,1)}, u32[]{:S(2)}) %copy-start) | copy-done | bytes 73752
  14.8 0.8 %collective-permute-start.11 = (bf16[144,256]{1,0:T(8,128)(2,1)S(1)}, bf16[144,256]{1,0:T(8,128)(2,1)S(1)}, u32[]{:S(2)}, u32[]{:S(2)}) collective-permute-start(bf16[144,256]{1,0:T(8,128)(2,1)S(1)} %after.4), channel_id=1, source_target_pairs={{0,2},{1,3},{2,0},{3,1},{4,6},{5,7},{6,4},{7,5},{8,10},{9,11},{10,... | collective-permute-start | bytes 221192 | tf_op jit(solution)/shard_map/ppermute | solution.py:501
  15.6 0.7 %collective-permute-start.5 = (bf16[144,256]{1,0:T(8,128)(2,1)S(1)}, bf16[144,256]{1,0:T(8,128)(2,1)S(1)}, u32[]{:S(2)}, u32[]{:S(2)}) collective-permute-start(bf16[144,256]{1,0:T(8,128)(2,1)S(1)} %collective-permute-done.3.refs_4_), channel_id=1, source_target_pairs={{0,8},{4,12},{8,0},{12,4},{1,9},{5,13},{9,1},{13,5},{2,10},{6,14},... | collective-permute-start | bytes 221192 | tf_op jit(solution)/shard_map/ppermute | solution.py:501
  16.3 0.6 %collective-permute-done.1.refs_0_ = bf16[144,256]{1,0:T(8,128)(2,1)S(1)} collective-permute-done((bf16[144,256]{1,0:T(8,128)(2,1)}, bf16[144,256]{1,0:T(8,128)(2,1)S(1)}, u32[]{:S(2)}, u32[]{:S(2)}) %collective-permute-start.1) | collective-permute-done | bytes 73760 | tf_op jit(solution)/shard_map/ppermute | solution.py:501
  17.0 1.5 %collective-permute-start.9 = (bf16[144,256]{1,0:T(8,128)(2,1)S(1)}, bf16[144,256]{1,0:T(8,128)(2,1)S(1)}, u32[]{:S(2)}, u32[]{:S(2)}) collective-permute-start(bf16[144,256]{1,0:T(8,128)(2,1)S(1)} %collective-permute-done.7.refs_8_.refs_1_), channel_id=1, source_target_pairs={{0,8},{4,12},{8,0},{12,4},{1,9},{5,13},{9,1},{13,5},{2,10},{6,14},... | collective-permute-start | bytes 221192 | tf_op jit(solution)/shard_map/ppermute | solution.py:501
  18.5 2.5 %prepare.1 = (bf16[256,256]{1,0:T(8,128)(2,1)S(1)}, bf16[4,192,2048]{2,1,0:T(8,128)(2,1)S(1)}) custom-call(f32[4]{0:T(128)S(1)} %copy-done.3, s32[4,4]{1,0:T(4,128)S(1)} %copy-done.2, bf16[2,256,256]{2,1,0:T(8,128)(2,1)S(1)} %copy-done.4), custom_call_target="tpu_custom_call" | custom-call | flops 2147483648 | bytes 6291456 | tf_op jit(solution)/shard_map/prepare/pallas_call | solution.py:373
  21.0 0.0 collective-permute-done.refs_1_
  21.1 0.1 collective-permute-start.2
  21.1 0.0 collective-permute-done.5.refs_6_
  21.1 0.5 %collective-permute-start.8 = (bf16[144,256]{1,0:T(8,128)(2,1)S(1)}, bf16[144,256]{1,0:T(8,128)(2,1)S(1)}, u32[]{:S(2)}, u32[]{:S(2)}) collective-permute-start(bf16[144,256]{1,0:T(8,128)(2,1)S(1)} %collective-permute-done.7.refs_8_.refs_1_), channel_id=1, source_target_pairs={{0,4},{4,0},{8,12},{12,8},{1,5},{5,1},{9,13},{13,9},{2,6},{6,2},{1... | collective-permute-start | bytes 221192 | tf_op jit(solution)/shard_map/ppermute | solution.py:501
  21.6 0.1 collective-permute-start.6
  21.7 0.0 collective-permute-done.9.refs_10_
  21.7 0.4 %collective-permute-start.10 = (bf16[144,256]{1,0:T(8,128)(2,1)S(1)}, bf16[144,256]{1,0:T(8,128)(2,1)S(1)}, u32[]{:S(2)}, u32[]{:S(2)}) collective-permute-start(bf16[144,256]{1,0:T(8,128)(2,1)S(1)} %collective-permute-done.9.refs_10_), channel_id=1, source_target_pairs={{0,4},{4,0},{8,12},{12,8},{1,5},{5,1},{9,13},{13,9},{2,6},{6,2},{1... | collective-permute-start | bytes 221192 | tf_op jit(solution)/shard_map/ppermute | solution.py:501
  22.2 0.9 %collective-permute-start.13 = (bf16[144,256]{1,0:T(8,128)(2,1)S(1)}, bf16[144,256]{1,0:T(8,128)(2,1)S(1)}, u32[]{:S(2)}, u32[]{:S(2)}) collective-permute-start(bf16[144,256]{1,0:T(8,128)(2,1)S(1)} %collective-permute-done.11.refs_0_), channel_id=1, source_target_pairs={{0,8},{4,12},{8,0},{12,4},{1,9},{5,13},{9,1},{13,5},{2,10},{6,14},... | collective-permute-start | bytes 221192 | tf_op jit(solution)/shard_map/ppermute | solution.py:501
  23.1 1.2 %sum_early_tilts.1.refs_1_.total_ref = f32[256,2048]{1,0:T(8,128)S(1)} custom-call(bf16[256,256]{1,0:T(8,128)(2,1)S(1)} %get-tuple-element.12.refs_1_.rows_ref, bf16[4,192,2048]{2,1,0:T(8,128)(2,1)S(1)} %get-tuple-element.13.weights_ref, bf16[144,256]{1,0:T(8,128)(2,1)S(1)} %copy-done.1, bf16[144,256]{1,0:T(8,128)(2,1)S(1)} %collective-permute-done.refs_1_, ...), custom_call_target="tpu_custom_call" | custom-call | flops 603979776 | bytes 3145728 | tf_op jit(solution)/shard_map/sum_early_tilts/pallas_call | solution.py:460
  24.3 2.2 %collective-permute-done.13.refs_0_ = bf16[144,256]{1,0:T(8,128)(2,1)S(1)} collective-permute-done((bf16[144,256]{1,0:T(8,128)(2,1)S(1)}, bf16[144,256]{1,0:T(8,128)(2,1)S(1)}, u32[]{:S(2)}, u32[]{:S(2)}) %collective-permute-start.13) | collective-permute-done | bytes 73760 | tf_op jit(solution)/shard_map/ppermute | solution.py:501
  26.5 1.3 %collective-permute-done.14.refs_3_ = bf16[144,256]{1,0:T(8,128)(2,1)S(1)} collective-permute-done((bf16[144,256]{1,0:T(8,128)(2,1)S(1)}, bf16[144,256]{1,0:T(8,128)(2,1)S(1)}, u32[]{:S(2)}, u32[]{:S(2)}) %collective-permute-start.14) | collective-permute-done | bytes 73760 | tf_op jit(solution)/shard_map/ppermute | solution.py:501
  27.8 1.4 %finish_volume.1 = bf16[16,64,512]{2,1,0:T(8,128)(2,1)} custom-call(bf16[256,256]{1,0:T(8,128)(2,1)S(1)} %get-tuple-element.12.refs_1_.rows_ref, bf16[4,192,2048]{2,1,0:T(8,128)(2,1)S(1)} %get-tuple-element.13.weights_ref, f32[256,2048]{1,0:T(8,128)S(1)} %sum_early_tilts.1.refs_1_.total_ref, bf16[144,256]{1,0:T(8,128)(2,1)S(1)} %collective-permute-done.11.refs_0_, ...), custom_call_target="tpu_custom_call" | custom-call | flops 201326592 | bytes 3145728 | tf_op jit(solution)/shard_map/finish_volume/pallas_call | solution.py:460
  (24 shorter events, 0.1 us)
Async XLA Ops:
  0.0 18.5 %copy-start.2 = (s32[4,4]{1,0:T(4,128)S(1)}, s32[4,4]{1,0:T(4,128)}, u32[]{:S(2)}) copy-start(s32[4,4]{1,0:T(4,128)} %defocus_ref.3) | copy-start | bytes 196
  0.0 18.5 %copy-start.3 = (f32[4]{0:T(128)S(1)}, f32[4]{0:T(128)}, u32[]{:S(2)}) copy-start(f32[4]{0:T(128)} %angle_ref.3) | copy-start | bytes 52
  0.0 18.5 %copy-start.4 = (bf16[2,256,256]{2,1,0:T(8,128)(2,1)S(1)}, bf16[2,256,256]{2,1,0:T(8,128)(2,1)}, u32[]{:S(2)}) copy-start(bf16[2,256,256]{2,1,0:T(8,128)(2,1)} %constant.5.clone.waves) | copy-start | bytes 786436
  4.2 11.4 %collective-permute-start.3 = (bf16[144,256]{1,0:T(8,128)(2,1)}, bf16[144,256]{1,0:T(8,128)(2,1)S(1)}, u32[]{:S(2)}, u32[]{:S(2)}) collective-permute-start(bf16[144,256]{1,0:T(8,128)(2,1)} %get-tuple-element.16), channel_id=1, source_target_pairs={{0,3},{1,2},{2,1},{3,0},{4,7},{5,6},{6,5},{7,4},{8,11},{9,10},{10,... | collective-permute-start | bytes 221192 | tf_op jit(solution)/shard_map/ppermute | solution.py:501
  9.3 4.7 %collective-permute-start.7 = (bf16[144,256]{1,0:T(8,128)(2,1)}, bf16[144,256]{1,0:T(8,128)(2,1)S(1)}, u32[]{:S(2)}, u32[]{:S(2)}) collective-permute-start(bf16[144,256]{1,0:T(8,128)(2,1)} %get-tuple-element.17), channel_id=1, source_target_pairs={{0,1},{1,0},{2,3},{3,2},{4,5},{5,4},{6,7},{7,6},{8,9},{9,8},{10,11... | collective-permute-start | bytes 221192 | tf_op jit(solution)/shard_map/ppermute | solution.py:501
  12.3 4.6 %collective-permute-start.1 = (bf16[144,256]{1,0:T(8,128)(2,1)}, bf16[144,256]{1,0:T(8,128)(2,1)S(1)}, u32[]{:S(2)}, u32[]{:S(2)}) collective-permute-start(bf16[144,256]{1,0:T(8,128)(2,1)} %get-tuple-element.15.refs_0_), channel_id=1, source_target_pairs={{0,8},{4,12},{8,0},{12,4},{1,9},{5,13},{9,1},{13,5},{2,10},{6,14},... | collective-permute-start | bytes 221192 | tf_op jit(solution)/shard_map/ppermute | solution.py:501
  13.9 7.1 %collective-permute-start = (bf16[144,256]{1,0:T(8,128)(2,1)}, bf16[144,256]{1,0:T(8,128)(2,1)S(1)}, u32[]{:S(2)}, u32[]{:S(2)}) collective-permute-start(bf16[144,256]{1,0:T(8,128)(2,1)} %get-tuple-element.15.refs_0_), channel_id=1, source_target_pairs={{0,4},{4,0},{8,12},{12,8},{1,5},{5,1},{9,13},{13,9},{2,6},{6,2},{1... | collective-permute-start | bytes 221192 | tf_op jit(solution)/shard_map/ppermute | solution.py:501
  13.9 0.9 %copy-start = (bf16[144,256]{1,0:T(8,128)(2,1)S(1)}, bf16[144,256]{1,0:T(8,128)(2,1)}, u32[]{:S(2)}) copy-start(bf16[144,256]{1,0:T(8,128)(2,1)} %get-tuple-element.18.refs_0_) | copy-start | bytes 221188
  14.8 8.3 %copy-start.1 = (bf16[144,256]{1,0:T(8,128)(2,1)S(1)}, bf16[144,256]{1,0:T(8,128)(2,1)}, u32[]{:S(2)}) copy-start(bf16[144,256]{1,0:T(8,128)(2,1)} %get-tuple-element.15.refs_0_) | copy-start | bytes 221188
  14.8 7.3 %collective-permute-start.11 = (bf16[144,256]{1,0:T(8,128)(2,1)S(1)}, bf16[144,256]{1,0:T(8,128)(2,1)S(1)}, u32[]{:S(2)}, u32[]{:S(2)}) collective-permute-start(bf16[144,256]{1,0:T(8,128)(2,1)S(1)} %after.4), channel_id=1, source_target_pairs={{0,2},{1,3},{2,0},{3,1},{4,6},{5,7},{6,4},{7,5},{8,10},{9,11},{10,... | collective-permute-start | bytes 221192 | tf_op jit(solution)/shard_map/ppermute | solution.py:501
  15.6 5.5 %collective-permute-start.5 = (bf16[144,256]{1,0:T(8,128)(2,1)S(1)}, bf16[144,256]{1,0:T(8,128)(2,1)S(1)}, u32[]{:S(2)}, u32[]{:S(2)}) collective-permute-start(bf16[144,256]{1,0:T(8,128)(2,1)S(1)} %collective-permute-done.3.refs_4_), channel_id=1, source_target_pairs={{0,8},{4,12},{8,0},{12,4},{1,9},{5,13},{9,1},{13,5},{2,10},{6,14},... | collective-permute-start | bytes 221192 | tf_op jit(solution)/shard_map/ppermute | solution.py:501
  16.3 5.3 %collective-permute-start.4 = (bf16[144,256]{1,0:T(8,128)(2,1)S(1)}, bf16[144,256]{1,0:T(8,128)(2,1)S(1)}, u32[]{:S(2)}, u32[]{:S(2)}) collective-permute-start(bf16[144,256]{1,0:T(8,128)(2,1)S(1)} %collective-permute-done.3.refs_4_), channel_id=1, source_target_pairs={{0,4},{4,0},{8,12},{12,8},{1,5},{5,1},{9,13},{13,9},{2,6},{6,2},{1... | collective-permute-start | bytes 221192 | tf_op jit(solution)/shard_map/ppermute | solution.py:501
  17.0 4.8 %collective-permute-start.9 = (bf16[144,256]{1,0:T(8,128)(2,1)S(1)}, bf16[144,256]{1,0:T(8,128)(2,1)S(1)}, u32[]{:S(2)}, u32[]{:S(2)}) collective-permute-start(bf16[144,256]{1,0:T(8,128)(2,1)S(1)} %collective-permute-done.7.refs_8_.refs_1_), channel_id=1, source_target_pairs={{0,8},{4,12},{8,0},{12,4},{1,9},{5,13},{9,1},{13,5},{2,10},{6,14},... | collective-permute-start | bytes 221192 | tf_op jit(solution)/shard_map/ppermute | solution.py:501
  21.1 2.0 %collective-permute-start.2 = (bf16[144,256]{1,0:T(8,128)(2,1)S(1)}, bf16[144,256]{1,0:T(8,128)(2,1)S(1)}, u32[]{:S(2)}, u32[]{:S(2)}) collective-permute-start(bf16[144,256]{1,0:T(8,128)(2,1)S(1)} %after.3.refs_2_), channel_id=1, source_target_pairs={{0,4},{4,0},{8,12},{12,8},{1,5},{5,1},{9,13},{13,9},{2,6},{6,2},{1... | collective-permute-start | bytes 221192 | tf_op jit(solution)/shard_map/ppermute | solution.py:501
  21.1 1.9 %collective-permute-start.8 = (bf16[144,256]{1,0:T(8,128)(2,1)S(1)}, bf16[144,256]{1,0:T(8,128)(2,1)S(1)}, u32[]{:S(2)}, u32[]{:S(2)}) collective-permute-start(bf16[144,256]{1,0:T(8,128)(2,1)S(1)} %collective-permute-done.7.refs_8_.refs_1_), channel_id=1, source_target_pairs={{0,4},{4,0},{8,12},{12,8},{1,5},{5,1},{9,13},{13,9},{2,6},{6,2},{1... | collective-permute-start | bytes 221192 | tf_op jit(solution)/shard_map/ppermute | solution.py:501
  21.6 1.5 %collective-permute-start.6 = (bf16[144,256]{1,0:T(8,128)(2,1)S(1)}, bf16[144,256]{1,0:T(8,128)(2,1)S(1)}, u32[]{:S(2)}, u32[]{:S(2)}) collective-permute-start(bf16[144,256]{1,0:T(8,128)(2,1)S(1)} %collective-permute-done.5.refs_6_), channel_id=1, source_target_pairs={{0,4},{4,0},{8,12},{12,8},{1,5},{5,1},{9,13},{13,9},{2,6},{6,2},{1... | collective-permute-start | bytes 221192 | tf_op jit(solution)/shard_map/ppermute | solution.py:501
  21.7 1.4 %collective-permute-start.10 = (bf16[144,256]{1,0:T(8,128)(2,1)S(1)}, bf16[144,256]{1,0:T(8,128)(2,1)S(1)}, u32[]{:S(2)}, u32[]{:S(2)}) collective-permute-start(bf16[144,256]{1,0:T(8,128)(2,1)S(1)} %collective-permute-done.9.refs_10_), channel_id=1, source_target_pairs={{0,4},{4,0},{8,12},{12,8},{1,5},{5,1},{9,13},{13,9},{2,6},{6,2},{1... | collective-permute-start | bytes 221192 | tf_op jit(solution)/shard_map/ppermute | solution.py:501
  22.2 4.4 %collective-permute-start.13 = (bf16[144,256]{1,0:T(8,128)(2,1)S(1)}, bf16[144,256]{1,0:T(8,128)(2,1)S(1)}, u32[]{:S(2)}, u32[]{:S(2)}) collective-permute-start(bf16[144,256]{1,0:T(8,128)(2,1)S(1)} %collective-permute-done.11.refs_0_), channel_id=1, source_target_pairs={{0,8},{4,12},{8,0},{12,4},{1,9},{5,13},{9,1},{13,5},{2,10},{6,14},... | collective-permute-start | bytes 221192 | tf_op jit(solution)/shard_map/ppermute | solution.py:501
  23.1 3.4 %collective-permute-start.12 = (bf16[144,256]{1,0:T(8,128)(2,1)S(1)}, bf16[144,256]{1,0:T(8,128)(2,1)S(1)}, u32[]{:S(2)}, u32[]{:S(2)}) collective-permute-start(bf16[144,256]{1,0:T(8,128)(2,1)S(1)} %collective-permute-done.11.refs_0_), channel_id=1, source_target_pairs={{0,4},{4,0},{8,12},{12,8},{1,5},{5,1},{9,13},{13,9},{2,6},{6,2},{1... | collective-permute-start | bytes 221192 | tf_op jit(solution)/shard_map/ppermute | solution.py:501
  26.5 1.3 %collective-permute-start.14 = (bf16[144,256]{1,0:T(8,128)(2,1)S(1)}, bf16[144,256]{1,0:T(8,128)(2,1)S(1)}, u32[]{:S(2)}, u32[]{:S(2)}) collective-permute-start(bf16[144,256]{1,0:T(8,128)(2,1)S(1)} %after.5.refs_2_), channel_id=1, source_target_pairs={{0,4},{4,0},{8,12},{12,8},{1,5},{5,1},{9,13},{13,9},{2,6},{6,2},{1... | collective-permute-start | bytes 221192 | tf_op jit(solution)/shard_map/ppermute | solution.py:501

commit v8 on v7

--- a/solution.py
+++ b/solution.py
@@ -182,10 +182,10 @@
     return sends
 
 
-def first_kernel(slots, slices_owned, image_ref, matrix_ref, angle_ref, defocus_ref, starts_ref, *refs):
+def column_kernel(slots, slices_owned, image_ref, matrix_ref, angle_ref, defocus_ref, starts_ref, *refs):
     count = len(slots)
-    out_refs, spectrum_ref = refs[:count], refs[count]
-    image, matrix, angles, defocus, starts, zhi, zlo, held, *scratch, sems, held_sem = refs[count + 1 :]
+    out_refs = refs[:count]
+    image, matrix, angles, defocus, starts, zhi, zlo, *scratch, sems = refs[count:]
     rows, columns = image.shape
     size = columns // RADIX
     copies = fetched(
@@ -212,103 +212,46 @@
     for j in range(3):
         real, imag = mixed[2 * j * rows : (2 * j + 1) * rows], mixed[(2 * j + 1) * rows : (2 * j + 2) * rows]
         spectrum += [real[:, :size] + imag[:, size:], imag[:, :size] - real[:, size:]]
-    for i in range(8):
-        held[i] = spectrum[i]
-    keep = pltpu.make_async_copy(held, spectrum_ref, held_sem)
-    keep.start()
     facts = (squares, ramp, turns, angles, defocus, starts)
     sends = send_patches(
         slots, slices_owned, spectrum, matrix.at[2], matrix.at[4], columns, facts, scratch, out_refs
     )
-    for copy in sends + [keep]:
-        copy.wait()
-
-
-def second_kernel(slots, slices_owned, spectrum_ref, matrix_ref, angle_ref, defocus_ref, starts_ref, *refs):
-    count = len(slots)
-    out_refs = refs[:count]
-    held, matrix, angles, defocus, starts, *scratch, sems = refs[count:]
-    columns = RADIX * held.shape[2]
-    copies = fetched(
-        [spectrum_ref, angle_ref, defocus_ref, starts_ref, matrix_ref.at[2], matrix_ref.at[4]],
-        [held, angles, defocus, starts, matrix.at[0], matrix.at[1]],
-        sems,
-    )
-    squares, ramp, cosine_turns, sine_turns = column_lines(columns)
-    turns = [t[j : j + 1, :] for j in range(3) for t in (cosine_turns, sine_turns)]
-    for copy in copies:
-        copy.wait()
-    facts = (squares, ramp, turns, angles, defocus, starts)
-    sends = send_patches(
-        slots, slices_owned, [held[i] for i in range(8)], matrix.at[0], matrix.at[1], columns, facts, scratch, out_refs
-    )
     for copy in sends:
         copy.wait()
 
 
-def column_filtered(slots, later, slices_owned, image, angles, defocus, starts):
+def column_filtered(slots, slices_owned, image, angles, defocus, starts):
     rows, columns = image.shape
     size = columns // RADIX
+    count = len(slots)
     matrices = jnp.asarray(column_tables(columns))
     away = pl.BlockSpec(memory_space=pl.ANY)
-    spectrum = jax.ShapeDtypeStruct((8, rows, size), jnp.float32)
-    patch = jax.ShapeDtypeStruct(packed_shape(rows), jnp.bfloat16)
-    small = [
-        pltpu.SMEM(angles.shape, jnp.float32),
-        pltpu.SMEM(defocus.shape, jnp.int32),
-        pltpu.SMEM(starts.shape, jnp.int32),
-    ]
-
-    def buffers(count):
-        return [
+    flops = 2 * rows * size * size * (42 + 14 * count)
+    sent = pl.pallas_call(
+        functools.partial(column_kernel, slots, slices_owned),
+        out_shape=[jax.ShapeDtypeStruct(packed_shape(rows), jnp.bfloat16)] * count,
+        in_specs=[away] * 5,
+        out_specs=[away] * count,
+        scratch_shapes=[
+            pltpu.VMEM((rows, columns), jnp.bfloat16),
+            pltpu.VMEM(matrices.shape, jnp.bfloat16),
+            pltpu.SMEM(angles.shape, jnp.float32),
+            pltpu.SMEM(defocus.shape, jnp.int32),
+            pltpu.SMEM(starts.shape, jnp.int32),
+            pltpu.VMEM((8, rows, size), jnp.bfloat16),
+            pltpu.VMEM((8, rows, size), jnp.bfloat16),
             pltpu.VMEM((2, count * rows, size), jnp.float32),
             pltpu.VMEM((6, count * rows, 2 * size), jnp.float32),
             pltpu.VMEM((count * rows, columns), jnp.float32),
             pltpu.VMEM((count, *packed_shape(rows)), jnp.bfloat16),
             pltpu.SemaphoreType.DMA((count,)),
-        ]
-
-    def cost(products):
-        return pl.CostEstimate(flops=2 * rows * size * size * products, bytes_accessed=3 * 2**20, transcendentals=0)
-
-    params = pltpu.CompilerParams(vmem_limit_bytes=60 * 2**20)
-    *first, held = pl.pallas_call(
-        functools.partial(first_kernel, slots, slices_owned),
-        out_shape=[patch] * len(slots) + [spectrum],
-        in_specs=[away] * 5,
-        out_specs=[away] * (len(slots) + 1),
-        scratch_shapes=[
-            pltpu.VMEM((rows, columns), jnp.bfloat16),
-            pltpu.VMEM(matrices.shape, jnp.bfloat16),
-            *small,
-            pltpu.VMEM((8, rows, size), jnp.bfloat16),
-            pltpu.VMEM((8, rows, size), jnp.bfloat16),
-            pltpu.VMEM(spectrum.shape, jnp.float32),
-            *buffers(len(slots)),
             pltpu.SemaphoreType.DMA((9,)),
-            pltpu.SemaphoreType.DMA,
         ],
-        compiler_params=params,
-        cost_estimate=cost(42 + 14 * len(slots)),
-        name="forward_and_first_slots",
+        compiler_params=pltpu.CompilerParams(vmem_limit_bytes=60 * 2**20),
+        cost_estimate=pl.CostEstimate(flops=flops, bytes_accessed=3 * 2**20, transcendentals=0),
+        name="column_filter",
     )(image, matrices, angles, defocus, starts)
-    second = pl.pallas_call(
-        functools.partial(second_kernel, later, slices_owned),
-        out_shape=[patch] * len(later),
-        in_specs=[away] * 5,
-        out_specs=[away] * len(later),
-        scratch_shapes=[
-            pltpu.VMEM(spectrum.shape, jnp.float32),
-            pltpu.VMEM((2,) + matrices.shape[1:], jnp.bfloat16),
-            *small,
-            *buffers(len(later)),
-            pltpu.SemaphoreType.DMA((6,)),
-        ],
-        compiler_params=params,
-        cost_estimate=cost(14 * len(later)),
-        name="later_slots",
-    )(held, matrices, angles, defocus, starts)
-    return dict(zip(slots, first)) | dict(zip(later, second))
+    return dict(zip(slots, sent))
 
 
 def after(array, *others):
@@ -516,16 +459,15 @@
     _, rows, _ = projections.shape
     row_devices, tilt_devices = lax.axis_size("row"), lax.axis_size("tilt")
     slices_owned = SLICES // tilt_devices
-    odd, even = list(range(tilt_devices - 1, 0, -2)), list(range(tilt_devices - 2, 0, -2))
-    sent = column_filtered(odd, even + [0], slices_owned, projections[0], tilt_angle, defocus, band_start)
-    arrived = {0: sent[0]} | {d: exchange(sent[d], "tilt", d) for d in odd}
+    far, near = list(range(tilt_devices - 1, 1, -1)), list(range(min(2, tilt_devices) - 1, -1, -1))
+    sent = column_filtered(far + near, slices_owned, projections[0], tilt_angle, defocus, band_start)
+    arrived = {d: exchange(sent[d], "tilt", d) if d else sent[d] for d in far + near}
     row_filters, weights = prepared(tilt_devices, slices_owned, rows, rows * row_devices, tilt_angle, defocus)
-    patches = {0: gather_rows(arrived[0], (row_filters,))} | {d: gather_rows(arrived[d]) for d in odd}
-    total = summed(row_filters, weights, patches, [0] + odd)
-    for d in even:
-        arrived[d] = exchange(after(sent[d], arrived[1]), "tilt", d)
-        patches[d] = gather_rows(arrived[d], (total,))
-    return finished(row_filters, weights, total, patches, even, 1.0 / math.sqrt(tilt_devices))
+    patches = {d: gather_rows(after(arrived[d], row_filters) if d else arrived[d]) for d in near}
+    total = summed(row_filters, weights, patches, near)
+    for d in far:
+        patches[d] = gather_rows(arrived[d], (total,) if d == far[-1] else ())
+    return finished(row_filters, weights, total, patches, far, 1.0 / math.sqrt(tilt_devices))
 
 
 def solution(mesh):

time: 29.4 us -> 27.6 us (0.939)
  waiting for transfers between devices: 4.1 us -> 7.43 us
  Pallas kernels: 12.3 us -> 9.99 us
  starting transfers between devices: 11.7 us -> 9.95 us
  local copies, waits for them, and re-layouts: 0.9 us -> 0.01 us
    ppermute x15, waiting for transfers between devices: 4.1 us -> 7.43 us  [exchange(): return lax.ppermute(array, axis, [(i, i ^ distance) for i in range(count)])]
    pallas_call x2 -> x1, Pallas kernels: 7.2 us -> 4.92 us  [column_filtered(): pl.pallas_call(functools.partial(column_kernel, slots, slices_owned), out...]
    ppermute x15, starting transfers between devices: 11.7 us -> 9.95 us  [exchange(): return lax.ppermute(array, axis, [(i, i ^ distance) for i in range(count)])]
    unnamed x10 -> x8, local copies, waits for them, and re-layouts: 0.9 us -> 0.01 us
  transfers between devices with their start and end apart: 15 -> 15, of which waited for: 3 -> 6; matrix products, arithmetic and copies ran while one was open for 0% -> 0% of each run, Pallas kernels for 23% -> 12%
where the time goes in v8:
time: 27.6 us; the launch traced here: 27.5 us
  Pallas kernels  9.99 us (36%)
  starting transfers between devices  9.95 us (36%)
  waiting for transfers between devices  7.43 us (27%)
    ppermute x15, starting transfers between devices, exchange(): return lax.ppermute(array, axis, [(i, i ^ distance) for i in range(count)])  9.95 us
    ppermute x15, waiting for transfers between devices, exchange(): return lax.ppermute(array, axis, [(i, i ^ distance) for i in range(count)])  7.43 us
    pallas_call x1, Pallas kernels, column_filtered(): pl.pallas_call(functools.partial(column_kernel, slots, slices_owned), out...  4.92 us
    pallas_call x2, Pallas kernels, interpolation(): pl.pallas_call(functools.partial(kernel, slots, len(patches[0])), in_spec...  2.54 us
    pallas_call x1, Pallas kernels, prepared(): pl.pallas_call(functools.partial(prepare_kernel, slots, slices_owned), ou...  2.53 us
  transfers between devices with their start and end apart: 15, of which 6 were waited for; matrix products, arithmetic and copies ran while one was open for 0% of the time, Pallas kernels for 12%

profile of v8, /device:TPU:0, one launch (start us, length us, event | category | flops | bytes accessed | tf_op | source)
XLA Modules:
  0.0 27.5 jit_solution(4307181720956625708)
XLA Ops:
  0.0 4.9 %column_filter.1 = (bf16[144,256]{1,0:T(8,128)(2,1)}, bf16[144,256]{1,0:T(8,128)(2,1)}, bf16[144,256]{1,0:T(8,128)(2,1)}, bf16[144,256]{1,0:T(8,128)(2,1)}) custom-call(bf16[64,2048]{1,0:T(8,128)(2,1)} %bitcast.1, bf16[5,256,512]{2,1,0:T(8,128)(2,1)} %constant.4.clone.matrix_ref, f32[4]{0:T(128)} %angle_ref.1, s32[4,4]{1,0:T(4,128)} %defocus_ref.1, ...), custom_call_target="tpu_custom_call" | custom-call | flops 822083584 | bytes 3145728 | tf_op jit(solution)/shard_map/column_filter/pallas_call | solution.py:230
  4.9 3.1 %collective-permute-start = (bf16[144,256]{1,0:T(8,128)(2,1)}, bf16[144,256]{1,0:T(8,128)(2,1)S(1)}, u32[]{:S(2)}, u32[]{:S(2)}) collective-permute-start(bf16[144,256]{1,0:T(8,128)(2,1)} %get-tuple-element.13), channel_id=1, source_target_pairs={{0,1},{1,0},{2,3},{3,2},{4,5},{5,4},{6,7},{7,6},{8,9},{9,8},{10,11... | collective-permute-start | bytes 221192 | tf_op jit(solution)/shard_map/ppermute | solution.py:444
  8.0 2.5 %collective-permute-start.7 = (bf16[144,256]{1,0:T(8,128)(2,1)}, bf16[144,256]{1,0:T(8,128)(2,1)S(1)}, u32[]{:S(2)}, u32[]{:S(2)}) collective-permute-start(bf16[144,256]{1,0:T(8,128)(2,1)} %get-tuple-element.15), channel_id=1, source_target_pairs={{0,3},{1,2},{2,1},{3,0},{4,7},{5,6},{6,5},{7,4},{8,11},{9,10},{10,... | collective-permute-start | bytes 221192 | tf_op jit(solution)/shard_map/ppermute | solution.py:444
  10.5 0.1 collective-permute-start.11
  10.6 1.5 %collective-permute-start.5 = (bf16[144,256]{1,0:T(8,128)(2,1)}, bf16[144,256]{1,0:T(8,128)(2,1)S(1)}, u32[]{:S(2)}, u32[]{:S(2)}) collective-permute-start(bf16[144,256]{1,0:T(8,128)(2,1)} %get-tuple-element.14.refs_4_), channel_id=1, source_target_pairs={{0,8},{4,12},{8,0},{12,4},{1,9},{5,13},{9,1},{13,5},{2,10},{6,14},... | collective-permute-start | bytes 221192 | tf_op jit(solution)/shard_map/ppermute | solution.py:444
  12.2 2.5 %prepare.1 = (bf16[256,256]{1,0:T(8,128)(2,1)S(1)}, bf16[4,192,2048]{2,1,0:T(8,128)(2,1)S(1)}) custom-call(f32[4]{0:T(128)S(1)} %copy-done.2, s32[4,4]{1,0:T(4,128)S(1)} %copy-done.1, bf16[2,256,256]{2,1,0:T(8,128)(2,1)S(1)} %copy-done.3), custom_call_target="tpu_custom_call" | custom-call | flops 2147483648 | bytes 6291456 | tf_op jit(solution)/shard_map/prepare/pallas_call | solution.py:316
  14.7 0.0 collective-permute-done.refs_0_
  14.7 0.6 %collective-permute-start.2 = (bf16[144,256]{1,0:T(8,128)(2,1)S(1)}, bf16[144,256]{1,0:T(8,128)(2,1)S(1)}, u32[]{:S(2)}, u32[]{:S(2)}) collective-permute-start(bf16[144,256]{1,0:T(8,128)(2,1)S(1)} %after.2.refs_0_), channel_id=1, source_target_pairs={{0,8},{4,12},{8,0},{12,4},{1,9},{5,13},{9,1},{13,5},{2,10},{6,14},... | collective-permute-start | bytes 221192 | tf_op jit(solution)/shard_map/ppermute | solution.py:444
  15.3 0.0 collective-permute-start.4
  15.3 0.2 collective-permute-done.7.refs_0_
  15.5 1.5 %collective-permute-start.9 = (bf16[144,256]{1,0:T(8,128)(2,1)S(1)}, bf16[144,256]{1,0:T(8,128)(2,1)S(1)}, u32[]{:S(2)}, u32[]{:S(2)}) collective-permute-start(bf16[144,256]{1,0:T(8,128)(2,1)S(1)} %collective-permute-done.7.refs_0_), channel_id=1, source_target_pairs={{0,8},{4,12},{8,0},{12,4},{1,9},{5,13},{9,1},{13,5},{2,10},{6,14},... | collective-permute-start | bytes 221192 | tf_op jit(solution)/shard_map/ppermute | solution.py:444
  17.0 0.1 collective-permute-start.6
  17.0 0.7 %collective-permute-done.11.refs_4_ = bf16[144,256]{1,0:T(8,128)(2,1)S(1)} collective-permute-done((bf16[144,256]{1,0:T(8,128)(2,1)}, bf16[144,256]{1,0:T(8,128)(2,1)S(1)}, u32[]{:S(2)}, u32[]{:S(2)}) %collective-permute-start.11) | collective-permute-done | bytes 73760 | tf_op jit(solution)/shard_map/ppermute | solution.py:444
  17.8 0.0 collective-permute-start.1
  17.8 2.1 %collective-permute-done.2.refs_2_ = bf16[144,256]{1,0:T(8,128)(2,1)S(1)} collective-permute-done((bf16[144,256]{1,0:T(8,128)(2,1)S(1)}, bf16[144,256]{1,0:T(8,128)(2,1)S(1)}, u32[]{:S(2)}, u32[]{:S(2)}) %collective-permute-start.2) | collective-permute-done | bytes 73760 | tf_op jit(solution)/shard_map/ppermute | solution.py:444
  19.9 0.0 collective-permute-start.3
  19.9 0.8 %collective-permute-done.9.refs_2_ = bf16[144,256]{1,0:T(8,128)(2,1)S(1)} collective-permute-done((bf16[144,256]{1,0:T(8,128)(2,1)S(1)}, bf16[144,256]{1,0:T(8,128)(2,1)S(1)}, u32[]{:S(2)}, u32[]{:S(2)}) %collective-permute-start.9) | collective-permute-done | bytes 73760 | tf_op jit(solution)/shard_map/ppermute | solution.py:444
  20.7 0.5 %collective-permute-start.12 = (bf16[144,256]{1,0:T(8,128)(2,1)S(1)}, bf16[144,256]{1,0:T(8,128)(2,1)S(1)}, u32[]{:S(2)}, u32[]{:S(2)}) collective-permute-start(bf16[144,256]{1,0:T(8,128)(2,1)S(1)} %collective-permute-done.11.refs_4_), channel_id=1, source_target_pairs={{0,4},{4,0},{8,12},{12,8},{1,5},{5,1},{9,13},{13,9},{2,6},{6,2},{1... | collective-permute-start | bytes 221192 | tf_op jit(solution)/shard_map/ppermute | solution.py:444
  21.2 0.1 collective-permute-start.10
  21.3 0.9 %sum_early_tilts.1.refs_1_.total_ref = f32[256,2048]{1,0:T(8,128)S(1)} custom-call(bf16[256,256]{1,0:T(8,128)(2,1)S(1)} %get-tuple-element.11.refs_1_.rows_ref, bf16[4,192,2048]{2,1,0:T(8,128)(2,1)S(1)} %get-tuple-element.12.weights_ref, bf16[144,256]{1,0:T(8,128)(2,1)S(1)} %after.2.refs_0_, bf16[144,256]{1,0:T(8,128)(2,1)S(1)} %collective-permute-done.1.refs_1_, ...), custom_call_target="tpu_custom_call" | custom-call | flops 402653184 | bytes 3145728 | tf_op jit(solution)/shard_map/sum_early_tilts/pallas_call | solution.py:403
  22.2 2.3 %collective-permute-done.13.refs_0_ = bf16[144,256]{1,0:T(8,128)(2,1)S(1)} collective-permute-done((bf16[144,256]{1,0:T(8,128)(2,1)S(1)}, bf16[144,256]{1,0:T(8,128)(2,1)S(1)}, u32[]{:S(2)}, u32[]{:S(2)}) %collective-permute-start.13) | collective-permute-done | bytes 73760 | tf_op jit(solution)/shard_map/ppermute | solution.py:444
  24.6 0.0 collective-permute-start.14
  24.6 1.2 %collective-permute-done.14.refs_7_ = bf16[144,256]{1,0:T(8,128)(2,1)S(1)} collective-permute-done((bf16[144,256]{1,0:T(8,128)(2,1)S(1)}, bf16[144,256]{1,0:T(8,128)(2,1)S(1)}, u32[]{:S(2)}, u32[]{:S(2)}) %collective-permute-start.14) | collective-permute-done | bytes 73760 | tf_op jit(solution)/shard_map/ppermute | solution.py:444
  25.8 1.6 %finish_volume.1 = bf16[16,64,512]{2,1,0:T(8,128)(2,1)} custom-call(bf16[256,256]{1,0:T(8,128)(2,1)S(1)} %get-tuple-element.11.refs_1_.rows_ref, bf16[4,192,2048]{2,1,0:T(8,128)(2,1)S(1)} %get-tuple-element.12.weights_ref, f32[256,2048]{1,0:T(8,128)S(1)} %sum_early_tilts.1.refs_1_.total_ref, bf16[144,256]{1,0:T(8,128)(2,1)S(1)} %collective-permute-done.7.refs_0_, ...), custom_call_target="tpu_custom_call" | custom-call | flops 402653184 | bytes 3145728 | tf_op jit(solution)/shard_map/finish_volume/pallas_call | solution.py:403
  (20 shorter events, 0.0 us)
Async XLA Ops:
  0.0 12.1 %copy-start.3 = (bf16[2,256,256]{2,1,0:T(8,128)(2,1)S(1)}, bf16[2,256,256]{2,1,0:T(8,128)(2,1)}, u32[]{:S(2)}) copy-start(bf16[2,256,256]{2,1,0:T(8,128)(2,1)} %constant.5.clone.waves) | copy-start | bytes 786436
  0.0 12.2 %copy-start.1 = (s32[4,4]{1,0:T(4,128)S(1)}, s32[4,4]{1,0:T(4,128)}, u32[]{:S(2)}) copy-start(s32[4,4]{1,0:T(4,128)} %defocus_ref.1) | copy-start | bytes 196
  0.0 12.2 %copy-start.2 = (f32[4]{0:T(128)S(1)}, f32[4]{0:T(128)}, u32[]{:S(2)}) copy-start(f32[4]{0:T(128)} %angle_ref.1) | copy-start | bytes 52
  4.9 9.8 %collective-permute-start = (bf16[144,256]{1,0:T(8,128)(2,1)}, bf16[144,256]{1,0:T(8,128)(2,1)S(1)}, u32[]{:S(2)}, u32[]{:S(2)}) collective-permute-start(bf16[144,256]{1,0:T(8,128)(2,1)} %get-tuple-element.13), channel_id=1, source_target_pairs={{0,1},{1,0},{2,3},{3,2},{4,5},{5,4},{6,7},{7,6},{8,9},{9,8},{10,11... | collective-permute-start | bytes 221192 | tf_op jit(solution)/shard_map/ppermute | solution.py:444
  8.0 7.4 %collective-permute-start.7 = (bf16[144,256]{1,0:T(8,128)(2,1)}, bf16[144,256]{1,0:T(8,128)(2,1)S(1)}, u32[]{:S(2)}, u32[]{:S(2)}) collective-permute-start(bf16[144,256]{1,0:T(8,128)(2,1)} %get-tuple-element.15), channel_id=1, source_target_pairs={{0,3},{1,2},{2,1},{3,0},{4,7},{5,6},{6,5},{7,4},{8,11},{9,10},{10,... | collective-permute-start | bytes 221192 | tf_op jit(solution)/shard_map/ppermute | solution.py:444
  10.5 7.3 %collective-permute-start.11 = (bf16[144,256]{1,0:T(8,128)(2,1)}, bf16[144,256]{1,0:T(8,128)(2,1)S(1)}, u32[]{:S(2)}, u32[]{:S(2)}) collective-permute-start(bf16[144,256]{1,0:T(8,128)(2,1)} %get-tuple-element.16), channel_id=1, source_target_pairs={{0,2},{1,3},{2,0},{3,1},{4,6},{5,7},{6,4},{7,5},{8,10},{9,11},{10,... | collective-permute-start | bytes 221192 | tf_op jit(solution)/shard_map/ppermute | solution.py:444
  10.6 4.7 %copy-start = (bf16[144,256]{1,0:T(8,128)(2,1)S(1)}, bf16[144,256]{1,0:T(8,128)(2,1)}, u32[]{:S(2)}) copy-start(bf16[144,256]{1,0:T(8,128)(2,1)} %get-tuple-element.14.refs_4_) | copy-start | bytes 221188
  10.6 6.3 %collective-permute-start.5 = (bf16[144,256]{1,0:T(8,128)(2,1)}, bf16[144,256]{1,0:T(8,128)(2,1)S(1)}, u32[]{:S(2)}, u32[]{:S(2)}) collective-permute-start(bf16[144,256]{1,0:T(8,128)(2,1)} %get-tuple-element.14.refs_4_), channel_id=1, source_target_pairs={{0,8},{4,12},{8,0},{12,4},{1,9},{5,13},{9,1},{13,5},{2,10},{6,14},... | collective-permute-start | bytes 221192 | tf_op jit(solution)/shard_map/ppermute | solution.py:444
  14.7 5.2 %collective-permute-start.2 = (bf16[144,256]{1,0:T(8,128)(2,1)S(1)}, bf16[144,256]{1,0:T(8,128)(2,1)S(1)}, u32[]{:S(2)}, u32[]{:S(2)}) collective-permute-start(bf16[144,256]{1,0:T(8,128)(2,1)S(1)} %after.2.refs_0_), channel_id=1, source_target_pairs={{0,8},{4,12},{8,0},{12,4},{1,9},{5,13},{9,1},{13,5},{2,10},{6,14},... | collective-permute-start | bytes 221192 | tf_op jit(solution)/shard_map/ppermute | solution.py:444
  15.3 4.6 %collective-permute-start.4 = (bf16[144,256]{1,0:T(8,128)(2,1)S(1)}, bf16[144,256]{1,0:T(8,128)(2,1)S(1)}, u32[]{:S(2)}, u32[]{:S(2)}) collective-permute-start(bf16[144,256]{1,0:T(8,128)(2,1)S(1)} %copy-done), channel_id=1, source_target_pairs={{0,4},{4,0},{8,12},{12,8},{1,5},{5,1},{9,13},{13,9},{2,6},{6,2},{1... | collective-permute-start | bytes 221192 | tf_op jit(solution)/shard_map/ppermute | solution.py:444
  15.5 5.3 %collective-permute-start.9 = (bf16[144,256]{1,0:T(8,128)(2,1)S(1)}, bf16[144,256]{1,0:T(8,128)(2,1)S(1)}, u32[]{:S(2)}, u32[]{:S(2)}) collective-permute-start(bf16[144,256]{1,0:T(8,128)(2,1)S(1)} %collective-permute-done.7.refs_0_), channel_id=1, source_target_pairs={{0,8},{4,12},{8,0},{12,4},{1,9},{5,13},{9,1},{13,5},{2,10},{6,14},... | collective-permute-start | bytes 221192 | tf_op jit(solution)/shard_map/ppermute | solution.py:444
  17.0 3.7 %collective-permute-start.6 = (bf16[144,256]{1,0:T(8,128)(2,1)S(1)}, bf16[144,256]{1,0:T(8,128)(2,1)S(1)}, u32[]{:S(2)}, u32[]{:S(2)}) collective-permute-start(bf16[144,256]{1,0:T(8,128)(2,1)S(1)} %collective-permute-done.5.refs_6_), channel_id=1, source_target_pairs={{0,4},{4,0},{8,12},{12,8},{1,5},{5,1},{9,13},{13,9},{2,6},{6,2},{1... | collective-permute-start | bytes 221192 | tf_op jit(solution)/shard_map/ppermute | solution.py:444
  17.8 3.4 %collective-permute-start.1 = (bf16[144,256]{1,0:T(8,128)(2,1)S(1)}, bf16[144,256]{1,0:T(8,128)(2,1)S(1)}, u32[]{:S(2)}, u32[]{:S(2)}) collective-permute-start(bf16[144,256]{1,0:T(8,128)(2,1)S(1)} %after.2.refs_0_), channel_id=1, source_target_pairs={{0,4},{4,0},{8,12},{12,8},{1,5},{5,1},{9,13},{13,9},{2,6},{6,2},{1... | collective-permute-start | bytes 221192 | tf_op jit(solution)/shard_map/ppermute | solution.py:444
  19.9 1.4 %collective-permute-start.3 = (bf16[144,256]{1,0:T(8,128)(2,1)S(1)}, bf16[144,256]{1,0:T(8,128)(2,1)S(1)}, u32[]{:S(2)}, u32[]{:S(2)}) collective-permute-start(bf16[144,256]{1,0:T(8,128)(2,1)S(1)} %collective-permute-done.2.refs_2_), channel_id=1, source_target_pairs={{0,4},{4,0},{8,12},{12,8},{1,5},{5,1},{9,13},{13,9},{2,6},{6,2},{1... | collective-permute-start | bytes 221192 | tf_op jit(solution)/shard_map/ppermute | solution.py:444
  19.9 4.7 %collective-permute-start.13 = (bf16[144,256]{1,0:T(8,128)(2,1)S(1)}, bf16[144,256]{1,0:T(8,128)(2,1)S(1)}, u32[]{:S(2)}, u32[]{:S(2)}) collective-permute-start(bf16[144,256]{1,0:T(8,128)(2,1)S(1)} %collective-permute-done.11.refs_4_), channel_id=1, source_target_pairs={{0,8},{4,12},{8,0},{12,4},{1,9},{5,13},{9,1},{13,5},{2,10},{6,14},... | collective-permute-start | bytes 221192 | tf_op jit(solution)/shard_map/ppermute | solution.py:444
  20.7 3.9 %collective-permute-start.8 = (bf16[144,256]{1,0:T(8,128)(2,1)S(1)}, bf16[144,256]{1,0:T(8,128)(2,1)S(1)}, u32[]{:S(2)}, u32[]{:S(2)}) collective-permute-start(bf16[144,256]{1,0:T(8,128)(2,1)S(1)} %collective-permute-done.7.refs_0_), channel_id=1, source_target_pairs={{0,4},{4,0},{8,12},{12,8},{1,5},{5,1},{9,13},{13,9},{2,6},{6,2},{1... | collective-permute-start | bytes 221192 | tf_op jit(solution)/shard_map/ppermute | solution.py:444
  20.7 3.8 %collective-permute-start.12 = (bf16[144,256]{1,0:T(8,128)(2,1)S(1)}, bf16[144,256]{1,0:T(8,128)(2,1)S(1)}, u32[]{:S(2)}, u32[]{:S(2)}) collective-permute-start(bf16[144,256]{1,0:T(8,128)(2,1)S(1)} %collective-permute-done.11.refs_4_), channel_id=1, source_target_pairs={{0,4},{4,0},{8,12},{12,8},{1,5},{5,1},{9,13},{13,9},{2,6},{6,2},{1... | collective-permute-start | bytes 221192 | tf_op jit(solution)/shard_map/ppermute | solution.py:444
  21.2 3.3 %collective-permute-start.10 = (bf16[144,256]{1,0:T(8,128)(2,1)S(1)}, bf16[144,256]{1,0:T(8,128)(2,1)S(1)}, u32[]{:S(2)}, u32[]{:S(2)}) collective-permute-start(bf16[144,256]{1,0:T(8,128)(2,1)S(1)} %collective-permute-done.9.refs_2_), channel_id=1, source_target_pairs={{0,4},{4,0},{8,12},{12,8},{1,5},{5,1},{9,13},{13,9},{2,6},{6,2},{1... | collective-permute-start | bytes 221192 | tf_op jit(solution)/shard_map/ppermute | solution.py:444
  24.6 1.3 %collective-permute-start.14 = (bf16[144,256]{1,0:T(8,128)(2,1)S(1)}, bf16[144,256]{1,0:T(8,128)(2,1)S(1)}, u32[]{:S(2)}, u32[]{:S(2)}) collective-permute-start(bf16[144,256]{1,0:T(8,128)(2,1)S(1)} %after.3.refs_6_), channel_id=1, source_target_pairs={{0,4},{4,0},{8,12},{12,8},{1,5},{5,1},{9,13},{13,9},{2,6},{6,2},{1... | collective-permute-start | bytes 221192 | tf_op jit(solution)/shard_map/ppermute | solution.py:444

commit v9 on v8

--- a/solution.py
+++ b/solution.py
@@ -404,7 +404,7 @@
         functools.partial(kernel, slots, len(patches[0])),
         in_specs=[vmem] * len(operands),
         compiler_params=pltpu.CompilerParams(vmem_limit_bytes=32 * 2**20),
-        cost_estimate=pl.CostEstimate(flops=flops, bytes_accessed=3 * 2**20, transcendentals=0),
+        cost_estimate=pl.CostEstimate(flops=0, bytes_accessed=0, transcendentals=0),
         **call,
     )(*operands)
 
@@ -466,7 +466,7 @@
     patches = {d: gather_rows(after(arrived[d], row_filters) if d else arrived[d]) for d in near}
     total = summed(row_filters, weights, patches, near)
     for d in far:
-        patches[d] = gather_rows(arrived[d], (total,) if d == far[-1] else ())
+        patches[d] = gather_rows(arrived[d])
     return finished(row_filters, weights, total, patches, far, 1.0 / math.sqrt(tilt_devices))
 
 

time: 27.6 us -> 27.6 us (level)
  starting transfers between devices: 9.95 us -> 10.8 us
  waiting for transfers between devices: 7.43 us -> 6.6 us
    ppermute x15, starting transfers between devices: 9.95 us -> 10.8 us  [exchange(): return lax.ppermute(array, axis, [(i, i ^ distance) for i in range(count)])]
    ppermute x15, waiting for transfers between devices: 7.43 us -> 6.6 us  [exchange(): return lax.ppermute(array, axis, [(i, i ^ distance) for i in range(count)])]
where the time goes in v9:
time: 27.6 us; the launch traced here: 27.5 us
  starting transfers between devices  10.8 us (39%)
  Pallas kernels  9.99 us (36%)
  waiting for transfers between devices  6.6 us (24%)
    ppermute x15, starting transfers between devices, exchange(): return lax.ppermute(array, axis, [(i, i ^ distance) for i in range(count)])  10.8 us
    ppermute x15, waiting for transfers between devices, exchange(): return lax.ppermute(array, axis, [(i, i ^ distance) for i in range(count)])  6.6 us
    pallas_call x1, Pallas kernels, column_filtered(): pl.pallas_call(functools.partial(column_kernel, slots, slices_owned), out...  4.93 us
    pallas_call x2, Pallas kernels, interpolation(): pl.pallas_call(functools.partial(kernel, slots, len(patches[0])), in_spec...  2.54 us
    pallas_call x1, Pallas kernels, prepared(): pl.pallas_call(functools.partial(prepare_kernel, slots, slices_owned), ou...  2.52 us
  transfers between devices with their start and end apart: 15, of which 6 were waited for; matrix products, arithmetic and copies ran while one was open for 0% of the time, Pallas kernels for 12%

profile of v9, /device:TPU:0, one launch (start us, length us, event | category | flops | bytes accessed | tf_op | source)
XLA Modules:
  0.0 27.5 jit_solution(7477978970433425395)
XLA Ops:
  0.0 4.9 %column_filter.1 = (bf16[144,256]{1,0:T(8,128)(2,1)}, bf16[144,256]{1,0:T(8,128)(2,1)}, bf16[144,256]{1,0:T(8,128)(2,1)}, bf16[144,256]{1,0:T(8,128)(2,1)}) custom-call(bf16[64,2048]{1,0:T(8,128)(2,1)} %bitcast.1, bf16[5,256,512]{2,1,0:T(8,128)(2,1)} %constant.4.clone.matrix_ref, f32[4]{0:T(128)} %angle_ref.1, s32[4,4]{1,0:T(4,128)} %defocus_ref.1, ...), custom_call_target="tpu_custom_call" | custom-call | flops 822083584 | bytes 3145728 | tf_op jit(solution)/shard_map/column_filter/pallas_call | solution.py:230
  4.9 3.0 %collective-permute-start.5 = (bf16[144,256]{1,0:T(8,128)(2,1)}, bf16[144,256]{1,0:T(8,128)(2,1)S(1)}, u32[]{:S(2)}, u32[]{:S(2)}) collective-permute-start(bf16[144,256]{1,0:T(8,128)(2,1)} %get-tuple-element.14.refs_4_), channel_id=1, source_target_pairs={{0,8},{4,12},{8,0},{12,4},{1,9},{5,13},{9,1},{13,5},{2,10},{6,14},... | collective-permute-start | bytes 221192 | tf_op jit(solution)/shard_map/ppermute | solution.py:444
  8.0 0.0 collective-permute-start.4
  8.0 1.6 %collective-permute-start = (bf16[144,256]{1,0:T(8,128)(2,1)}, bf16[144,256]{1,0:T(8,128)(2,1)S(1)}, u32[]{:S(2)}, u32[]{:S(2)}) collective-permute-start(bf16[144,256]{1,0:T(8,128)(2,1)} %get-tuple-element.13), channel_id=1, source_target_pairs={{0,1},{1,0},{2,3},{3,2},{4,5},{5,4},{6,7},{7,6},{8,9},{9,8},{10,11... | collective-permute-start | bytes 221192 | tf_op jit(solution)/shard_map/ppermute | solution.py:444
  9.6 2.5 %collective-permute-start.7 = (bf16[144,256]{1,0:T(8,128)(2,1)}, bf16[144,256]{1,0:T(8,128)(2,1)S(1)}, u32[]{:S(2)}, u32[]{:S(2)}) collective-permute-start(bf16[144,256]{1,0:T(8,128)(2,1)} %get-tuple-element.15), channel_id=1, source_target_pairs={{0,3},{1,2},{2,1},{3,0},{4,7},{5,6},{6,5},{7,4},{8,11},{9,10},{10,... | collective-permute-start | bytes 221192 | tf_op jit(solution)/shard_map/ppermute | solution.py:444
  12.0 0.1 collective-permute-start.11
  12.2 2.5 %prepare.1 = (bf16[256,256]{1,0:T(8,128)(2,1)S(1)}, bf16[4,192,2048]{2,1,0:T(8,128)(2,1)S(1)}) custom-call(f32[4]{0:T(128)S(1)} %copy-done.2, s32[4,4]{1,0:T(4,128)S(1)} %copy-done.1, bf16[2,256,256]{2,1,0:T(8,128)(2,1)S(1)} %copy-done.3), custom_call_target="tpu_custom_call" | custom-call | flops 2147483648 | bytes 6291456 | tf_op jit(solution)/shard_map/prepare/pallas_call | solution.py:316
  14.7 2.3 %collective-permute-done.7.refs_0_ = bf16[144,256]{1,0:T(8,128)(2,1)S(1)} collective-permute-done((bf16[144,256]{1,0:T(8,128)(2,1)}, bf16[144,256]{1,0:T(8,128)(2,1)S(1)}, u32[]{:S(2)}, u32[]{:S(2)}) %collective-permute-start.7) | collective-permute-done | bytes 73760 | tf_op jit(solution)/shard_map/ppermute | solution.py:444
  17.0 0.5 %collective-permute-start.9 = (bf16[144,256]{1,0:T(8,128)(2,1)S(1)}, bf16[144,256]{1,0:T(8,128)(2,1)S(1)}, u32[]{:S(2)}, u32[]{:S(2)}) collective-permute-start(bf16[144,256]{1,0:T(8,128)(2,1)S(1)} %collective-permute-done.7.refs_0_), channel_id=1, source_target_pairs={{0,8},{4,12},{8,0},{12,4},{1,9},{5,13},{9,1},{13,5},{2,10},{6,14},... | collective-permute-start | bytes 221192 | tf_op jit(solution)/shard_map/ppermute | solution.py:444
  17.5 1.5 %collective-permute-start.2 = (bf16[144,256]{1,0:T(8,128)(2,1)S(1)}, bf16[144,256]{1,0:T(8,128)(2,1)S(1)}, u32[]{:S(2)}, u32[]{:S(2)}) collective-permute-start(bf16[144,256]{1,0:T(8,128)(2,1)S(1)} %after.1.refs_0_), channel_id=1, source_target_pairs={{0,8},{4,12},{8,0},{12,4},{1,9},{5,13},{9,1},{13,5},{2,10},{6,14},... | collective-permute-start | bytes 221192 | tf_op jit(solution)/shard_map/ppermute | solution.py:444
  19.0 0.7 %collective-permute-done.11.refs_4_ = bf16[144,256]{1,0:T(8,128)(2,1)S(1)} collective-permute-done((bf16[144,256]{1,0:T(8,128)(2,1)}, bf16[144,256]{1,0:T(8,128)(2,1)S(1)}, u32[]{:S(2)}, u32[]{:S(2)}) %collective-permute-start.11) | collective-permute-done | bytes 73760 | tf_op jit(solution)/shard_map/ppermute | solution.py:444
  19.7 0.5 %collective-permute-start.13 = (bf16[144,256]{1,0:T(8,128)(2,1)S(1)}, bf16[144,256]{1,0:T(8,128)(2,1)S(1)}, u32[]{:S(2)}, u32[]{:S(2)}) collective-permute-start(bf16[144,256]{1,0:T(8,128)(2,1)S(1)} %collective-permute-done.11.refs_4_), channel_id=1, source_target_pairs={{0,8},{4,12},{8,0},{12,4},{1,9},{5,13},{9,1},{13,5},{2,10},{6,14},... | collective-permute-start | bytes 221192 | tf_op jit(solution)/shard_map/ppermute | solution.py:444
  20.2 0.5 %collective-permute-start.1 = (bf16[144,256]{1,0:T(8,128)(2,1)S(1)}, bf16[144,256]{1,0:T(8,128)(2,1)S(1)}, u32[]{:S(2)}, u32[]{:S(2)}) collective-permute-start(bf16[144,256]{1,0:T(8,128)(2,1)S(1)} %after.1.refs_0_), channel_id=1, source_target_pairs={{0,4},{4,0},{8,12},{12,8},{1,5},{5,1},{9,13},{13,9},{2,6},{6,2},{1... | collective-permute-start | bytes 221192 | tf_op jit(solution)/shard_map/ppermute | solution.py:444
  20.7 0.6 %collective-permute-done.9.refs_2_ = bf16[144,256]{1,0:T(8,128)(2,1)S(1)} collective-permute-done((bf16[144,256]{1,0:T(8,128)(2,1)S(1)}, bf16[144,256]{1,0:T(8,128)(2,1)S(1)}, u32[]{:S(2)}, u32[]{:S(2)}) %collective-permute-start.9) | collective-permute-done | bytes 73760 | tf_op jit(solution)/shard_map/ppermute | solution.py:444
  21.3 0.0 collective-permute-start.8
  21.3 0.8 %collective-permute-done.2.refs_2_ = bf16[144,256]{1,0:T(8,128)(2,1)S(1)} collective-permute-done((bf16[144,256]{1,0:T(8,128)(2,1)S(1)}, bf16[144,256]{1,0:T(8,128)(2,1)S(1)}, u32[]{:S(2)}, u32[]{:S(2)}) %collective-permute-start.2) | collective-permute-done | bytes 73760 | tf_op jit(solution)/shard_map/ppermute | solution.py:444
  22.1 0.0 collective-permute-start.3
  22.1 2.0 %collective-permute-done.13.refs_6_ = bf16[144,256]{1,0:T(8,128)(2,1)S(1)} collective-permute-done((bf16[144,256]{1,0:T(8,128)(2,1)S(1)}, bf16[144,256]{1,0:T(8,128)(2,1)S(1)}, u32[]{:S(2)}, u32[]{:S(2)}) %collective-permute-start.13) | collective-permute-done | bytes 73760 | tf_op jit(solution)/shard_map/ppermute | solution.py:444
  24.1 0.0 collective-permute-start.12
  24.1 0.5 %collective-permute-start.10 = (bf16[144,256]{1,0:T(8,128)(2,1)S(1)}, bf16[144,256]{1,0:T(8,128)(2,1)S(1)}, u32[]{:S(2)}, u32[]{:S(2)}) collective-permute-start(bf16[144,256]{1,0:T(8,128)(2,1)S(1)} %collective-permute-done.9.refs_2_), channel_id=1, source_target_pairs={{0,4},{4,0},{8,12},{12,8},{1,5},{5,1},{9,13},{13,9},{2,6},{6,2},{1... | collective-permute-start | bytes 221192 | tf_op jit(solution)/shard_map/ppermute | solution.py:444
  24.6 0.1 collective-permute-start.14
  24.7 0.9 %sum_early_tilts.1.total_ref = f32[256,2048]{1,0:T(8,128)S(1)} custom-call(bf16[256,256]{1,0:T(8,128)(2,1)S(1)} %get-tuple-element.11.refs_1_.rows_ref, bf16[4,192,2048]{2,1,0:T(8,128)(2,1)S(1)} %get-tuple-element.12.weights_ref, bf16[144,256]{1,0:T(8,128)(2,1)S(1)} %after.1.refs_0_, bf16[144,256]{1,0:T(8,128)(2,1)S(1)} %collective-permute-done.1.refs_1_, ...), custom_call_target="tpu_custom_call" | custom-call | tf_op jit(solution)/shard_map/sum_early_tilts/pallas_call | solution.py:403
  25.6 0.3 collective-permute-done.14.refs_7_
  25.9 1.6 %finish_volume.1 = bf16[16,64,512]{2,1,0:T(8,128)(2,1)} custom-call(bf16[256,256]{1,0:T(8,128)(2,1)S(1)} %get-tuple-element.11.refs_1_.rows_ref, bf16[4,192,2048]{2,1,0:T(8,128)(2,1)S(1)} %get-tuple-element.12.weights_ref, f32[256,2048]{1,0:T(8,128)S(1)} %sum_early_tilts.1.total_ref, bf16[144,256]{1,0:T(8,128)(2,1)S(1)} %collective-permute-done.7.refs_0_, ...), custom_call_target="tpu_custom_call" | custom-call | tf_op jit(solution)/shard_map/finish_volume/pallas_call | solution.py:403
  (19 shorter events, 0.0 us)
Async XLA Ops:
  0.0 12.2 %copy-start.3 = (bf16[2,256,256]{2,1,0:T(8,128)(2,1)S(1)}, bf16[2,256,256]{2,1,0:T(8,128)(2,1)}, u32[]{:S(2)}) copy-start(bf16[2,256,256]{2,1,0:T(8,128)(2,1)} %constant.5.clone.waves) | copy-start | bytes 786436
  0.0 12.2 %copy-start.1 = (s32[4,4]{1,0:T(4,128)S(1)}, s32[4,4]{1,0:T(4,128)}, u32[]{:S(2)}) copy-start(s32[4,4]{1,0:T(4,128)} %defocus_ref.1) | copy-start | bytes 196
  0.0 12.2 %copy-start.2 = (f32[4]{0:T(128)S(1)}, f32[4]{0:T(128)}, u32[]{:S(2)}) copy-start(f32[4]{0:T(128)} %angle_ref.1) | copy-start | bytes 52
  4.9 15.3 %collective-permute-start.5 = (bf16[144,256]{1,0:T(8,128)(2,1)}, bf16[144,256]{1,0:T(8,128)(2,1)S(1)}, u32[]{:S(2)}, u32[]{:S(2)}) collective-permute-start(bf16[144,256]{1,0:T(8,128)(2,1)} %get-tuple-element.14.refs_4_), channel_id=1, source_target_pairs={{0,8},{4,12},{8,0},{12,4},{1,9},{5,13},{9,1},{13,5},{2,10},{6,14},... | collective-permute-start | bytes 221192 | tf_op jit(solution)/shard_map/ppermute | solution.py:444
  8.0 12.2 %collective-permute-start.4 = (bf16[144,256]{1,0:T(8,128)(2,1)}, bf16[144,256]{1,0:T(8,128)(2,1)S(1)}, u32[]{:S(2)}, u32[]{:S(2)}) collective-permute-start(bf16[144,256]{1,0:T(8,128)(2,1)} %get-tuple-element.14.refs_4_), channel_id=1, source_target_pairs={{0,4},{4,0},{8,12},{12,8},{1,5},{5,1},{9,13},{13,9},{2,6},{6,2},{1... | collective-permute-start | bytes 221192 | tf_op jit(solution)/shard_map/ppermute | solution.py:444
  8.0 9.5 %collective-permute-start = (bf16[144,256]{1,0:T(8,128)(2,1)}, bf16[144,256]{1,0:T(8,128)(2,1)S(1)}, u32[]{:S(2)}, u32[]{:S(2)}) collective-permute-start(bf16[144,256]{1,0:T(8,128)(2,1)} %get-tuple-element.13), channel_id=1, source_target_pairs={{0,1},{1,0},{2,3},{3,2},{4,5},{5,4},{6,7},{7,6},{8,9},{9,8},{10,11... | collective-permute-start | bytes 221192 | tf_op jit(solution)/shard_map/ppermute | solution.py:444
  9.6 7.4 %collective-permute-start.7 = (bf16[144,256]{1,0:T(8,128)(2,1)}, bf16[144,256]{1,0:T(8,128)(2,1)S(1)}, u32[]{:S(2)}, u32[]{:S(2)}) collective-permute-start(bf16[144,256]{1,0:T(8,128)(2,1)} %get-tuple-element.15), channel_id=1, source_target_pairs={{0,3},{1,2},{2,1},{3,0},{4,7},{5,6},{6,5},{7,4},{8,11},{9,10},{10,... | collective-permute-start | bytes 221192 | tf_op jit(solution)/shard_map/ppermute | solution.py:444
  12.0 12.6 %copy-start = (bf16[144,256]{1,0:T(8,128)(2,1)S(1)}, bf16[144,256]{1,0:T(8,128)(2,1)}, u32[]{:S(2)}) copy-start(bf16[144,256]{1,0:T(8,128)(2,1)} %get-tuple-element.14.refs_4_) | copy-start | bytes 221188
  12.0 7.7 %collective-permute-start.11 = (bf16[144,256]{1,0:T(8,128)(2,1)}, bf16[144,256]{1,0:T(8,128)(2,1)S(1)}, u32[]{:S(2)}, u32[]{:S(2)}) collective-permute-start(bf16[144,256]{1,0:T(8,128)(2,1)} %get-tuple-element.16), channel_id=1, source_target_pairs={{0,2},{1,3},{2,0},{3,1},{4,6},{5,7},{6,4},{7,5},{8,10},{9,11},{10,... | collective-permute-start | bytes 221192 | tf_op jit(solution)/shard_map/ppermute | solution.py:444
  17.0 4.4 %collective-permute-start.9 = (bf16[144,256]{1,0:T(8,128)(2,1)S(1)}, bf16[144,256]{1,0:T(8,128)(2,1)S(1)}, u32[]{:S(2)}, u32[]{:S(2)}) collective-permute-start(bf16[144,256]{1,0:T(8,128)(2,1)S(1)} %collective-permute-done.7.refs_0_), channel_id=1, source_target_pairs={{0,8},{4,12},{8,0},{12,4},{1,9},{5,13},{9,1},{13,5},{2,10},{6,14},... | collective-permute-start | bytes 221192 | tf_op jit(solution)/shard_map/ppermute | solution.py:444
  17.5 4.6 %collective-permute-start.2 = (bf16[144,256]{1,0:T(8,128)(2,1)S(1)}, bf16[144,256]{1,0:T(8,128)(2,1)S(1)}, u32[]{:S(2)}, u32[]{:S(2)}) collective-permute-start(bf16[144,256]{1,0:T(8,128)(2,1)S(1)} %after.1.refs_0_), channel_id=1, source_target_pairs={{0,8},{4,12},{8,0},{12,4},{1,9},{5,13},{9,1},{13,5},{2,10},{6,14},... | collective-permute-start | bytes 221192 | tf_op jit(solution)/shard_map/ppermute | solution.py:444
  19.7 4.4 %collective-permute-start.13 = (bf16[144,256]{1,0:T(8,128)(2,1)S(1)}, bf16[144,256]{1,0:T(8,128)(2,1)S(1)}, u32[]{:S(2)}, u32[]{:S(2)}) collective-permute-start(bf16[144,256]{1,0:T(8,128)(2,1)S(1)} %collective-permute-done.11.refs_4_), channel_id=1, source_target_pairs={{0,8},{4,12},{8,0},{12,4},{1,9},{5,13},{9,1},{13,5},{2,10},{6,14},... | collective-permute-start | bytes 221192 | tf_op jit(solution)/shard_map/ppermute | solution.py:444
  20.2 3.9 %collective-permute-start.6 = (bf16[144,256]{1,0:T(8,128)(2,1)S(1)}, bf16[144,256]{1,0:T(8,128)(2,1)S(1)}, u32[]{:S(2)}, u32[]{:S(2)}) collective-permute-start(bf16[144,256]{1,0:T(8,128)(2,1)S(1)} %collective-permute-done.5.refs_6_), channel_id=1, source_target_pairs={{0,4},{4,0},{8,12},{12,8},{1,5},{5,1},{9,13},{13,9},{2,6},{6,2},{1... | collective-permute-start | bytes 221192 | tf_op jit(solution)/shard_map/ppermute | solution.py:444
  20.2 4.4 %collective-permute-start.1 = (bf16[144,256]{1,0:T(8,128)(2,1)S(1)}, bf16[144,256]{1,0:T(8,128)(2,1)S(1)}, u32[]{:S(2)}, u32[]{:S(2)}) collective-permute-start(bf16[144,256]{1,0:T(8,128)(2,1)S(1)} %after.1.refs_0_), channel_id=1, source_target_pairs={{0,4},{4,0},{8,12},{12,8},{1,5},{5,1},{9,13},{13,9},{2,6},{6,2},{1... | collective-permute-start | bytes 221192 | tf_op jit(solution)/shard_map/ppermute | solution.py:444
  21.3 4.3 %collective-permute-start.8 = (bf16[144,256]{1,0:T(8,128)(2,1)S(1)}, bf16[144,256]{1,0:T(8,128)(2,1)S(1)}, u32[]{:S(2)}, u32[]{:S(2)}) collective-permute-start(bf16[144,256]{1,0:T(8,128)(2,1)S(1)} %collective-permute-done.7.refs_0_), channel_id=1, source_target_pairs={{0,4},{4,0},{8,12},{12,8},{1,5},{5,1},{9,13},{13,9},{2,6},{6,2},{1... | collective-permute-start | bytes 221192 | tf_op jit(solution)/shard_map/ppermute | solution.py:444
  22.1 2.6 %collective-permute-start.3 = (bf16[144,256]{1,0:T(8,128)(2,1)S(1)}, bf16[144,256]{1,0:T(8,128)(2,1)S(1)}, u32[]{:S(2)}, u32[]{:S(2)}) collective-permute-start(bf16[144,256]{1,0:T(8,128)(2,1)S(1)} %collective-permute-done.2.refs_2_), channel_id=1, source_target_pairs={{0,4},{4,0},{8,12},{12,8},{1,5},{5,1},{9,13},{13,9},{2,6},{6,2},{1... | collective-permute-start | bytes 221192 | tf_op jit(solution)/shard_map/ppermute | solution.py:444
  24.1 1.5 %collective-permute-start.12 = (bf16[144,256]{1,0:T(8,128)(2,1)S(1)}, bf16[144,256]{1,0:T(8,128)(2,1)S(1)}, u32[]{:S(2)}, u32[]{:S(2)}) collective-permute-start(bf16[144,256]{1,0:T(8,128)(2,1)S(1)} %collective-permute-done.11.refs_4_), channel_id=1, source_target_pairs={{0,4},{4,0},{8,12},{12,8},{1,5},{5,1},{9,13},{13,9},{2,6},{6,2},{1... | collective-permute-start | bytes 221192 | tf_op jit(solution)/shard_map/ppermute | solution.py:444
  24.1 1.5 %collective-permute-start.10 = (bf16[144,256]{1,0:T(8,128)(2,1)S(1)}, bf16[144,256]{1,0:T(8,128)(2,1)S(1)}, u32[]{:S(2)}, u32[]{:S(2)}) collective-permute-start(bf16[144,256]{1,0:T(8,128)(2,1)S(1)} %collective-permute-done.9.refs_2_), channel_id=1, source_target_pairs={{0,4},{4,0},{8,12},{12,8},{1,5},{5,1},{9,13},{13,9},{2,6},{6,2},{1... | collective-permute-start | bytes 221192 | tf_op jit(solution)/shard_map/ppermute | solution.py:444
  24.6 1.3 %collective-permute-start.14 = (bf16[144,256]{1,0:T(8,128)(2,1)S(1)}, bf16[144,256]{1,0:T(8,128)(2,1)S(1)}, u32[]{:S(2)}, u32[]{:S(2)}) collective-permute-start(bf16[144,256]{1,0:T(8,128)(2,1)S(1)} %collective-permute-done.13.refs_6_), channel_id=1, source_target_pairs={{0,4},{4,0},{8,12},{12,8},{1,5},{5,1},{9,13},{13,9},{2,6},{6,2},{1... | collective-permute-start | bytes 221192 | tf_op jit(solution)/shard_map/ppermute | solution.py:444

commit v10 on v9

--- a/solution.py
+++ b/solution.py
@@ -342,28 +342,32 @@
     return jnp.concatenate([packed[:rows], packed[rows : 2 * rows], rest], 1)
 
 
-def corrected_patches(slot, rows_ref, patch_refs):
-    patches = jnp.concatenate([unpacked(ref[...]) for ref in patch_refs], 0)
-    rows = patches.shape[0] // len(patch_refs)
-    image = jnp.dot(rows_ref[slot * rows : (slot + 1) * rows, :], patches, preferred_element_type=jnp.float32)
-    lane = lax.broadcasted_iota(jnp.int32, (rows, MAIN), 1) // REST
-    main = jnp.concatenate([image[:, block * MAIN : (block + 1) * MAIN] for block in range(XBLK)], 0)
-    rest = jnp.concatenate([jnp.where(lane == block, image[:, XBLK * MAIN :], 0.0) for block in range(XBLK)], 0)
-    return jnp.concatenate([main, rest[:, : XBLK * REST]], 1).astype(jnp.bfloat16)
+def corrected_patches(slots, row_devices, rows_ref, patch_refs):
+    parts = []
+    for group in slots:
+        refs, patch_refs = patch_refs[:row_devices], patch_refs[row_devices:]
+        height = refs[0].shape[0] // len(group)
+        for i, slot in enumerate(group):
+            patches = jnp.concatenate([unpacked(ref[i * height : (i + 1) * height]) for ref in refs], 0)
+            rows = patches.shape[0] // row_devices
+            image = jnp.dot(rows_ref[slot * rows : (slot + 1) * rows, :], patches, preferred_element_type=jnp.float32)
+            lane = lax.broadcasted_iota(jnp.int32, (rows, MAIN), 1) // REST
+            main = jnp.concatenate([image[:, block * MAIN : (block + 1) * MAIN] for block in range(XBLK)], 0)
+            rest = [jnp.where(lane == block, image[:, XBLK * MAIN :], 0.0) for block in range(XBLK)]
+            rest = jnp.concatenate(rest, 0)[:, : XBLK * REST]
+            parts.append((slot, jnp.concatenate([main, rest], 1).astype(jnp.bfloat16)))
+    return parts
 
 
 def sum_kernel(slots, row_devices, rows_ref, weights_ref, *refs):
-    patch_refs, total_ref = refs[:-1], refs[-1]
-    parts = [
-        corrected_patches(slot, rows_ref, patch_refs[i * row_devices : (i + 1) * row_devices])
-        for i, slot in enumerate(slots)
-    ]
+    total_ref = refs[-1]
+    (slot, part), *others = corrected_patches(slots, row_devices, rows_ref, refs[:-1])
     step = 4 * XBW
     for first in range(0, total_ref.shape[1], step):
         here = slice(first, first + step)
-        total = jnp.dot(parts[0], weights_ref[slots[0], :, here], preferred_element_type=jnp.float32)
-        for part, slot in zip(parts[1:], slots[1:]):
-            total += jnp.dot(part, weights_ref[slot, :, here], preferred_element_type=jnp.float32)
+        total = jnp.dot(part, weights_ref[slot, :, here], preferred_element_type=jnp.float32)
+        for other, more in others:
+            total += jnp.dot(more, weights_ref[other, :, here], preferred_element_type=jnp.float32)
         total_ref[:, here] = total
 
 
@@ -371,16 +375,13 @@
     patch_refs = refs[: len(slots) * row_devices]
     out_ref, out, sems = refs[len(slots) * row_devices :]
     rows = total_ref.shape[0] // XBLK
-    parts = [
-        corrected_patches(slot, rows_ref, patch_refs[i * row_devices : (i + 1) * row_devices])
-        for i, slot in enumerate(slots)
-    ]
+    parts = corrected_patches(slots, row_devices, rows_ref, patch_refs)
     step = 4
     copies = []
     for group in range(out.shape[0] // step):
         here = slice(group * step * XBW, (group + 1) * step * XBW)
         total = total_ref[:, here]
-        for part, slot in zip(parts, slots):
+        for slot, part in parts:
             total += jnp.dot(part, weights_ref[slot, :, here], preferred_element_type=jnp.float32)
         for c in range(step):
             for block in range(XBLK):
@@ -395,11 +396,8 @@
 
 
 def interpolation(kernel, slots, weights, row_filters, patches, totals, **call):
-    _, taps, width = weights.shape
-    rows = row_filters.shape[0] // weights.shape[0]
     vmem = pl.BlockSpec(memory_space=pltpu.VMEM)
-    operands = [row_filters, weights, *totals, *(block for slot in slots for block in patches[slot])]
-    flops = 2 * len(slots) * taps * width * XBLK * rows
+    operands = [row_filters, weights, *totals, *(block for group in patches for block in group)]
     return pl.pallas_call(
         functools.partial(kernel, slots, len(patches[0])),
         in_specs=[vmem] * len(operands),
@@ -459,15 +457,14 @@
     _, rows, _ = projections.shape
     row_devices, tilt_devices = lax.axis_size("row"), lax.axis_size("tilt")
     slices_owned = SLICES // tilt_devices
-    far, near = list(range(tilt_devices - 1, 1, -1)), list(range(min(2, tilt_devices) - 1, -1, -1))
+    far, near = list(range(tilt_devices - 1, 1, -1)), list(range(min(2, tilt_devices)))
     sent = column_filtered(far + near, slices_owned, projections[0], tilt_angle, defocus, band_start)
     arrived = {d: exchange(sent[d], "tilt", d) if d else sent[d] for d in far + near}
     row_filters, weights = prepared(tilt_devices, slices_owned, rows, rows * row_devices, tilt_angle, defocus)
-    patches = {d: gather_rows(after(arrived[d], row_filters) if d else arrived[d]) for d in near}
-    total = summed(row_filters, weights, patches, near)
-    for d in far:
-        patches[d] = gather_rows(arrived[d])
-    return finished(row_filters, weights, total, patches, far, 1.0 / math.sqrt(tilt_devices))
+    early = [gather_rows(jnp.concatenate([arrived[d] for d in near]))]
+    total = summed(row_filters, weights, early, [near])
+    late = [gather_rows(after(arrived[d], row_filters) if d == far[-1] else arrived[d]) for d in far]
+    return finished(row_filters, weights, total, late, [[d] for d in far], 1.0 / math.sqrt(tilt_devices))
 
 
 def solution(mesh):

time: 27.6 us -> 25.4 us (0.920)
  waiting for transfers between devices: 6.6 us -> 3.65 us
  local copies, waits for them, and re-layouts: 0.01 us -> 0.91 us
    ppermute x15 -> x12, waiting for transfers between devices: 6.6 us -> 3.65 us  [exchange(): return lax.ppermute(array, axis, [(i, i ^ distance) for i in range(count)])]
    unnamed x8 -> x7, local copies, waits for them, and re-layouts: 0.01 us -> 0.9 us
    ppermute x15 -> x12, starting transfers between devices: 10.8 us -> 10.6 us  [exchange(): return lax.ppermute(array, axis, [(i, i ^ distance) for i in range(count)])]
  transfers between devices with their start and end apart: 15 -> 12, of which waited for: 6 -> 3; matrix products, arithmetic and copies ran while one was open for 0% -> 4% of each run, Pallas kernels for 12% -> 14%
where the time goes in v10:
time: 25.4 us; the launch traced here: 25.2 us
  starting transfers between devices  10.6 us (42%)
  Pallas kernels  10 us (39%)
  waiting for transfers between devices  3.65 us (14%)
  local copies, waits for them, and re-layouts  0.91 us (4%)
    ppermute x12, starting transfers between devices, exchange(): return lax.ppermute(array, axis, [(i, i ^ distance) for i in range(count)])  10.6 us
    pallas_call x1, Pallas kernels, column_filtered(): pl.pallas_call(functools.partial(column_kernel, slots, slices_owned), out...  4.93 us
    ppermute x12, waiting for transfers between devices, exchange(): return lax.ppermute(array, axis, [(i, i ^ distance) for i in range(count)])  3.65 us
    pallas_call x2, Pallas kernels, interpolation(): pl.pallas_call(functools.partial(kernel, slots, len(patches[0])), in_spec...  2.54 us
    pallas_call x1, Pallas kernels, prepared(): pl.pallas_call(functools.partial(prepare_kernel, slots, slices_owned), ou...  2.53 us
    unnamed x7, local copies, waits for them, and re-layouts  0.9 us
  transfers between devices with their start and end apart: 12, of which 3 were waited for; matrix products, arithmetic and copies ran while one was open for 4% of the time, Pallas kernels for 14%

profile of v10, /device:TPU:0, one launch (start us, length us, event | category | flops | bytes accessed | tf_op | source)
XLA Modules:
  0.0 25.2 jit_solution(3851368070334021900)
XLA Ops:
  0.0 4.9 %column_filter.1 = (bf16[144,256]{1,0:T(8,128)(2,1)}, bf16[144,256]{1,0:T(8,128)(2,1)}, bf16[144,256]{1,0:T(8,128)(2,1)}, bf16[144,256]{1,0:T(8,128)(2,1)}) custom-call(bf16[64,2048]{1,0:T(8,128)(2,1)} %bitcast.1, bf16[5,256,512]{2,1,0:T(8,128)(2,1)} %constant.4.clone.matrix_ref, f32[4]{0:T(128)} %angle_ref.1, s32[4,4]{1,0:T(4,128)} %defocus_ref.1, ...), custom_call_target="tpu_custom_call" | custom-call | flops 822083584 | bytes 3145728 | tf_op jit(solution)/shard_map/column_filter/pallas_call | solution.py:230
  4.9 3.1 %collective-permute-start = (bf16[144,256]{1,0:T(8,128)(2,1)}, bf16[144,256]{1,0:T(8,128)(2,1)S(1)}, u32[]{:S(2)}, u32[]{:S(2)}) collective-permute-start(bf16[144,256]{1,0:T(8,128)(2,1)} %get-tuple-element.14), channel_id=1, source_target_pairs={{0,1},{1,0},{2,3},{3,2},{4,5},{5,4},{6,7},{7,6},{8,9},{9,8},{10,11... | collective-permute-start | bytes 221192 | tf_op jit(solution)/shard_map/ppermute | solution.py:442
  8.0 2.5 %collective-permute-start.4 = (bf16[144,256]{1,0:T(8,128)(2,1)}, bf16[144,256]{1,0:T(8,128)(2,1)S(1)}, u32[]{:S(2)}, u32[]{:S(2)}) collective-permute-start(bf16[144,256]{1,0:T(8,128)(2,1)} %get-tuple-element.15), channel_id=1, source_target_pairs={{0,3},{1,2},{2,1},{3,0},{4,7},{5,6},{6,5},{7,4},{8,11},{9,10},{10,... | collective-permute-start | bytes 221192 | tf_op jit(solution)/shard_map/ppermute | solution.py:442
  10.5 0.1 collective-permute-start.8
  10.6 0.9 %constant_dynamic-update-slice_fusion.1 = bf16[288,256]{1,0:T(8,128)(2,1)S(1)} fusion(bf16[144,256]{1,0:T(8,128)(2,1)} %get-tuple-element.13), kind=kLoop, calls=%fused_computation.1 | loop fusion | bytes 147456
  11.5 0.0 collective-permute-done
  11.5 1.6 %collective-permute-start.2 = (bf16[288,256]{1,0:T(8,128)(2,1)S(1)}, bf16[288,256]{1,0:T(8,128)(2,1)S(1)}, u32[]{:S(2)}, u32[]{:S(2)}) collective-permute-start(bf16[288,256]{1,0:T(8,128)(2,1)S(1)} %constant_dynamic-update-slice_fusion.refs_0_), channel_id=1, source_target_pairs={{0,8},{4,12},{8,0},{12,4},{1,9},{5,13},{9,1},{13,5},{2,10},{6,14},... | collective-permute-start | bytes 442376 | tf_op jit(solution)/shard_map/ppermute | solution.py:442
  13.1 0.0 collective-permute-start.1
  13.1 2.5 %prepare.1 = (bf16[256,256]{1,0:T(8,128)(2,1)S(1)}, bf16[4,192,2048]{2,1,0:T(8,128)(2,1)S(1)}) custom-call(f32[4]{0:T(128)S(1)} %copy-done.1, s32[4,4]{1,0:T(4,128)S(1)} %copy-done, bf16[2,256,256]{2,1,0:T(8,128)(2,1)S(1)} %copy-done.2), custom_call_target="tpu_custom_call" | custom-call | flops 2147483648 | bytes 6291456 | tf_op jit(solution)/shard_map/prepare/pallas_call | solution.py:316
  15.7 0.0 collective-permute-done.4.refs_0_
  15.7 1.3 %collective-permute-start.6 = (bf16[144,256]{1,0:T(8,128)(2,1)S(1)}, bf16[144,256]{1,0:T(8,128)(2,1)S(1)}, u32[]{:S(2)}, u32[]{:S(2)}) collective-permute-start(bf16[144,256]{1,0:T(8,128)(2,1)S(1)} %collective-permute-done.4.refs_0_), channel_id=1, source_target_pairs={{0,8},{4,12},{8,0},{12,4},{1,9},{5,13},{9,1},{13,5},{2,10},{6,14},... | collective-permute-start | bytes 221192 | tf_op jit(solution)/shard_map/ppermute | solution.py:442
  17.0 0.0 collective-permute-start.3
  17.0 0.8 %collective-permute-done.8.refs_0_ = bf16[144,256]{1,0:T(8,128)(2,1)S(1)} collective-permute-done((bf16[144,256]{1,0:T(8,128)(2,1)}, bf16[144,256]{1,0:T(8,128)(2,1)S(1)}, u32[]{:S(2)}, u32[]{:S(2)}) %collective-permute-start.8) | collective-permute-done | bytes 73760 | tf_op jit(solution)/shard_map/ppermute | solution.py:442
  17.8 1.5 %collective-permute-start.10 = (bf16[144,256]{1,0:T(8,128)(2,1)S(1)}, bf16[144,256]{1,0:T(8,128)(2,1)S(1)}, u32[]{:S(2)}, u32[]{:S(2)}) collective-permute-start(bf16[144,256]{1,0:T(8,128)(2,1)S(1)} %after.1.refs_4_), channel_id=1, source_target_pairs={{0,8},{4,12},{8,0},{12,4},{1,9},{5,13},{9,1},{13,5},{2,10},{6,14},... | collective-permute-start | bytes 221192 | tf_op jit(solution)/shard_map/ppermute | solution.py:442
  19.3 0.0 collective-permute-start.9
  19.3 1.3 %collective-permute-done.6.refs_2_ = bf16[144,256]{1,0:T(8,128)(2,1)S(1)} collective-permute-done((bf16[144,256]{1,0:T(8,128)(2,1)S(1)}, bf16[144,256]{1,0:T(8,128)(2,1)S(1)}, u32[]{:S(2)}, u32[]{:S(2)}) %collective-permute-start.6) | collective-permute-done | bytes 73760 | tf_op jit(solution)/shard_map/ppermute | solution.py:442
  20.6 1.5 %collective-permute-done.10.refs_6_ = bf16[144,256]{1,0:T(8,128)(2,1)S(1)} collective-permute-done((bf16[144,256]{1,0:T(8,128)(2,1)S(1)}, bf16[144,256]{1,0:T(8,128)(2,1)S(1)}, u32[]{:S(2)}, u32[]{:S(2)}) %collective-permute-start.10) | collective-permute-done | bytes 73760 | tf_op jit(solution)/shard_map/ppermute | solution.py:442
  22.1 0.0 collective-permute-start.7
  22.1 0.0 collective-permute-done.1.refs_1_
  22.1 0.5 %collective-permute-start.11 = (bf16[144,256]{1,0:T(8,128)(2,1)S(1)}, bf16[144,256]{1,0:T(8,128)(2,1)S(1)}, u32[]{:S(2)}, u32[]{:S(2)}) collective-permute-start(bf16[144,256]{1,0:T(8,128)(2,1)S(1)} %collective-permute-done.10.refs_6_), channel_id=1, source_target_pairs={{0,4},{4,0},{8,12},{12,8},{1,5},{5,1},{9,13},{13,9},{2,6},{6,2},{1... | collective-permute-start | bytes 221192 | tf_op jit(solution)/shard_map/ppermute | solution.py:442
  22.6 0.0 collective-permute-done.3.refs_3_
  22.7 0.9 %sum_early_tilts.1.total_ref = f32[256,2048]{1,0:T(8,128)S(1)} custom-call(bf16[256,256]{1,0:T(8,128)(2,1)S(1)} %get-tuple-element.11.rows_ref.refs_1_, bf16[4,192,2048]{2,1,0:T(8,128)(2,1)S(1)} %get-tuple-element.12.weights_ref, bf16[288,256]{1,0:T(8,128)(2,1)S(1)} %constant_dynamic-update-slice_fusion.refs_0_, ...), custom_call_target="tpu_custom_call" | custom-call | tf_op jit(solution)/shard_map/sum_early_tilts/pallas_call | solution.py:401
  23.6 0.0 collective-permute-done.7.refs_3_
  23.6 1.6 %finish_volume.1 = bf16[16,64,512]{2,1,0:T(8,128)(2,1)} custom-call(bf16[256,256]{1,0:T(8,128)(2,1)S(1)} %get-tuple-element.11.rows_ref.refs_1_, bf16[4,192,2048]{2,1,0:T(8,128)(2,1)S(1)} %get-tuple-element.12.weights_ref, f32[256,2048]{1,0:T(8,128)S(1)} %sum_early_tilts.1.total_ref, bf16[144,256]{1,0:T(8,128)(2,1)S(1)} %collective-permute-done.4.refs_0_, ...), custom_call_target="tpu_custom_call" | custom-call | tf_op jit(solution)/shard_map/finish_volume/pallas_call | solution.py:401
  (13 shorter events, 0.0 us)
Async XLA Ops:
  0.0 13.1 %copy-start.2 = (bf16[2,256,256]{2,1,0:T(8,128)(2,1)S(1)}, bf16[2,256,256]{2,1,0:T(8,128)(2,1)}, u32[]{:S(2)}) copy-start(bf16[2,256,256]{2,1,0:T(8,128)(2,1)} %constant.5.clone.waves) | copy-start | bytes 786436
  0.0 13.1 %copy-start = (s32[4,4]{1,0:T(4,128)S(1)}, s32[4,4]{1,0:T(4,128)}, u32[]{:S(2)}) copy-start(s32[4,4]{1,0:T(4,128)} %defocus_ref.1) | copy-start | bytes 196
  0.0 13.1 %copy-start.1 = (f32[4]{0:T(128)S(1)}, f32[4]{0:T(128)}, u32[]{:S(2)}) copy-start(f32[4]{0:T(128)} %angle_ref.1) | copy-start | bytes 52
  4.9 6.6 %collective-permute-start = (bf16[144,256]{1,0:T(8,128)(2,1)}, bf16[144,256]{1,0:T(8,128)(2,1)S(1)}, u32[]{:S(2)}, u32[]{:S(2)}) collective-permute-start(bf16[144,256]{1,0:T(8,128)(2,1)} %get-tuple-element.14), channel_id=1, source_target_pairs={{0,1},{1,0},{2,3},{3,2},{4,5},{5,4},{6,7},{7,6},{8,9},{9,8},{10,11... | collective-permute-start | bytes 221192 | tf_op jit(solution)/shard_map/ppermute | solution.py:442
  8.0 7.6 %collective-permute-start.4 = (bf16[144,256]{1,0:T(8,128)(2,1)}, bf16[144,256]{1,0:T(8,128)(2,1)S(1)}, u32[]{:S(2)}, u32[]{:S(2)}) collective-permute-start(bf16[144,256]{1,0:T(8,128)(2,1)} %get-tuple-element.15), channel_id=1, source_target_pairs={{0,3},{1,2},{2,1},{3,0},{4,7},{5,6},{6,5},{7,4},{8,11},{9,10},{10,... | collective-permute-start | bytes 221192 | tf_op jit(solution)/shard_map/ppermute | solution.py:442
  10.5 7.3 %collective-permute-start.8 = (bf16[144,256]{1,0:T(8,128)(2,1)}, bf16[144,256]{1,0:T(8,128)(2,1)S(1)}, u32[]{:S(2)}, u32[]{:S(2)}) collective-permute-start(bf16[144,256]{1,0:T(8,128)(2,1)} %get-tuple-element.16), channel_id=1, source_target_pairs={{0,2},{1,3},{2,0},{3,1},{4,6},{5,7},{6,4},{7,5},{8,10},{9,11},{10,... | collective-permute-start | bytes 221192 | tf_op jit(solution)/shard_map/ppermute | solution.py:442
  11.5 5.4 %collective-permute-start.2 = (bf16[288,256]{1,0:T(8,128)(2,1)S(1)}, bf16[288,256]{1,0:T(8,128)(2,1)S(1)}, u32[]{:S(2)}, u32[]{:S(2)}) collective-permute-start(bf16[288,256]{1,0:T(8,128)(2,1)S(1)} %constant_dynamic-update-slice_fusion.refs_0_), channel_id=1, source_target_pairs={{0,8},{4,12},{8,0},{12,4},{1,9},{5,13},{9,1},{13,5},{2,10},{6,14},... | collective-permute-start | bytes 442376 | tf_op jit(solution)/shard_map/ppermute | solution.py:442
  13.1 9.0 %collective-permute-start.1 = (bf16[288,256]{1,0:T(8,128)(2,1)S(1)}, bf16[288,256]{1,0:T(8,128)(2,1)S(1)}, u32[]{:S(2)}, u32[]{:S(2)}) collective-permute-start(bf16[288,256]{1,0:T(8,128)(2,1)S(1)} %constant_dynamic-update-slice_fusion.refs_0_), channel_id=1, source_target_pairs={{0,4},{4,0},{8,12},{12,8},{1,5},{5,1},{9,13},{13,9},{2,6},{6,2},{1... | collective-permute-start | bytes 442376 | tf_op jit(solution)/shard_map/ppermute | solution.py:442
  15.7 4.9 %collective-permute-start.6 = (bf16[144,256]{1,0:T(8,128)(2,1)S(1)}, bf16[144,256]{1,0:T(8,128)(2,1)S(1)}, u32[]{:S(2)}, u32[]{:S(2)}) collective-permute-start(bf16[144,256]{1,0:T(8,128)(2,1)S(1)} %collective-permute-done.4.refs_0_), channel_id=1, source_target_pairs={{0,8},{4,12},{8,0},{12,4},{1,9},{5,13},{9,1},{13,5},{2,10},{6,14},... | collective-permute-start | bytes 221192 | tf_op jit(solution)/shard_map/ppermute | solution.py:442
  17.0 5.7 %collective-permute-start.3 = (bf16[288,256]{1,0:T(8,128)(2,1)S(1)}, bf16[288,256]{1,0:T(8,128)(2,1)S(1)}, u32[]{:S(2)}, u32[]{:S(2)}) collective-permute-start(bf16[288,256]{1,0:T(8,128)(2,1)S(1)} %collective-permute-done.2.refs_2_), channel_id=1, source_target_pairs={{0,4},{4,0},{8,12},{12,8},{1,5},{5,1},{9,13},{13,9},{2,6},{6,2},{1... | collective-permute-start | bytes 442376 | tf_op jit(solution)/shard_map/ppermute | solution.py:442
  17.8 4.4 %collective-permute-start.10 = (bf16[144,256]{1,0:T(8,128)(2,1)S(1)}, bf16[144,256]{1,0:T(8,128)(2,1)S(1)}, u32[]{:S(2)}, u32[]{:S(2)}) collective-permute-start(bf16[144,256]{1,0:T(8,128)(2,1)S(1)} %after.1.refs_4_), channel_id=1, source_target_pairs={{0,8},{4,12},{8,0},{12,4},{1,9},{5,13},{9,1},{13,5},{2,10},{6,14},... | collective-permute-start | bytes 221192 | tf_op jit(solution)/shard_map/ppermute | solution.py:442
  19.3 4.3 %collective-permute-start.9 = (bf16[144,256]{1,0:T(8,128)(2,1)S(1)}, bf16[144,256]{1,0:T(8,128)(2,1)S(1)}, u32[]{:S(2)}, u32[]{:S(2)}) collective-permute-start(bf16[144,256]{1,0:T(8,128)(2,1)S(1)} %after.1.refs_4_), channel_id=1, source_target_pairs={{0,4},{4,0},{8,12},{12,8},{1,5},{5,1},{9,13},{13,9},{2,6},{6,2},{1... | collective-permute-start | bytes 221192 | tf_op jit(solution)/shard_map/ppermute | solution.py:442
  20.6 3.0 %collective-permute-start.5 = (bf16[144,256]{1,0:T(8,128)(2,1)S(1)}, bf16[144,256]{1,0:T(8,128)(2,1)S(1)}, u32[]{:S(2)}, u32[]{:S(2)}) collective-permute-start(bf16[144,256]{1,0:T(8,128)(2,1)S(1)} %collective-permute-done.4.refs_0_), channel_id=1, source_target_pairs={{0,4},{4,0},{8,12},{12,8},{1,5},{5,1},{9,13},{13,9},{2,6},{6,2},{1... | collective-permute-start | bytes 221192 | tf_op jit(solution)/shard_map/ppermute | solution.py:442
  22.1 1.4 %collective-permute-start.7 = (bf16[144,256]{1,0:T(8,128)(2,1)S(1)}, bf16[144,256]{1,0:T(8,128)(2,1)S(1)}, u32[]{:S(2)}, u32[]{:S(2)}) collective-permute-start(bf16[144,256]{1,0:T(8,128)(2,1)S(1)} %collective-permute-done.6.refs_2_), channel_id=1, source_target_pairs={{0,4},{4,0},{8,12},{12,8},{1,5},{5,1},{9,13},{13,9},{2,6},{6,2},{1... | collective-permute-start | bytes 221192 | tf_op jit(solution)/shard_map/ppermute | solution.py:442
  22.1 1.4 %collective-permute-start.11 = (bf16[144,256]{1,0:T(8,128)(2,1)S(1)}, bf16[144,256]{1,0:T(8,128)(2,1)S(1)}, u32[]{:S(2)}, u32[]{:S(2)}) collective-permute-start(bf16[144,256]{1,0:T(8,128)(2,1)S(1)} %collective-permute-done.10.refs_6_), channel_id=1, source_target_pairs={{0,4},{4,0},{8,12},{12,8},{1,5},{5,1},{9,13},{13,9},{2,6},{6,2},{1... | collective-permute-start | bytes 221192 | tf_op jit(solution)/shard_map/ppermute | solution.py:442

commit v11 on v10

--- a/solution.py
+++ b/solution.py
@@ -461,9 +461,9 @@
     sent = column_filtered(far + near, slices_owned, projections[0], tilt_angle, defocus, band_start)
     arrived = {d: exchange(sent[d], "tilt", d) if d else sent[d] for d in far + near}
     row_filters, weights = prepared(tilt_devices, slices_owned, rows, rows * row_devices, tilt_angle, defocus)
-    early = [gather_rows(jnp.concatenate([arrived[d] for d in near]))]
-    total = summed(row_filters, weights, early, [near])
-    late = [gather_rows(after(arrived[d], row_filters) if d == far[-1] else arrived[d]) for d in far]
+    early = [gather_rows(arrived[d], (row_filters,)) for d in near]
+    total = summed(row_filters, weights, early, [[d] for d in near])
+    late = [gather_rows(arrived[d], (row_filters,) if d == far[0] else ()) for d in far]
     return finished(row_filters, weights, total, late, [[d] for d in far], 1.0 / math.sqrt(tilt_devices))
 
 

time: 25.4 us -> 27.3 us (1.075)
  waiting for transfers between devices: 3.65 us -> 5.85 us
  local copies, waits for them, and re-layouts: 0.91 us -> 0.01 us
  starting transfers between devices: 10.6 us -> 11.3 us
    ppermute x12 -> x15, waiting for transfers between devices: 3.65 us -> 5.85 us  [exchange(): return lax.ppermute(array, axis, [(i, i ^ distance) for i in range(count)])]
    unnamed x7 -> x8, local copies, waits for them, and re-layouts: 0.9 us -> 0.01 us
    ppermute x12 -> x15, starting transfers between devices: 10.6 us -> 11.3 us  [exchange(): return lax.ppermute(array, axis, [(i, i ^ distance) for i in range(count)])]
  transfers between devices with their start and end apart: 12 -> 15, of which waited for: 3 -> 3; matrix products, arithmetic and copies ran while one was open for 4% -> 0% of each run, Pallas kernels for 14% -> 13%
where the time goes in v11:
time: 27.3 us; the launch traced here: 27.2 us
  starting transfers between devices  11.3 us (41%)
  Pallas kernels  9.99 us (37%)
  waiting for transfers between devices  5.85 us (21%)
    ppermute x15, starting transfers between devices, exchange(): return lax.ppermute(array, axis, [(i, i ^ distance) for i in range(count)])  11.3 us
    ppermute x15, waiting for transfers between devices, exchange(): return lax.ppermute(array, axis, [(i, i ^ distance) for i in range(count)])  5.85 us
    pallas_call x1, Pallas kernels, column_filtered(): pl.pallas_call(functools.partial(column_kernel, slots, slices_owned), out...  4.93 us
    pallas_call x2, Pallas kernels, interpolation(): pl.pallas_call(functools.partial(kernel, slots, len(patches[0])), in_spec...  2.54 us
    pallas_call x1, Pallas kernels, prepared(): pl.pallas_call(functools.partial(prepare_kernel, slots, slices_owned), ou...  2.52 us
  transfers between devices with their start and end apart: 15, of which 3 were waited for; matrix products, arithmetic and copies ran while one was open for 0% of the time, Pallas kernels for 13%

profile of v11, /device:TPU:0, one launch (start us, length us, event | category | flops | bytes accessed | tf_op | source)
XLA Modules:
  0.0 27.2 jit_solution(10079118260389447057)
XLA Ops:
  0.0 4.9 %column_filter.1 = (bf16[144,256]{1,0:T(8,128)(2,1)}, bf16[144,256]{1,0:T(8,128)(2,1)}, bf16[144,256]{1,0:T(8,128)(2,1)}, bf16[144,256]{1,0:T(8,128)(2,1)}) custom-call(bf16[64,2048]{1,0:T(8,128)(2,1)} %bitcast.1, bf16[5,256,512]{2,1,0:T(8,128)(2,1)} %constant.4.clone.matrix_ref, f32[4]{0:T(128)} %angle_ref.1, s32[4,4]{1,0:T(4,128)} %defocus_ref.1, ...), custom_call_target="tpu_custom_call" | custom-call | flops 822083584 | bytes 3145728 | tf_op jit(solution)/shard_map/column_filter/pallas_call | solution.py:230
  4.9 3.1 %collective-permute-start.3 = (bf16[144,256]{1,0:T(8,128)(2,1)}, bf16[144,256]{1,0:T(8,128)(2,1)S(1)}, u32[]{:S(2)}, u32[]{:S(2)}) collective-permute-start(bf16[144,256]{1,0:T(8,128)(2,1)} %get-tuple-element.14), channel_id=1, source_target_pairs={{0,1},{1,0},{2,3},{3,2},{4,5},{5,4},{6,7},{7,6},{8,9},{9,8},{10,11... | collective-permute-start | bytes 221192 | tf_op jit(solution)/shard_map/ppermute | solution.py:442
  8.0 2.5 %collective-permute-start.7 = (bf16[144,256]{1,0:T(8,128)(2,1)}, bf16[144,256]{1,0:T(8,128)(2,1)S(1)}, u32[]{:S(2)}, u32[]{:S(2)}) collective-permute-start(bf16[144,256]{1,0:T(8,128)(2,1)} %get-tuple-element.15), channel_id=1, source_target_pairs={{0,3},{1,2},{2,1},{3,0},{4,7},{5,6},{6,5},{7,4},{8,11},{9,10},{10,... | collective-permute-start | bytes 221192 | tf_op jit(solution)/shard_map/ppermute | solution.py:442
  10.5 1.5 %collective-permute-start.1 = (bf16[144,256]{1,0:T(8,128)(2,1)}, bf16[144,256]{1,0:T(8,128)(2,1)S(1)}, u32[]{:S(2)}, u32[]{:S(2)}) collective-permute-start(bf16[144,256]{1,0:T(8,128)(2,1)} %get-tuple-element.13.refs_0_), channel_id=1, source_target_pairs={{0,8},{4,12},{8,0},{12,4},{1,9},{5,13},{9,1},{13,5},{2,10},{6,14},... | collective-permute-start | bytes 221192 | tf_op jit(solution)/shard_map/ppermute | solution.py:442
  12.0 0.1 collective-permute-start.11
  12.1 0.0 collective-permute-done.3.refs_4_
  12.2 0.5 %collective-permute-start.5 = (bf16[144,256]{1,0:T(8,128)(2,1)S(1)}, bf16[144,256]{1,0:T(8,128)(2,1)S(1)}, u32[]{:S(2)}, u32[]{:S(2)}) collective-permute-start(bf16[144,256]{1,0:T(8,128)(2,1)S(1)} %collective-permute-done.3.refs_4_), channel_id=1, source_target_pairs={{0,8},{4,12},{8,0},{12,4},{1,9},{5,13},{9,1},{13,5},{2,10},{6,14},... | collective-permute-start | bytes 221192 | tf_op jit(solution)/shard_map/ppermute | solution.py:442
  12.7 2.0 %collective-permute-done.7.refs_0_ = bf16[144,256]{1,0:T(8,128)(2,1)S(1)} collective-permute-done((bf16[144,256]{1,0:T(8,128)(2,1)}, bf16[144,256]{1,0:T(8,128)(2,1)S(1)}, u32[]{:S(2)}, u32[]{:S(2)}) %collective-permute-start.7) | collective-permute-done | bytes 73760 | tf_op jit(solution)/shard_map/ppermute | solution.py:442
  14.6 1.5 %collective-permute-start.9 = (bf16[144,256]{1,0:T(8,128)(2,1)S(1)}, bf16[144,256]{1,0:T(8,128)(2,1)S(1)}, u32[]{:S(2)}, u32[]{:S(2)}) collective-permute-start(bf16[144,256]{1,0:T(8,128)(2,1)S(1)} %collective-permute-done.7.refs_0_), channel_id=1, source_target_pairs={{0,8},{4,12},{8,0},{12,4},{1,9},{5,13},{9,1},{13,5},{2,10},{6,14},... | collective-permute-start | bytes 221192 | tf_op jit(solution)/shard_map/ppermute | solution.py:442
  16.1 2.5 %prepare.1 = (bf16[256,256]{1,0:T(8,128)(2,1)S(1)}, bf16[4,192,2048]{2,1,0:T(8,128)(2,1)S(1)}) custom-call(f32[4]{0:T(128)S(1)} %copy-done.2, s32[4,4]{1,0:T(4,128)S(1)} %copy-done.1, bf16[2,256,256]{2,1,0:T(8,128)(2,1)S(1)} %copy-done.3), custom_call_target="tpu_custom_call" | custom-call | flops 2147483648 | bytes 6291456 | tf_op jit(solution)/shard_map/prepare/pallas_call | solution.py:316
  18.7 0.7 %collective-permute-done.11.refs_4_ = bf16[144,256]{1,0:T(8,128)(2,1)S(1)} collective-permute-done((bf16[144,256]{1,0:T(8,128)(2,1)}, bf16[144,256]{1,0:T(8,128)(2,1)S(1)}, u32[]{:S(2)}, u32[]{:S(2)}) %collective-permute-start.11) | collective-permute-done | bytes 73760 | tf_op jit(solution)/shard_map/ppermute | solution.py:442
  19.4 0.0 collective-permute-start.4
  19.4 0.0 collective-permute-done.1.refs_0_
  19.4 0.5 %collective-permute-start.13 = (bf16[144,256]{1,0:T(8,128)(2,1)S(1)}, bf16[144,256]{1,0:T(8,128)(2,1)S(1)}, u32[]{:S(2)}, u32[]{:S(2)}) collective-permute-start(bf16[144,256]{1,0:T(8,128)(2,1)S(1)} %collective-permute-done.11.refs_4_), channel_id=1, source_target_pairs={{0,8},{4,12},{8,0},{12,4},{1,9},{5,13},{9,1},{13,5},{2,10},{6,14},... | collective-permute-start | bytes 221192 | tf_op jit(solution)/shard_map/ppermute | solution.py:442
  19.9 0.0 collective-permute-done.9.refs_0_
  19.9 0.2 collective-permute-start.2
  20.2 0.0 collective-permute-done.5.refs_0_
  20.2 0.3 %collective-permute-start.8 = (bf16[144,256]{1,0:T(8,128)(2,1)S(1)}, bf16[144,256]{1,0:T(8,128)(2,1)S(1)}, u32[]{:S(2)}, u32[]{:S(2)}) collective-permute-start(bf16[144,256]{1,0:T(8,128)(2,1)S(1)} %collective-permute-done.7.refs_0_), channel_id=1, source_target_pairs={{0,4},{4,0},{8,12},{12,8},{1,5},{5,1},{9,13},{13,9},{2,6},{6,2},{1... | collective-permute-start | bytes 221192 | tf_op jit(solution)/shard_map/ppermute | solution.py:442
  20.4 0.2 collective-permute-start.6
  20.7 0.3 %collective-permute-start.12 = (bf16[144,256]{1,0:T(8,128)(2,1)S(1)}, bf16[144,256]{1,0:T(8,128)(2,1)S(1)}, u32[]{:S(2)}, u32[]{:S(2)}) collective-permute-start(bf16[144,256]{1,0:T(8,128)(2,1)S(1)} %collective-permute-done.11.refs_4_), channel_id=1, source_target_pairs={{0,4},{4,0},{8,12},{12,8},{1,5},{5,1},{9,13},{13,9},{2,6},{6,2},{1... | collective-permute-start | bytes 221192 | tf_op jit(solution)/shard_map/ppermute | solution.py:442
  21.0 3.1 %collective-permute-done.13.refs_6_ = bf16[144,256]{1,0:T(8,128)(2,1)S(1)} collective-permute-done((bf16[144,256]{1,0:T(8,128)(2,1)S(1)}, bf16[144,256]{1,0:T(8,128)(2,1)S(1)}, u32[]{:S(2)}, u32[]{:S(2)}) %collective-permute-start.13) | collective-permute-done | bytes 73760 | tf_op jit(solution)/shard_map/ppermute | solution.py:442
  24.1 0.5 %collective-permute-start.10 = (bf16[144,256]{1,0:T(8,128)(2,1)S(1)}, bf16[144,256]{1,0:T(8,128)(2,1)S(1)}, u32[]{:S(2)}, u32[]{:S(2)}) collective-permute-start(bf16[144,256]{1,0:T(8,128)(2,1)S(1)} %after.5.refs_2_), channel_id=1, source_target_pairs={{0,4},{4,0},{8,12},{12,8},{1,5},{5,1},{9,13},{13,9},{2,6},{6,2},{1... | collective-permute-start | bytes 221192 | tf_op jit(solution)/shard_map/ppermute | solution.py:442
  24.6 0.9 %sum_early_tilts.1.total_ref = f32[256,2048]{1,0:T(8,128)S(1)} custom-call(bf16[256,256]{1,0:T(8,128)(2,1)S(1)} %get-tuple-element.11.refs_1_.rows_ref, bf16[4,192,2048]{2,1,0:T(8,128)(2,1)S(1)} %get-tuple-element.12.weights_ref, bf16[144,256]{1,0:T(8,128)(2,1)S(1)} %copy-done, bf16[144,256]{1,0:T(8,128)(2,1)S(1)} %collective-permute-done.refs_1_, ...), custom_call_target="tpu_custom_call" | custom-call | tf_op jit(solution)/shard_map/sum_early_tilts/pallas_call | solution.py:401
  25.6 1.6 %finish_volume.1 = bf16[16,64,512]{2,1,0:T(8,128)(2,1)} custom-call(bf16[256,256]{1,0:T(8,128)(2,1)S(1)} %get-tuple-element.11.refs_1_.rows_ref, bf16[4,192,2048]{2,1,0:T(8,128)(2,1)S(1)} %get-tuple-element.12.weights_ref, f32[256,2048]{1,0:T(8,128)S(1)} %sum_early_tilts.1.total_ref, bf16[144,256]{1,0:T(8,128)(2,1)S(1)} %collective-permute-done.7.refs_0_, ...), custom_call_target="tpu_custom_call" | custom-call | tf_op jit(solution)/shard_map/finish_volume/pallas_call | solution.py:401
  (21 shorter events, 0.0 us)
Async XLA Ops:
  0.0 16.1 %copy-start.3 = (bf16[2,256,256]{2,1,0:T(8,128)(2,1)S(1)}, bf16[2,256,256]{2,1,0:T(8,128)(2,1)}, u32[]{:S(2)}) copy-start(bf16[2,256,256]{2,1,0:T(8,128)(2,1)} %constant.5.clone.waves) | copy-start | bytes 786436
  0.0 16.1 %copy-start.1 = (s32[4,4]{1,0:T(4,128)S(1)}, s32[4,4]{1,0:T(4,128)}, u32[]{:S(2)}) copy-start(s32[4,4]{1,0:T(4,128)} %defocus_ref.1) | copy-start | bytes 196
  0.0 16.1 %copy-start.2 = (f32[4]{0:T(128)S(1)}, f32[4]{0:T(128)}, u32[]{:S(2)}) copy-start(f32[4]{0:T(128)} %angle_ref.1) | copy-start | bytes 52
  4.9 7.2 %collective-permute-start.3 = (bf16[144,256]{1,0:T(8,128)(2,1)}, bf16[144,256]{1,0:T(8,128)(2,1)S(1)}, u32[]{:S(2)}, u32[]{:S(2)}) collective-permute-start(bf16[144,256]{1,0:T(8,128)(2,1)} %get-tuple-element.14), channel_id=1, source_target_pairs={{0,1},{1,0},{2,3},{3,2},{4,5},{5,4},{6,7},{7,6},{8,9},{9,8},{10,11... | collective-permute-start | bytes 221192 | tf_op jit(solution)/shard_map/ppermute | solution.py:442
  8.0 6.6 %collective-permute-start.7 = (bf16[144,256]{1,0:T(8,128)(2,1)}, bf16[144,256]{1,0:T(8,128)(2,1)S(1)}, u32[]{:S(2)}, u32[]{:S(2)}) collective-permute-start(bf16[144,256]{1,0:T(8,128)(2,1)} %get-tuple-element.15), channel_id=1, source_target_pairs={{0,3},{1,2},{2,1},{3,0},{4,7},{5,6},{6,5},{7,4},{8,11},{9,10},{10,... | collective-permute-start | bytes 221192 | tf_op jit(solution)/shard_map/ppermute | solution.py:442
  10.5 8.9 %collective-permute-start.1 = (bf16[144,256]{1,0:T(8,128)(2,1)}, bf16[144,256]{1,0:T(8,128)(2,1)S(1)}, u32[]{:S(2)}, u32[]{:S(2)}) collective-permute-start(bf16[144,256]{1,0:T(8,128)(2,1)} %get-tuple-element.13.refs_0_), channel_id=1, source_target_pairs={{0,8},{4,12},{8,0},{12,4},{1,9},{5,13},{9,1},{13,5},{2,10},{6,14},... | collective-permute-start | bytes 221192 | tf_op jit(solution)/shard_map/ppermute | solution.py:442
  12.0 8.4 %collective-permute-start = (bf16[144,256]{1,0:T(8,128)(2,1)}, bf16[144,256]{1,0:T(8,128)(2,1)S(1)}, u32[]{:S(2)}, u32[]{:S(2)}) collective-permute-start(bf16[144,256]{1,0:T(8,128)(2,1)} %get-tuple-element.13.refs_0_), channel_id=1, source_target_pairs={{0,4},{4,0},{8,12},{12,8},{1,5},{5,1},{9,13},{13,9},{2,6},{6,2},{1... | collective-permute-start | bytes 221192 | tf_op jit(solution)/shard_map/ppermute | solution.py:442
  12.0 12.6 %copy-start = (bf16[144,256]{1,0:T(8,128)(2,1)S(1)}, bf16[144,256]{1,0:T(8,128)(2,1)}, u32[]{:S(2)}) copy-start(bf16[144,256]{1,0:T(8,128)(2,1)} %get-tuple-element.13.refs_0_) | copy-start | bytes 221188
  12.0 7.4 %collective-permute-start.11 = (bf16[144,256]{1,0:T(8,128)(2,1)}, bf16[144,256]{1,0:T(8,128)(2,1)S(1)}, u32[]{:S(2)}, u32[]{:S(2)}) collective-permute-start(bf16[144,256]{1,0:T(8,128)(2,1)} %get-tuple-element.16), channel_id=1, source_target_pairs={{0,2},{1,3},{2,0},{3,1},{4,6},{5,7},{6,4},{7,5},{8,10},{9,11},{10,... | collective-permute-start | bytes 221192 | tf_op jit(solution)/shard_map/ppermute | solution.py:442
  12.2 8.0 %collective-permute-start.5 = (bf16[144,256]{1,0:T(8,128)(2,1)S(1)}, bf16[144,256]{1,0:T(8,128)(2,1)S(1)}, u32[]{:S(2)}, u32[]{:S(2)}) collective-permute-start(bf16[144,256]{1,0:T(8,128)(2,1)S(1)} %collective-permute-done.3.refs_4_), channel_id=1, source_target_pairs={{0,8},{4,12},{8,0},{12,4},{1,9},{5,13},{9,1},{13,5},{2,10},{6,14},... | collective-permute-start | bytes 221192 | tf_op jit(solution)/shard_map/ppermute | solution.py:442
  14.6 5.3 %collective-permute-start.9 = (bf16[144,256]{1,0:T(8,128)(2,1)S(1)}, bf16[144,256]{1,0:T(8,128)(2,1)S(1)}, u32[]{:S(2)}, u32[]{:S(2)}) collective-permute-start(bf16[144,256]{1,0:T(8,128)(2,1)S(1)} %collective-permute-done.7.refs_0_), channel_id=1, source_target_pairs={{0,8},{4,12},{8,0},{12,4},{1,9},{5,13},{9,1},{13,5},{2,10},{6,14},... | collective-permute-start | bytes 221192 | tf_op jit(solution)/shard_map/ppermute | solution.py:442
  19.4 1.3 %collective-permute-start.4 = (bf16[144,256]{1,0:T(8,128)(2,1)S(1)}, bf16[144,256]{1,0:T(8,128)(2,1)S(1)}, u32[]{:S(2)}, u32[]{:S(2)}) collective-permute-start(bf16[144,256]{1,0:T(8,128)(2,1)S(1)} %collective-permute-done.3.refs_4_), channel_id=1, source_target_pairs={{0,4},{4,0},{8,12},{12,8},{1,5},{5,1},{9,13},{13,9},{2,6},{6,2},{1... | collective-permute-start | bytes 221192 | tf_op jit(solution)/shard_map/ppermute | solution.py:442
  19.4 4.7 %collective-permute-start.13 = (bf16[144,256]{1,0:T(8,128)(2,1)S(1)}, bf16[144,256]{1,0:T(8,128)(2,1)S(1)}, u32[]{:S(2)}, u32[]{:S(2)}) collective-permute-start(bf16[144,256]{1,0:T(8,128)(2,1)S(1)} %collective-permute-done.11.refs_4_), channel_id=1, source_target_pairs={{0,8},{4,12},{8,0},{12,4},{1,9},{5,13},{9,1},{13,5},{2,10},{6,14},... | collective-permute-start | bytes 221192 | tf_op jit(solution)/shard_map/ppermute | solution.py:442
  19.9 4.2 %collective-permute-start.2 = (bf16[144,256]{1,0:T(8,128)(2,1)S(1)}, bf16[144,256]{1,0:T(8,128)(2,1)S(1)}, u32[]{:S(2)}, u32[]{:S(2)}) collective-permute-start(bf16[144,256]{1,0:T(8,128)(2,1)S(1)} %after.3.refs_2_), channel_id=1, source_target_pairs={{0,4},{4,0},{8,12},{12,8},{1,5},{5,1},{9,13},{13,9},{2,6},{6,2},{1... | collective-permute-start | bytes 221192 | tf_op jit(solution)/shard_map/ppermute | solution.py:442
  20.2 5.4 %collective-permute-start.8 = (bf16[144,256]{1,0:T(8,128)(2,1)S(1)}, bf16[144,256]{1,0:T(8,128)(2,1)S(1)}, u32[]{:S(2)}, u32[]{:S(2)}) collective-permute-start(bf16[144,256]{1,0:T(8,128)(2,1)S(1)} %collective-permute-done.7.refs_0_), channel_id=1, source_target_pairs={{0,4},{4,0},{8,12},{12,8},{1,5},{5,1},{9,13},{13,9},{2,6},{6,2},{1... | collective-permute-start | bytes 221192 | tf_op jit(solution)/shard_map/ppermute | solution.py:442
  20.4 4.2 %collective-permute-start.6 = (bf16[144,256]{1,0:T(8,128)(2,1)S(1)}, bf16[144,256]{1,0:T(8,128)(2,1)S(1)}, u32[]{:S(2)}, u32[]{:S(2)}) collective-permute-start(bf16[144,256]{1,0:T(8,128)(2,1)S(1)} %after.4.refs_6_), channel_id=1, source_target_pairs={{0,4},{4,0},{8,12},{12,8},{1,5},{5,1},{9,13},{13,9},{2,6},{6,2},{1... | collective-permute-start | bytes 221192 | tf_op jit(solution)/shard_map/ppermute | solution.py:442
  20.7 4.9 %collective-permute-start.12 = (bf16[144,256]{1,0:T(8,128)(2,1)S(1)}, bf16[144,256]{1,0:T(8,128)(2,1)S(1)}, u32[]{:S(2)}, u32[]{:S(2)}) collective-permute-start(bf16[144,256]{1,0:T(8,128)(2,1)S(1)} %collective-permute-done.11.refs_4_), channel_id=1, source_target_pairs={{0,4},{4,0},{8,12},{12,8},{1,5},{5,1},{9,13},{13,9},{2,6},{6,2},{1... | collective-permute-start | bytes 221192 | tf_op jit(solution)/shard_map/ppermute | solution.py:442
  24.1 1.4 %collective-permute-start.14 = (bf16[144,256]{1,0:T(8,128)(2,1)S(1)}, bf16[144,256]{1,0:T(8,128)(2,1)S(1)}, u32[]{:S(2)}, u32[]{:S(2)}) collective-permute-start(bf16[144,256]{1,0:T(8,128)(2,1)S(1)} %collective-permute-done.13.refs_6_), channel_id=1, source_target_pairs={{0,4},{4,0},{8,12},{12,8},{1,5},{5,1},{9,13},{13,9},{2,6},{6,2},{1... | collective-permute-start | bytes 221192 | tf_op jit(solution)/shard_map/ppermute | solution.py:442
  24.1 1.4 %collective-permute-start.10 = (bf16[144,256]{1,0:T(8,128)(2,1)S(1)}, bf16[144,256]{1,0:T(8,128)(2,1)S(1)}, u32[]{:S(2)}, u32[]{:S(2)}) collective-permute-start(bf16[144,256]{1,0:T(8,128)(2,1)S(1)} %after.5.refs_2_), channel_id=1, source_target_pairs={{0,4},{4,0},{8,12},{12,8},{1,5},{5,1},{9,13},{13,9},{2,6},{6,2},{1... | collective-permute-start | bytes 221192 | tf_op jit(solution)/shard_map/ppermute | solution.py:442

commit v12 on v11

--- a/solution.py
+++ b/solution.py
@@ -457,14 +457,14 @@
     _, rows, _ = projections.shape
     row_devices, tilt_devices = lax.axis_size("row"), lax.axis_size("tilt")
     slices_owned = SLICES // tilt_devices
-    far, near = list(range(tilt_devices - 1, 1, -1)), list(range(min(2, tilt_devices)))
-    sent = column_filtered(far + near, slices_owned, projections[0], tilt_angle, defocus, band_start)
-    arrived = {d: exchange(sent[d], "tilt", d) if d else sent[d] for d in far + near}
+    first, later = [0, tilt_devices - 1], list(range(1, tilt_devices - 1))
+    sent = column_filtered(first[::-1] + later, slices_owned, projections[0], tilt_angle, defocus, band_start)
+    arrived = {d: exchange(sent[d], "tilt", d) if d else sent[d] for d in first[::-1] + later}
     row_filters, weights = prepared(tilt_devices, slices_owned, rows, rows * row_devices, tilt_angle, defocus)
-    early = [gather_rows(arrived[d], (row_filters,)) for d in near]
-    total = summed(row_filters, weights, early, [[d] for d in near])
-    late = [gather_rows(arrived[d], (row_filters,) if d == far[0] else ()) for d in far]
-    return finished(row_filters, weights, total, late, [[d] for d in far], 1.0 / math.sqrt(tilt_devices))
+    early = [gather_rows(jnp.concatenate([arrived[d] for d in first]))]
+    total = summed(row_filters, weights, early, [first])
+    late = [gather_rows(after(arrived[d], row_filters) if d == later[-1] else arrived[d]) for d in later]
+    return finished(row_filters, weights, total, late, [[d] for d in later], 1.0 / math.sqrt(tilt_devices))
 
 
 def solution(mesh):

time: 27.3 us -> 27.1 us (level)
  starting transfers between devices: 11.3 us -> 10.1 us
  local copies, waits for them, and re-layouts: 0.01 us -> 0.91 us
    ppermute x15 -> x12, starting transfers between devices: 11.3 us -> 10.1 us  [exchange(): return lax.ppermute(array, axis, [(i, i ^ distance) for i in range(count)])]
    unnamed x8 -> x7, local copies, waits for them, and re-layouts: 0.01 us -> 0.9 us
    ppermute x15 -> x12, waiting for transfers between devices: 5.85 us -> 5.84 us  [exchange(): return lax.ppermute(array, axis, [(i, i ^ distance) for i in range(count)])]
  transfers between devices with their start and end apart: 15 -> 12, of which waited for: 3 -> 4; matrix products, arithmetic and copies ran while one was open for 0% -> 3% of each run, Pallas kernels for 13% -> 13%
where the time goes in v12:
time: 27.1 us; the launch traced here: 26.9 us
  starting transfers between devices  10.1 us (37%)
  Pallas kernels  10 us (37%)
  waiting for transfers between devices  5.84 us (22%)
  local copies, waits for them, and re-layouts  0.91 us (3%)
    ppermute x12, starting transfers between devices, exchange(): return lax.ppermute(array, axis, [(i, i ^ distance) for i in range(count)])  10.1 us
    ppermute x12, waiting for transfers between devices, exchange(): return lax.ppermute(array, axis, [(i, i ^ distance) for i in range(count)])  5.84 us
    pallas_call x1, Pallas kernels, column_filtered(): pl.pallas_call(functools.partial(column_kernel, slots, slices_owned), out...  4.93 us
    pallas_call x2, Pallas kernels, interpolation(): pl.pallas_call(functools.partial(kernel, slots, len(patches[0])), in_spec...  2.54 us
    pallas_call x1, Pallas kernels, prepared(): pl.pallas_call(functools.partial(prepare_kernel, slots, slices_owned), ou...  2.53 us
    unnamed x7, local copies, waits for them, and re-layouts  0.9 us
  transfers between devices with their start and end apart: 12, of which 4 were waited for; matrix products, arithmetic and copies ran while one was open for 3% of the time, Pallas kernels for 13%

profile of v12, /device:TPU:0, one launch (start us, length us, event | category | flops | bytes accessed | tf_op | source)
XLA Modules:
  0.0 26.9 jit_solution(16119276080224260042)
XLA Ops:
  0.0 4.9 %column_filter.1 = (bf16[144,256]{1,0:T(8,128)(2,1)}, bf16[144,256]{1,0:T(8,128)(2,1)}, bf16[144,256]{1,0:T(8,128)(2,1)}, bf16[144,256]{1,0:T(8,128)(2,1)}) custom-call(bf16[64,2048]{1,0:T(8,128)(2,1)} %bitcast.1, bf16[5,256,512]{2,1,0:T(8,128)(2,1)} %constant.4.clone.matrix_ref, f32[4]{0:T(128)} %angle_ref.1, s32[4,4]{1,0:T(4,128)} %defocus_ref.1, ...), custom_call_target="tpu_custom_call" | custom-call | flops 822083584 | bytes 3145728 | tf_op jit(solution)/shard_map/column_filter/pallas_call | solution.py:230
  4.9 5.1 %collective-permute-start = (bf16[144,256]{1,0:T(8,128)(2,1)}, bf16[144,256]{1,0:T(8,128)(2,1)S(1)}, u32[]{:S(2)}, u32[]{:S(2)}) collective-permute-start(bf16[144,256]{1,0:T(8,128)(2,1)} %get-tuple-element.14), channel_id=1, source_target_pairs={{0,3},{1,2},{2,1},{3,0},{4,7},{5,6},{6,5},{7,4},{8,11},{9,10},{10,... | collective-permute-start | bytes 221192 | tf_op jit(solution)/shard_map/ppermute | solution.py:442
  10.1 0.0 collective-permute-start.4
  10.1 0.6 %collective-permute-start.8 = (bf16[144,256]{1,0:T(8,128)(2,1)}, bf16[144,256]{1,0:T(8,128)(2,1)S(1)}, u32[]{:S(2)}, u32[]{:S(2)}) collective-permute-start(bf16[144,256]{1,0:T(8,128)(2,1)} %get-tuple-element.16), channel_id=1, source_target_pairs={{0,2},{1,3},{2,0},{3,1},{4,6},{5,7},{6,4},{7,5},{8,10},{9,11},{10,... | collective-permute-start | bytes 221192 | tf_op jit(solution)/shard_map/ppermute | solution.py:442
  10.7 0.9 %constant_dynamic-update-slice_fusion.1 = bf16[288,256]{1,0:T(8,128)(2,1)S(1)} fusion(bf16[144,256]{1,0:T(8,128)(2,1)} %get-tuple-element.13), kind=kLoop, calls=%fused_computation.1 | loop fusion | bytes 147456
  11.6 1.8 %collective-permute-done = bf16[144,256]{1,0:T(8,128)(2,1)S(1)} collective-permute-done((bf16[144,256]{1,0:T(8,128)(2,1)}, bf16[144,256]{1,0:T(8,128)(2,1)S(1)}, u32[]{:S(2)}, u32[]{:S(2)}) %collective-permute-start) | collective-permute-done | bytes 73760 | tf_op jit(solution)/shard_map/ppermute | solution.py:442
  13.4 1.5 %collective-permute-start.2 = (bf16[288,256]{1,0:T(8,128)(2,1)S(1)}, bf16[288,256]{1,0:T(8,128)(2,1)S(1)}, u32[]{:S(2)}, u32[]{:S(2)}) collective-permute-start(bf16[288,256]{1,0:T(8,128)(2,1)S(1)} %constant_dynamic-update-slice_fusion.refs_0_), channel_id=1, source_target_pairs={{0,8},{4,12},{8,0},{12,4},{1,9},{5,13},{9,1},{13,5},{2,10},{6,14},... | collective-permute-start | bytes 442376 | tf_op jit(solution)/shard_map/ppermute | solution.py:442
  15.0 0.0 collective-permute-start.1
  15.0 2.5 %prepare.1 = (bf16[256,256]{1,0:T(8,128)(2,1)S(1)}, bf16[4,192,2048]{2,1,0:T(8,128)(2,1)S(1)}) custom-call(f32[4]{0:T(128)S(1)} %copy-done.1, s32[4,4]{1,0:T(4,128)S(1)} %copy-done, bf16[2,256,256]{2,1,0:T(8,128)(2,1)S(1)} %copy-done.2), custom_call_target="tpu_custom_call" | custom-call | flops 2147483648 | bytes 6291456 | tf_op jit(solution)/shard_map/prepare/pallas_call | solution.py:316
  17.5 0.0 collective-permute-done.4.refs_0_
  17.5 0.6 %collective-permute-start.6 = (bf16[144,256]{1,0:T(8,128)(2,1)S(1)}, bf16[144,256]{1,0:T(8,128)(2,1)S(1)}, u32[]{:S(2)}, u32[]{:S(2)}) collective-permute-start(bf16[144,256]{1,0:T(8,128)(2,1)S(1)} %collective-permute-done.4.refs_0_), channel_id=1, source_target_pairs={{0,8},{4,12},{8,0},{12,4},{1,9},{5,13},{9,1},{13,5},{2,10},{6,14},... | collective-permute-start | bytes 221192 | tf_op jit(solution)/shard_map/ppermute | solution.py:442
  18.1 0.5 %collective-permute-done.2.refs_2_ = bf16[288,256]{1,0:T(8,128)(2,1)S(1)} collective-permute-done((bf16[288,256]{1,0:T(8,128)(2,1)S(1)}, bf16[288,256]{1,0:T(8,128)(2,1)S(1)}, u32[]{:S(2)}, u32[]{:S(2)}) %collective-permute-start.2) | collective-permute-done | bytes 147488 | tf_op jit(solution)/shard_map/ppermute | solution.py:442
  18.6 0.0 collective-permute-start.3
  18.6 0.0 collective-permute-done.8.refs_0_
  18.6 1.6 %collective-permute-start.10 = (bf16[144,256]{1,0:T(8,128)(2,1)S(1)}, bf16[144,256]{1,0:T(8,128)(2,1)S(1)}, u32[]{:S(2)}, u32[]{:S(2)}) collective-permute-start(bf16[144,256]{1,0:T(8,128)(2,1)S(1)} %after.1.refs_4_), channel_id=1, source_target_pairs={{0,8},{4,12},{8,0},{12,4},{1,9},{5,13},{9,1},{13,5},{2,10},{6,14},... | collective-permute-start | bytes 221192 | tf_op jit(solution)/shard_map/ppermute | solution.py:442
  20.2 0.2 collective-permute-start.9
  20.3 2.3 %collective-permute-done.6.refs_2_ = bf16[144,256]{1,0:T(8,128)(2,1)S(1)} collective-permute-done((bf16[144,256]{1,0:T(8,128)(2,1)S(1)}, bf16[144,256]{1,0:T(8,128)(2,1)S(1)}, u32[]{:S(2)}, u32[]{:S(2)}) %collective-permute-start.6) | collective-permute-done | bytes 73760 | tf_op jit(solution)/shard_map/ppermute | solution.py:442
  22.7 1.2 %collective-permute-done.10.refs_6_ = bf16[144,256]{1,0:T(8,128)(2,1)S(1)} collective-permute-done((bf16[144,256]{1,0:T(8,128)(2,1)S(1)}, bf16[144,256]{1,0:T(8,128)(2,1)S(1)}, u32[]{:S(2)}, u32[]{:S(2)}) %collective-permute-start.10) | collective-permute-done | bytes 73760 | tf_op jit(solution)/shard_map/ppermute | solution.py:442
  23.8 0.5 %collective-permute-start.11 = (bf16[144,256]{1,0:T(8,128)(2,1)S(1)}, bf16[144,256]{1,0:T(8,128)(2,1)S(1)}, u32[]{:S(2)}, u32[]{:S(2)}) collective-permute-start(bf16[144,256]{1,0:T(8,128)(2,1)S(1)} %collective-permute-done.10.refs_6_), channel_id=1, source_target_pairs={{0,4},{4,0},{8,12},{12,8},{1,5},{5,1},{9,13},{13,9},{2,6},{6,2},{1... | collective-permute-start | bytes 221192 | tf_op jit(solution)/shard_map/ppermute | solution.py:442
  24.4 0.9 %sum_early_tilts.1.total_ref = f32[256,2048]{1,0:T(8,128)S(1)} custom-call(bf16[256,256]{1,0:T(8,128)(2,1)S(1)} %get-tuple-element.11.rows_ref.refs_1_, bf16[4,192,2048]{2,1,0:T(8,128)(2,1)S(1)} %get-tuple-element.12.weights_ref, bf16[288,256]{1,0:T(8,128)(2,1)S(1)} %constant_dynamic-update-slice_fusion.refs_0_, ...), custom_call_target="tpu_custom_call" | custom-call | tf_op jit(solution)/shard_map/sum_early_tilts/pallas_call | solution.py:401
  25.3 0.0 collective-permute-done.5.refs_1_
  25.3 0.0 collective-permute-done.9.refs_5_
  25.3 0.0 collective-permute-done.11.refs_7_
  25.3 1.6 %finish_volume.1 = bf16[16,64,512]{2,1,0:T(8,128)(2,1)} custom-call(bf16[256,256]{1,0:T(8,128)(2,1)S(1)} %get-tuple-element.11.rows_ref.refs_1_, bf16[4,192,2048]{2,1,0:T(8,128)(2,1)S(1)} %get-tuple-element.12.weights_ref, f32[256,2048]{1,0:T(8,128)S(1)} %sum_early_tilts.1.total_ref, bf16[144,256]{1,0:T(8,128)(2,1)S(1)} %collective-permute-done.4.refs_0_, ...), custom_call_target="tpu_custom_call" | custom-call | tf_op jit(solution)/shard_map/finish_volume/pallas_call | solution.py:401
  (13 shorter events, 0.0 us)
Async XLA Ops:
  0.0 15.0 %copy-start.2 = (bf16[2,256,256]{2,1,0:T(8,128)(2,1)S(1)}, bf16[2,256,256]{2,1,0:T(8,128)(2,1)}, u32[]{:S(2)}) copy-start(bf16[2,256,256]{2,1,0:T(8,128)(2,1)} %constant.5.clone.waves) | copy-start | bytes 786436
  0.0 15.0 %copy-start = (s32[4,4]{1,0:T(4,128)S(1)}, s32[4,4]{1,0:T(4,128)}, u32[]{:S(2)}) copy-start(s32[4,4]{1,0:T(4,128)} %defocus_ref.1) | copy-start | bytes 196
  0.0 15.0 %copy-start.1 = (f32[4]{0:T(128)S(1)}, f32[4]{0:T(128)}, u32[]{:S(2)}) copy-start(f32[4]{0:T(128)} %angle_ref.1) | copy-start | bytes 52
  4.9 8.5 %collective-permute-start = (bf16[144,256]{1,0:T(8,128)(2,1)}, bf16[144,256]{1,0:T(8,128)(2,1)S(1)}, u32[]{:S(2)}, u32[]{:S(2)}) collective-permute-start(bf16[144,256]{1,0:T(8,128)(2,1)} %get-tuple-element.14), channel_id=1, source_target_pairs={{0,3},{1,2},{2,1},{3,0},{4,7},{5,6},{6,5},{7,4},{8,11},{9,10},{10,... | collective-permute-start | bytes 221192 | tf_op jit(solution)/shard_map/ppermute | solution.py:442
  10.1 7.5 %collective-permute-start.4 = (bf16[144,256]{1,0:T(8,128)(2,1)}, bf16[144,256]{1,0:T(8,128)(2,1)S(1)}, u32[]{:S(2)}, u32[]{:S(2)}) collective-permute-start(bf16[144,256]{1,0:T(8,128)(2,1)} %get-tuple-element.15), channel_id=1, source_target_pairs={{0,1},{1,0},{2,3},{3,2},{4,5},{5,4},{6,7},{7,6},{8,9},{9,8},{10,11... | collective-permute-start | bytes 221192 | tf_op jit(solution)/shard_map/ppermute | solution.py:442
  10.1 8.5 %collective-permute-start.8 = (bf16[144,256]{1,0:T(8,128)(2,1)}, bf16[144,256]{1,0:T(8,128)(2,1)S(1)}, u32[]{:S(2)}, u32[]{:S(2)}) collective-permute-start(bf16[144,256]{1,0:T(8,128)(2,1)} %get-tuple-element.16), channel_id=1, source_target_pairs={{0,2},{1,3},{2,0},{3,1},{4,6},{5,7},{6,4},{7,5},{8,10},{9,11},{10,... | collective-permute-start | bytes 221192 | tf_op jit(solution)/shard_map/ppermute | solution.py:442
  13.4 5.1 %collective-permute-start.2 = (bf16[288,256]{1,0:T(8,128)(2,1)S(1)}, bf16[288,256]{1,0:T(8,128)(2,1)S(1)}, u32[]{:S(2)}, u32[]{:S(2)}) collective-permute-start(bf16[288,256]{1,0:T(8,128)(2,1)S(1)} %constant_dynamic-update-slice_fusion.refs_0_), channel_id=1, source_target_pairs={{0,8},{4,12},{8,0},{12,4},{1,9},{5,13},{9,1},{13,5},{2,10},{6,14},... | collective-permute-start | bytes 442376 | tf_op jit(solution)/shard_map/ppermute | solution.py:442
  15.0 8.9 %collective-permute-start.1 = (bf16[288,256]{1,0:T(8,128)(2,1)S(1)}, bf16[288,256]{1,0:T(8,128)(2,1)S(1)}, u32[]{:S(2)}, u32[]{:S(2)}) collective-permute-start(bf16[288,256]{1,0:T(8,128)(2,1)S(1)} %constant_dynamic-update-slice_fusion.refs_0_), channel_id=1, source_target_pairs={{0,4},{4,0},{8,12},{12,8},{1,5},{5,1},{9,13},{13,9},{2,6},{6,2},{1... | collective-permute-start | bytes 442376 | tf_op jit(solution)/shard_map/ppermute | solution.py:442
  17.5 5.1 %collective-permute-start.6 = (bf16[144,256]{1,0:T(8,128)(2,1)S(1)}, bf16[144,256]{1,0:T(8,128)(2,1)S(1)}, u32[]{:S(2)}, u32[]{:S(2)}) collective-permute-start(bf16[144,256]{1,0:T(8,128)(2,1)S(1)} %collective-permute-done.4.refs_0_), channel_id=1, source_target_pairs={{0,8},{4,12},{8,0},{12,4},{1,9},{5,13},{9,1},{13,5},{2,10},{6,14},... | collective-permute-start | bytes 221192 | tf_op jit(solution)/shard_map/ppermute | solution.py:442
  18.6 5.8 %collective-permute-start.3 = (bf16[288,256]{1,0:T(8,128)(2,1)S(1)}, bf16[288,256]{1,0:T(8,128)(2,1)S(1)}, u32[]{:S(2)}, u32[]{:S(2)}) collective-permute-start(bf16[288,256]{1,0:T(8,128)(2,1)S(1)} %collective-permute-done.2.refs_2_), channel_id=1, source_target_pairs={{0,4},{4,0},{8,12},{12,8},{1,5},{5,1},{9,13},{13,9},{2,6},{6,2},{1... | collective-permute-start | bytes 442376 | tf_op jit(solution)/shard_map/ppermute | solution.py:442
  18.6 5.2 %collective-permute-start.10 = (bf16[144,256]{1,0:T(8,128)(2,1)S(1)}, bf16[144,256]{1,0:T(8,128)(2,1)S(1)}, u32[]{:S(2)}, u32[]{:S(2)}) collective-permute-start(bf16[144,256]{1,0:T(8,128)(2,1)S(1)} %after.1.refs_4_), channel_id=1, source_target_pairs={{0,8},{4,12},{8,0},{12,4},{1,9},{5,13},{9,1},{13,5},{2,10},{6,14},... | collective-permute-start | bytes 221192 | tf_op jit(solution)/shard_map/ppermute | solution.py:442
  20.2 5.1 %collective-permute-start.9 = (bf16[144,256]{1,0:T(8,128)(2,1)S(1)}, bf16[144,256]{1,0:T(8,128)(2,1)S(1)}, u32[]{:S(2)}, u32[]{:S(2)}) collective-permute-start(bf16[144,256]{1,0:T(8,128)(2,1)S(1)} %after.1.refs_4_), channel_id=1, source_target_pairs={{0,4},{4,0},{8,12},{12,8},{1,5},{5,1},{9,13},{13,9},{2,6},{6,2},{1... | collective-permute-start | bytes 221192 | tf_op jit(solution)/shard_map/ppermute | solution.py:442
  22.7 2.6 %collective-permute-start.5 = (bf16[144,256]{1,0:T(8,128)(2,1)S(1)}, bf16[144,256]{1,0:T(8,128)(2,1)S(1)}, u32[]{:S(2)}, u32[]{:S(2)}) collective-permute-start(bf16[144,256]{1,0:T(8,128)(2,1)S(1)} %collective-permute-done.4.refs_0_), channel_id=1, source_target_pairs={{0,4},{4,0},{8,12},{12,8},{1,5},{5,1},{9,13},{13,9},{2,6},{6,2},{1... | collective-permute-start | bytes 221192 | tf_op jit(solution)/shard_map/ppermute | solution.py:442
  23.8 1.4 %collective-permute-start.7 = (bf16[144,256]{1,0:T(8,128)(2,1)S(1)}, bf16[144,256]{1,0:T(8,128)(2,1)S(1)}, u32[]{:S(2)}, u32[]{:S(2)}) collective-permute-start(bf16[144,256]{1,0:T(8,128)(2,1)S(1)} %collective-permute-done.6.refs_2_), channel_id=1, source_target_pairs={{0,4},{4,0},{8,12},{12,8},{1,5},{5,1},{9,13},{13,9},{2,6},{6,2},{1... | collective-permute-start | bytes 221192 | tf_op jit(solution)/shard_map/ppermute | solution.py:442
  23.8 1.4 %collective-permute-start.11 = (bf16[144,256]{1,0:T(8,128)(2,1)S(1)}, bf16[144,256]{1,0:T(8,128)(2,1)S(1)}, u32[]{:S(2)}, u32[]{:S(2)}) collective-permute-start(bf16[144,256]{1,0:T(8,128)(2,1)S(1)} %collective-permute-done.10.refs_6_), channel_id=1, source_target_pairs={{0,4},{4,0},{8,12},{12,8},{1,5},{5,1},{9,13},{13,9},{2,6},{6,2},{1... | collective-permute-start | bytes 221192 | tf_op jit(solution)/shard_map/ppermute | solution.py:442

commit v13 on v10

--- a/solution.py
+++ b/solution.py
@@ -268,7 +268,7 @@
     )(array, *others)
 
 
-def prepare_kernel(slots, slices_owned, angles, defocus, waves, rows_ref, weights_ref, mine, order):
+def prepare_kernel(slots, slices_owned, angles, defocus, waves, awaited, rows_ref, weights_ref, mine, order):
     tilt, row = lax.axis_index("tilt"), lax.axis_index("row")
     slab, local_first = tilt * slices_owned // SLAB, tilt * slices_owned % SLAB
     full_rows = waves.shape[1]
@@ -311,7 +311,7 @@
         lax.fori_loop(0, slices_owned, one_slice, 0, unroll=2)
 
 
-def prepared(slots, slices_owned, rows, full_rows, angles, defocus):
+def prepared(slots, slices_owned, rows, full_rows, angles, defocus, awaited):
     smem, vmem = pl.BlockSpec(memory_space=pltpu.SMEM), pl.BlockSpec(memory_space=pltpu.VMEM)
     return pl.pallas_call(
         functools.partial(prepare_kernel, slots, slices_owned),
@@ -319,7 +319,7 @@
             jax.ShapeDtypeStruct((slots * rows, full_rows), jnp.bfloat16),
             jax.ShapeDtypeStruct((slots, MAIN + XBLK * REST, slices_owned * XBW), jnp.bfloat16),
         ],
-        in_specs=[smem] * 2 + [vmem],
+        in_specs=[smem] * 2 + [vmem, pl.BlockSpec(memory_space=pl.ANY)],
         out_specs=[vmem] * 2,
         scratch_shapes=[
             pltpu.VMEM((2, slots * rows, full_rows), jnp.bfloat16),
@@ -328,7 +328,7 @@
         compiler_params=pltpu.CompilerParams(vmem_limit_bytes=32 * 2**20),
         cost_estimate=pl.CostEstimate(flops=2**31, bytes_accessed=6 * 2**20, transcendentals=0),
         name="prepare",
-    )(angles, defocus, jnp.asarray(row_tables(full_rows)))
+    )(angles, defocus, jnp.asarray(row_tables(full_rows)), awaited)
 
 
 def unpacked(packed):
@@ -359,9 +359,9 @@
     return parts
 
 
-def sum_kernel(slots, row_devices, rows_ref, weights_ref, *refs):
-    total_ref = refs[-1]
-    (slot, part), *others = corrected_patches(slots, row_devices, rows_ref, refs[:-1])
+def sum_kernel(slots, row_devices, *refs):
+    *patch_refs, rows_ref, weights_ref, total_ref = refs
+    (slot, part), *others = corrected_patches(slots, row_devices, rows_ref, patch_refs)
     step = 4 * XBW
     for first in range(0, total_ref.shape[1], step):
         here = slice(first, first + step)
@@ -371,9 +371,8 @@
         total_ref[:, here] = total
 
 
-def finish_kernel(factor, slots, row_devices, rows_ref, weights_ref, total_ref, *refs):
-    patch_refs = refs[: len(slots) * row_devices]
-    out_ref, out, sems = refs[len(slots) * row_devices :]
+def finish_kernel(factor, slots, row_devices, total_ref, *refs):
+    *patch_refs, rows_ref, weights_ref, out_ref, out, sems = refs
     rows = total_ref.shape[0] // XBLK
     parts = corrected_patches(slots, row_devices, rows_ref, patch_refs)
     step = 4
@@ -397,7 +396,7 @@
 
 def interpolation(kernel, slots, weights, row_filters, patches, totals, **call):
     vmem = pl.BlockSpec(memory_space=pltpu.VMEM)
-    operands = [row_filters, weights, *totals, *(block for group in patches for block in group)]
+    operands = [*totals, *(block for group in patches for block in group), row_filters, weights]
     return pl.pallas_call(
         functools.partial(kernel, slots, len(patches[0])),
         in_specs=[vmem] * len(operands),
@@ -460,7 +459,7 @@
     far, near = list(range(tilt_devices - 1, 1, -1)), list(range(min(2, tilt_devices)))
     sent = column_filtered(far + near, slices_owned, projections[0], tilt_angle, defocus, band_start)
     arrived = {d: exchange(sent[d], "tilt", d) if d else sent[d] for d in far + near}
-    row_filters, weights = prepared(tilt_devices, slices_owned, rows, rows * row_devices, tilt_angle, defocus)
+    row_filters, weights = prepared(tilt_devices, slices_owned, rows, rows * row_devices, tilt_angle, defocus, arrived[far[0]])
     early = [gather_rows(jnp.concatenate([arrived[d] for d in near]))]
     total = summed(row_filters, weights, early, [near])
     late = [gather_rows(after(arrived[d], row_filters) if d == far[-1] else arrived[d]) for d in far]

time: 25.4 us -> 27.6 us (1.087)
  waiting for transfers between devices: 3.65 us -> 5.95 us
    ppermute x12, waiting for transfers between devices: 3.65 us -> 5.95 us  [exchange(): return lax.ppermute(array, axis, [(i, i ^ distance) for i in range(count)])]
  transfers between devices with their start and end apart: 12 -> 12, of which waited for: 3 -> 2; matrix products, arithmetic and copies ran while one was open for 4% -> 3% of each run, Pallas kernels for 14% -> 13%
where the time goes in v13:
time: 27.6 us; the launch traced here: 27.4 us
  starting transfers between devices  10.4 us (38%)
  Pallas kernels  10 us (36%)
  waiting for transfers between devices  5.95 us (22%)
  local copies, waits for them, and re-layouts  0.91 us (3%)
    ppermute x12, starting transfers between devices, exchange(): return lax.ppermute(array, axis, [(i, i ^ distance) for i in range(count)])  10.4 us
    ppermute x12, waiting for transfers between devices, exchange(): return lax.ppermute(array, axis, [(i, i ^ distance) for i in range(count)])  5.95 us
    pallas_call x1, Pallas kernels, column_filtered(): pl.pallas_call(functools.partial(column_kernel, slots, slices_owned), out...  4.93 us
    pallas_call x2, Pallas kernels, interpolation(): pl.pallas_call(functools.partial(kernel, slots, len(patches[0])), in_spec...  2.55 us
    pallas_call x1, Pallas kernels, prepared(): pl.pallas_call(functools.partial(prepare_kernel, slots, slices_owned), ou...  2.54 us
    unnamed x7, local copies, waits for them, and re-layouts  0.9 us
  transfers between devices with their start and end apart: 12, of which 2 were waited for; matrix products, arithmetic and copies ran while one was open for 3% of the time, Pallas kernels for 13%

profile of v13, /device:TPU:0, one launch (start us, length us, event | category | flops | bytes accessed | tf_op | source)
XLA Modules:
  0.0 27.4 jit_solution(6884959300283323591)
XLA Ops:
  0.0 4.9 %column_filter.1 = (bf16[144,256]{1,0:T(8,128)(2,1)}, bf16[144,256]{1,0:T(8,128)(2,1)}, bf16[144,256]{1,0:T(8,128)(2,1)}, bf16[144,256]{1,0:T(8,128)(2,1)}) custom-call(bf16[64,2048]{1,0:T(8,128)(2,1)} %bitcast.1, bf16[5,256,512]{2,1,0:T(8,128)(2,1)} %constant.4.clone.matrix_ref, f32[4]{0:T(128)} %angles.1, s32[4,4]{1,0:T(4,128)} %defocus.1, ...), custom_call_target="tpu_custom_call" | custom-call | flops 822083584 | bytes 3145728 | tf_op jit(solution)/shard_map/column_filter/pallas_call | solution.py:230
  4.9 3.1 %collective-permute-start = (bf16[144,256]{1,0:T(8,128)(2,1)}, bf16[144,256]{1,0:T(8,128)(2,1)S(1)}, u32[]{:S(2)}, u32[]{:S(2)}) collective-permute-start(bf16[144,256]{1,0:T(8,128)(2,1)} %get-tuple-element.12), channel_id=1, source_target_pairs={{0,1},{1,0},{2,3},{3,2},{4,5},{5,4},{6,7},{7,6},{8,9},{9,8},{10,11... | collective-permute-start | bytes 221192 | tf_op jit(solution)/shard_map/ppermute | solution.py:441
  8.0 2.5 %collective-permute-start.4 = (bf16[144,256]{1,0:T(8,128)(2,1)}, bf16[144,256]{1,0:T(8,128)(2,1)S(1)}, u32[]{:S(2)}, u32[]{:S(2)}) collective-permute-start(bf16[144,256]{1,0:T(8,128)(2,1)} %get-tuple-element.13), channel_id=1, source_target_pairs={{0,3},{1,2},{2,1},{3,0},{4,7},{5,6},{6,5},{7,4},{8,11},{9,10},{10,... | collective-permute-start | bytes 221192 | tf_op jit(solution)/shard_map/ppermute | solution.py:441
  10.5 0.1 collective-permute-start.8
  10.6 0.9 %constant_dynamic-update-slice_fusion.1 = bf16[288,256]{1,0:T(8,128)(2,1)S(1)} fusion(bf16[144,256]{1,0:T(8,128)(2,1)} %get-tuple-element.11), kind=kLoop, calls=%fused_computation.1 | loop fusion | bytes 147456
  11.5 0.0 collective-permute-done
  11.5 1.6 %collective-permute-start.2 = (bf16[288,256]{1,0:T(8,128)(2,1)S(1)}, bf16[288,256]{1,0:T(8,128)(2,1)S(1)}, u32[]{:S(2)}, u32[]{:S(2)}) collective-permute-start(bf16[288,256]{1,0:T(8,128)(2,1)S(1)} %constant_dynamic-update-slice_fusion.refs_0_), channel_id=1, source_target_pairs={{0,8},{4,12},{8,0},{12,4},{1,9},{5,13},{9,1},{13,5},{2,10},{6,14},... | collective-permute-start | bytes 442376 | tf_op jit(solution)/shard_map/ppermute | solution.py:441
  13.1 0.0 collective-permute-start.1
  13.1 2.3 %collective-permute-done.4.awaited.refs_0_ = bf16[144,256]{1,0:T(8,128)(2,1)S(1)} collective-permute-done((bf16[144,256]{1,0:T(8,128)(2,1)}, bf16[144,256]{1,0:T(8,128)(2,1)S(1)}, u32[]{:S(2)}, u32[]{:S(2)}) %collective-permute-start.4) | collective-permute-done | bytes 73760 | tf_op jit(solution)/shard_map/ppermute | solution.py:441
  15.5 1.5 %collective-permute-start.6 = (bf16[144,256]{1,0:T(8,128)(2,1)S(1)}, bf16[144,256]{1,0:T(8,128)(2,1)S(1)}, u32[]{:S(2)}, u32[]{:S(2)}) collective-permute-start(bf16[144,256]{1,0:T(8,128)(2,1)S(1)} %collective-permute-done.4.awaited.refs_0_), channel_id=1, source_target_pairs={{0,8},{4,12},{8,0},{12,4},{1,9},{5,13},{9,1},{13,5},{2,10},{6,14},... | collective-permute-start | bytes 221192 | tf_op jit(solution)/shard_map/ppermute | solution.py:441
  17.0 2.5 %prepare.1 = (bf16[256,256]{1,0:T(8,128)(2,1)S(1)}, bf16[4,192,2048]{2,1,0:T(8,128)(2,1)S(1)}) custom-call(f32[4]{0:T(128)S(1)} %copy-done.1, s32[4,4]{1,0:T(4,128)S(1)} %copy-done, bf16[2,256,256]{2,1,0:T(8,128)(2,1)S(1)} %copy-done.2, bf16[144,256]{1,0:T(8,128)(2,1)S(1)} %collective-permute-done.4.awaited.refs_0_), custom_call_target="tpu_custom_call" | custom-call | flops 2147483648 | bytes 6291456 | tf_op jit(solution)/shard_map/prepare/pallas_call | solution.py:316
  19.5 0.0 collective-permute-done.2.refs_2_
  19.5 0.1 collective-permute-start.3
  19.6 0.6 %collective-permute-start.10 = (bf16[144,256]{1,0:T(8,128)(2,1)S(1)}, bf16[144,256]{1,0:T(8,128)(2,1)S(1)}, u32[]{:S(2)}, u32[]{:S(2)}) collective-permute-start(bf16[144,256]{1,0:T(8,128)(2,1)S(1)} %after.1.refs_4_), channel_id=1, source_target_pairs={{0,8},{4,12},{8,0},{12,4},{1,9},{5,13},{9,1},{13,5},{2,10},{6,14},... | collective-permute-start | bytes 221192 | tf_op jit(solution)/shard_map/ppermute | solution.py:441
  20.2 0.1 collective-permute-start.9
  20.3 0.0 collective-permute-done.6.refs_2_
  20.4 0.4 %collective-permute-start.5 = (bf16[144,256]{1,0:T(8,128)(2,1)S(1)}, bf16[144,256]{1,0:T(8,128)(2,1)S(1)}, u32[]{:S(2)}, u32[]{:S(2)}) collective-permute-start(bf16[144,256]{1,0:T(8,128)(2,1)S(1)} %collective-permute-done.4.awaited.refs_0_), channel_id=1, source_target_pairs={{0,4},{4,0},{8,12},{12,8},{1,5},{5,1},{9,13},{13,9},{2,6},{6,2},{1... | collective-permute-start | bytes 221192 | tf_op jit(solution)/shard_map/ppermute | solution.py:441
  20.7 3.6 %collective-permute-done.10.refs_6_ = bf16[144,256]{1,0:T(8,128)(2,1)S(1)} collective-permute-done((bf16[144,256]{1,0:T(8,128)(2,1)S(1)}, bf16[144,256]{1,0:T(8,128)(2,1)S(1)}, u32[]{:S(2)}, u32[]{:S(2)}) %collective-permute-start.10) | collective-permute-done | bytes 73760 | tf_op jit(solution)/shard_map/ppermute | solution.py:441
  24.3 0.0 collective-permute-done.1.refs_1_
  24.3 0.5 %collective-permute-start.11 = (bf16[144,256]{1,0:T(8,128)(2,1)S(1)}, bf16[144,256]{1,0:T(8,128)(2,1)S(1)}, u32[]{:S(2)}, u32[]{:S(2)}) collective-permute-start(bf16[144,256]{1,0:T(8,128)(2,1)S(1)} %collective-permute-done.10.refs_6_), channel_id=1, source_target_pairs={{0,4},{4,0},{8,12},{12,8},{1,5},{5,1},{9,13},{13,9},{2,6},{6,2},{1... | collective-permute-start | bytes 221192 | tf_op jit(solution)/shard_map/ppermute | solution.py:441
  24.8 0.0 collective-permute-done.3.refs_3_
  24.8 0.9 %sum_early_tilts.1.total_ref = f32[256,2048]{1,0:T(8,128)S(1)} custom-call(bf16[288,256]{1,0:T(8,128)(2,1)S(1)} %constant_dynamic-update-slice_fusion.refs_0_, bf16[288,256]{1,0:T(8,128)(2,1)S(1)} %collective-permute-done.1.refs_1_, bf16[288,256]{1,0:T(8,128)(2,1)S(1)} %collective-permute-done.2.refs_2_, ...), custom_call_target="tpu_custom_call" | custom-call | tf_op jit(solution)/shard_map/sum_early_tilts/pallas_call | solution.py:400
  25.7 0.0 collective-permute-done.5.refs_1_
  25.8 1.7 %finish_volume.1 = bf16[16,64,512]{2,1,0:T(8,128)(2,1)} custom-call(f32[256,2048]{1,0:T(8,128)S(1)} %sum_early_tilts.1.total_ref, bf16[144,256]{1,0:T(8,128)(2,1)S(1)} %collective-permute-done.4.awaited.refs_0_, bf16[144,256]{1,0:T(8,128)(2,1)S(1)} %collective-permute-done.5.refs_1_, bf16[144,256]{1,0:T(8,128)(2,1)S(1)} %collective-permute-done.6.refs_2_, ...), custom_call_target="tpu_custom_call" | custom-call | tf_op jit(solution)/shard_map/finish_volume/pallas_call | solution.py:400
  (13 shorter events, 0.0 us)
Async XLA Ops:
  0.0 17.0 %copy-start.2 = (bf16[2,256,256]{2,1,0:T(8,128)(2,1)S(1)}, bf16[2,256,256]{2,1,0:T(8,128)(2,1)}, u32[]{:S(2)}) copy-start(bf16[2,256,256]{2,1,0:T(8,128)(2,1)} %constant.5.clone.waves) | copy-start | bytes 786436
  0.0 17.0 %copy-start = (s32[4,4]{1,0:T(4,128)S(1)}, s32[4,4]{1,0:T(4,128)}, u32[]{:S(2)}) copy-start(s32[4,4]{1,0:T(4,128)} %defocus.1) | copy-start | bytes 196
  0.0 17.0 %copy-start.1 = (f32[4]{0:T(128)S(1)}, f32[4]{0:T(128)}, u32[]{:S(2)}) copy-start(f32[4]{0:T(128)} %angles.1) | copy-start | bytes 52
  4.9 6.6 %collective-permute-start = (bf16[144,256]{1,0:T(8,128)(2,1)}, bf16[144,256]{1,0:T(8,128)(2,1)S(1)}, u32[]{:S(2)}, u32[]{:S(2)}) collective-permute-start(bf16[144,256]{1,0:T(8,128)(2,1)} %get-tuple-element.12), channel_id=1, source_target_pairs={{0,1},{1,0},{2,3},{3,2},{4,5},{5,4},{6,7},{7,6},{8,9},{9,8},{10,11... | collective-permute-start | bytes 221192 | tf_op jit(solution)/shard_map/ppermute | solution.py:441
  8.0 7.4 %collective-permute-start.4 = (bf16[144,256]{1,0:T(8,128)(2,1)}, bf16[144,256]{1,0:T(8,128)(2,1)S(1)}, u32[]{:S(2)}, u32[]{:S(2)}) collective-permute-start(bf16[144,256]{1,0:T(8,128)(2,1)} %get-tuple-element.13), channel_id=1, source_target_pairs={{0,3},{1,2},{2,1},{3,0},{4,7},{5,6},{6,5},{7,4},{8,11},{9,10},{10,... | collective-permute-start | bytes 221192 | tf_op jit(solution)/shard_map/ppermute | solution.py:441
  10.5 9.1 %collective-permute-start.8 = (bf16[144,256]{1,0:T(8,128)(2,1)}, bf16[144,256]{1,0:T(8,128)(2,1)S(1)}, u32[]{:S(2)}, u32[]{:S(2)}) collective-permute-start(bf16[144,256]{1,0:T(8,128)(2,1)} %get-tuple-element.16), channel_id=1, source_target_pairs={{0,2},{1,3},{2,0},{3,1},{4,6},{5,7},{6,4},{7,5},{8,10},{9,11},{10,... | collective-permute-start | bytes 221192 | tf_op jit(solution)/shard_map/ppermute | solution.py:441
  11.5 8.0 %collective-permute-start.2 = (bf16[288,256]{1,0:T(8,128)(2,1)S(1)}, bf16[288,256]{1,0:T(8,128)(2,1)S(1)}, u32[]{:S(2)}, u32[]{:S(2)}) collective-permute-start(bf16[288,256]{1,0:T(8,128)(2,1)S(1)} %constant_dynamic-update-slice_fusion.refs_0_), channel_id=1, source_target_pairs={{0,8},{4,12},{8,0},{12,4},{1,9},{5,13},{9,1},{13,5},{2,10},{6,14},... | collective-permute-start | bytes 442376 | tf_op jit(solution)/shard_map/ppermute | solution.py:441
  13.1 11.2 %collective-permute-start.1 = (bf16[288,256]{1,0:T(8,128)(2,1)S(1)}, bf16[288,256]{1,0:T(8,128)(2,1)S(1)}, u32[]{:S(2)}, u32[]{:S(2)}) collective-permute-start(bf16[288,256]{1,0:T(8,128)(2,1)S(1)} %constant_dynamic-update-slice_fusion.refs_0_), channel_id=1, source_target_pairs={{0,4},{4,0},{8,12},{12,8},{1,5},{5,1},{9,13},{13,9},{2,6},{6,2},{1... | collective-permute-start | bytes 442376 | tf_op jit(solution)/shard_map/ppermute | solution.py:441
  15.5 4.9 %collective-permute-start.6 = (bf16[144,256]{1,0:T(8,128)(2,1)S(1)}, bf16[144,256]{1,0:T(8,128)(2,1)S(1)}, u32[]{:S(2)}, u32[]{:S(2)}) collective-permute-start(bf16[144,256]{1,0:T(8,128)(2,1)S(1)} %collective-permute-done.4.awaited.refs_0_), channel_id=1, source_target_pairs={{0,8},{4,12},{8,0},{12,4},{1,9},{5,13},{9,1},{13,5},{2,10},{6,14},... | collective-permute-start | bytes 221192 | tf_op jit(solution)/shard_map/ppermute | solution.py:441
  19.5 5.3 %collective-permute-start.3 = (bf16[288,256]{1,0:T(8,128)(2,1)S(1)}, bf16[288,256]{1,0:T(8,128)(2,1)S(1)}, u32[]{:S(2)}, u32[]{:S(2)}) collective-permute-start(bf16[288,256]{1,0:T(8,128)(2,1)S(1)} %collective-permute-done.2.refs_2_), channel_id=1, source_target_pairs={{0,4},{4,0},{8,12},{12,8},{1,5},{5,1},{9,13},{13,9},{2,6},{6,2},{1... | collective-permute-start | bytes 442376 | tf_op jit(solution)/shard_map/ppermute | solution.py:441
  19.6 4.7 %collective-permute-start.10 = (bf16[144,256]{1,0:T(8,128)(2,1)S(1)}, bf16[144,256]{1,0:T(8,128)(2,1)S(1)}, u32[]{:S(2)}, u32[]{:S(2)}) collective-permute-start(bf16[144,256]{1,0:T(8,128)(2,1)S(1)} %after.1.refs_4_), channel_id=1, source_target_pairs={{0,8},{4,12},{8,0},{12,4},{1,9},{5,13},{9,1},{13,5},{2,10},{6,14},... | collective-permute-start | bytes 221192 | tf_op jit(solution)/shard_map/ppermute | solution.py:441
  20.2 5.5 %collective-permute-start.9 = (bf16[144,256]{1,0:T(8,128)(2,1)S(1)}, bf16[144,256]{1,0:T(8,128)(2,1)S(1)}, u32[]{:S(2)}, u32[]{:S(2)}) collective-permute-start(bf16[144,256]{1,0:T(8,128)(2,1)S(1)} %after.1.refs_4_), channel_id=1, source_target_pairs={{0,4},{4,0},{8,12},{12,8},{1,5},{5,1},{9,13},{13,9},{2,6},{6,2},{1... | collective-permute-start | bytes 221192 | tf_op jit(solution)/shard_map/ppermute | solution.py:441
  20.4 5.4 %collective-permute-start.5 = (bf16[144,256]{1,0:T(8,128)(2,1)S(1)}, bf16[144,256]{1,0:T(8,128)(2,1)S(1)}, u32[]{:S(2)}, u32[]{:S(2)}) collective-permute-start(bf16[144,256]{1,0:T(8,128)(2,1)S(1)} %collective-permute-done.4.awaited.refs_0_), channel_id=1, source_target_pairs={{0,4},{4,0},{8,12},{12,8},{1,5},{5,1},{9,13},{13,9},{2,6},{6,2},{1... | collective-permute-start | bytes 221192 | tf_op jit(solution)/shard_map/ppermute | solution.py:441
  24.3 1.4 %collective-permute-start.7 = (bf16[144,256]{1,0:T(8,128)(2,1)S(1)}, bf16[144,256]{1,0:T(8,128)(2,1)S(1)}, u32[]{:S(2)}, u32[]{:S(2)}) collective-permute-start(bf16[144,256]{1,0:T(8,128)(2,1)S(1)} %collective-permute-done.6.refs_2_), channel_id=1, source_target_pairs={{0,4},{4,0},{8,12},{12,8},{1,5},{5,1},{9,13},{13,9},{2,6},{6,2},{1... | collective-permute-start | bytes 221192 | tf_op jit(solution)/shard_map/ppermute | solution.py:441
  24.3 1.4 %collective-permute-start.11 = (bf16[144,256]{1,0:T(8,128)(2,1)S(1)}, bf16[144,256]{1,0:T(8,128)(2,1)S(1)}, u32[]{:S(2)}, u32[]{:S(2)}) collective-permute-start(bf16[144,256]{1,0:T(8,128)(2,1)S(1)} %collective-permute-done.10.refs_6_), channel_id=1, source_target_pairs={{0,4},{4,0},{8,12},{12,8},{1,5},{5,1},{9,13},{13,9},{2,6},{6,2},{1... | collective-permute-start | bytes 221192 | tf_op jit(solution)/shard_map/ppermute | solution.py:441

commit v14 on v10

--- a/solution.py
+++ b/solution.py
@@ -117,12 +117,11 @@
     lax.fori_loop(0, rows // 16, step, 0)
 
 
-def inverse_butterflies(ends, waves, turns, turned):
-    rows, columns = turned.shape
-    size = columns // RADIX
-
-    def step(i, carry):
-        here = pl.ds(pl.multiple_of(i * 8, 8), 8)
+def inverse_butterflies(ends, waves, turns, turned, first, rows):
+    columns = turned.shape[1]
+    size = columns // RADIX
+    for top in range(first, first + rows, 8):
+        here = slice(top, top + 8)
         r, s = [], []
         for j in range(3):
             c, d = turns[2 * j], turns[2 * j + 1]
@@ -137,9 +136,6 @@
         out = [even0 + a, odd1 + g, even2 - d, odd3 - h, even0 - a, odd1 - g, even2 + d, odd3 + h]
         for m in range(8):
             turned[here, m * size : (m + 1) * size] = out[m]
-        return carry
-
-    lax.fori_loop(0, rows // 8, step, 0)
 
 
 def send_patches(slots, slices_owned, spectrum, wave_table, end_table, columns, facts, scratch, out_refs):
@@ -147,37 +143,44 @@
     ends, waves, turned, out, out_sems = scratch
     rows, size = spectrum[0].shape
     tilt = lax.axis_index("tilt")
-    slabs = [(tilt ^ slot) * slices_owned // SLAB for slot in slots]
-    gains = [flip_sign(squares, defocus[tilt, slab], columns) * ramp for slab in slabs]
-    filtered = [
-        jnp.concatenate([(spectrum[i] * gain[i : i + 1, :]).astype(jnp.bfloat16) for gain in gains], 0) for i in range(8)
-    ]
-    for i in range(2):
-        ends[i] = jnp.dot(filtered[i], end_table[:, i * size : (i + 1) * size], preferred_element_type=jnp.float32)
-    for i in range(6):
-        waves[i] = jnp.dot(filtered[2 + i], wave_table[...], preferred_element_type=jnp.float32)
-    inverse_butterflies(ends, waves, turns, turned)
     lane = lax.broadcasted_iota(jnp.int32, (rows, MAIN), 1) // REST
     _, _, first_tap = reach_of(angles[tilt])
+    slabs = [(tilt ^ slot) * slices_owned // SLAB for slot in slots]
+
+    def transform(k):
+        slab = slabs[k]
+        mine = slice(k * rows, (k + 1) * rows)
+        gain = flip_sign(squares, defocus[tilt, slab], columns) * ramp
+        filtered = [(spectrum[i] * gain[i : i + 1, :]).astype(jnp.bfloat16) for i in range(8)]
+        for i in range(2):
+            table = end_table[:, i * size : (i + 1) * size]
+            ends[i, mine, :] = jnp.dot(filtered[i], table, preferred_element_type=jnp.float32)
+        both = jnp.dot(jnp.concatenate(filtered[2:], 0), wave_table[...], preferred_element_type=jnp.float32)
+        for i in range(6):
+            waves[i, mine, :] = both[i * rows : (i + 1) * rows]
     sends = []
-    for i, slab in enumerate(slabs):
+    transform(0)
+    for k, slab in enumerate(slabs):
+        if k + 1 < len(slabs):
+            transform(k + 1)
+        inverse_butterflies(ends, waves, turns, turned, k * rows, rows)
         rest = jnp.zeros((rows, MAIN), jnp.float32)
         for block in range(XBLK):
             start = starts[tilt, slab, block] + first_tap
             base = pl.multiple_of(jnp.minimum((start // 128) * 128, columns - WINDOW), 128)
-            window = turned[i * rows : (i + 1) * rows, pl.ds(base, WINDOW)]
+            window = turned[k * rows : (k + 1) * rows, pl.ds(base, WINDOW)]
             shift = base - start
             reach = pltpu.roll(window, jnp.where(shift < 0, shift + WINDOW, shift), 1)[:, : 2 * MAIN]
             there = slice(block // 2 * rows, (block // 2 + 1) * rows), slice(block % 2 * MAIN, (block % 2 + 1) * MAIN)
-            out[i, *there] = reach[:, :MAIN].astype(jnp.bfloat16)
+            out[k, *there] = reach[:, :MAIN].astype(jnp.bfloat16)
             last = reach[:, MAIN:]
             rest = jnp.where(lane == block, pltpu.roll(last, block * REST, 1) if block else last, rest)
         quarters = [rest[q * rows // 4 : (q + 1) * rows // 4] for q in range(4)]
         for tile in range(2):
             right = pltpu.roll(quarters[2 * tile + 1], XBLK * REST, 1)
             both = jnp.where(lane[: rows // 4] < XBLK, quarters[2 * tile], right)
-            out[i, 2 * rows :, tile * MAIN : (tile + 1) * MAIN] = both.astype(jnp.bfloat16)
-        sends.append(pltpu.make_async_copy(out.at[i], out_refs[i], out_sems.at[i]))
+            out[k, 2 * rows :, tile * MAIN : (tile + 1) * MAIN] = both.astype(jnp.bfloat16)
+        sends.append(pltpu.make_async_copy(out.at[k], out_refs[k], out_sems.at[k]))
         sends[-1].start()
     return sends
 
@@ -197,7 +200,7 @@
     turns = [t[j : j + 1, :] for j in range(3) for t in (cosine_turns, sine_turns)]
     copies[0].wait()
     butterflies(image, turns, zhi, zlo)
-    for copy in copies[1:]:
+    for copy in copies[4:8]:
         copy.wait()
 
     def product(first, lines, table, here):
@@ -212,6 +215,8 @@
     for j in range(3):
         real, imag = mixed[2 * j * rows : (2 * j + 1) * rows], mixed[(2 * j + 1) * rows : (2 * j + 2) * rows]
         spectrum += [real[:, :size] + imag[:, size:], imag[:, :size] - real[:, size:]]
+    for copy in copies[1:4] + copies[8:]:
+        copy.wait()
     facts = (squares, ramp, turns, angles, defocus, starts)
     sends = send_patches(
         slots, slices_owned, spectrum, matrix.at[2], matrix.at[4], columns, facts, scratch, out_refs

time: 25.4 us -> 25 us (0.984)
  Pallas kernels: 10 us -> 9.6 us
    pallas_call x1, Pallas kernels: 4.93 us -> 4.53 us  [column_filtered(): pl.pallas_call(functools.partial(column_kernel, slots, slices_owned), out...]
where the time goes in v14:
time: 25 us; the launch traced here: 24.8 us
  starting transfers between devices  10.6 us (42%)
  Pallas kernels  9.6 us (38%)
  waiting for transfers between devices  3.65 us (15%)
  local copies, waits for them, and re-layouts  0.91 us (4%)
    ppermute x12, starting transfers between devices, exchange(): return lax.ppermute(array, axis, [(i, i ^ distance) for i in range(count)])  10.6 us
    pallas_call x1, Pallas kernels, column_filtered(): pl.pallas_call(functools.partial(column_kernel, slots, slices_owned), out...  4.53 us
    ppermute x12, waiting for transfers between devices, exchange(): return lax.ppermute(array, axis, [(i, i ^ distance) for i in range(count)])  3.65 us
    pallas_call x2, Pallas kernels, interpolation(): pl.pallas_call(functools.partial(kernel, slots, len(patches[0])), in_spec...  2.54 us
    pallas_call x1, Pallas kernels, prepared(): pl.pallas_call(functools.partial(prepare_kernel, slots, slices_owned), ou...  2.52 us
    unnamed x7, local copies, waits for them, and re-layouts  0.9 us
  transfers between devices with their start and end apart: 12, of which 3 were waited for; matrix products, arithmetic and copies ran while one was open for 4% of the time, Pallas kernels for 14%

profile of v14, /device:TPU:0, one launch (start us, length us, event | category | flops | bytes accessed | tf_op | source)
XLA Modules:
  0.0 24.8 jit_solution(12650646676547763638)
XLA Ops:
  0.0 4.5 %column_filter.1 = (bf16[144,256]{1,0:T(8,128)(2,1)}, bf16[144,256]{1,0:T(8,128)(2,1)}, bf16[144,256]{1,0:T(8,128)(2,1)}, bf16[144,256]{1,0:T(8,128)(2,1)}) custom-call(bf16[64,2048]{1,0:T(8,128)(2,1)} %bitcast.1, bf16[5,256,512]{2,1,0:T(8,128)(2,1)} %constant.4.clone.matrix_ref, f32[4]{0:T(128)} %angle_ref.1, s32[4,4]{1,0:T(4,128)} %defocus_ref.1, ...), custom_call_target="tpu_custom_call" | custom-call | flops 822083584 | bytes 3145728 | tf_op jit(solution)/shard_map/column_filter/pallas_call | solution.py:235
  4.5 3.1 %collective-permute-start = (bf16[144,256]{1,0:T(8,128)(2,1)}, bf16[144,256]{1,0:T(8,128)(2,1)S(1)}, u32[]{:S(2)}, u32[]{:S(2)}) collective-permute-start(bf16[144,256]{1,0:T(8,128)(2,1)} %get-tuple-element.14), channel_id=1, source_target_pairs={{0,1},{1,0},{2,3},{3,2},{4,5},{5,4},{6,7},{7,6},{8,9},{9,8},{10,11... | collective-permute-start | bytes 221192 | tf_op jit(solution)/shard_map/ppermute | solution.py:447
  7.6 2.5 %collective-permute-start.4 = (bf16[144,256]{1,0:T(8,128)(2,1)}, bf16[144,256]{1,0:T(8,128)(2,1)S(1)}, u32[]{:S(2)}, u32[]{:S(2)}) collective-permute-start(bf16[144,256]{1,0:T(8,128)(2,1)} %get-tuple-element.15), channel_id=1, source_target_pairs={{0,3},{1,2},{2,1},{3,0},{4,7},{5,6},{6,5},{7,4},{8,11},{9,10},{10,... | collective-permute-start | bytes 221192 | tf_op jit(solution)/shard_map/ppermute | solution.py:447
  10.1 0.1 collective-permute-start.8
  10.2 0.9 %constant_dynamic-update-slice_fusion.1 = bf16[288,256]{1,0:T(8,128)(2,1)S(1)} fusion(bf16[144,256]{1,0:T(8,128)(2,1)} %get-tuple-element.13), kind=kLoop, calls=%fused_computation.1 | loop fusion | bytes 147456
  11.1 0.0 collective-permute-done
  11.1 1.6 %collective-permute-start.2 = (bf16[288,256]{1,0:T(8,128)(2,1)S(1)}, bf16[288,256]{1,0:T(8,128)(2,1)S(1)}, u32[]{:S(2)}, u32[]{:S(2)}) collective-permute-start(bf16[288,256]{1,0:T(8,128)(2,1)S(1)} %constant_dynamic-update-slice_fusion.refs_0_), channel_id=1, source_target_pairs={{0,8},{4,12},{8,0},{12,4},{1,9},{5,13},{9,1},{13,5},{2,10},{6,14},... | collective-permute-start | bytes 442376 | tf_op jit(solution)/shard_map/ppermute | solution.py:447
  12.7 0.0 collective-permute-start.1
  12.7 2.5 %prepare.1 = (bf16[256,256]{1,0:T(8,128)(2,1)S(1)}, bf16[4,192,2048]{2,1,0:T(8,128)(2,1)S(1)}) custom-call(f32[4]{0:T(128)S(1)} %copy-done.1, s32[4,4]{1,0:T(4,128)S(1)} %copy-done, bf16[2,256,256]{2,1,0:T(8,128)(2,1)S(1)} %copy-done.2), custom_call_target="tpu_custom_call" | custom-call | flops 2147483648 | bytes 6291456 | tf_op jit(solution)/shard_map/prepare/pallas_call | solution.py:321
  15.3 0.0 collective-permute-done.4.refs_0_
  15.3 1.3 %collective-permute-start.6 = (bf16[144,256]{1,0:T(8,128)(2,1)S(1)}, bf16[144,256]{1,0:T(8,128)(2,1)S(1)}, u32[]{:S(2)}, u32[]{:S(2)}) collective-permute-start(bf16[144,256]{1,0:T(8,128)(2,1)S(1)} %collective-permute-done.4.refs_0_), channel_id=1, source_target_pairs={{0,8},{4,12},{8,0},{12,4},{1,9},{5,13},{9,1},{13,5},{2,10},{6,14},... | collective-permute-start | bytes 221192 | tf_op jit(solution)/shard_map/ppermute | solution.py:447
  16.6 0.0 collective-permute-done.2.refs_2_
  16.6 0.0 collective-permute-start.3
  16.6 0.8 %collective-permute-done.8.refs_0_ = bf16[144,256]{1,0:T(8,128)(2,1)S(1)} collective-permute-done((bf16[144,256]{1,0:T(8,128)(2,1)}, bf16[144,256]{1,0:T(8,128)(2,1)S(1)}, u32[]{:S(2)}, u32[]{:S(2)}) %collective-permute-start.8) | collective-permute-done | bytes 73760 | tf_op jit(solution)/shard_map/ppermute | solution.py:447
  17.4 1.5 %collective-permute-start.10 = (bf16[144,256]{1,0:T(8,128)(2,1)S(1)}, bf16[144,256]{1,0:T(8,128)(2,1)S(1)}, u32[]{:S(2)}, u32[]{:S(2)}) collective-permute-start(bf16[144,256]{1,0:T(8,128)(2,1)S(1)} %after.1.refs_4_), channel_id=1, source_target_pairs={{0,8},{4,12},{8,0},{12,4},{1,9},{5,13},{9,1},{13,5},{2,10},{6,14},... | collective-permute-start | bytes 221192 | tf_op jit(solution)/shard_map/ppermute | solution.py:447
  18.9 0.0 collective-permute-start.9
  18.9 1.3 %collective-permute-done.6.refs_2_ = bf16[144,256]{1,0:T(8,128)(2,1)S(1)} collective-permute-done((bf16[144,256]{1,0:T(8,128)(2,1)S(1)}, bf16[144,256]{1,0:T(8,128)(2,1)S(1)}, u32[]{:S(2)}, u32[]{:S(2)}) %collective-permute-start.6) | collective-permute-done | bytes 73760 | tf_op jit(solution)/shard_map/ppermute | solution.py:447
  20.2 0.0 collective-permute-start.5
  20.2 1.6 %collective-permute-done.10.refs_6_ = bf16[144,256]{1,0:T(8,128)(2,1)S(1)} collective-permute-done((bf16[144,256]{1,0:T(8,128)(2,1)S(1)}, bf16[144,256]{1,0:T(8,128)(2,1)S(1)}, u32[]{:S(2)}, u32[]{:S(2)}) %collective-permute-start.10) | collective-permute-done | bytes 73760 | tf_op jit(solution)/shard_map/ppermute | solution.py:447
  21.7 0.5 %collective-permute-start.11 = (bf16[144,256]{1,0:T(8,128)(2,1)S(1)}, bf16[144,256]{1,0:T(8,128)(2,1)S(1)}, u32[]{:S(2)}, u32[]{:S(2)}) collective-permute-start(bf16[144,256]{1,0:T(8,128)(2,1)S(1)} %collective-permute-done.10.refs_6_), channel_id=1, source_target_pairs={{0,4},{4,0},{8,12},{12,8},{1,5},{5,1},{9,13},{13,9},{2,6},{6,2},{1... | collective-permute-start | bytes 221192 | tf_op jit(solution)/shard_map/ppermute | solution.py:447
  22.2 0.9 %sum_early_tilts.1.total_ref = f32[256,2048]{1,0:T(8,128)S(1)} custom-call(bf16[256,256]{1,0:T(8,128)(2,1)S(1)} %get-tuple-element.11.rows_ref.refs_1_, bf16[4,192,2048]{2,1,0:T(8,128)(2,1)S(1)} %get-tuple-element.12.weights_ref, bf16[288,256]{1,0:T(8,128)(2,1)S(1)} %constant_dynamic-update-slice_fusion.refs_0_, ...), custom_call_target="tpu_custom_call" | custom-call | tf_op jit(solution)/shard_map/sum_early_tilts/pallas_call | solution.py:406
  23.2 0.0 collective-permute-done.9.refs_5_
  23.2 0.0 collective-permute-done.7.refs_3_
  23.2 1.6 %finish_volume.1 = bf16[16,64,512]{2,1,0:T(8,128)(2,1)} custom-call(bf16[256,256]{1,0:T(8,128)(2,1)S(1)} %get-tuple-element.11.rows_ref.refs_1_, bf16[4,192,2048]{2,1,0:T(8,128)(2,1)S(1)} %get-tuple-element.12.weights_ref, f32[256,2048]{1,0:T(8,128)S(1)} %sum_early_tilts.1.total_ref, bf16[144,256]{1,0:T(8,128)(2,1)S(1)} %collective-permute-done.4.refs_0_, ...), custom_call_target="tpu_custom_call" | custom-call | tf_op jit(solution)/shard_map/finish_volume/pallas_call | solution.py:406
  (13 shorter events, 0.0 us)
Async XLA Ops:
  0.0 12.7 %copy-start.2 = (bf16[2,256,256]{2,1,0:T(8,128)(2,1)S(1)}, bf16[2,256,256]{2,1,0:T(8,128)(2,1)}, u32[]{:S(2)}) copy-start(bf16[2,256,256]{2,1,0:T(8,128)(2,1)} %constant.5.clone.waves) | copy-start | bytes 786436
  0.0 12.7 %copy-start = (s32[4,4]{1,0:T(4,128)S(1)}, s32[4,4]{1,0:T(4,128)}, u32[]{:S(2)}) copy-start(s32[4,4]{1,0:T(4,128)} %defocus_ref.1) | copy-start | bytes 196
  0.0 12.7 %copy-start.1 = (f32[4]{0:T(128)S(1)}, f32[4]{0:T(128)}, u32[]{:S(2)}) copy-start(f32[4]{0:T(128)} %angle_ref.1) | copy-start | bytes 52
  4.5 6.6 %collective-permute-start = (bf16[144,256]{1,0:T(8,128)(2,1)}, bf16[144,256]{1,0:T(8,128)(2,1)S(1)}, u32[]{:S(2)}, u32[]{:S(2)}) collective-permute-start(bf16[144,256]{1,0:T(8,128)(2,1)} %get-tuple-element.14), channel_id=1, source_target_pairs={{0,1},{1,0},{2,3},{3,2},{4,5},{5,4},{6,7},{7,6},{8,9},{9,8},{10,11... | collective-permute-start | bytes 221192 | tf_op jit(solution)/shard_map/ppermute | solution.py:447
  7.6 7.6 %collective-permute-start.4 = (bf16[144,256]{1,0:T(8,128)(2,1)}, bf16[144,256]{1,0:T(8,128)(2,1)S(1)}, u32[]{:S(2)}, u32[]{:S(2)}) collective-permute-start(bf16[144,256]{1,0:T(8,128)(2,1)} %get-tuple-element.15), channel_id=1, source_target_pairs={{0,3},{1,2},{2,1},{3,0},{4,7},{5,6},{6,5},{7,4},{8,11},{9,10},{10,... | collective-permute-start | bytes 221192 | tf_op jit(solution)/shard_map/ppermute | solution.py:447
  10.1 7.3 %collective-permute-start.8 = (bf16[144,256]{1,0:T(8,128)(2,1)}, bf16[144,256]{1,0:T(8,128)(2,1)S(1)}, u32[]{:S(2)}, u32[]{:S(2)}) collective-permute-start(bf16[144,256]{1,0:T(8,128)(2,1)} %get-tuple-element.16), channel_id=1, source_target_pairs={{0,2},{1,3},{2,0},{3,1},{4,6},{5,7},{6,4},{7,5},{8,10},{9,11},{10,... | collective-permute-start | bytes 221192 | tf_op jit(solution)/shard_map/ppermute | solution.py:447
  11.1 5.4 %collective-permute-start.2 = (bf16[288,256]{1,0:T(8,128)(2,1)S(1)}, bf16[288,256]{1,0:T(8,128)(2,1)S(1)}, u32[]{:S(2)}, u32[]{:S(2)}) collective-permute-start(bf16[288,256]{1,0:T(8,128)(2,1)S(1)} %constant_dynamic-update-slice_fusion.refs_0_), channel_id=1, source_target_pairs={{0,8},{4,12},{8,0},{12,4},{1,9},{5,13},{9,1},{13,5},{2,10},{6,14},... | collective-permute-start | bytes 442376 | tf_op jit(solution)/shard_map/ppermute | solution.py:447
  12.7 9.0 %collective-permute-start.1 = (bf16[288,256]{1,0:T(8,128)(2,1)S(1)}, bf16[288,256]{1,0:T(8,128)(2,1)S(1)}, u32[]{:S(2)}, u32[]{:S(2)}) collective-permute-start(bf16[288,256]{1,0:T(8,128)(2,1)S(1)} %constant_dynamic-update-slice_fusion.refs_0_), channel_id=1, source_target_pairs={{0,4},{4,0},{8,12},{12,8},{1,5},{5,1},{9,13},{13,9},{2,6},{6,2},{1... | collective-permute-start | bytes 442376 | tf_op jit(solution)/shard_map/ppermute | solution.py:447
  15.3 4.9 %collective-permute-start.6 = (bf16[144,256]{1,0:T(8,128)(2,1)S(1)}, bf16[144,256]{1,0:T(8,128)(2,1)S(1)}, u32[]{:S(2)}, u32[]{:S(2)}) collective-permute-start(bf16[144,256]{1,0:T(8,128)(2,1)S(1)} %collective-permute-done.4.refs_0_), channel_id=1, source_target_pairs={{0,8},{4,12},{8,0},{12,4},{1,9},{5,13},{9,1},{13,5},{2,10},{6,14},... | collective-permute-start | bytes 221192 | tf_op jit(solution)/shard_map/ppermute | solution.py:447
  16.6 5.7 %collective-permute-start.3 = (bf16[288,256]{1,0:T(8,128)(2,1)S(1)}, bf16[288,256]{1,0:T(8,128)(2,1)S(1)}, u32[]{:S(2)}, u32[]{:S(2)}) collective-permute-start(bf16[288,256]{1,0:T(8,128)(2,1)S(1)} %collective-permute-done.2.refs_2_), channel_id=1, source_target_pairs={{0,4},{4,0},{8,12},{12,8},{1,5},{5,1},{9,13},{13,9},{2,6},{6,2},{1... | collective-permute-start | bytes 442376 | tf_op jit(solution)/shard_map/ppermute | solution.py:447
  17.4 4.4 %collective-permute-start.10 = (bf16[144,256]{1,0:T(8,128)(2,1)S(1)}, bf16[144,256]{1,0:T(8,128)(2,1)S(1)}, u32[]{:S(2)}, u32[]{:S(2)}) collective-permute-start(bf16[144,256]{1,0:T(8,128)(2,1)S(1)} %after.1.refs_4_), channel_id=1, source_target_pairs={{0,8},{4,12},{8,0},{12,4},{1,9},{5,13},{9,1},{13,5},{2,10},{6,14},... | collective-permute-start | bytes 221192 | tf_op jit(solution)/shard_map/ppermute | solution.py:447
  18.9 4.3 %collective-permute-start.9 = (bf16[144,256]{1,0:T(8,128)(2,1)S(1)}, bf16[144,256]{1,0:T(8,128)(2,1)S(1)}, u32[]{:S(2)}, u32[]{:S(2)}) collective-permute-start(bf16[144,256]{1,0:T(8,128)(2,1)S(1)} %after.1.refs_4_), channel_id=1, source_target_pairs={{0,4},{4,0},{8,12},{12,8},{1,5},{5,1},{9,13},{13,9},{2,6},{6,2},{1... | collective-permute-start | bytes 221192 | tf_op jit(solution)/shard_map/ppermute | solution.py:447
  20.2 3.0 %collective-permute-start.5 = (bf16[144,256]{1,0:T(8,128)(2,1)S(1)}, bf16[144,256]{1,0:T(8,128)(2,1)S(1)}, u32[]{:S(2)}, u32[]{:S(2)}) collective-permute-start(bf16[144,256]{1,0:T(8,128)(2,1)S(1)} %collective-permute-done.4.refs_0_), channel_id=1, source_target_pairs={{0,4},{4,0},{8,12},{12,8},{1,5},{5,1},{9,13},{13,9},{2,6},{6,2},{1... | collective-permute-start | bytes 221192 | tf_op jit(solution)/shard_map/ppermute | solution.py:447
  21.7 1.4 %collective-permute-start.7 = (bf16[144,256]{1,0:T(8,128)(2,1)S(1)}, bf16[144,256]{1,0:T(8,128)(2,1)S(1)}, u32[]{:S(2)}, u32[]{:S(2)}) collective-permute-start(bf16[144,256]{1,0:T(8,128)(2,1)S(1)} %collective-permute-done.6.refs_2_), channel_id=1, source_target_pairs={{0,4},{4,0},{8,12},{12,8},{1,5},{5,1},{9,13},{13,9},{2,6},{6,2},{1... | collective-permute-start | bytes 221192 | tf_op jit(solution)/shard_map/ppermute | solution.py:447
  21.7 1.4 %collective-permute-start.11 = (bf16[144,256]{1,0:T(8,128)(2,1)S(1)}, bf16[144,256]{1,0:T(8,128)(2,1)S(1)}, u32[]{:S(2)}, u32[]{:S(2)}) collective-permute-start(bf16[144,256]{1,0:T(8,128)(2,1)S(1)} %collective-permute-done.10.refs_6_), channel_id=1, source_target_pairs={{0,4},{4,0},{8,12},{12,8},{1,5},{5,1},{9,13},{13,9},{2,6},{6,2},{1... | collective-permute-start | bytes 221192 | tf_op jit(solution)/shard_map/ppermute | solution.py:447

commit v15 on v14

--- a/solution.py
+++ b/solution.py
@@ -16,7 +16,7 @@
 SLICES = 64
 RADIX = 8
 MAIN = 128
-REST = 16
+REST = 8
 REACH = MAIN + REST
 WINDOW = 384
 ROOT = math.sqrt(0.5)
@@ -70,7 +70,7 @@
 
 
 def packed_shape(rows):
-    return (2 * rows + rows // 4, 2 * MAIN)
+    return (XBLK * rows + rows // 4, MAIN)
 
 
 def flip_sign(squares, defocus, length):
@@ -89,7 +89,7 @@
     line = jnp.full((8, XBW), angle, jnp.float32)
     cosine, sine = jnp.cos(line), jnp.sin(line)
     lowest = 0.5 * XBW + jnp.minimum((XBW - 1) * cosine, 0.0) - 0.5 * (SLAB - 1) * jnp.abs(sine)
-    first = jnp.clip(jnp.floor(lowest) - 4.0, 0.0, float(BAND - REACH))
+    first = jnp.clip(jnp.floor(lowest) - 2.0, 0.0, float(BAND - REACH))
     return cosine[:1], sine[:1], jnp.max(first).astype(jnp.int32)
 
 
@@ -171,15 +171,15 @@
             window = turned[k * rows : (k + 1) * rows, pl.ds(base, WINDOW)]
             shift = base - start
             reach = pltpu.roll(window, jnp.where(shift < 0, shift + WINDOW, shift), 1)[:, : 2 * MAIN]
-            there = slice(block // 2 * rows, (block // 2 + 1) * rows), slice(block % 2 * MAIN, (block % 2 + 1) * MAIN)
-            out[k, *there] = reach[:, :MAIN].astype(jnp.bfloat16)
+            out[k, block * rows : (block + 1) * rows, :] = reach[:, :MAIN].astype(jnp.bfloat16)
             last = reach[:, MAIN:]
             rest = jnp.where(lane == block, pltpu.roll(last, block * REST, 1) if block else last, rest)
-        quarters = [rest[q * rows // 4 : (q + 1) * rows // 4] for q in range(4)]
-        for tile in range(2):
-            right = pltpu.roll(quarters[2 * tile + 1], XBLK * REST, 1)
-            both = jnp.where(lane[: rows // 4] < XBLK, quarters[2 * tile], right)
-            out[k, 2 * rows :, tile * MAIN : (tile + 1) * MAIN] = both.astype(jnp.bfloat16)
+        quarter = rows // 4
+        beside = rest[:quarter]
+        for q in range(1, 4):
+            moved = pltpu.roll(rest[q * quarter : (q + 1) * quarter], q * XBLK * REST, 1)
+            beside = jnp.where(lane[:quarter] // XBLK == q, moved, beside)
+        out[k, XBLK * rows :, :] = beside.astype(jnp.bfloat16)
         sends.append(pltpu.make_async_copy(out.at[k], out_refs[k], out_sems.at[k]))
         sends[-1].start()
     return sends
@@ -307,10 +307,10 @@
             offset = (local_first + c).astype(jnp.float32) - 0.5 * (SLAB - 1)
             centre = 0.5 * XBW + across * cosine + offset * sine
             there = pl.ds(pl.multiple_of(c * XBW, XBW), XBW)
-            weights = jnp.maximum(0.0, 1.0 - jnp.abs(tap - centre)).astype(jnp.bfloat16)
-            weights_ref[slot, :REACH, there] = weights
-            for block in range(1, XBLK):
-                weights_ref[slot, MAIN + block * REST : MAIN + (block + 1) * REST, there] = weights[MAIN:]
+            weights = jnp.maximum(0.0, 1.0 - jnp.abs(tap - centre))
+            weights_ref[slot, :MAIN, there] = weights[:MAIN].astype(jnp.bfloat16)
+            rest = jnp.concatenate([weights[MAIN:]] * XBLK, 0)
+            weights_ref[slot, MAIN:, there] = rest.astype(jnp.bfloat16)
             return carry
 
         lax.fori_loop(0, slices_owned, one_slice, 0, unroll=2)
@@ -337,14 +337,11 @@
 
 
 def unpacked(packed):
-    rows = 4 * packed.shape[0] // 9
-    rest = packed[2 * rows :].astype(jnp.float32)
-    quarters = []
-    for tile in range(2):
-        both = rest[:, tile * MAIN : (tile + 1) * MAIN]
-        quarters += [both, pltpu.roll(both, MAIN - XBLK * REST, 1)]
+    rows = 4 * packed.shape[0] // (4 * XBLK + 1)
+    beside = packed[XBLK * rows :].astype(jnp.float32)
+    quarters = [pltpu.roll(beside, MAIN - q * XBLK * REST, 1) if q else beside for q in range(4)]
     rest = jnp.concatenate(quarters, 0).astype(jnp.bfloat16)
-    return jnp.concatenate([packed[:rows], packed[rows : 2 * rows], rest], 1)
+    return jnp.concatenate([packed[block * rows : (block + 1) * rows] for block in range(XBLK)] + [rest], 1)
 
 
 def corrected_patches(slots, row_devices, rows_ref, patch_refs):

time: 25 us -> 24.7 us (0.988)
    pallas_call x1, Pallas kernels: 2.52 us -> 2.25 us  [prepared(): pl.pallas_call(functools.partial(prepare_kernel, slots, slices_owned), ou...]
  transfers between devices with their start and end apart: 12 -> 12, of which waited for: 3 -> 3; matrix products, arithmetic and copies ran while one was open for 4% -> 4% of each run, Pallas kernels for 14% -> 13%
where the time goes in v15:
time: 24.7 us; the launch traced here: 24.5 us
  starting transfers between devices  10.7 us (43%)
  Pallas kernels  9.36 us (38%)
  waiting for transfers between devices  3.47 us (14%)
  local copies, waits for them, and re-layouts  0.91 us (4%)
    ppermute x12, starting transfers between devices, exchange(): return lax.ppermute(array, axis, [(i, i ^ distance) for i in range(count)])  10.7 us
    pallas_call x1, Pallas kernels, column_filtered(): pl.pallas_call(functools.partial(column_kernel, slots, slices_owned), out...  4.54 us
    ppermute x12, waiting for transfers between devices, exchange(): return lax.ppermute(array, axis, [(i, i ^ distance) for i in range(count)])  3.47 us
    pallas_call x2, Pallas kernels, interpolation(): pl.pallas_call(functools.partial(kernel, slots, len(patches[0])), in_spec...  2.57 us
    pallas_call x1, Pallas kernels, prepared(): pl.pallas_call(functools.partial(prepare_kernel, slots, slices_owned), ou...  2.25 us
    unnamed x7, local copies, waits for them, and re-layouts  0.9 us
  transfers between devices with their start and end apart: 12, of which 3 were waited for; matrix products, arithmetic and copies ran while one was open for 4% of the time, Pallas kernels for 13%

profile of v15, /device:TPU:0, one launch (start us, length us, event | category | flops | bytes accessed | tf_op | source)
XLA Modules:
  0.0 24.5 jit_solution(7090877225923544875)
XLA Ops:
  0.0 4.5 %column_filter.1 = (bf16[272,128]{1,0:T(8,128)(2,1)}, bf16[272,128]{1,0:T(8,128)(2,1)}, bf16[272,128]{1,0:T(8,128)(2,1)}, bf16[272,128]{1,0:T(8,128)(2,1)}) custom-call(bf16[64,2048]{1,0:T(8,128)(2,1)} %bitcast.1, bf16[5,256,512]{2,1,0:T(8,128)(2,1)} %constant.4.clone.matrix_ref, f32[4]{0:T(128)} %angle_ref.1, s32[4,4]{1,0:T(4,128)} %defocus_ref.1, ...), custom_call_target="tpu_custom_call" | custom-call | flops 822083584 | bytes 3145728 | tf_op jit(solution)/shard_map/column_filter/pallas_call | solution.py:235
  4.6 3.1 %collective-permute-start = (bf16[272,128]{1,0:T(8,128)(2,1)}, bf16[272,128]{1,0:T(8,128)(2,1)S(1)}, u32[]{:S(2)}, u32[]{:S(2)}) collective-permute-start(bf16[272,128]{1,0:T(8,128)(2,1)} %get-tuple-element.14), channel_id=1, source_target_pairs={{0,1},{1,0},{2,3},{3,2},{4,5},{5,4},{6,7},{7,6},{8,9},{9,8},{10,11... | collective-permute-start | bytes 208904 | tf_op jit(solution)/shard_map/ppermute | solution.py:444
  7.6 2.5 %collective-permute-start.4 = (bf16[272,128]{1,0:T(8,128)(2,1)}, bf16[272,128]{1,0:T(8,128)(2,1)S(1)}, u32[]{:S(2)}, u32[]{:S(2)}) collective-permute-start(bf16[272,128]{1,0:T(8,128)(2,1)} %get-tuple-element.15), channel_id=1, source_target_pairs={{0,3},{1,2},{2,1},{3,0},{4,7},{5,6},{6,5},{7,4},{8,11},{9,10},{10,... | collective-permute-start | bytes 208904 | tf_op jit(solution)/shard_map/ppermute | solution.py:444
  10.1 0.1 collective-permute-start.8
  10.2 0.9 %constant_dynamic-update-slice_fusion.1 = bf16[544,128]{1,0:T(8,128)(2,1)S(1)} fusion(bf16[272,128]{1,0:T(8,128)(2,1)} %get-tuple-element.13), kind=kLoop, calls=%fused_computation.1 | loop fusion | bytes 139264
  11.1 0.0 collective-permute-done
  11.1 1.6 %collective-permute-start.2 = (bf16[544,128]{1,0:T(8,128)(2,1)S(1)}, bf16[544,128]{1,0:T(8,128)(2,1)S(1)}, u32[]{:S(2)}, u32[]{:S(2)}) collective-permute-start(bf16[544,128]{1,0:T(8,128)(2,1)S(1)} %constant_dynamic-update-slice_fusion.refs_0_), channel_id=1, source_target_pairs={{0,8},{4,12},{8,0},{12,4},{1,9},{5,13},{9,1},{13,5},{2,10},{6,14},... | collective-permute-start | bytes 417800 | tf_op jit(solution)/shard_map/ppermute | solution.py:444
  12.7 0.0 collective-permute-start.1
  12.7 2.2 %prepare.1 = (bf16[256,256]{1,0:T(8,128)(2,1)S(1)}, bf16[4,160,2048]{2,1,0:T(8,128)(2,1)S(1)}) custom-call(f32[4]{0:T(128)S(1)} %copy-done.1, s32[4,4]{1,0:T(4,128)S(1)} %copy-done, bf16[2,256,256]{2,1,0:T(8,128)(2,1)S(1)} %copy-done.2), custom_call_target="tpu_custom_call" | custom-call | flops 2147483648 | bytes 6291456 | tf_op jit(solution)/shard_map/prepare/pallas_call | solution.py:321
  15.0 0.0 collective-permute-done.4.refs_0_
  15.0 1.4 %collective-permute-start.6 = (bf16[272,128]{1,0:T(8,128)(2,1)S(1)}, bf16[272,128]{1,0:T(8,128)(2,1)S(1)}, u32[]{:S(2)}, u32[]{:S(2)}) collective-permute-start(bf16[272,128]{1,0:T(8,128)(2,1)S(1)} %collective-permute-done.4.refs_0_), channel_id=1, source_target_pairs={{0,8},{4,12},{8,0},{12,4},{1,9},{5,13},{9,1},{13,5},{2,10},{6,14},... | collective-permute-start | bytes 208904 | tf_op jit(solution)/shard_map/ppermute | solution.py:444
  16.4 0.7 %collective-permute-done.8.refs_0_ = bf16[272,128]{1,0:T(8,128)(2,1)S(1)} collective-permute-done((bf16[272,128]{1,0:T(8,128)(2,1)}, bf16[272,128]{1,0:T(8,128)(2,1)S(1)}, u32[]{:S(2)}, u32[]{:S(2)}) %collective-permute-start.8) | collective-permute-done | bytes 69664 | tf_op jit(solution)/shard_map/ppermute | solution.py:444
  17.1 1.5 %collective-permute-start.10 = (bf16[272,128]{1,0:T(8,128)(2,1)S(1)}, bf16[272,128]{1,0:T(8,128)(2,1)S(1)}, u32[]{:S(2)}, u32[]{:S(2)}) collective-permute-start(bf16[272,128]{1,0:T(8,128)(2,1)S(1)} %after.1.refs_4_), channel_id=1, source_target_pairs={{0,8},{4,12},{8,0},{12,4},{1,9},{5,13},{9,1},{13,5},{2,10},{6,14},... | collective-permute-start | bytes 208904 | tf_op jit(solution)/shard_map/ppermute | solution.py:444
  18.6 0.0 collective-permute-start.9
  18.6 1.1 %collective-permute-done.6.refs_2_ = bf16[272,128]{1,0:T(8,128)(2,1)S(1)} collective-permute-done((bf16[272,128]{1,0:T(8,128)(2,1)S(1)}, bf16[272,128]{1,0:T(8,128)(2,1)S(1)}, u32[]{:S(2)}, u32[]{:S(2)}) %collective-permute-start.6) | collective-permute-done | bytes 69664 | tf_op jit(solution)/shard_map/ppermute | solution.py:444
  19.7 1.7 %collective-permute-done.10.refs_6_ = bf16[272,128]{1,0:T(8,128)(2,1)S(1)} collective-permute-done((bf16[272,128]{1,0:T(8,128)(2,1)S(1)}, bf16[272,128]{1,0:T(8,128)(2,1)S(1)}, u32[]{:S(2)}, u32[]{:S(2)}) %collective-permute-start.10) | collective-permute-done | bytes 69664 | tf_op jit(solution)/shard_map/ppermute | solution.py:444
  21.4 0.0 collective-permute-start.7
  21.4 0.0 collective-permute-done.1.refs_1_
  21.4 0.5 %collective-permute-start.11 = (bf16[272,128]{1,0:T(8,128)(2,1)S(1)}, bf16[272,128]{1,0:T(8,128)(2,1)S(1)}, u32[]{:S(2)}, u32[]{:S(2)}) collective-permute-start(bf16[272,128]{1,0:T(8,128)(2,1)S(1)} %collective-permute-done.10.refs_6_), channel_id=1, source_target_pairs={{0,4},{4,0},{8,12},{12,8},{1,5},{5,1},{9,13},{13,9},{2,6},{6,2},{1... | collective-permute-start | bytes 208904 | tf_op jit(solution)/shard_map/ppermute | solution.py:444
  21.9 0.0 collective-permute-done.3.refs_3_
  21.9 0.9 %sum_early_tilts.1.total_ref = f32[256,2048]{1,0:T(8,128)S(1)} custom-call(bf16[256,256]{1,0:T(8,128)(2,1)S(1)} %get-tuple-element.11.rows_ref.refs_1_, bf16[4,160,2048]{2,1,0:T(8,128)(2,1)S(1)} %get-tuple-element.12.weights_ref, bf16[544,128]{1,0:T(8,128)(2,1)S(1)} %constant_dynamic-update-slice_fusion.refs_0_, ...), custom_call_target="tpu_custom_call" | custom-call | tf_op jit(solution)/shard_map/sum_early_tilts/pallas_call | solution.py:403
  22.8 0.0 collective-permute-done.5.refs_1_
  22.8 0.0 collective-permute-done.7.refs_3_
  22.9 1.7 %finish_volume.1 = bf16[16,64,512]{2,1,0:T(8,128)(2,1)} custom-call(bf16[256,256]{1,0:T(8,128)(2,1)S(1)} %get-tuple-element.11.rows_ref.refs_1_, bf16[4,160,2048]{2,1,0:T(8,128)(2,1)S(1)} %get-tuple-element.12.weights_ref, f32[256,2048]{1,0:T(8,128)S(1)} %sum_early_tilts.1.total_ref, bf16[272,128]{1,0:T(8,128)(2,1)S(1)} %collective-permute-done.4.refs_0_, ...), custom_call_target="tpu_custom_call" | custom-call | tf_op jit(solution)/shard_map/finish_volume/pallas_call | solution.py:403
  (13 shorter events, 0.0 us)
Async XLA Ops:
  0.0 12.7 %copy-start.2 = (bf16[2,256,256]{2,1,0:T(8,128)(2,1)S(1)}, bf16[2,256,256]{2,1,0:T(8,128)(2,1)}, u32[]{:S(2)}) copy-start(bf16[2,256,256]{2,1,0:T(8,128)(2,1)} %constant.5.clone.waves) | copy-start | bytes 786436
  0.0 12.7 %copy-start = (s32[4,4]{1,0:T(4,128)S(1)}, s32[4,4]{1,0:T(4,128)}, u32[]{:S(2)}) copy-start(s32[4,4]{1,0:T(4,128)} %defocus_ref.1) | copy-start | bytes 196
  0.0 12.7 %copy-start.1 = (f32[4]{0:T(128)S(1)}, f32[4]{0:T(128)}, u32[]{:S(2)}) copy-start(f32[4]{0:T(128)} %angle_ref.1) | copy-start | bytes 52
  4.6 6.6 %collective-permute-start = (bf16[272,128]{1,0:T(8,128)(2,1)}, bf16[272,128]{1,0:T(8,128)(2,1)S(1)}, u32[]{:S(2)}, u32[]{:S(2)}) collective-permute-start(bf16[272,128]{1,0:T(8,128)(2,1)} %get-tuple-element.14), channel_id=1, source_target_pairs={{0,1},{1,0},{2,3},{3,2},{4,5},{5,4},{6,7},{7,6},{8,9},{9,8},{10,11... | collective-permute-start | bytes 208904 | tf_op jit(solution)/shard_map/ppermute | solution.py:444
  7.6 7.4 %collective-permute-start.4 = (bf16[272,128]{1,0:T(8,128)(2,1)}, bf16[272,128]{1,0:T(8,128)(2,1)S(1)}, u32[]{:S(2)}, u32[]{:S(2)}) collective-permute-start(bf16[272,128]{1,0:T(8,128)(2,1)} %get-tuple-element.15), channel_id=1, source_target_pairs={{0,3},{1,2},{2,1},{3,0},{4,7},{5,6},{6,5},{7,4},{8,11},{9,10},{10,... | collective-permute-start | bytes 208904 | tf_op jit(solution)/shard_map/ppermute | solution.py:444
  10.1 7.0 %collective-permute-start.8 = (bf16[272,128]{1,0:T(8,128)(2,1)}, bf16[272,128]{1,0:T(8,128)(2,1)S(1)}, u32[]{:S(2)}, u32[]{:S(2)}) collective-permute-start(bf16[272,128]{1,0:T(8,128)(2,1)} %get-tuple-element.16), channel_id=1, source_target_pairs={{0,2},{1,3},{2,0},{3,1},{4,6},{5,7},{6,4},{7,5},{8,10},{9,11},{10,... | collective-permute-start | bytes 208904 | tf_op jit(solution)/shard_map/ppermute | solution.py:444
  11.1 5.3 %collective-permute-start.2 = (bf16[544,128]{1,0:T(8,128)(2,1)S(1)}, bf16[544,128]{1,0:T(8,128)(2,1)S(1)}, u32[]{:S(2)}, u32[]{:S(2)}) collective-permute-start(bf16[544,128]{1,0:T(8,128)(2,1)S(1)} %constant_dynamic-update-slice_fusion.refs_0_), channel_id=1, source_target_pairs={{0,8},{4,12},{8,0},{12,4},{1,9},{5,13},{9,1},{13,5},{2,10},{6,14},... | collective-permute-start | bytes 417800 | tf_op jit(solution)/shard_map/ppermute | solution.py:444
  12.7 8.7 %collective-permute-start.1 = (bf16[544,128]{1,0:T(8,128)(2,1)S(1)}, bf16[544,128]{1,0:T(8,128)(2,1)S(1)}, u32[]{:S(2)}, u32[]{:S(2)}) collective-permute-start(bf16[544,128]{1,0:T(8,128)(2,1)S(1)} %constant_dynamic-update-slice_fusion.refs_0_), channel_id=1, source_target_pairs={{0,4},{4,0},{8,12},{12,8},{1,5},{5,1},{9,13},{13,9},{2,6},{6,2},{1... | collective-permute-start | bytes 417800 | tf_op jit(solution)/shard_map/ppermute | solution.py:444
  15.0 4.7 %collective-permute-start.6 = (bf16[272,128]{1,0:T(8,128)(2,1)S(1)}, bf16[272,128]{1,0:T(8,128)(2,1)S(1)}, u32[]{:S(2)}, u32[]{:S(2)}) collective-permute-start(bf16[272,128]{1,0:T(8,128)(2,1)S(1)} %collective-permute-done.4.refs_0_), channel_id=1, source_target_pairs={{0,8},{4,12},{8,0},{12,4},{1,9},{5,13},{9,1},{13,5},{2,10},{6,14},... | collective-permute-start | bytes 208904 | tf_op jit(solution)/shard_map/ppermute | solution.py:444
  16.4 5.5 %collective-permute-start.3 = (bf16[544,128]{1,0:T(8,128)(2,1)S(1)}, bf16[544,128]{1,0:T(8,128)(2,1)S(1)}, u32[]{:S(2)}, u32[]{:S(2)}) collective-permute-start(bf16[544,128]{1,0:T(8,128)(2,1)S(1)} %collective-permute-done.2.refs_2_), channel_id=1, source_target_pairs={{0,4},{4,0},{8,12},{12,8},{1,5},{5,1},{9,13},{13,9},{2,6},{6,2},{1... | collective-permute-start | bytes 417800 | tf_op jit(solution)/shard_map/ppermute | solution.py:444
  17.1 4.3 %collective-permute-start.10 = (bf16[272,128]{1,0:T(8,128)(2,1)S(1)}, bf16[272,128]{1,0:T(8,128)(2,1)S(1)}, u32[]{:S(2)}, u32[]{:S(2)}) collective-permute-start(bf16[272,128]{1,0:T(8,128)(2,1)S(1)} %after.1.refs_4_), channel_id=1, source_target_pairs={{0,8},{4,12},{8,0},{12,4},{1,9},{5,13},{9,1},{13,5},{2,10},{6,14},... | collective-permute-start | bytes 208904 | tf_op jit(solution)/shard_map/ppermute | solution.py:444
  18.6 4.2 %collective-permute-start.9 = (bf16[272,128]{1,0:T(8,128)(2,1)S(1)}, bf16[272,128]{1,0:T(8,128)(2,1)S(1)}, u32[]{:S(2)}, u32[]{:S(2)}) collective-permute-start(bf16[272,128]{1,0:T(8,128)(2,1)S(1)} %after.1.refs_4_), channel_id=1, source_target_pairs={{0,4},{4,0},{8,12},{12,8},{1,5},{5,1},{9,13},{13,9},{2,6},{6,2},{1... | collective-permute-start | bytes 208904 | tf_op jit(solution)/shard_map/ppermute | solution.py:444
  19.7 3.1 %collective-permute-start.5 = (bf16[272,128]{1,0:T(8,128)(2,1)S(1)}, bf16[272,128]{1,0:T(8,128)(2,1)S(1)}, u32[]{:S(2)}, u32[]{:S(2)}) collective-permute-start(bf16[272,128]{1,0:T(8,128)(2,1)S(1)} %collective-permute-done.4.refs_0_), channel_id=1, source_target_pairs={{0,4},{4,0},{8,12},{12,8},{1,5},{5,1},{9,13},{13,9},{2,6},{6,2},{1... | collective-permute-start | bytes 208904 | tf_op jit(solution)/shard_map/ppermute | solution.py:444
  21.4 1.5 %collective-permute-start.7 = (bf16[272,128]{1,0:T(8,128)(2,1)S(1)}, bf16[272,128]{1,0:T(8,128)(2,1)S(1)}, u32[]{:S(2)}, u32[]{:S(2)}) collective-permute-start(bf16[272,128]{1,0:T(8,128)(2,1)S(1)} %collective-permute-done.6.refs_2_), channel_id=1, source_target_pairs={{0,4},{4,0},{8,12},{12,8},{1,5},{5,1},{9,13},{13,9},{2,6},{6,2},{1... | collective-permute-start | bytes 208904 | tf_op jit(solution)/shard_map/ppermute | solution.py:444
  21.4 1.5 %collective-permute-start.11 = (bf16[272,128]{1,0:T(8,128)(2,1)S(1)}, bf16[272,128]{1,0:T(8,128)(2,1)S(1)}, u32[]{:S(2)}, u32[]{:S(2)}) collective-permute-start(bf16[272,128]{1,0:T(8,128)(2,1)S(1)} %collective-permute-done.10.refs_6_), channel_id=1, source_target_pairs={{0,4},{4,0},{8,12},{12,8},{1,5},{5,1},{9,13},{13,9},{2,6},{6,2},{1... | collective-permute-start | bytes 208904 | tf_op jit(solution)/shard_map/ppermute | solution.py:444

commit v16 on v15

--- a/solution.py
+++ b/solution.py
@@ -93,12 +93,10 @@
     return cosine[:1], sine[:1], jnp.max(first).astype(jnp.int32)
 
 
-def butterflies(image, turns, zhi, zlo):
-    rows, columns = image.shape
-    size = columns // RADIX
-
-    def step(i, carry):
-        here = pl.ds(pl.multiple_of(i * 16, 16), 16)
+def butterflies(image, turns, zhi, zlo, first, count):
+    size = image.shape[1] // RADIX
+    for top_row in range(first, first + count, 16):
+        here = slice(top_row, top_row + 16)
         x = [image[here, m * size : (m + 1) * size].astype(jnp.float32) for m in range(8)]
         p0, p1, p2, p3 = (x[m] + x[m + 4] for m in range(4))
         q0, q1, q2, q3 = (x[m] - x[m + 4] for m in range(4))
@@ -112,9 +110,6 @@
             top = z[line].astype(jnp.bfloat16)
             zhi[line, here, :] = top
             zlo[line, here, :] = (z[line] - top.astype(jnp.float32)).astype(jnp.bfloat16)
-        return carry
-
-    lax.fori_loop(0, rows // 16, step, 0)
 
 
 def inverse_butterflies(ends, waves, turns, turned, first, rows):
@@ -191,16 +186,19 @@
     image, matrix, angles, defocus, starts, zhi, zlo, *scratch, sems = refs[count:]
     rows, columns = image.shape
     size = columns // RADIX
+    halves = [pl.ds(0, rows // 2), pl.ds(rows // 2, rows // 2)]
+    order = [2, 3, 0, 1, 4]
     copies = fetched(
-        [image_ref, angle_ref, defocus_ref, starts_ref] + [matrix_ref.at[i] for i in range(5)],
-        [image, angles, defocus, starts] + [matrix.at[i] for i in range(5)],
+        [image_ref.at[h] for h in halves] + [matrix_ref.at[i] for i in order] + [angle_ref, defocus_ref, starts_ref],
+        [image.at[h] for h in halves] + [matrix.at[i] for i in order] + [angles, defocus, starts],
         sems,
     )
     squares, ramp, cosine_turns, sine_turns = column_lines(columns)
     turns = [t[j : j + 1, :] for j in range(3) for t in (cosine_turns, sine_turns)]
-    copies[0].wait()
-    butterflies(image, turns, zhi, zlo)
-    for copy in copies[4:8]:
+    for i in range(2):
+        copies[i].wait()
+        butterflies(image, turns, zhi, zlo, i * rows // 2, rows // 2)
+    for copy in copies[2:4]:
         copy.wait()
 
     def product(first, lines, table, here):
@@ -210,13 +208,13 @@
         total += jnp.dot(top, matrix[table + 1, :, here], preferred_element_type=jnp.float32)
         return total + jnp.dot(rest, matrix[table, :, here], preferred_element_type=jnp.float32)
 
+    mixed = product(2, 6, 2, slice(None))
+    for copy in copies[4:]:
+        copy.wait()
     spectrum = [product(0, 1, 0, slice(0, size)), product(1, 1, 0, slice(size, 2 * size))]
-    mixed = product(2, 6, 2, slice(None))
     for j in range(3):
         real, imag = mixed[2 * j * rows : (2 * j + 1) * rows], mixed[(2 * j + 1) * rows : (2 * j + 2) * rows]
         spectrum += [real[:, :size] + imag[:, size:], imag[:, :size] - real[:, size:]]
-    for copy in copies[1:4] + copies[8:]:
-        copy.wait()
     facts = (squares, ramp, turns, angles, defocus, starts)
     sends = send_patches(
         slots, slices_owned, spectrum, matrix.at[2], matrix.at[4], columns, facts, scratch, out_refs
@@ -250,7 +248,7 @@
             pltpu.VMEM((count * rows, columns), jnp.float32),
             pltpu.VMEM((count, *packed_shape(rows)), jnp.bfloat16),
             pltpu.SemaphoreType.DMA((count,)),
-            pltpu.SemaphoreType.DMA((9,)),
+            pltpu.SemaphoreType.DMA((10,)),
         ],
         compiler_params=pltpu.CompilerParams(vmem_limit_bytes=60 * 2**20),
         cost_estimate=pl.CostEstimate(flops=flops, bytes_accessed=3 * 2**20, transcendentals=0),
@@ -378,7 +376,7 @@
     out_ref, out, sems = refs[len(slots) * row_devices :]
     rows = total_ref.shape[0] // XBLK
     parts = corrected_patches(slots, row_devices, rows_ref, patch_refs)
-    step = 4
+    step = 2
     copies = []
     for group in range(out.shape[0] // step):
         here = slice(group * step * XBW, (group + 1) * step * XBW)
@@ -434,7 +432,7 @@
         [total],
         out_shape=jax.ShapeDtypeStruct(shape, jnp.bfloat16),
         out_specs=pl.BlockSpec(memory_space=pl.ANY),
-        scratch_shapes=[pltpu.VMEM(shape, jnp.bfloat16), pltpu.SemaphoreType.DMA((shape[0] // 4,))],
+        scratch_shapes=[pltpu.VMEM(shape, jnp.bfloat16), pltpu.SemaphoreType.DMA((shape[0] // 2,))],
         name="finish_volume",
     )
 

time: 24.7 us -> 24.7 us (level)
  no operation moved by 1% of the time
where the time goes in v16:
time: 24.7 us; the launch traced here: 24.5 us
  starting transfers between devices  10.7 us (43%)
  Pallas kernels  9.36 us (38%)
  waiting for transfers between devices  3.48 us (14%)
  local copies, waits for them, and re-layouts  0.91 us (4%)
    ppermute x12, starting transfers between devices, exchange(): return lax.ppermute(array, axis, [(i, i ^ distance) for i in range(count)])  10.7 us
    pallas_call x1, Pallas kernels, column_filtered(): pl.pallas_call(functools.partial(column_kernel, slots, slices_owned), out...  4.51 us
    ppermute x12, waiting for transfers between devices, exchange(): return lax.ppermute(array, axis, [(i, i ^ distance) for i in range(count)])  3.48 us
    pallas_call x2, Pallas kernels, interpolation(): pl.pallas_call(functools.partial(kernel, slots, len(patches[0])), in_spec...  2.6 us
    pallas_call x1, Pallas kernels, prepared(): pl.pallas_call(functools.partial(prepare_kernel, slots, slices_owned), ou...  2.25 us
    unnamed x7, local copies, waits for them, and re-layouts  0.9 us
  transfers between devices with their start and end apart: 12, of which 3 were waited for; matrix products, arithmetic and copies ran while one was open for 4% of the time, Pallas kernels for 13%

profile of v16, /device:TPU:0, one launch (start us, length us, event | category | flops | bytes accessed | tf_op | source)
XLA Modules:
  0.0 24.5 jit_solution(12650148898978533903)
XLA Ops:
  0.0 4.5 %column_filter.1 = (bf16[272,128]{1,0:T(8,128)(2,1)}, bf16[272,128]{1,0:T(8,128)(2,1)}, bf16[272,128]{1,0:T(8,128)(2,1)}, bf16[272,128]{1,0:T(8,128)(2,1)}) custom-call(bf16[64,2048]{1,0:T(8,128)(2,1)} %bitcast.1, bf16[5,256,512]{2,1,0:T(8,128)(2,1)} %constant.4.clone.matrix_ref, f32[4]{0:T(128)} %angle_ref.1, s32[4,4]{1,0:T(4,128)} %defocus_ref.1, ...), custom_call_target="tpu_custom_call" | custom-call | flops 822083584 | bytes 3145728 | tf_op jit(solution)/shard_map/column_filter/pallas_call | solution.py:233
  4.5 3.1 %collective-permute-start = (bf16[272,128]{1,0:T(8,128)(2,1)}, bf16[272,128]{1,0:T(8,128)(2,1)S(1)}, u32[]{:S(2)}, u32[]{:S(2)}) collective-permute-start(bf16[272,128]{1,0:T(8,128)(2,1)} %get-tuple-element.14), channel_id=1, source_target_pairs={{0,1},{1,0},{2,3},{3,2},{4,5},{5,4},{6,7},{7,6},{8,9},{9,8},{10,11... | collective-permute-start | bytes 208904 | tf_op jit(solution)/shard_map/ppermute | solution.py:442
  7.6 2.5 %collective-permute-start.4 = (bf16[272,128]{1,0:T(8,128)(2,1)}, bf16[272,128]{1,0:T(8,128)(2,1)S(1)}, u32[]{:S(2)}, u32[]{:S(2)}) collective-permute-start(bf16[272,128]{1,0:T(8,128)(2,1)} %get-tuple-element.15), channel_id=1, source_target_pairs={{0,3},{1,2},{2,1},{3,0},{4,7},{5,6},{6,5},{7,4},{8,11},{9,10},{10,... | collective-permute-start | bytes 208904 | tf_op jit(solution)/shard_map/ppermute | solution.py:442
  10.1 0.1 collective-permute-start.8
  10.2 0.9 %constant_dynamic-update-slice_fusion.1 = bf16[544,128]{1,0:T(8,128)(2,1)S(1)} fusion(bf16[272,128]{1,0:T(8,128)(2,1)} %get-tuple-element.13), kind=kLoop, calls=%fused_computation.1 | loop fusion | bytes 139264
  11.1 0.0 collective-permute-done
  11.1 1.6 %collective-permute-start.2 = (bf16[544,128]{1,0:T(8,128)(2,1)S(1)}, bf16[544,128]{1,0:T(8,128)(2,1)S(1)}, u32[]{:S(2)}, u32[]{:S(2)}) collective-permute-start(bf16[544,128]{1,0:T(8,128)(2,1)S(1)} %constant_dynamic-update-slice_fusion.refs_0_), channel_id=1, source_target_pairs={{0,8},{4,12},{8,0},{12,4},{1,9},{5,13},{9,1},{13,5},{2,10},{6,14},... | collective-permute-start | bytes 417800 | tf_op jit(solution)/shard_map/ppermute | solution.py:442
  12.7 2.2 %prepare.1 = (bf16[256,256]{1,0:T(8,128)(2,1)S(1)}, bf16[4,160,2048]{2,1,0:T(8,128)(2,1)S(1)}) custom-call(f32[4]{0:T(128)S(1)} %copy-done.1, s32[4,4]{1,0:T(4,128)S(1)} %copy-done, bf16[2,256,256]{2,1,0:T(8,128)(2,1)S(1)} %copy-done.2), custom_call_target="tpu_custom_call" | custom-call | flops 2147483648 | bytes 6291456 | tf_op jit(solution)/shard_map/prepare/pallas_call | solution.py:319
  15.0 0.0 collective-permute-done.4.refs_0_
  15.0 1.4 %collective-permute-start.6 = (bf16[272,128]{1,0:T(8,128)(2,1)S(1)}, bf16[272,128]{1,0:T(8,128)(2,1)S(1)}, u32[]{:S(2)}, u32[]{:S(2)}) collective-permute-start(bf16[272,128]{1,0:T(8,128)(2,1)S(1)} %collective-permute-done.4.refs_0_), channel_id=1, source_target_pairs={{0,8},{4,12},{8,0},{12,4},{1,9},{5,13},{9,1},{13,5},{2,10},{6,14},... | collective-permute-start | bytes 208904 | tf_op jit(solution)/shard_map/ppermute | solution.py:442
  16.4 0.0 collective-permute-done.2.refs_2_
  16.4 0.0 collective-permute-start.3
  16.4 0.7 %collective-permute-done.8.refs_0_ = bf16[272,128]{1,0:T(8,128)(2,1)S(1)} collective-permute-done((bf16[272,128]{1,0:T(8,128)(2,1)}, bf16[272,128]{1,0:T(8,128)(2,1)S(1)}, u32[]{:S(2)}, u32[]{:S(2)}) %collective-permute-start.8) | collective-permute-done | bytes 69664 | tf_op jit(solution)/shard_map/ppermute | solution.py:442
  17.1 1.5 %collective-permute-start.10 = (bf16[272,128]{1,0:T(8,128)(2,1)S(1)}, bf16[272,128]{1,0:T(8,128)(2,1)S(1)}, u32[]{:S(2)}, u32[]{:S(2)}) collective-permute-start(bf16[272,128]{1,0:T(8,128)(2,1)S(1)} %after.1.refs_4_), channel_id=1, source_target_pairs={{0,8},{4,12},{8,0},{12,4},{1,9},{5,13},{9,1},{13,5},{2,10},{6,14},... | collective-permute-start | bytes 208904 | tf_op jit(solution)/shard_map/ppermute | solution.py:442
  18.6 1.1 %collective-permute-done.6.refs_2_ = bf16[272,128]{1,0:T(8,128)(2,1)S(1)} collective-permute-done((bf16[272,128]{1,0:T(8,128)(2,1)S(1)}, bf16[272,128]{1,0:T(8,128)(2,1)S(1)}, u32[]{:S(2)}, u32[]{:S(2)}) %collective-permute-start.6) | collective-permute-done | bytes 69664 | tf_op jit(solution)/shard_map/ppermute | solution.py:442
  19.7 0.0 collective-permute-start.5
  19.7 1.7 %collective-permute-done.10.refs_6_ = bf16[272,128]{1,0:T(8,128)(2,1)S(1)} collective-permute-done((bf16[272,128]{1,0:T(8,128)(2,1)S(1)}, bf16[272,128]{1,0:T(8,128)(2,1)S(1)}, u32[]{:S(2)}, u32[]{:S(2)}) %collective-permute-start.10) | collective-permute-done | bytes 69664 | tf_op jit(solution)/shard_map/ppermute | solution.py:442
  21.4 0.0 collective-permute-start.7
  21.4 0.0 collective-permute-done.1.refs_1_
  21.4 0.5 %collective-permute-start.11 = (bf16[272,128]{1,0:T(8,128)(2,1)S(1)}, bf16[272,128]{1,0:T(8,128)(2,1)S(1)}, u32[]{:S(2)}, u32[]{:S(2)}) collective-permute-start(bf16[272,128]{1,0:T(8,128)(2,1)S(1)} %collective-permute-done.10.refs_6_), channel_id=1, source_target_pairs={{0,4},{4,0},{8,12},{12,8},{1,5},{5,1},{9,13},{13,9},{2,6},{6,2},{1... | collective-permute-start | bytes 208904 | tf_op jit(solution)/shard_map/ppermute | solution.py:442
  21.9 0.9 %sum_early_tilts.1.total_ref = f32[256,2048]{1,0:T(8,128)S(1)} custom-call(bf16[256,256]{1,0:T(8,128)(2,1)S(1)} %get-tuple-element.11.rows_ref.refs_1_, bf16[4,160,2048]{2,1,0:T(8,128)(2,1)S(1)} %get-tuple-element.12.weights_ref, bf16[544,128]{1,0:T(8,128)(2,1)S(1)} %constant_dynamic-update-slice_fusion.refs_0_, ...), custom_call_target="tpu_custom_call" | custom-call | tf_op jit(solution)/shard_map/sum_early_tilts/pallas_call | solution.py:401
  22.8 0.0 collective-permute-done.5.refs_1_
  22.8 0.0 collective-permute-done.9.refs_5_
  22.8 1.7 %finish_volume.1 = bf16[16,64,512]{2,1,0:T(8,128)(2,1)} custom-call(bf16[256,256]{1,0:T(8,128)(2,1)S(1)} %get-tuple-element.11.rows_ref.refs_1_, bf16[4,160,2048]{2,1,0:T(8,128)(2,1)S(1)} %get-tuple-element.12.weights_ref, f32[256,2048]{1,0:T(8,128)S(1)} %sum_early_tilts.1.total_ref, bf16[272,128]{1,0:T(8,128)(2,1)S(1)} %collective-permute-done.4.refs_0_, ...), custom_call_target="tpu_custom_call" | custom-call | tf_op jit(solution)/shard_map/finish_volume/pallas_call | solution.py:401
  (13 shorter events, 0.0 us)
Async XLA Ops:
  0.0 12.7 %copy-start.2 = (bf16[2,256,256]{2,1,0:T(8,128)(2,1)S(1)}, bf16[2,256,256]{2,1,0:T(8,128)(2,1)}, u32[]{:S(2)}) copy-start(bf16[2,256,256]{2,1,0:T(8,128)(2,1)} %constant.5.clone.waves) | copy-start | bytes 786436
  0.0 12.7 %copy-start = (s32[4,4]{1,0:T(4,128)S(1)}, s32[4,4]{1,0:T(4,128)}, u32[]{:S(2)}) copy-start(s32[4,4]{1,0:T(4,128)} %defocus_ref.1) | copy-start | bytes 196
  0.0 12.7 %copy-start.1 = (f32[4]{0:T(128)S(1)}, f32[4]{0:T(128)}, u32[]{:S(2)}) copy-start(f32[4]{0:T(128)} %angle_ref.1) | copy-start | bytes 52
  4.5 6.6 %collective-permute-start = (bf16[272,128]{1,0:T(8,128)(2,1)}, bf16[272,128]{1,0:T(8,128)(2,1)S(1)}, u32[]{:S(2)}, u32[]{:S(2)}) collective-permute-start(bf16[272,128]{1,0:T(8,128)(2,1)} %get-tuple-element.14), channel_id=1, source_target_pairs={{0,1},{1,0},{2,3},{3,2},{4,5},{5,4},{6,7},{7,6},{8,9},{9,8},{10,11... | collective-permute-start | bytes 208904 | tf_op jit(solution)/shard_map/ppermute | solution.py:442
  7.6 7.4 %collective-permute-start.4 = (bf16[272,128]{1,0:T(8,128)(2,1)}, bf16[272,128]{1,0:T(8,128)(2,1)S(1)}, u32[]{:S(2)}, u32[]{:S(2)}) collective-permute-start(bf16[272,128]{1,0:T(8,128)(2,1)} %get-tuple-element.15), channel_id=1, source_target_pairs={{0,3},{1,2},{2,1},{3,0},{4,7},{5,6},{6,5},{7,4},{8,11},{9,10},{10,... | collective-permute-start | bytes 208904 | tf_op jit(solution)/shard_map/ppermute | solution.py:442
  10.1 7.0 %collective-permute-start.8 = (bf16[272,128]{1,0:T(8,128)(2,1)}, bf16[272,128]{1,0:T(8,128)(2,1)S(1)}, u32[]{:S(2)}, u32[]{:S(2)}) collective-permute-start(bf16[272,128]{1,0:T(8,128)(2,1)} %get-tuple-element.16), channel_id=1, source_target_pairs={{0,2},{1,3},{2,0},{3,1},{4,6},{5,7},{6,4},{7,5},{8,10},{9,11},{10,... | collective-permute-start | bytes 208904 | tf_op jit(solution)/shard_map/ppermute | solution.py:442
  11.1 5.3 %collective-permute-start.2 = (bf16[544,128]{1,0:T(8,128)(2,1)S(1)}, bf16[544,128]{1,0:T(8,128)(2,1)S(1)}, u32[]{:S(2)}, u32[]{:S(2)}) collective-permute-start(bf16[544,128]{1,0:T(8,128)(2,1)S(1)} %constant_dynamic-update-slice_fusion.refs_0_), channel_id=1, source_target_pairs={{0,8},{4,12},{8,0},{12,4},{1,9},{5,13},{9,1},{13,5},{2,10},{6,14},... | collective-permute-start | bytes 417800 | tf_op jit(solution)/shard_map/ppermute | solution.py:442
  12.7 8.7 %collective-permute-start.1 = (bf16[544,128]{1,0:T(8,128)(2,1)S(1)}, bf16[544,128]{1,0:T(8,128)(2,1)S(1)}, u32[]{:S(2)}, u32[]{:S(2)}) collective-permute-start(bf16[544,128]{1,0:T(8,128)(2,1)S(1)} %constant_dynamic-update-slice_fusion.refs_0_), channel_id=1, source_target_pairs={{0,4},{4,0},{8,12},{12,8},{1,5},{5,1},{9,13},{13,9},{2,6},{6,2},{1... | collective-permute-start | bytes 417800 | tf_op jit(solution)/shard_map/ppermute | solution.py:442
  15.0 4.7 %collective-permute-start.6 = (bf16[272,128]{1,0:T(8,128)(2,1)S(1)}, bf16[272,128]{1,0:T(8,128)(2,1)S(1)}, u32[]{:S(2)}, u32[]{:S(2)}) collective-permute-start(bf16[272,128]{1,0:T(8,128)(2,1)S(1)} %collective-permute-done.4.refs_0_), channel_id=1, source_target_pairs={{0,8},{4,12},{8,0},{12,4},{1,9},{5,13},{9,1},{13,5},{2,10},{6,14},... | collective-permute-start | bytes 208904 | tf_op jit(solution)/shard_map/ppermute | solution.py:442
  16.4 5.5 %collective-permute-start.3 = (bf16[544,128]{1,0:T(8,128)(2,1)S(1)}, bf16[544,128]{1,0:T(8,128)(2,1)S(1)}, u32[]{:S(2)}, u32[]{:S(2)}) collective-permute-start(bf16[544,128]{1,0:T(8,128)(2,1)S(1)} %collective-permute-done.2.refs_2_), channel_id=1, source_target_pairs={{0,4},{4,0},{8,12},{12,8},{1,5},{5,1},{9,13},{13,9},{2,6},{6,2},{1... | collective-permute-start | bytes 417800 | tf_op jit(solution)/shard_map/ppermute | solution.py:442
  17.1 4.3 %collective-permute-start.10 = (bf16[272,128]{1,0:T(8,128)(2,1)S(1)}, bf16[272,128]{1,0:T(8,128)(2,1)S(1)}, u32[]{:S(2)}, u32[]{:S(2)}) collective-permute-start(bf16[272,128]{1,0:T(8,128)(2,1)S(1)} %after.1.refs_4_), channel_id=1, source_target_pairs={{0,8},{4,12},{8,0},{12,4},{1,9},{5,13},{9,1},{13,5},{2,10},{6,14},... | collective-permute-start | bytes 208904 | tf_op jit(solution)/shard_map/ppermute | solution.py:442
  18.6 4.2 %collective-permute-start.9 = (bf16[272,128]{1,0:T(8,128)(2,1)S(1)}, bf16[272,128]{1,0:T(8,128)(2,1)S(1)}, u32[]{:S(2)}, u32[]{:S(2)}) collective-permute-start(bf16[272,128]{1,0:T(8,128)(2,1)S(1)} %after.1.refs_4_), channel_id=1, source_target_pairs={{0,4},{4,0},{8,12},{12,8},{1,5},{5,1},{9,13},{13,9},{2,6},{6,2},{1... | collective-permute-start | bytes 208904 | tf_op jit(solution)/shard_map/ppermute | solution.py:442
  19.7 3.1 %collective-permute-start.5 = (bf16[272,128]{1,0:T(8,128)(2,1)S(1)}, bf16[272,128]{1,0:T(8,128)(2,1)S(1)}, u32[]{:S(2)}, u32[]{:S(2)}) collective-permute-start(bf16[272,128]{1,0:T(8,128)(2,1)S(1)} %collective-permute-done.4.refs_0_), channel_id=1, source_target_pairs={{0,4},{4,0},{8,12},{12,8},{1,5},{5,1},{9,13},{13,9},{2,6},{6,2},{1... | collective-permute-start | bytes 208904 | tf_op jit(solution)/shard_map/ppermute | solution.py:442
  21.4 1.5 %collective-permute-start.7 = (bf16[272,128]{1,0:T(8,128)(2,1)S(1)}, bf16[272,128]{1,0:T(8,128)(2,1)S(1)}, u32[]{:S(2)}, u32[]{:S(2)}) collective-permute-start(bf16[272,128]{1,0:T(8,128)(2,1)S(1)} %collective-permute-done.6.refs_2_), channel_id=1, source_target_pairs={{0,4},{4,0},{8,12},{12,8},{1,5},{5,1},{9,13},{13,9},{2,6},{6,2},{1... | collective-permute-start | bytes 208904 | tf_op jit(solution)/shard_map/ppermute | solution.py:442
  21.4 1.5 %collective-permute-start.11 = (bf16[272,128]{1,0:T(8,128)(2,1)S(1)}, bf16[272,128]{1,0:T(8,128)(2,1)S(1)}, u32[]{:S(2)}, u32[]{:S(2)}) collective-permute-start(bf16[272,128]{1,0:T(8,128)(2,1)S(1)} %collective-permute-done.10.refs_6_), channel_id=1, source_target_pairs={{0,4},{4,0},{8,12},{12,8},{1,5},{5,1},{9,13},{13,9},{2,6},{6,2},{1... | collective-permute-start | bytes 208904 | tf_op jit(solution)/shard_map/ppermute | solution.py:442

commit v17 on v15

--- a/solution.py
+++ b/solution.py
@@ -461,7 +461,8 @@
     slices_owned = SLICES // tilt_devices
     far, near = list(range(tilt_devices - 1, 1, -1)), list(range(min(2, tilt_devices)))
     sent = column_filtered(far + near, slices_owned, projections[0], tilt_angle, defocus, band_start)
-    arrived = {d: exchange(sent[d], "tilt", d) if d else sent[d] for d in far + near}
+    arrived = {d: exchange(sent[d], "tilt", d) if d else sent[d] for d in far[:-1] + near}
+    arrived[far[-1]] = exchange(after(sent[far[-1]], arrived[1]), "tilt", far[-1])
     row_filters, weights = prepared(tilt_devices, slices_owned, rows, rows * row_devices, tilt_angle, defocus)
     early = [gather_rows(jnp.concatenate([arrived[d] for d in near]))]
     total = summed(row_filters, weights, early, [near])

time: 24.7 us -> 29 us (1.17)
  waiting for transfers between devices: 3.47 us -> 5.09 us
  local copies, waits for them, and re-layouts: 0.91 us -> 2.44 us
  starting transfers between devices: 10.7 us -> 11.8 us
    ppermute x12, waiting for transfers between devices: 3.47 us -> 5.09 us  [exchange(): return lax.ppermute(array, axis, [(i, i ^ distance) for i in range(count)])]
    unnamed x7 -> x11, local copies, waits for them, and re-layouts: 0.9 us -> 2.43 us
    ppermute x12, starting transfers between devices: 10.7 us -> 11.8 us  [exchange(): return lax.ppermute(array, axis, [(i, i ^ distance) for i in range(count)])]
  transfers between devices with their start and end apart: 12 -> 12, of which waited for: 3 -> 4; matrix products, arithmetic and copies ran while one was open for 4% -> 3% of each run, Pallas kernels for 13% -> 11%
where the time goes in v17:
time: 29 us; the launch traced here: 28.8 us
  starting transfers between devices  11.8 us (41%)
  Pallas kernels  9.34 us (32%)
  waiting for transfers between devices  5.09 us (18%)
  local copies, waits for them, and re-layouts  2.44 us (8%)
    ppermute x12, starting transfers between devices, exchange(): return lax.ppermute(array, axis, [(i, i ^ distance) for i in range(count)])  11.8 us
    ppermute x12, waiting for transfers between devices, exchange(): return lax.ppermute(array, axis, [(i, i ^ distance) for i in range(count)])  5.09 us
    pallas_call x1, Pallas kernels, column_filtered(): pl.pallas_call(functools.partial(column_kernel, slots, slices_owned), out...  4.53 us
    pallas_call x2, Pallas kernels, interpolation(): pl.pallas_call(functools.partial(kernel, slots, len(patches[0])), in_spec...  2.56 us
    unnamed x11, local copies, waits for them, and re-layouts  2.43 us
    pallas_call x1, Pallas kernels, prepared(): pl.pallas_call(functools.partial(prepare_kernel, slots, slices_owned), ou...  2.25 us
  transfers between devices with their start and end apart: 12, of which 4 were waited for; matrix products, arithmetic and copies ran while one was open for 3% of the time, Pallas kernels for 11%

profile of v17, /device:TPU:0, one launch (start us, length us, event | category | flops | bytes accessed | tf_op | source)
XLA Modules:
  0.0 28.8 jit_solution(8471644131078134069)
XLA Ops:
  0.0 4.5 %column_filter.1 = (bf16[272,128]{1,0:T(8,128)(2,1)}, bf16[272,128]{1,0:T(8,128)(2,1)}, bf16[272,128]{1,0:T(8,128)(2,1)}, bf16[272,128]{1,0:T(8,128)(2,1)}) custom-call(bf16[64,2048]{1,0:T(8,128)(2,1)} %bitcast.1, bf16[5,256,512]{2,1,0:T(8,128)(2,1)} %constant.4.clone.matrix_ref, f32[4]{0:T(128)} %angle_ref.1, s32[4,4]{1,0:T(4,128)} %defocus_ref.1, ...), custom_call_target="tpu_custom_call" | custom-call | flops 822083584 | bytes 3145728 | tf_op jit(solution)/shard_map/column_filter/pallas_call | solution.py:235
  4.5 3.1 %collective-permute-start = (bf16[272,128]{1,0:T(8,128)(2,1)}, bf16[272,128]{1,0:T(8,128)(2,1)S(1)}, u32[]{:S(2)}, u32[]{:S(2)}) collective-permute-start(bf16[272,128]{1,0:T(8,128)(2,1)} %get-tuple-element.14), channel_id=1, source_target_pairs={{0,1},{1,0},{2,3},{3,2},{4,5},{5,4},{6,7},{7,6},{8,9},{9,8},{10,11... | collective-permute-start | bytes 208904 | tf_op jit(solution)/shard_map/ppermute | solution.py:444
  7.6 2.5 %collective-permute-start.4 = (bf16[272,128]{1,0:T(8,128)(2,1)}, bf16[272,128]{1,0:T(8,128)(2,1)S(1)}, u32[]{:S(2)}, u32[]{:S(2)}) collective-permute-start(bf16[272,128]{1,0:T(8,128)(2,1)} %get-tuple-element.15), channel_id=1, source_target_pairs={{0,3},{1,2},{2,1},{3,0},{4,7},{5,6},{6,5},{7,4},{8,11},{9,10},{10,... | collective-permute-start | bytes 208904 | tf_op jit(solution)/shard_map/ppermute | solution.py:444
  10.1 0.9 %constant_dynamic-update-slice_fusion.1 = bf16[544,128]{1,0:T(8,128)(2,1)S(1)} fusion(bf16[272,128]{1,0:T(8,128)(2,1)} %get-tuple-element.13), kind=kLoop, calls=%fused_computation.1 | loop fusion | bytes 139264
  11.0 0.0 collective-permute-done.refs_1_
  11.0 1.6 %collective-permute-start.2 = (bf16[544,128]{1,0:T(8,128)(2,1)S(1)}, bf16[544,128]{1,0:T(8,128)(2,1)S(1)}, u32[]{:S(2)}, u32[]{:S(2)}) collective-permute-start(bf16[544,128]{1,0:T(8,128)(2,1)S(1)} %constant_dynamic-update-slice_fusion.refs_0_), channel_id=1, source_target_pairs={{0,8},{4,12},{8,0},{12,4},{1,9},{5,13},{9,1},{13,5},{2,10},{6,14},... | collective-permute-start | bytes 417800 | tf_op jit(solution)/shard_map/ppermute | solution.py:444
  12.6 0.0 collective-permute-start.1
  12.6 0.9 %copy-done = bf16[272,128]{1,0:T(8,128)(2,1)S(1)} copy-done((bf16[272,128]{1,0:T(8,128)(2,1)S(1)}, bf16[272,128]{1,0:T(8,128)(2,1)}, u32[]{:S(2)}) %copy-start) | copy-done | bytes 69656
  13.5 0.6 %copy-done.1 = bf16[272,128]{1,0:T(8,128)(2,1)} copy-done((bf16[272,128]{1,0:T(8,128)(2,1)}, bf16[272,128]{1,0:T(8,128)(2,1)S(1)}, u32[]{:S(2)}) %copy-start.1) | copy-done | bytes 69656
  14.1 2.8 %collective-permute-start.8 = (bf16[272,128]{1,0:T(8,128)(2,1)}, bf16[272,128]{1,0:T(8,128)(2,1)S(1)}, u32[]{:S(2)}, u32[]{:S(2)}) collective-permute-start(bf16[272,128]{1,0:T(8,128)(2,1)} %copy-done.1), channel_id=1, source_target_pairs={{0,2},{1,3},{2,0},{3,1},{4,6},{5,7},{6,4},{7,5},{8,10},{9,11},{10,... | collective-permute-start | bytes 208904 | tf_op jit(solution)/shard_map/ppermute | solution.py:444
  17.0 2.2 %prepare.1 = (bf16[256,256]{1,0:T(8,128)(2,1)S(1)}, bf16[4,160,2048]{2,1,0:T(8,128)(2,1)S(1)}) custom-call(f32[4]{0:T(128)S(1)} %copy-done.3, s32[4,4]{1,0:T(4,128)S(1)} %copy-done.2, bf16[2,256,256]{2,1,0:T(8,128)(2,1)S(1)} %copy-done.4), custom_call_target="tpu_custom_call" | custom-call | flops 2147483648 | bytes 6291456 | tf_op jit(solution)/shard_map/prepare/pallas_call | solution.py:321
  19.3 0.3 %collective-permute-start.3 = (bf16[544,128]{1,0:T(8,128)(2,1)S(1)}, bf16[544,128]{1,0:T(8,128)(2,1)S(1)}, u32[]{:S(2)}, u32[]{:S(2)}) collective-permute-start(bf16[544,128]{1,0:T(8,128)(2,1)S(1)} %collective-permute-done.2.refs_2_), channel_id=1, source_target_pairs={{0,4},{4,0},{8,12},{12,8},{1,5},{5,1},{9,13},{13,9},{2,6},{6,2},{1... | collective-permute-start | bytes 417800 | tf_op jit(solution)/shard_map/ppermute | solution.py:444
  19.5 0.0 collective-permute-done.4.refs_0_
  19.6 0.5 %collective-permute-start.6 = (bf16[272,128]{1,0:T(8,128)(2,1)S(1)}, bf16[272,128]{1,0:T(8,128)(2,1)S(1)}, u32[]{:S(2)}, u32[]{:S(2)}) collective-permute-start(bf16[272,128]{1,0:T(8,128)(2,1)S(1)} %collective-permute-done.4.refs_0_), channel_id=1, source_target_pairs={{0,8},{4,12},{8,0},{12,4},{1,9},{5,13},{9,1},{13,5},{2,10},{6,14},... | collective-permute-start | bytes 208904 | tf_op jit(solution)/shard_map/ppermute | solution.py:444
  20.1 1.5 %collective-permute-done.8.refs_0_ = bf16[272,128]{1,0:T(8,128)(2,1)S(1)} collective-permute-done((bf16[272,128]{1,0:T(8,128)(2,1)}, bf16[272,128]{1,0:T(8,128)(2,1)S(1)}, u32[]{:S(2)}, u32[]{:S(2)}) %collective-permute-start.8) | collective-permute-done | bytes 69664 | tf_op jit(solution)/shard_map/ppermute | solution.py:444
  21.5 0.5 %collective-permute-start.10 = (bf16[272,128]{1,0:T(8,128)(2,1)S(1)}, bf16[272,128]{1,0:T(8,128)(2,1)S(1)}, u32[]{:S(2)}, u32[]{:S(2)}) collective-permute-start(bf16[272,128]{1,0:T(8,128)(2,1)S(1)} %after.3.refs_4_), channel_id=1, source_target_pairs={{0,8},{4,12},{8,0},{12,4},{1,9},{5,13},{9,1},{13,5},{2,10},{6,14},... | collective-permute-start | bytes 208904 | tf_op jit(solution)/shard_map/ppermute | solution.py:444
  22.0 1.9 %collective-permute-done.6.refs_2_ = bf16[272,128]{1,0:T(8,128)(2,1)S(1)} collective-permute-done((bf16[272,128]{1,0:T(8,128)(2,1)S(1)}, bf16[272,128]{1,0:T(8,128)(2,1)S(1)}, u32[]{:S(2)}, u32[]{:S(2)}) %collective-permute-start.6) | collective-permute-done | bytes 69664 | tf_op jit(solution)/shard_map/ppermute | solution.py:444
  23.9 0.0 collective-permute-start.9
  23.9 0.0 collective-permute-done.1.refs_1_
  23.9 0.5 %collective-permute-start.7 = (bf16[272,128]{1,0:T(8,128)(2,1)S(1)}, bf16[272,128]{1,0:T(8,128)(2,1)S(1)}, u32[]{:S(2)}, u32[]{:S(2)}) collective-permute-start(bf16[272,128]{1,0:T(8,128)(2,1)S(1)} %collective-permute-done.6.refs_2_), channel_id=1, source_target_pairs={{0,4},{4,0},{8,12},{12,8},{1,5},{5,1},{9,13},{13,9},{2,6},{6,2},{1... | collective-permute-start | bytes 208904 | tf_op jit(solution)/shard_map/ppermute | solution.py:444
  24.4 1.4 %collective-permute-done.10.refs_6_ = bf16[272,128]{1,0:T(8,128)(2,1)S(1)} collective-permute-done((bf16[272,128]{1,0:T(8,128)(2,1)S(1)}, bf16[272,128]{1,0:T(8,128)(2,1)S(1)}, u32[]{:S(2)}, u32[]{:S(2)}) %collective-permute-start.10) | collective-permute-done | bytes 69664 | tf_op jit(solution)/shard_map/ppermute | solution.py:444
  25.9 0.9 %sum_early_tilts.1.total_ref = f32[256,2048]{1,0:T(8,128)S(1)} custom-call(bf16[256,256]{1,0:T(8,128)(2,1)S(1)} %get-tuple-element.11.rows_ref.refs_1_, bf16[4,160,2048]{2,1,0:T(8,128)(2,1)S(1)} %get-tuple-element.12.weights_ref, bf16[544,128]{1,0:T(8,128)(2,1)S(1)} %constant_dynamic-update-slice_fusion.refs_0_, ...), custom_call_target="tpu_custom_call" | custom-call | tf_op jit(solution)/shard_map/sum_early_tilts/pallas_call | solution.py:403
  26.8 0.3 %collective-permute-done.11.refs_7_ = bf16[272,128]{1,0:T(8,128)(2,1)S(1)} collective-permute-done((bf16[272,128]{1,0:T(8,128)(2,1)S(1)}, bf16[272,128]{1,0:T(8,128)(2,1)S(1)}, u32[]{:S(2)}, u32[]{:S(2)}) %collective-permute-start.11) | collective-permute-done | bytes 69664 | tf_op jit(solution)/shard_map/ppermute | solution.py:444
  27.1 1.7 %finish_volume.1 = bf16[16,64,512]{2,1,0:T(8,128)(2,1)} custom-call(bf16[256,256]{1,0:T(8,128)(2,1)S(1)} %get-tuple-element.11.rows_ref.refs_1_, bf16[4,160,2048]{2,1,0:T(8,128)(2,1)S(1)} %get-tuple-element.12.weights_ref, f32[256,2048]{1,0:T(8,128)S(1)} %sum_early_tilts.1.total_ref, bf16[272,128]{1,0:T(8,128)(2,1)S(1)} %collective-permute-done.4.refs_0_, ...), custom_call_target="tpu_custom_call" | custom-call | tf_op jit(solution)/shard_map/finish_volume/pallas_call | solution.py:403
  (18 shorter events, 0.0 us)
Async XLA Ops:
  0.0 17.0 %copy-start.4 = (bf16[2,256,256]{2,1,0:T(8,128)(2,1)S(1)}, bf16[2,256,256]{2,1,0:T(8,128)(2,1)}, u32[]{:S(2)}) copy-start(bf16[2,256,256]{2,1,0:T(8,128)(2,1)} %constant.5.clone.waves) | copy-start | bytes 786436
  0.0 17.0 %copy-start.2 = (s32[4,4]{1,0:T(4,128)S(1)}, s32[4,4]{1,0:T(4,128)}, u32[]{:S(2)}) copy-start(s32[4,4]{1,0:T(4,128)} %defocus_ref.1) | copy-start | bytes 196
  0.0 17.0 %copy-start.3 = (f32[4]{0:T(128)S(1)}, f32[4]{0:T(128)}, u32[]{:S(2)}) copy-start(f32[4]{0:T(128)} %angle_ref.1) | copy-start | bytes 52
  4.5 6.5 %collective-permute-start = (bf16[272,128]{1,0:T(8,128)(2,1)}, bf16[272,128]{1,0:T(8,128)(2,1)S(1)}, u32[]{:S(2)}, u32[]{:S(2)}) collective-permute-start(bf16[272,128]{1,0:T(8,128)(2,1)} %get-tuple-element.14), channel_id=1, source_target_pairs={{0,1},{1,0},{2,3},{3,2},{4,5},{5,4},{6,7},{7,6},{8,9},{9,8},{10,11... | collective-permute-start | bytes 208904 | tf_op jit(solution)/shard_map/ppermute | solution.py:444
  7.6 11.9 %collective-permute-start.4 = (bf16[272,128]{1,0:T(8,128)(2,1)}, bf16[272,128]{1,0:T(8,128)(2,1)S(1)}, u32[]{:S(2)}, u32[]{:S(2)}) collective-permute-start(bf16[272,128]{1,0:T(8,128)(2,1)} %get-tuple-element.15), channel_id=1, source_target_pairs={{0,3},{1,2},{2,1},{3,0},{4,7},{5,6},{6,5},{7,4},{8,11},{9,10},{10,... | collective-permute-start | bytes 208904 | tf_op jit(solution)/shard_map/ppermute | solution.py:444
  11.0 8.2 %collective-permute-start.2 = (bf16[544,128]{1,0:T(8,128)(2,1)S(1)}, bf16[544,128]{1,0:T(8,128)(2,1)S(1)}, u32[]{:S(2)}, u32[]{:S(2)}) collective-permute-start(bf16[544,128]{1,0:T(8,128)(2,1)S(1)} %constant_dynamic-update-slice_fusion.refs_0_), channel_id=1, source_target_pairs={{0,8},{4,12},{8,0},{12,4},{1,9},{5,13},{9,1},{13,5},{2,10},{6,14},... | collective-permute-start | bytes 417800 | tf_op jit(solution)/shard_map/ppermute | solution.py:444
  12.6 11.3 %collective-permute-start.1 = (bf16[544,128]{1,0:T(8,128)(2,1)S(1)}, bf16[544,128]{1,0:T(8,128)(2,1)S(1)}, u32[]{:S(2)}, u32[]{:S(2)}) collective-permute-start(bf16[544,128]{1,0:T(8,128)(2,1)S(1)} %constant_dynamic-update-slice_fusion.refs_0_), channel_id=1, source_target_pairs={{0,4},{4,0},{8,12},{12,8},{1,5},{5,1},{9,13},{13,9},{2,6},{6,2},{1... | collective-permute-start | bytes 417800 | tf_op jit(solution)/shard_map/ppermute | solution.py:444
  12.6 0.9 %copy-start = (bf16[272,128]{1,0:T(8,128)(2,1)S(1)}, bf16[272,128]{1,0:T(8,128)(2,1)}, u32[]{:S(2)}) copy-start(bf16[272,128]{1,0:T(8,128)(2,1)} %get-tuple-element.16.refs_0_) | copy-start | bytes 208900
  13.5 0.6 %copy-start.1 = (bf16[272,128]{1,0:T(8,128)(2,1)}, bf16[272,128]{1,0:T(8,128)(2,1)S(1)}, u32[]{:S(2)}) copy-start(bf16[272,128]{1,0:T(8,128)(2,1)S(1)} %after.2) | copy-start | bytes 208900
  14.1 7.4 %collective-permute-start.8 = (bf16[272,128]{1,0:T(8,128)(2,1)}, bf16[272,128]{1,0:T(8,128)(2,1)S(1)}, u32[]{:S(2)}, u32[]{:S(2)}) collective-permute-start(bf16[272,128]{1,0:T(8,128)(2,1)} %copy-done.1), channel_id=1, source_target_pairs={{0,2},{1,3},{2,0},{3,1},{4,6},{5,7},{6,4},{7,5},{8,10},{9,11},{10,... | collective-permute-start | bytes 208904 | tf_op jit(solution)/shard_map/ppermute | solution.py:444
  19.3 6.6 %collective-permute-start.3 = (bf16[544,128]{1,0:T(8,128)(2,1)S(1)}, bf16[544,128]{1,0:T(8,128)(2,1)S(1)}, u32[]{:S(2)}, u32[]{:S(2)}) collective-permute-start(bf16[544,128]{1,0:T(8,128)(2,1)S(1)} %collective-permute-done.2.refs_2_), channel_id=1, source_target_pairs={{0,4},{4,0},{8,12},{12,8},{1,5},{5,1},{9,13},{13,9},{2,6},{6,2},{1... | collective-permute-start | bytes 417800 | tf_op jit(solution)/shard_map/ppermute | solution.py:444
  19.6 4.4 %collective-permute-start.6 = (bf16[272,128]{1,0:T(8,128)(2,1)S(1)}, bf16[272,128]{1,0:T(8,128)(2,1)S(1)}, u32[]{:S(2)}, u32[]{:S(2)}) collective-permute-start(bf16[272,128]{1,0:T(8,128)(2,1)S(1)} %collective-permute-done.4.refs_0_), channel_id=1, source_target_pairs={{0,8},{4,12},{8,0},{12,4},{1,9},{5,13},{9,1},{13,5},{2,10},{6,14},... | collective-permute-start | bytes 208904 | tf_op jit(solution)/shard_map/ppermute | solution.py:444
  21.5 4.3 %collective-permute-start.10 = (bf16[272,128]{1,0:T(8,128)(2,1)S(1)}, bf16[272,128]{1,0:T(8,128)(2,1)S(1)}, u32[]{:S(2)}, u32[]{:S(2)}) collective-permute-start(bf16[272,128]{1,0:T(8,128)(2,1)S(1)} %after.3.refs_4_), channel_id=1, source_target_pairs={{0,8},{4,12},{8,0},{12,4},{1,9},{5,13},{9,1},{13,5},{2,10},{6,14},... | collective-permute-start | bytes 208904 | tf_op jit(solution)/shard_map/ppermute | solution.py:444
  22.0 4.7 %collective-permute-start.5 = (bf16[272,128]{1,0:T(8,128)(2,1)S(1)}, bf16[272,128]{1,0:T(8,128)(2,1)S(1)}, u32[]{:S(2)}, u32[]{:S(2)}) collective-permute-start(bf16[272,128]{1,0:T(8,128)(2,1)S(1)} %collective-permute-done.4.refs_0_), channel_id=1, source_target_pairs={{0,4},{4,0},{8,12},{12,8},{1,5},{5,1},{9,13},{13,9},{2,6},{6,2},{1... | collective-permute-start | bytes 208904 | tf_op jit(solution)/shard_map/ppermute | solution.py:444
  23.9 2.9 %collective-permute-start.9 = (bf16[272,128]{1,0:T(8,128)(2,1)S(1)}, bf16[272,128]{1,0:T(8,128)(2,1)S(1)}, u32[]{:S(2)}, u32[]{:S(2)}) collective-permute-start(bf16[272,128]{1,0:T(8,128)(2,1)S(1)} %after.3.refs_4_), channel_id=1, source_target_pairs={{0,4},{4,0},{8,12},{12,8},{1,5},{5,1},{9,13},{13,9},{2,6},{6,2},{1... | collective-permute-start | bytes 208904 | tf_op jit(solution)/shard_map/ppermute | solution.py:444
  23.9 2.9 %collective-permute-start.7 = (bf16[272,128]{1,0:T(8,128)(2,1)S(1)}, bf16[272,128]{1,0:T(8,128)(2,1)S(1)}, u32[]{:S(2)}, u32[]{:S(2)}) collective-permute-start(bf16[272,128]{1,0:T(8,128)(2,1)S(1)} %collective-permute-done.6.refs_2_), channel_id=1, source_target_pairs={{0,4},{4,0},{8,12},{12,8},{1,5},{5,1},{9,13},{13,9},{2,6},{6,2},{1... | collective-permute-start | bytes 208904 | tf_op jit(solution)/shard_map/ppermute | solution.py:444
  25.8 1.3 %collective-permute-start.11 = (bf16[272,128]{1,0:T(8,128)(2,1)S(1)}, bf16[272,128]{1,0:T(8,128)(2,1)S(1)}, u32[]{:S(2)}, u32[]{:S(2)}) collective-permute-start(bf16[272,128]{1,0:T(8,128)(2,1)S(1)} %collective-permute-done.10.refs_6_), channel_id=1, source_target_pairs={{0,4},{4,0},{8,12},{12,8},{1,5},{5,1},{9,13},{13,9},{2,6},{6,2},{1... | collective-permute-start | bytes 208904 | tf_op jit(solution)/shard_map/ppermute | solution.py:444

commit v18 on v15

--- a/solution.py
+++ b/solution.py
@@ -252,7 +252,7 @@
             pltpu.SemaphoreType.DMA((count,)),
             pltpu.SemaphoreType.DMA((9,)),
         ],
-        compiler_params=pltpu.CompilerParams(vmem_limit_bytes=60 * 2**20),
+        compiler_params=pltpu.CompilerParams(vmem_limit_bytes=215 * 2**18),
         cost_estimate=pl.CostEstimate(flops=flops, bytes_accessed=3 * 2**20, transcendentals=0),
         name="column_filter",
     )(image, matrices, angles, defocus, starts)

time: 24.7 us -> 27.2 us (1.10)
  local copies, waits for them, and re-layouts: 0.91 us -> 2.94 us
  Pallas kernels: 9.36 us -> 9.96 us
  starting transfers between devices: 10.7 us -> 10.4 us
    unnamed x7 -> x9, local copies, waits for them, and re-layouts: 0.9 us -> 2.92 us
    pallas_call x1, Pallas kernels: 4.54 us -> 5.16 us  [column_filtered(): pl.pallas_call(functools.partial(column_kernel, slots, slices_owned), out...]
    ppermute x12, starting transfers between devices: 10.7 us -> 10.4 us  [exchange(): return lax.ppermute(array, axis, [(i, i ^ distance) for i in range(count)])]
  transfers between devices with their start and end apart: 12 -> 12, of which waited for: 3 -> 4; matrix products, arithmetic and copies ran while one was open for 4% -> 3% of each run, Pallas kernels for 13% -> 12%
where the time goes in v18:
time: 27.2 us; the launch traced here: 26.9 us
  starting transfers between devices  10.4 us (38%)
  Pallas kernels  9.96 us (37%)
  waiting for transfers between devices  3.55 us (13%)
  local copies, waits for them, and re-layouts  2.94 us (11%)
    ppermute x12, starting transfers between devices, exchange(): return lax.ppermute(array, axis, [(i, i ^ distance) for i in range(count)])  10.4 us
    pallas_call x1, Pallas kernels, column_filtered(): pl.pallas_call(functools.partial(column_kernel, slots, slices_owned), out...  5.16 us
    ppermute x12, waiting for transfers between devices, exchange(): return lax.ppermute(array, axis, [(i, i ^ distance) for i in range(count)])  3.55 us
    unnamed x9, local copies, waits for them, and re-layouts  2.92 us
    pallas_call x2, Pallas kernels, interpolation(): pl.pallas_call(functools.partial(kernel, slots, len(patches[0])), in_spec...  2.55 us
    pallas_call x1, Pallas kernels, prepared(): pl.pallas_call(functools.partial(prepare_kernel, slots, slices_owned), ou...  2.25 us
  transfers between devices with their start and end apart: 12, of which 4 were waited for; matrix products, arithmetic and copies ran while one was open for 3% of the time, Pallas kernels for 12%

profile of v18, /device:TPU:0, one launch (start us, length us, event | category | flops | bytes accessed | tf_op | source)
XLA Modules:
  0.0 26.9 jit_solution(4152740460876537556)
XLA Ops:
  0.0 0.7 %copy-done = s32[4,4,4]{2,1,0:T(4,128)S(1)} copy-done((s32[4,4,4]{2,1,0:T(4,128)S(1)}, s32[4,4,4]{2,1,0:T(4,128)}, u32[]{:S(2)}) %copy-start) | copy-done | bytes 280
  0.7 0.7 %copy-done.1 = s32[4,4]{1,0:T(4,128)S(1)} copy-done((s32[4,4]{1,0:T(4,128)S(1)}, s32[4,4]{1,0:T(4,128)}, u32[]{:S(2)}) %copy-start.1) | copy-done | bytes 88
  1.4 0.7 %copy-done.2 = f32[4]{0:T(128)S(1)} copy-done((f32[4]{0:T(128)S(1)}, f32[4]{0:T(128)}, u32[]{:S(2)}) %copy-start.2) | copy-done | bytes 40
  2.0 5.2 %column_filter.1 = (bf16[272,128]{1,0:T(8,128)(2,1)S(1)}, bf16[272,128]{1,0:T(8,128)(2,1)S(1)}, bf16[272,128]{1,0:T(8,128)(2,1)}, bf16[272,128]{1,0:T(8,128)(2,1)}) custom-call(bf16[64,2048]{1,0:T(8,128)(2,1)} %bitcast.1, bf16[5,256,512]{2,1,0:T(8,128)(2,1)} %constant.4.clone.matrix_ref, f32[4]{0:T(128)S(1)} %copy-done.2, s32[4,4]{1,0:T(4,128)S(1)} %copy-done.1, ...), custom_call_target="tpu_custom_call" | custom-call | flops 822083584 | bytes 3145728 | tf_op jit(solution)/shard_map/column_filter/pallas_call | solution.py:235
  7.2 3.1 %collective-permute-start = (bf16[272,128]{1,0:T(8,128)(2,1)}, bf16[272,128]{1,0:T(8,128)(2,1)S(1)}, u32[]{:S(2)}, u32[]{:S(2)}) collective-permute-start(bf16[272,128]{1,0:T(8,128)(2,1)} %get-tuple-element.14), channel_id=1, source_target_pairs={{0,1},{1,0},{2,3},{3,2},{4,5},{5,4},{6,7},{7,6},{8,9},{9,8},{10,11... | collective-permute-start | bytes 208904 | tf_op jit(solution)/shard_map/ppermute | solution.py:444
  10.3 2.5 %collective-permute-start.4 = (bf16[272,128]{1,0:T(8,128)(2,1)S(1)}, bf16[272,128]{1,0:T(8,128)(2,1)S(1)}, u32[]{:S(2)}, u32[]{:S(2)}) collective-permute-start(bf16[272,128]{1,0:T(8,128)(2,1)S(1)} %get-tuple-element.15), channel_id=1, source_target_pairs={{0,3},{1,2},{2,1},{3,0},{4,7},{5,6},{6,5},{7,4},{8,11},{9,10},{10,... | collective-permute-start | bytes 208904 | tf_op jit(solution)/shard_map/ppermute | solution.py:444
  12.8 0.1 collective-permute-start.8
  12.9 0.9 %constant_dynamic-update-slice_fusion.1 = bf16[544,128]{1,0:T(8,128)(2,1)S(1)} fusion(bf16[272,128]{1,0:T(8,128)(2,1)} %get-tuple-element.13), kind=kLoop, calls=%fused_computation.1 | loop fusion | bytes 139264
  13.8 1.6 %collective-permute-start.2 = (bf16[544,128]{1,0:T(8,128)(2,1)S(1)}, bf16[544,128]{1,0:T(8,128)(2,1)S(1)}, u32[]{:S(2)}, u32[]{:S(2)}) collective-permute-start(bf16[544,128]{1,0:T(8,128)(2,1)S(1)} %constant_dynamic-update-slice_fusion.refs_0_), channel_id=1, source_target_pairs={{0,8},{4,12},{8,0},{12,4},{1,9},{5,13},{9,1},{13,5},{2,10},{6,14},... | collective-permute-start | bytes 417800 | tf_op jit(solution)/shard_map/ppermute | solution.py:444
  15.4 2.2 %prepare.1 = (bf16[256,256]{1,0:T(8,128)(2,1)S(1)}, bf16[4,160,2048]{2,1,0:T(8,128)(2,1)S(1)}) custom-call(f32[4]{0:T(128)S(1)} %copy-done.2, s32[4,4]{1,0:T(4,128)S(1)} %copy-done.1, bf16[2,256,256]{2,1,0:T(8,128)(2,1)S(1)} %copy-done.3), custom_call_target="tpu_custom_call" | custom-call | flops 2147483648 | bytes 6291456 | tf_op jit(solution)/shard_map/prepare/pallas_call | solution.py:321
  17.7 1.1 %collective-permute-start.6 = (bf16[272,128]{1,0:T(8,128)(2,1)S(1)}, bf16[272,128]{1,0:T(8,128)(2,1)S(1)}, u32[]{:S(2)}, u32[]{:S(2)}) collective-permute-start(bf16[272,128]{1,0:T(8,128)(2,1)S(1)} %collective-permute-done.4.refs_0_), channel_id=1, source_target_pairs={{0,8},{4,12},{8,0},{12,4},{1,9},{5,13},{9,1},{13,5},{2,10},{6,14},... | collective-permute-start | bytes 208904 | tf_op jit(solution)/shard_map/ppermute | solution.py:444
  18.7 0.2 collective-permute-done.2.refs_2_
  18.9 0.0 collective-permute-start.3
  18.9 0.5 %collective-permute-done.8.refs_0_ = bf16[272,128]{1,0:T(8,128)(2,1)S(1)} collective-permute-done((bf16[272,128]{1,0:T(8,128)(2,1)S(1)}, bf16[272,128]{1,0:T(8,128)(2,1)S(1)}, u32[]{:S(2)}, u32[]{:S(2)}) %collective-permute-start.8) | collective-permute-done | bytes 69664 | tf_op jit(solution)/shard_map/ppermute | solution.py:444
  19.5 1.5 %collective-permute-start.10 = (bf16[272,128]{1,0:T(8,128)(2,1)S(1)}, bf16[272,128]{1,0:T(8,128)(2,1)S(1)}, u32[]{:S(2)}, u32[]{:S(2)}) collective-permute-start(bf16[272,128]{1,0:T(8,128)(2,1)S(1)} %after.1.refs_4_), channel_id=1, source_target_pairs={{0,8},{4,12},{8,0},{12,4},{1,9},{5,13},{9,1},{13,5},{2,10},{6,14},... | collective-permute-start | bytes 208904 | tf_op jit(solution)/shard_map/ppermute | solution.py:444
  21.0 0.0 collective-permute-start.9
  21.0 1.6 %collective-permute-done.6.refs_2_ = bf16[272,128]{1,0:T(8,128)(2,1)S(1)} collective-permute-done((bf16[272,128]{1,0:T(8,128)(2,1)S(1)}, bf16[272,128]{1,0:T(8,128)(2,1)S(1)}, u32[]{:S(2)}, u32[]{:S(2)}) %collective-permute-start.6) | collective-permute-done | bytes 69664 | tf_op jit(solution)/shard_map/ppermute | solution.py:444
  22.6 1.2 %collective-permute-done.10.refs_6_ = bf16[272,128]{1,0:T(8,128)(2,1)S(1)} collective-permute-done((bf16[272,128]{1,0:T(8,128)(2,1)S(1)}, bf16[272,128]{1,0:T(8,128)(2,1)S(1)}, u32[]{:S(2)}, u32[]{:S(2)}) %collective-permute-start.10) | collective-permute-done | bytes 69664 | tf_op jit(solution)/shard_map/ppermute | solution.py:444
  23.8 0.0 collective-permute-start.7
  23.8 0.0 collective-permute-done.1.refs_1_
  23.8 0.5 %collective-permute-start.11 = (bf16[272,128]{1,0:T(8,128)(2,1)S(1)}, bf16[272,128]{1,0:T(8,128)(2,1)S(1)}, u32[]{:S(2)}, u32[]{:S(2)}) collective-permute-start(bf16[272,128]{1,0:T(8,128)(2,1)S(1)} %collective-permute-done.10.refs_6_), channel_id=1, source_target_pairs={{0,4},{4,0},{8,12},{12,8},{1,5},{5,1},{9,13},{13,9},{2,6},{6,2},{1... | collective-permute-start | bytes 208904 | tf_op jit(solution)/shard_map/ppermute | solution.py:444
  24.3 0.0 collective-permute-done.3.refs_3_
  24.3 0.9 %sum_early_tilts.1.total_ref = f32[256,2048]{1,0:T(8,128)S(1)} custom-call(bf16[256,256]{1,0:T(8,128)(2,1)S(1)} %get-tuple-element.11.rows_ref.refs_1_, bf16[4,160,2048]{2,1,0:T(8,128)(2,1)S(1)} %get-tuple-element.12.weights_ref, bf16[544,128]{1,0:T(8,128)(2,1)S(1)} %constant_dynamic-update-slice_fusion.refs_0_, ...), custom_call_target="tpu_custom_call" | custom-call | tf_op jit(solution)/shard_map/sum_early_tilts/pallas_call | solution.py:403
  25.3 1.6 %finish_volume.1 = bf16[16,64,512]{2,1,0:T(8,128)(2,1)} custom-call(bf16[256,256]{1,0:T(8,128)(2,1)S(1)} %get-tuple-element.11.rows_ref.refs_1_, bf16[4,160,2048]{2,1,0:T(8,128)(2,1)S(1)} %get-tuple-element.12.weights_ref, f32[256,2048]{1,0:T(8,128)S(1)} %sum_early_tilts.1.total_ref, bf16[272,128]{1,0:T(8,128)(2,1)S(1)} %collective-permute-done.4.refs_0_, ...), custom_call_target="tpu_custom_call" | custom-call | tf_op jit(solution)/shard_map/finish_volume/pallas_call | solution.py:403
  (15 shorter events, 0.0 us)
Async XLA Ops:
  0.0 0.7 %copy-start = (s32[4,4,4]{2,1,0:T(4,128)S(1)}, s32[4,4,4]{2,1,0:T(4,128)}, u32[]{:S(2)}) copy-start(s32[4,4,4]{2,1,0:T(4,128)} %starts_ref.1) | copy-start | bytes 772
  0.7 0.7 %copy-start.1 = (s32[4,4]{1,0:T(4,128)S(1)}, s32[4,4]{1,0:T(4,128)}, u32[]{:S(2)}) copy-start(s32[4,4]{1,0:T(4,128)} %defocus_ref.1) | copy-start | bytes 196
  1.4 0.7 %copy-start.2 = (f32[4]{0:T(128)S(1)}, f32[4]{0:T(128)}, u32[]{:S(2)}) copy-start(f32[4]{0:T(128)} %angle_ref.1) | copy-start | bytes 52
  2.0 13.4 %copy-start.3 = (bf16[2,256,256]{2,1,0:T(8,128)(2,1)S(1)}, bf16[2,256,256]{2,1,0:T(8,128)(2,1)}, u32[]{:S(2)}) copy-start(bf16[2,256,256]{2,1,0:T(8,128)(2,1)} %constant.5.clone.waves) | copy-start | bytes 786436
  7.2 6.6 %collective-permute-start = (bf16[272,128]{1,0:T(8,128)(2,1)}, bf16[272,128]{1,0:T(8,128)(2,1)S(1)}, u32[]{:S(2)}, u32[]{:S(2)}) collective-permute-start(bf16[272,128]{1,0:T(8,128)(2,1)} %get-tuple-element.14), channel_id=1, source_target_pairs={{0,1},{1,0},{2,3},{3,2},{4,5},{5,4},{6,7},{7,6},{8,9},{9,8},{10,11... | collective-permute-start | bytes 208904 | tf_op jit(solution)/shard_map/ppermute | solution.py:444
  10.3 7.4 %collective-permute-start.4 = (bf16[272,128]{1,0:T(8,128)(2,1)S(1)}, bf16[272,128]{1,0:T(8,128)(2,1)S(1)}, u32[]{:S(2)}, u32[]{:S(2)}) collective-permute-start(bf16[272,128]{1,0:T(8,128)(2,1)S(1)} %get-tuple-element.15), channel_id=1, source_target_pairs={{0,3},{1,2},{2,1},{3,0},{4,7},{5,6},{6,5},{7,4},{8,11},{9,10},{10,... | collective-permute-start | bytes 208904 | tf_op jit(solution)/shard_map/ppermute | solution.py:444
  12.8 6.7 %collective-permute-start.8 = (bf16[272,128]{1,0:T(8,128)(2,1)S(1)}, bf16[272,128]{1,0:T(8,128)(2,1)S(1)}, u32[]{:S(2)}, u32[]{:S(2)}) collective-permute-start(bf16[272,128]{1,0:T(8,128)(2,1)S(1)} %get-tuple-element.16), channel_id=1, source_target_pairs={{0,2},{1,3},{2,0},{3,1},{4,6},{5,7},{6,4},{7,5},{8,10},{9,11},{10,... | collective-permute-start | bytes 208904 | tf_op jit(solution)/shard_map/ppermute | solution.py:444
  13.8 5.1 %collective-permute-start.2 = (bf16[544,128]{1,0:T(8,128)(2,1)S(1)}, bf16[544,128]{1,0:T(8,128)(2,1)S(1)}, u32[]{:S(2)}, u32[]{:S(2)}) collective-permute-start(bf16[544,128]{1,0:T(8,128)(2,1)S(1)} %constant_dynamic-update-slice_fusion.refs_0_), channel_id=1, source_target_pairs={{0,8},{4,12},{8,0},{12,4},{1,9},{5,13},{9,1},{13,5},{2,10},{6,14},... | collective-permute-start | bytes 417800 | tf_op jit(solution)/shard_map/ppermute | solution.py:444
  15.4 8.4 %collective-permute-start.1 = (bf16[544,128]{1,0:T(8,128)(2,1)S(1)}, bf16[544,128]{1,0:T(8,128)(2,1)S(1)}, u32[]{:S(2)}, u32[]{:S(2)}) collective-permute-start(bf16[544,128]{1,0:T(8,128)(2,1)S(1)} %constant_dynamic-update-slice_fusion.refs_0_), channel_id=1, source_target_pairs={{0,4},{4,0},{8,12},{12,8},{1,5},{5,1},{9,13},{13,9},{2,6},{6,2},{1... | collective-permute-start | bytes 417800 | tf_op jit(solution)/shard_map/ppermute | solution.py:444
  17.7 5.0 %collective-permute-start.6 = (bf16[272,128]{1,0:T(8,128)(2,1)S(1)}, bf16[272,128]{1,0:T(8,128)(2,1)S(1)}, u32[]{:S(2)}, u32[]{:S(2)}) collective-permute-start(bf16[272,128]{1,0:T(8,128)(2,1)S(1)} %collective-permute-done.4.refs_0_), channel_id=1, source_target_pairs={{0,8},{4,12},{8,0},{12,4},{1,9},{5,13},{9,1},{13,5},{2,10},{6,14},... | collective-permute-start | bytes 208904 | tf_op jit(solution)/shard_map/ppermute | solution.py:444
  18.9 5.4 %collective-permute-start.3 = (bf16[544,128]{1,0:T(8,128)(2,1)S(1)}, bf16[544,128]{1,0:T(8,128)(2,1)S(1)}, u32[]{:S(2)}, u32[]{:S(2)}) collective-permute-start(bf16[544,128]{1,0:T(8,128)(2,1)S(1)} %collective-permute-done.2.refs_2_), channel_id=1, source_target_pairs={{0,4},{4,0},{8,12},{12,8},{1,5},{5,1},{9,13},{13,9},{2,6},{6,2},{1... | collective-permute-start | bytes 417800 | tf_op jit(solution)/shard_map/ppermute | solution.py:444
  19.5 4.3 %collective-permute-start.10 = (bf16[272,128]{1,0:T(8,128)(2,1)S(1)}, bf16[272,128]{1,0:T(8,128)(2,1)S(1)}, u32[]{:S(2)}, u32[]{:S(2)}) collective-permute-start(bf16[272,128]{1,0:T(8,128)(2,1)S(1)} %after.1.refs_4_), channel_id=1, source_target_pairs={{0,8},{4,12},{8,0},{12,4},{1,9},{5,13},{9,1},{13,5},{2,10},{6,14},... | collective-permute-start | bytes 208904 | tf_op jit(solution)/shard_map/ppermute | solution.py:444
  21.0 4.3 %collective-permute-start.9 = (bf16[272,128]{1,0:T(8,128)(2,1)S(1)}, bf16[272,128]{1,0:T(8,128)(2,1)S(1)}, u32[]{:S(2)}, u32[]{:S(2)}) collective-permute-start(bf16[272,128]{1,0:T(8,128)(2,1)S(1)} %after.1.refs_4_), channel_id=1, source_target_pairs={{0,4},{4,0},{8,12},{12,8},{1,5},{5,1},{9,13},{13,9},{2,6},{6,2},{1... | collective-permute-start | bytes 208904 | tf_op jit(solution)/shard_map/ppermute | solution.py:444
  22.6 2.6 %collective-permute-start.5 = (bf16[272,128]{1,0:T(8,128)(2,1)S(1)}, bf16[272,128]{1,0:T(8,128)(2,1)S(1)}, u32[]{:S(2)}, u32[]{:S(2)}) collective-permute-start(bf16[272,128]{1,0:T(8,128)(2,1)S(1)} %collective-permute-done.4.refs_0_), channel_id=1, source_target_pairs={{0,4},{4,0},{8,12},{12,8},{1,5},{5,1},{9,13},{13,9},{2,6},{6,2},{1... | collective-permute-start | bytes 208904 | tf_op jit(solution)/shard_map/ppermute | solution.py:444
  23.8 1.5 %collective-permute-start.7 = (bf16[272,128]{1,0:T(8,128)(2,1)S(1)}, bf16[272,128]{1,0:T(8,128)(2,1)S(1)}, u32[]{:S(2)}, u32[]{:S(2)}) collective-permute-start(bf16[272,128]{1,0:T(8,128)(2,1)S(1)} %collective-permute-done.6.refs_2_), channel_id=1, source_target_pairs={{0,4},{4,0},{8,12},{12,8},{1,5},{5,1},{9,13},{13,9},{2,6},{6,2},{1... | collective-permute-start | bytes 208904 | tf_op jit(solution)/shard_map/ppermute | solution.py:444
  23.8 1.5 %collective-permute-start.11 = (bf16[272,128]{1,0:T(8,128)(2,1)S(1)}, bf16[272,128]{1,0:T(8,128)(2,1)S(1)}, u32[]{:S(2)}, u32[]{:S(2)}) collective-permute-start(bf16[272,128]{1,0:T(8,128)(2,1)S(1)} %collective-permute-done.10.refs_6_), channel_id=1, source_target_pairs={{0,4},{4,0},{8,12},{12,8},{1,5},{5,1},{9,13},{13,9},{2,6},{6,2},{1... | collective-permute-start | bytes 208904 | tf_op jit(solution)/shard_map/ppermute | solution.py:444

commit v19 on v16

--- a/solution.py
+++ b/solution.py
@@ -311,7 +311,7 @@
             weights_ref[slot, MAIN:, there] = rest.astype(jnp.bfloat16)
             return carry
 
-        lax.fori_loop(0, slices_owned, one_slice, 0, unroll=2)
+        lax.fori_loop(0, slices_owned, one_slice, 0, unroll=4)
 
 
 def prepared(slots, slices_owned, rows, full_rows, angles, defocus):
@@ -376,7 +376,7 @@
     out_ref, out, sems = refs[len(slots) * row_devices :]
     rows = total_ref.shape[0] // XBLK
     parts = corrected_patches(slots, row_devices, rows_ref, patch_refs)
-    step = 2
+    step = 4
     copies = []
     for group in range(out.shape[0] // step):
         here = slice(group * step * XBW, (group + 1) * step * XBW)
@@ -432,7 +432,7 @@
         [total],
         out_shape=jax.ShapeDtypeStruct(shape, jnp.bfloat16),
         out_specs=pl.BlockSpec(memory_space=pl.ANY),
-        scratch_shapes=[pltpu.VMEM(shape, jnp.bfloat16), pltpu.SemaphoreType.DMA((shape[0] // 2,))],
+        scratch_shapes=[pltpu.VMEM(shape, jnp.bfloat16), pltpu.SemaphoreType.DMA((shape[0] // 4,))],
         name="finish_volume",
     )
 

time: 24.7 us -> 24.7 us (level)
  no operation moved by 1% of the time
where the time goes in v19:
time: 24.7 us; the launch traced here: 24.5 us
  starting transfers between devices  10.7 us (43%)
  Pallas kernels  9.33 us (38%)
  waiting for transfers between devices  3.48 us (14%)
  local copies, waits for them, and re-layouts  0.91 us (4%)
    ppermute x12, starting transfers between devices, exchange(): return lax.ppermute(array, axis, [(i, i ^ distance) for i in range(count)])  10.7 us
    pallas_call x1, Pallas kernels, column_filtered(): pl.pallas_call(functools.partial(column_kernel, slots, slices_owned), out...  4.5 us
    ppermute x12, waiting for transfers between devices, exchange(): return lax.ppermute(array, axis, [(i, i ^ distance) for i in range(count)])  3.48 us
    pallas_call x2, Pallas kernels, interpolation(): pl.pallas_call(functools.partial(kernel, slots, len(patches[0])), in_spec...  2.56 us
    pallas_call x1, Pallas kernels, prepared(): pl.pallas_call(functools.partial(prepare_kernel, slots, slices_owned), ou...  2.27 us
    unnamed x7, local copies, waits for them, and re-layouts  0.9 us
  transfers between devices with their start and end apart: 12, of which 3 were waited for; matrix products, arithmetic and copies ran while one was open for 4% of the time, Pallas kernels for 13%

profile of v19, /device:TPU:0, one launch (start us, length us, event | category | flops | bytes accessed | tf_op | source)
XLA Modules:
  0.0 24.5 jit_solution(2964955158129559548)
XLA Ops:
  0.0 4.5 %column_filter.1 = (bf16[272,128]{1,0:T(8,128)(2,1)}, bf16[272,128]{1,0:T(8,128)(2,1)}, bf16[272,128]{1,0:T(8,128)(2,1)}, bf16[272,128]{1,0:T(8,128)(2,1)}) custom-call(bf16[64,2048]{1,0:T(8,128)(2,1)} %bitcast.1, bf16[5,256,512]{2,1,0:T(8,128)(2,1)} %constant.4.clone.matrix_ref, f32[4]{0:T(128)} %angle_ref.1, s32[4,4]{1,0:T(4,128)} %defocus_ref.1, ...), custom_call_target="tpu_custom_call" | custom-call | flops 822083584 | bytes 3145728 | tf_op jit(solution)/shard_map/column_filter/pallas_call | solution.py:233
  4.5 3.1 %collective-permute-start = (bf16[272,128]{1,0:T(8,128)(2,1)}, bf16[272,128]{1,0:T(8,128)(2,1)S(1)}, u32[]{:S(2)}, u32[]{:S(2)}) collective-permute-start(bf16[272,128]{1,0:T(8,128)(2,1)} %get-tuple-element.14), channel_id=1, source_target_pairs={{0,1},{1,0},{2,3},{3,2},{4,5},{5,4},{6,7},{7,6},{8,9},{9,8},{10,11... | collective-permute-start | bytes 208904 | tf_op jit(solution)/shard_map/ppermute | solution.py:442
  7.6 2.5 %collective-permute-start.4 = (bf16[272,128]{1,0:T(8,128)(2,1)}, bf16[272,128]{1,0:T(8,128)(2,1)S(1)}, u32[]{:S(2)}, u32[]{:S(2)}) collective-permute-start(bf16[272,128]{1,0:T(8,128)(2,1)} %get-tuple-element.15), channel_id=1, source_target_pairs={{0,3},{1,2},{2,1},{3,0},{4,7},{5,6},{6,5},{7,4},{8,11},{9,10},{10,... | collective-permute-start | bytes 208904 | tf_op jit(solution)/shard_map/ppermute | solution.py:442
  10.1 0.1 collective-permute-start.8
  10.2 0.9 %constant_dynamic-update-slice_fusion.1 = bf16[544,128]{1,0:T(8,128)(2,1)S(1)} fusion(bf16[272,128]{1,0:T(8,128)(2,1)} %get-tuple-element.13), kind=kLoop, calls=%fused_computation.1 | loop fusion | bytes 139264
  11.1 0.0 collective-permute-done
  11.1 1.6 %collective-permute-start.2 = (bf16[544,128]{1,0:T(8,128)(2,1)S(1)}, bf16[544,128]{1,0:T(8,128)(2,1)S(1)}, u32[]{:S(2)}, u32[]{:S(2)}) collective-permute-start(bf16[544,128]{1,0:T(8,128)(2,1)S(1)} %constant_dynamic-update-slice_fusion.refs_0_), channel_id=1, source_target_pairs={{0,8},{4,12},{8,0},{12,4},{1,9},{5,13},{9,1},{13,5},{2,10},{6,14},... | collective-permute-start | bytes 417800 | tf_op jit(solution)/shard_map/ppermute | solution.py:442
  12.7 0.0 collective-permute-start.1
  12.7 2.3 %prepare.1 = (bf16[256,256]{1,0:T(8,128)(2,1)S(1)}, bf16[4,160,2048]{2,1,0:T(8,128)(2,1)S(1)}) custom-call(f32[4]{0:T(128)S(1)} %copy-done.1, s32[4,4]{1,0:T(4,128)S(1)} %copy-done, bf16[2,256,256]{2,1,0:T(8,128)(2,1)S(1)} %copy-done.2), custom_call_target="tpu_custom_call" | custom-call | flops 2147483648 | bytes 6291456 | tf_op jit(solution)/shard_map/prepare/pallas_call | solution.py:319
  15.0 0.0 collective-permute-done.4.refs_0_
  15.0 1.4 %collective-permute-start.6 = (bf16[272,128]{1,0:T(8,128)(2,1)S(1)}, bf16[272,128]{1,0:T(8,128)(2,1)S(1)}, u32[]{:S(2)}, u32[]{:S(2)}) collective-permute-start(bf16[272,128]{1,0:T(8,128)(2,1)S(1)} %collective-permute-done.4.refs_0_), channel_id=1, source_target_pairs={{0,8},{4,12},{8,0},{12,4},{1,9},{5,13},{9,1},{13,5},{2,10},{6,14},... | collective-permute-start | bytes 208904 | tf_op jit(solution)/shard_map/ppermute | solution.py:442
  16.4 0.0 collective-permute-done.2.refs_2_
  16.4 0.7 %collective-permute-done.8.refs_0_ = bf16[272,128]{1,0:T(8,128)(2,1)S(1)} collective-permute-done((bf16[272,128]{1,0:T(8,128)(2,1)}, bf16[272,128]{1,0:T(8,128)(2,1)S(1)}, u32[]{:S(2)}, u32[]{:S(2)}) %collective-permute-start.8) | collective-permute-done | bytes 69664 | tf_op jit(solution)/shard_map/ppermute | solution.py:442
  17.1 1.5 %collective-permute-start.10 = (bf16[272,128]{1,0:T(8,128)(2,1)S(1)}, bf16[272,128]{1,0:T(8,128)(2,1)S(1)}, u32[]{:S(2)}, u32[]{:S(2)}) collective-permute-start(bf16[272,128]{1,0:T(8,128)(2,1)S(1)} %after.1.refs_4_), channel_id=1, source_target_pairs={{0,8},{4,12},{8,0},{12,4},{1,9},{5,13},{9,1},{13,5},{2,10},{6,14},... | collective-permute-start | bytes 208904 | tf_op jit(solution)/shard_map/ppermute | solution.py:442
  18.6 0.0 collective-permute-start.9
  18.6 1.2 %collective-permute-done.6.refs_2_ = bf16[272,128]{1,0:T(8,128)(2,1)S(1)} collective-permute-done((bf16[272,128]{1,0:T(8,128)(2,1)S(1)}, bf16[272,128]{1,0:T(8,128)(2,1)S(1)}, u32[]{:S(2)}, u32[]{:S(2)}) %collective-permute-start.6) | collective-permute-done | bytes 69664 | tf_op jit(solution)/shard_map/ppermute | solution.py:442
  19.7 0.0 collective-permute-start.5
  19.7 1.6 %collective-permute-done.10.refs_6_ = bf16[272,128]{1,0:T(8,128)(2,1)S(1)} collective-permute-done((bf16[272,128]{1,0:T(8,128)(2,1)S(1)}, bf16[272,128]{1,0:T(8,128)(2,1)S(1)}, u32[]{:S(2)}, u32[]{:S(2)}) %collective-permute-start.10) | collective-permute-done | bytes 69664 | tf_op jit(solution)/shard_map/ppermute | solution.py:442
  21.4 0.5 %collective-permute-start.11 = (bf16[272,128]{1,0:T(8,128)(2,1)S(1)}, bf16[272,128]{1,0:T(8,128)(2,1)S(1)}, u32[]{:S(2)}, u32[]{:S(2)}) collective-permute-start(bf16[272,128]{1,0:T(8,128)(2,1)S(1)} %collective-permute-done.10.refs_6_), channel_id=1, source_target_pairs={{0,4},{4,0},{8,12},{12,8},{1,5},{5,1},{9,13},{13,9},{2,6},{6,2},{1... | collective-permute-start | bytes 208904 | tf_op jit(solution)/shard_map/ppermute | solution.py:442
  21.9 0.9 %sum_early_tilts.1.total_ref = f32[256,2048]{1,0:T(8,128)S(1)} custom-call(bf16[256,256]{1,0:T(8,128)(2,1)S(1)} %get-tuple-element.11.rows_ref.refs_1_, bf16[4,160,2048]{2,1,0:T(8,128)(2,1)S(1)} %get-tuple-element.12.weights_ref, bf16[544,128]{1,0:T(8,128)(2,1)S(1)} %constant_dynamic-update-slice_fusion.refs_0_, ...), custom_call_target="tpu_custom_call" | custom-call | tf_op jit(solution)/shard_map/sum_early_tilts/pallas_call | solution.py:401
  22.8 0.0 collective-permute-done.5.refs_1_
  22.8 0.0 collective-permute-done.9.refs_5_
  22.8 0.0 collective-permute-done.11.refs_7_
  22.8 1.7 %finish_volume.1 = bf16[16,64,512]{2,1,0:T(8,128)(2,1)} custom-call(bf16[256,256]{1,0:T(8,128)(2,1)S(1)} %get-tuple-element.11.rows_ref.refs_1_, bf16[4,160,2048]{2,1,0:T(8,128)(2,1)S(1)} %get-tuple-element.12.weights_ref, f32[256,2048]{1,0:T(8,128)S(1)} %sum_early_tilts.1.total_ref, bf16[272,128]{1,0:T(8,128)(2,1)S(1)} %collective-permute-done.4.refs_0_, ...), custom_call_target="tpu_custom_call" | custom-call | tf_op jit(solution)/shard_map/finish_volume/pallas_call | solution.py:401
  (13 shorter events, 0.0 us)
Async XLA Ops:
  0.0 12.7 %copy-start.2 = (bf16[2,256,256]{2,1,0:T(8,128)(2,1)S(1)}, bf16[2,256,256]{2,1,0:T(8,128)(2,1)}, u32[]{:S(2)}) copy-start(bf16[2,256,256]{2,1,0:T(8,128)(2,1)} %constant.5.clone.waves) | copy-start | bytes 786436
  0.0 12.7 %copy-start = (s32[4,4]{1,0:T(4,128)S(1)}, s32[4,4]{1,0:T(4,128)}, u32[]{:S(2)}) copy-start(s32[4,4]{1,0:T(4,128)} %defocus_ref.1) | copy-start | bytes 196
  0.0 12.7 %copy-start.1 = (f32[4]{0:T(128)S(1)}, f32[4]{0:T(128)}, u32[]{:S(2)}) copy-start(f32[4]{0:T(128)} %angle_ref.1) | copy-start | bytes 52
  4.5 6.6 %collective-permute-start = (bf16[272,128]{1,0:T(8,128)(2,1)}, bf16[272,128]{1,0:T(8,128)(2,1)S(1)}, u32[]{:S(2)}, u32[]{:S(2)}) collective-permute-start(bf16[272,128]{1,0:T(8,128)(2,1)} %get-tuple-element.14), channel_id=1, source_target_pairs={{0,1},{1,0},{2,3},{3,2},{4,5},{5,4},{6,7},{7,6},{8,9},{9,8},{10,11... | collective-permute-start | bytes 208904 | tf_op jit(solution)/shard_map/ppermute | solution.py:442
  7.6 7.4 %collective-permute-start.4 = (bf16[272,128]{1,0:T(8,128)(2,1)}, bf16[272,128]{1,0:T(8,128)(2,1)S(1)}, u32[]{:S(2)}, u32[]{:S(2)}) collective-permute-start(bf16[272,128]{1,0:T(8,128)(2,1)} %get-tuple-element.15), channel_id=1, source_target_pairs={{0,3},{1,2},{2,1},{3,0},{4,7},{5,6},{6,5},{7,4},{8,11},{9,10},{10,... | collective-permute-start | bytes 208904 | tf_op jit(solution)/shard_map/ppermute | solution.py:442
  10.1 7.0 %collective-permute-start.8 = (bf16[272,128]{1,0:T(8,128)(2,1)}, bf16[272,128]{1,0:T(8,128)(2,1)S(1)}, u32[]{:S(2)}, u32[]{:S(2)}) collective-permute-start(bf16[272,128]{1,0:T(8,128)(2,1)} %get-tuple-element.16), channel_id=1, source_target_pairs={{0,2},{1,3},{2,0},{3,1},{4,6},{5,7},{6,4},{7,5},{8,10},{9,11},{10,... | collective-permute-start | bytes 208904 | tf_op jit(solution)/shard_map/ppermute | solution.py:442
  11.1 5.3 %collective-permute-start.2 = (bf16[544,128]{1,0:T(8,128)(2,1)S(1)}, bf16[544,128]{1,0:T(8,128)(2,1)S(1)}, u32[]{:S(2)}, u32[]{:S(2)}) collective-permute-start(bf16[544,128]{1,0:T(8,128)(2,1)S(1)} %constant_dynamic-update-slice_fusion.refs_0_), channel_id=1, source_target_pairs={{0,8},{4,12},{8,0},{12,4},{1,9},{5,13},{9,1},{13,5},{2,10},{6,14},... | collective-permute-start | bytes 417800 | tf_op jit(solution)/shard_map/ppermute | solution.py:442
  12.7 8.7 %collective-permute-start.1 = (bf16[544,128]{1,0:T(8,128)(2,1)S(1)}, bf16[544,128]{1,0:T(8,128)(2,1)S(1)}, u32[]{:S(2)}, u32[]{:S(2)}) collective-permute-start(bf16[544,128]{1,0:T(8,128)(2,1)S(1)} %constant_dynamic-update-slice_fusion.refs_0_), channel_id=1, source_target_pairs={{0,4},{4,0},{8,12},{12,8},{1,5},{5,1},{9,13},{13,9},{2,6},{6,2},{1... | collective-permute-start | bytes 417800 | tf_op jit(solution)/shard_map/ppermute | solution.py:442
  15.0 4.7 %collective-permute-start.6 = (bf16[272,128]{1,0:T(8,128)(2,1)S(1)}, bf16[272,128]{1,0:T(8,128)(2,1)S(1)}, u32[]{:S(2)}, u32[]{:S(2)}) collective-permute-start(bf16[272,128]{1,0:T(8,128)(2,1)S(1)} %collective-permute-done.4.refs_0_), channel_id=1, source_target_pairs={{0,8},{4,12},{8,0},{12,4},{1,9},{5,13},{9,1},{13,5},{2,10},{6,14},... | collective-permute-start | bytes 208904 | tf_op jit(solution)/shard_map/ppermute | solution.py:442
  16.4 5.5 %collective-permute-start.3 = (bf16[544,128]{1,0:T(8,128)(2,1)S(1)}, bf16[544,128]{1,0:T(8,128)(2,1)S(1)}, u32[]{:S(2)}, u32[]{:S(2)}) collective-permute-start(bf16[544,128]{1,0:T(8,128)(2,1)S(1)} %collective-permute-done.2.refs_2_), channel_id=1, source_target_pairs={{0,4},{4,0},{8,12},{12,8},{1,5},{5,1},{9,13},{13,9},{2,6},{6,2},{1... | collective-permute-start | bytes 417800 | tf_op jit(solution)/shard_map/ppermute | solution.py:442
  17.1 4.3 %collective-permute-start.10 = (bf16[272,128]{1,0:T(8,128)(2,1)S(1)}, bf16[272,128]{1,0:T(8,128)(2,1)S(1)}, u32[]{:S(2)}, u32[]{:S(2)}) collective-permute-start(bf16[272,128]{1,0:T(8,128)(2,1)S(1)} %after.1.refs_4_), channel_id=1, source_target_pairs={{0,8},{4,12},{8,0},{12,4},{1,9},{5,13},{9,1},{13,5},{2,10},{6,14},... | collective-permute-start | bytes 208904 | tf_op jit(solution)/shard_map/ppermute | solution.py:442
  18.6 4.2 %collective-permute-start.9 = (bf16[272,128]{1,0:T(8,128)(2,1)S(1)}, bf16[272,128]{1,0:T(8,128)(2,1)S(1)}, u32[]{:S(2)}, u32[]{:S(2)}) collective-permute-start(bf16[272,128]{1,0:T(8,128)(2,1)S(1)} %after.1.refs_4_), channel_id=1, source_target_pairs={{0,4},{4,0},{8,12},{12,8},{1,5},{5,1},{9,13},{13,9},{2,6},{6,2},{1... | collective-permute-start | bytes 208904 | tf_op jit(solution)/shard_map/ppermute | solution.py:442
  19.7 3.1 %collective-permute-start.5 = (bf16[272,128]{1,0:T(8,128)(2,1)S(1)}, bf16[272,128]{1,0:T(8,128)(2,1)S(1)}, u32[]{:S(2)}, u32[]{:S(2)}) collective-permute-start(bf16[272,128]{1,0:T(8,128)(2,1)S(1)} %collective-permute-done.4.refs_0_), channel_id=1, source_target_pairs={{0,4},{4,0},{8,12},{12,8},{1,5},{5,1},{9,13},{13,9},{2,6},{6,2},{1... | collective-permute-start | bytes 208904 | tf_op jit(solution)/shard_map/ppermute | solution.py:442
  21.4 1.5 %collective-permute-start.7 = (bf16[272,128]{1,0:T(8,128)(2,1)S(1)}, bf16[272,128]{1,0:T(8,128)(2,1)S(1)}, u32[]{:S(2)}, u32[]{:S(2)}) collective-permute-start(bf16[272,128]{1,0:T(8,128)(2,1)S(1)} %collective-permute-done.6.refs_2_), channel_id=1, source_target_pairs={{0,4},{4,0},{8,12},{12,8},{1,5},{5,1},{9,13},{13,9},{2,6},{6,2},{1... | collective-permute-start | bytes 208904 | tf_op jit(solution)/shard_map/ppermute | solution.py:442
  21.4 1.5 %collective-permute-start.11 = (bf16[272,128]{1,0:T(8,128)(2,1)S(1)}, bf16[272,128]{1,0:T(8,128)(2,1)S(1)}, u32[]{:S(2)}, u32[]{:S(2)}) collective-permute-start(bf16[272,128]{1,0:T(8,128)(2,1)S(1)} %collective-permute-done.10.refs_6_), channel_id=1, source_target_pairs={{0,4},{4,0},{8,12},{12,8},{1,5},{5,1},{9,13},{13,9},{2,6},{6,2},{1... | collective-permute-start | bytes 208904 | tf_op jit(solution)/shard_map/ppermute | solution.py:442

commit v20 on v15

--- a/solution.py
+++ b/solution.py
@@ -159,10 +159,9 @@
         for i in range(6):
             waves[i, mine, :] = both[i * rows : (i + 1) * rows]
     sends = []
-    transform(0)
+    for k in range(len(slabs)):
+        transform(k)
     for k, slab in enumerate(slabs):
-        if k + 1 < len(slabs):
-            transform(k + 1)
         inverse_butterflies(ends, waves, turns, turned, k * rows, rows)
         rest = jnp.zeros((rows, MAIN), jnp.float32)
         for block in range(XBLK):

time: 24.7 us -> 24.7 us (level)
  no operation moved by 1% of the time
where the time goes in v20:
time: 24.7 us; the launch traced here: 24.5 us
  starting transfers between devices  10.7 us (43%)
  Pallas kernels  9.34 us (38%)
  waiting for transfers between devices  3.47 us (14%)
  local copies, waits for them, and re-layouts  0.91 us (4%)
    ppermute x12, starting transfers between devices, exchange(): return lax.ppermute(array, axis, [(i, i ^ distance) for i in range(count)])  10.7 us
    pallas_call x1, Pallas kernels, column_filtered(): pl.pallas_call(functools.partial(column_kernel, slots, slices_owned), out...  4.54 us
    ppermute x12, waiting for transfers between devices, exchange(): return lax.ppermute(array, axis, [(i, i ^ distance) for i in range(count)])  3.47 us
    pallas_call x2, Pallas kernels, interpolation(): pl.pallas_call(functools.partial(kernel, slots, len(patches[0])), in_spec...  2.55 us
    pallas_call x1, Pallas kernels, prepared(): pl.pallas_call(functools.partial(prepare_kernel, slots, slices_owned), ou...  2.25 us
    unnamed x7, local copies, waits for them, and re-layouts  0.9 us
  transfers between devices with their start and end apart: 12, of which 3 were waited for; matrix products, arithmetic and copies ran while one was open for 4% of the time, Pallas kernels for 13%

profile of v20, /device:TPU:0, one launch (start us, length us, event | category | flops | bytes accessed | tf_op | source)
XLA Modules:
  0.0 24.5 jit_solution(7090877225923544875)
XLA Ops:
  0.0 4.5 %column_filter.1 = (bf16[272,128]{1,0:T(8,128)(2,1)}, bf16[272,128]{1,0:T(8,128)(2,1)}, bf16[272,128]{1,0:T(8,128)(2,1)}, bf16[272,128]{1,0:T(8,128)(2,1)}) custom-call(bf16[64,2048]{1,0:T(8,128)(2,1)} %bitcast.1, bf16[5,256,512]{2,1,0:T(8,128)(2,1)} %constant.4.clone.matrix_ref, f32[4]{0:T(128)} %angle_ref.1, s32[4,4]{1,0:T(4,128)} %defocus_ref.1, ...), custom_call_target="tpu_custom_call" | custom-call | flops 822083584 | bytes 3145728 | tf_op jit(solution)/shard_map/column_filter/pallas_call | solution.py:234
  4.6 3.1 %collective-permute-start = (bf16[272,128]{1,0:T(8,128)(2,1)}, bf16[272,128]{1,0:T(8,128)(2,1)S(1)}, u32[]{:S(2)}, u32[]{:S(2)}) collective-permute-start(bf16[272,128]{1,0:T(8,128)(2,1)} %get-tuple-element.14), channel_id=1, source_target_pairs={{0,1},{1,0},{2,3},{3,2},{4,5},{5,4},{6,7},{7,6},{8,9},{9,8},{10,11... | collective-permute-start | bytes 208904 | tf_op jit(solution)/shard_map/ppermute | solution.py:443
  7.6 2.5 %collective-permute-start.4 = (bf16[272,128]{1,0:T(8,128)(2,1)}, bf16[272,128]{1,0:T(8,128)(2,1)S(1)}, u32[]{:S(2)}, u32[]{:S(2)}) collective-permute-start(bf16[272,128]{1,0:T(8,128)(2,1)} %get-tuple-element.15), channel_id=1, source_target_pairs={{0,3},{1,2},{2,1},{3,0},{4,7},{5,6},{6,5},{7,4},{8,11},{9,10},{10,... | collective-permute-start | bytes 208904 | tf_op jit(solution)/shard_map/ppermute | solution.py:443
  10.1 0.1 collective-permute-start.8
  10.2 0.9 %constant_dynamic-update-slice_fusion.1 = bf16[544,128]{1,0:T(8,128)(2,1)S(1)} fusion(bf16[272,128]{1,0:T(8,128)(2,1)} %get-tuple-element.13), kind=kLoop, calls=%fused_computation.1 | loop fusion | bytes 139264
  11.1 0.0 collective-permute-done
  11.1 1.6 %collective-permute-start.2 = (bf16[544,128]{1,0:T(8,128)(2,1)S(1)}, bf16[544,128]{1,0:T(8,128)(2,1)S(1)}, u32[]{:S(2)}, u32[]{:S(2)}) collective-permute-start(bf16[544,128]{1,0:T(8,128)(2,1)S(1)} %constant_dynamic-update-slice_fusion.refs_0_), channel_id=1, source_target_pairs={{0,8},{4,12},{8,0},{12,4},{1,9},{5,13},{9,1},{13,5},{2,10},{6,14},... | collective-permute-start | bytes 417800 | tf_op jit(solution)/shard_map/ppermute | solution.py:443
  12.7 0.0 collective-permute-start.1
  12.7 2.2 %prepare.1 = (bf16[256,256]{1,0:T(8,128)(2,1)S(1)}, bf16[4,160,2048]{2,1,0:T(8,128)(2,1)S(1)}) custom-call(f32[4]{0:T(128)S(1)} %copy-done.1, s32[4,4]{1,0:T(4,128)S(1)} %copy-done, bf16[2,256,256]{2,1,0:T(8,128)(2,1)S(1)} %copy-done.2), custom_call_target="tpu_custom_call" | custom-call | flops 2147483648 | bytes 6291456 | tf_op jit(solution)/shard_map/prepare/pallas_call | solution.py:320
  15.0 0.0 collective-permute-done.4.refs_0_
  15.0 1.4 %collective-permute-start.6 = (bf16[272,128]{1,0:T(8,128)(2,1)S(1)}, bf16[272,128]{1,0:T(8,128)(2,1)S(1)}, u32[]{:S(2)}, u32[]{:S(2)}) collective-permute-start(bf16[272,128]{1,0:T(8,128)(2,1)S(1)} %collective-permute-done.4.refs_0_), channel_id=1, source_target_pairs={{0,8},{4,12},{8,0},{12,4},{1,9},{5,13},{9,1},{13,5},{2,10},{6,14},... | collective-permute-start | bytes 208904 | tf_op jit(solution)/shard_map/ppermute | solution.py:443
  16.4 0.0 collective-permute-done.2.refs_2_
  16.4 0.0 collective-permute-start.3
  16.4 0.7 %collective-permute-done.8.refs_0_ = bf16[272,128]{1,0:T(8,128)(2,1)S(1)} collective-permute-done((bf16[272,128]{1,0:T(8,128)(2,1)}, bf16[272,128]{1,0:T(8,128)(2,1)S(1)}, u32[]{:S(2)}, u32[]{:S(2)}) %collective-permute-start.8) | collective-permute-done | bytes 69664 | tf_op jit(solution)/shard_map/ppermute | solution.py:443
  17.1 1.5 %collective-permute-start.10 = (bf16[272,128]{1,0:T(8,128)(2,1)S(1)}, bf16[272,128]{1,0:T(8,128)(2,1)S(1)}, u32[]{:S(2)}, u32[]{:S(2)}) collective-permute-start(bf16[272,128]{1,0:T(8,128)(2,1)S(1)} %after.1.refs_4_), channel_id=1, source_target_pairs={{0,8},{4,12},{8,0},{12,4},{1,9},{5,13},{9,1},{13,5},{2,10},{6,14},... | collective-permute-start | bytes 208904 | tf_op jit(solution)/shard_map/ppermute | solution.py:443
  18.6 0.0 collective-permute-start.9
  18.6 1.1 %collective-permute-done.6.refs_2_ = bf16[272,128]{1,0:T(8,128)(2,1)S(1)} collective-permute-done((bf16[272,128]{1,0:T(8,128)(2,1)S(1)}, bf16[272,128]{1,0:T(8,128)(2,1)S(1)}, u32[]{:S(2)}, u32[]{:S(2)}) %collective-permute-start.6) | collective-permute-done | bytes 69664 | tf_op jit(solution)/shard_map/ppermute | solution.py:443
  19.7 0.0 collective-permute-start.5
  19.7 1.7 %collective-permute-done.10.refs_6_ = bf16[272,128]{1,0:T(8,128)(2,1)S(1)} collective-permute-done((bf16[272,128]{1,0:T(8,128)(2,1)S(1)}, bf16[272,128]{1,0:T(8,128)(2,1)S(1)}, u32[]{:S(2)}, u32[]{:S(2)}) %collective-permute-start.10) | collective-permute-done | bytes 69664 | tf_op jit(solution)/shard_map/ppermute | solution.py:443
  21.4 0.5 %collective-permute-start.11 = (bf16[272,128]{1,0:T(8,128)(2,1)S(1)}, bf16[272,128]{1,0:T(8,128)(2,1)S(1)}, u32[]{:S(2)}, u32[]{:S(2)}) collective-permute-start(bf16[272,128]{1,0:T(8,128)(2,1)S(1)} %collective-permute-done.10.refs_6_), channel_id=1, source_target_pairs={{0,4},{4,0},{8,12},{12,8},{1,5},{5,1},{9,13},{13,9},{2,6},{6,2},{1... | collective-permute-start | bytes 208904 | tf_op jit(solution)/shard_map/ppermute | solution.py:443
  21.9 0.9 %sum_early_tilts.1.total_ref = f32[256,2048]{1,0:T(8,128)S(1)} custom-call(bf16[256,256]{1,0:T(8,128)(2,1)S(1)} %get-tuple-element.11.rows_ref.refs_1_, bf16[4,160,2048]{2,1,0:T(8,128)(2,1)S(1)} %get-tuple-element.12.weights_ref, bf16[544,128]{1,0:T(8,128)(2,1)S(1)} %constant_dynamic-update-slice_fusion.refs_0_, ...), custom_call_target="tpu_custom_call" | custom-call | tf_op jit(solution)/shard_map/sum_early_tilts/pallas_call | solution.py:402
  22.8 0.0 collective-permute-done.9.refs_5_
  22.8 0.0 collective-permute-done.7.refs_3_
  22.9 1.6 %finish_volume.1 = bf16[16,64,512]{2,1,0:T(8,128)(2,1)} custom-call(bf16[256,256]{1,0:T(8,128)(2,1)S(1)} %get-tuple-element.11.rows_ref.refs_1_, bf16[4,160,2048]{2,1,0:T(8,128)(2,1)S(1)} %get-tuple-element.12.weights_ref, f32[256,2048]{1,0:T(8,128)S(1)} %sum_early_tilts.1.total_ref, bf16[272,128]{1,0:T(8,128)(2,1)S(1)} %collective-permute-done.4.refs_0_, ...), custom_call_target="tpu_custom_call" | custom-call | tf_op jit(solution)/shard_map/finish_volume/pallas_call | solution.py:402
  (13 shorter events, 0.0 us)
Async XLA Ops:
  0.0 12.7 %copy-start.2 = (bf16[2,256,256]{2,1,0:T(8,128)(2,1)S(1)}, bf16[2,256,256]{2,1,0:T(8,128)(2,1)}, u32[]{:S(2)}) copy-start(bf16[2,256,256]{2,1,0:T(8,128)(2,1)} %constant.5.clone.waves) | copy-start | bytes 786436
  0.0 12.7 %copy-start = (s32[4,4]{1,0:T(4,128)S(1)}, s32[4,4]{1,0:T(4,128)}, u32[]{:S(2)}) copy-start(s32[4,4]{1,0:T(4,128)} %defocus_ref.1) | copy-start | bytes 196
  0.0 12.7 %copy-start.1 = (f32[4]{0:T(128)S(1)}, f32[4]{0:T(128)}, u32[]{:S(2)}) copy-start(f32[4]{0:T(128)} %angle_ref.1) | copy-start | bytes 52
  4.6 6.6 %collective-permute-start = (bf16[272,128]{1,0:T(8,128)(2,1)}, bf16[272,128]{1,0:T(8,128)(2,1)S(1)}, u32[]{:S(2)}, u32[]{:S(2)}) collective-permute-start(bf16[272,128]{1,0:T(8,128)(2,1)} %get-tuple-element.14), channel_id=1, source_target_pairs={{0,1},{1,0},{2,3},{3,2},{4,5},{5,4},{6,7},{7,6},{8,9},{9,8},{10,11... | collective-permute-start | bytes 208904 | tf_op jit(solution)/shard_map/ppermute | solution.py:443
  7.6 7.4 %collective-permute-start.4 = (bf16[272,128]{1,0:T(8,128)(2,1)}, bf16[272,128]{1,0:T(8,128)(2,1)S(1)}, u32[]{:S(2)}, u32[]{:S(2)}) collective-permute-start(bf16[272,128]{1,0:T(8,128)(2,1)} %get-tuple-element.15), channel_id=1, source_target_pairs={{0,3},{1,2},{2,1},{3,0},{4,7},{5,6},{6,5},{7,4},{8,11},{9,10},{10,... | collective-permute-start | bytes 208904 | tf_op jit(solution)/shard_map/ppermute | solution.py:443
  10.1 7.0 %collective-permute-start.8 = (bf16[272,128]{1,0:T(8,128)(2,1)}, bf16[272,128]{1,0:T(8,128)(2,1)S(1)}, u32[]{:S(2)}, u32[]{:S(2)}) collective-permute-start(bf16[272,128]{1,0:T(8,128)(2,1)} %get-tuple-element.16), channel_id=1, source_target_pairs={{0,2},{1,3},{2,0},{3,1},{4,6},{5,7},{6,4},{7,5},{8,10},{9,11},{10,... | collective-permute-start | bytes 208904 | tf_op jit(solution)/shard_map/ppermute | solution.py:443
  11.1 5.3 %collective-permute-start.2 = (bf16[544,128]{1,0:T(8,128)(2,1)S(1)}, bf16[544,128]{1,0:T(8,128)(2,1)S(1)}, u32[]{:S(2)}, u32[]{:S(2)}) collective-permute-start(bf16[544,128]{1,0:T(8,128)(2,1)S(1)} %constant_dynamic-update-slice_fusion.refs_0_), channel_id=1, source_target_pairs={{0,8},{4,12},{8,0},{12,4},{1,9},{5,13},{9,1},{13,5},{2,10},{6,14},... | collective-permute-start | bytes 417800 | tf_op jit(solution)/shard_map/ppermute | solution.py:443
  12.7 8.7 %collective-permute-start.1 = (bf16[544,128]{1,0:T(8,128)(2,1)S(1)}, bf16[544,128]{1,0:T(8,128)(2,1)S(1)}, u32[]{:S(2)}, u32[]{:S(2)}) collective-permute-start(bf16[544,128]{1,0:T(8,128)(2,1)S(1)} %constant_dynamic-update-slice_fusion.refs_0_), channel_id=1, source_target_pairs={{0,4},{4,0},{8,12},{12,8},{1,5},{5,1},{9,13},{13,9},{2,6},{6,2},{1... | collective-permute-start | bytes 417800 | tf_op jit(solution)/shard_map/ppermute | solution.py:443
  15.0 4.7 %collective-permute-start.6 = (bf16[272,128]{1,0:T(8,128)(2,1)S(1)}, bf16[272,128]{1,0:T(8,128)(2,1)S(1)}, u32[]{:S(2)}, u32[]{:S(2)}) collective-permute-start(bf16[272,128]{1,0:T(8,128)(2,1)S(1)} %collective-permute-done.4.refs_0_), channel_id=1, source_target_pairs={{0,8},{4,12},{8,0},{12,4},{1,9},{5,13},{9,1},{13,5},{2,10},{6,14},... | collective-permute-start | bytes 208904 | tf_op jit(solution)/shard_map/ppermute | solution.py:443
  16.4 5.5 %collective-permute-start.3 = (bf16[544,128]{1,0:T(8,128)(2,1)S(1)}, bf16[544,128]{1,0:T(8,128)(2,1)S(1)}, u32[]{:S(2)}, u32[]{:S(2)}) collective-permute-start(bf16[544,128]{1,0:T(8,128)(2,1)S(1)} %collective-permute-done.2.refs_2_), channel_id=1, source_target_pairs={{0,4},{4,0},{8,12},{12,8},{1,5},{5,1},{9,13},{13,9},{2,6},{6,2},{1... | collective-permute-start | bytes 417800 | tf_op jit(solution)/shard_map/ppermute | solution.py:443
  17.1 4.3 %collective-permute-start.10 = (bf16[272,128]{1,0:T(8,128)(2,1)S(1)}, bf16[272,128]{1,0:T(8,128)(2,1)S(1)}, u32[]{:S(2)}, u32[]{:S(2)}) collective-permute-start(bf16[272,128]{1,0:T(8,128)(2,1)S(1)} %after.1.refs_4_), channel_id=1, source_target_pairs={{0,8},{4,12},{8,0},{12,4},{1,9},{5,13},{9,1},{13,5},{2,10},{6,14},... | collective-permute-start | bytes 208904 | tf_op jit(solution)/shard_map/ppermute | solution.py:443
  18.6 4.2 %collective-permute-start.9 = (bf16[272,128]{1,0:T(8,128)(2,1)S(1)}, bf16[272,128]{1,0:T(8,128)(2,1)S(1)}, u32[]{:S(2)}, u32[]{:S(2)}) collective-permute-start(bf16[272,128]{1,0:T(8,128)(2,1)S(1)} %after.1.refs_4_), channel_id=1, source_target_pairs={{0,4},{4,0},{8,12},{12,8},{1,5},{5,1},{9,13},{13,9},{2,6},{6,2},{1... | collective-permute-start | bytes 208904 | tf_op jit(solution)/shard_map/ppermute | solution.py:443
  19.7 3.1 %collective-permute-start.5 = (bf16[272,128]{1,0:T(8,128)(2,1)S(1)}, bf16[272,128]{1,0:T(8,128)(2,1)S(1)}, u32[]{:S(2)}, u32[]{:S(2)}) collective-permute-start(bf16[272,128]{1,0:T(8,128)(2,1)S(1)} %collective-permute-done.4.refs_0_), channel_id=1, source_target_pairs={{0,4},{4,0},{8,12},{12,8},{1,5},{5,1},{9,13},{13,9},{2,6},{6,2},{1... | collective-permute-start | bytes 208904 | tf_op jit(solution)/shard_map/ppermute | solution.py:443
  21.4 1.5 %collective-permute-start.7 = (bf16[272,128]{1,0:T(8,128)(2,1)S(1)}, bf16[272,128]{1,0:T(8,128)(2,1)S(1)}, u32[]{:S(2)}, u32[]{:S(2)}) collective-permute-start(bf16[272,128]{1,0:T(8,128)(2,1)S(1)} %collective-permute-done.6.refs_2_), channel_id=1, source_target_pairs={{0,4},{4,0},{8,12},{12,8},{1,5},{5,1},{9,13},{13,9},{2,6},{6,2},{1... | collective-permute-start | bytes 208904 | tf_op jit(solution)/shard_map/ppermute | solution.py:443
  21.4 1.5 %collective-permute-start.11 = (bf16[272,128]{1,0:T(8,128)(2,1)S(1)}, bf16[272,128]{1,0:T(8,128)(2,1)S(1)}, u32[]{:S(2)}, u32[]{:S(2)}) collective-permute-start(bf16[272,128]{1,0:T(8,128)(2,1)S(1)} %collective-permute-done.10.refs_6_), channel_id=1, source_target_pairs={{0,4},{4,0},{8,12},{12,8},{1,5},{5,1},{9,13},{13,9},{2,6},{6,2},{1... | collective-permute-start | bytes 208904 | tf_op jit(solution)/shard_map/ppermute | solution.py:443

commit v21 on v15

--- a/solution.py
+++ b/solution.py
@@ -378,7 +378,7 @@
     out_ref, out, sems = refs[len(slots) * row_devices :]
     rows = total_ref.shape[0] // XBLK
     parts = corrected_patches(slots, row_devices, rows_ref, patch_refs)
-    step = 4
+    step = 8
     copies = []
     for group in range(out.shape[0] // step):
         here = slice(group * step * XBW, (group + 1) * step * XBW)

time: 24.7 us -> 24.8 us (level)
  no operation moved by 1% of the time
where the time goes in v21:
time: 24.8 us; the launch traced here: 24.6 us
  starting transfers between devices  10.7 us (43%)
  Pallas kernels  9.43 us (38%)
  waiting for transfers between devices  3.47 us (14%)
  local copies, waits for them, and re-layouts  0.91 us (4%)
    ppermute x12, starting transfers between devices, exchange(): return lax.ppermute(array, axis, [(i, i ^ distance) for i in range(count)])  10.7 us
    pallas_call x1, Pallas kernels, column_filtered(): pl.pallas_call(functools.partial(column_kernel, slots, slices_owned), out...  4.53 us
    ppermute x12, waiting for transfers between devices, exchange(): return lax.ppermute(array, axis, [(i, i ^ distance) for i in range(count)])  3.47 us
    pallas_call x2, Pallas kernels, interpolation(): pl.pallas_call(functools.partial(kernel, slots, len(patches[0])), in_spec...  2.65 us
    pallas_call x1, Pallas kernels, prepared(): pl.pallas_call(functools.partial(prepare_kernel, slots, slices_owned), ou...  2.25 us
    unnamed x7, local copies, waits for them, and re-layouts  0.9 us
  transfers between devices with their start and end apart: 12, of which 3 were waited for; matrix products, arithmetic and copies ran while one was open for 4% of the time, Pallas kernels for 13%

profile of v21, /device:TPU:0, one launch (start us, length us, event | category | flops | bytes accessed | tf_op | source)
XLA Modules:
  0.0 24.6 jit_solution(12231825846446466928)
XLA Ops:
  0.0 4.5 %column_filter.1 = (bf16[272,128]{1,0:T(8,128)(2,1)}, bf16[272,128]{1,0:T(8,128)(2,1)}, bf16[272,128]{1,0:T(8,128)(2,1)}, bf16[272,128]{1,0:T(8,128)(2,1)}) custom-call(bf16[64,2048]{1,0:T(8,128)(2,1)} %bitcast.1, bf16[5,256,512]{2,1,0:T(8,128)(2,1)} %constant.4.clone.matrix_ref, f32[4]{0:T(128)} %angle_ref.1, s32[4,4]{1,0:T(4,128)} %defocus_ref.1, ...), custom_call_target="tpu_custom_call" | custom-call | flops 822083584 | bytes 3145728 | tf_op jit(solution)/shard_map/column_filter/pallas_call | solution.py:235
  4.5 3.1 %collective-permute-start = (bf16[272,128]{1,0:T(8,128)(2,1)}, bf16[272,128]{1,0:T(8,128)(2,1)S(1)}, u32[]{:S(2)}, u32[]{:S(2)}) collective-permute-start(bf16[272,128]{1,0:T(8,128)(2,1)} %get-tuple-element.14), channel_id=1, source_target_pairs={{0,1},{1,0},{2,3},{3,2},{4,5},{5,4},{6,7},{7,6},{8,9},{9,8},{10,11... | collective-permute-start | bytes 208904 | tf_op jit(solution)/shard_map/ppermute | solution.py:444
  7.6 2.5 %collective-permute-start.4 = (bf16[272,128]{1,0:T(8,128)(2,1)}, bf16[272,128]{1,0:T(8,128)(2,1)S(1)}, u32[]{:S(2)}, u32[]{:S(2)}) collective-permute-start(bf16[272,128]{1,0:T(8,128)(2,1)} %get-tuple-element.15), channel_id=1, source_target_pairs={{0,3},{1,2},{2,1},{3,0},{4,7},{5,6},{6,5},{7,4},{8,11},{9,10},{10,... | collective-permute-start | bytes 208904 | tf_op jit(solution)/shard_map/ppermute | solution.py:444
  10.1 0.1 collective-permute-start.8
  10.2 0.9 %constant_dynamic-update-slice_fusion.1 = bf16[544,128]{1,0:T(8,128)(2,1)S(1)} fusion(bf16[272,128]{1,0:T(8,128)(2,1)} %get-tuple-element.13), kind=kLoop, calls=%fused_computation.1 | loop fusion | bytes 139264
  11.1 0.0 collective-permute-done
  11.1 1.6 %collective-permute-start.2 = (bf16[544,128]{1,0:T(8,128)(2,1)S(1)}, bf16[544,128]{1,0:T(8,128)(2,1)S(1)}, u32[]{:S(2)}, u32[]{:S(2)}) collective-permute-start(bf16[544,128]{1,0:T(8,128)(2,1)S(1)} %constant_dynamic-update-slice_fusion.refs_0_), channel_id=1, source_target_pairs={{0,8},{4,12},{8,0},{12,4},{1,9},{5,13},{9,1},{13,5},{2,10},{6,14},... | collective-permute-start | bytes 417800 | tf_op jit(solution)/shard_map/ppermute | solution.py:444
  12.7 0.0 collective-permute-start.1
  12.7 2.2 %prepare.1 = (bf16[256,256]{1,0:T(8,128)(2,1)S(1)}, bf16[4,160,2048]{2,1,0:T(8,128)(2,1)S(1)}) custom-call(f32[4]{0:T(128)S(1)} %copy-done.1, s32[4,4]{1,0:T(4,128)S(1)} %copy-done, bf16[2,256,256]{2,1,0:T(8,128)(2,1)S(1)} %copy-done.2), custom_call_target="tpu_custom_call" | custom-call | flops 2147483648 | bytes 6291456 | tf_op jit(solution)/shard_map/prepare/pallas_call | solution.py:321
  15.0 0.0 collective-permute-done.4.refs_0_
  15.0 1.4 %collective-permute-start.6 = (bf16[272,128]{1,0:T(8,128)(2,1)S(1)}, bf16[272,128]{1,0:T(8,128)(2,1)S(1)}, u32[]{:S(2)}, u32[]{:S(2)}) collective-permute-start(bf16[272,128]{1,0:T(8,128)(2,1)S(1)} %collective-permute-done.4.refs_0_), channel_id=1, source_target_pairs={{0,8},{4,12},{8,0},{12,4},{1,9},{5,13},{9,1},{13,5},{2,10},{6,14},... | collective-permute-start | bytes 208904 | tf_op jit(solution)/shard_map/ppermute | solution.py:444
  16.4 0.0 collective-permute-done.2.refs_2_
  16.4 0.0 collective-permute-start.3
  16.4 0.7 %collective-permute-done.8.refs_0_ = bf16[272,128]{1,0:T(8,128)(2,1)S(1)} collective-permute-done((bf16[272,128]{1,0:T(8,128)(2,1)}, bf16[272,128]{1,0:T(8,128)(2,1)S(1)}, u32[]{:S(2)}, u32[]{:S(2)}) %collective-permute-start.8) | collective-permute-done | bytes 69664 | tf_op jit(solution)/shard_map/ppermute | solution.py:444
  17.1 1.5 %collective-permute-start.10 = (bf16[272,128]{1,0:T(8,128)(2,1)S(1)}, bf16[272,128]{1,0:T(8,128)(2,1)S(1)}, u32[]{:S(2)}, u32[]{:S(2)}) collective-permute-start(bf16[272,128]{1,0:T(8,128)(2,1)S(1)} %after.1.refs_4_), channel_id=1, source_target_pairs={{0,8},{4,12},{8,0},{12,4},{1,9},{5,13},{9,1},{13,5},{2,10},{6,14},... | collective-permute-start | bytes 208904 | tf_op jit(solution)/shard_map/ppermute | solution.py:444
  18.6 1.1 %collective-permute-done.6.refs_2_ = bf16[272,128]{1,0:T(8,128)(2,1)S(1)} collective-permute-done((bf16[272,128]{1,0:T(8,128)(2,1)S(1)}, bf16[272,128]{1,0:T(8,128)(2,1)S(1)}, u32[]{:S(2)}, u32[]{:S(2)}) %collective-permute-start.6) | collective-permute-done | bytes 69664 | tf_op jit(solution)/shard_map/ppermute | solution.py:444
  19.7 0.0 collective-permute-start.5
  19.7 1.7 %collective-permute-done.10.refs_6_ = bf16[272,128]{1,0:T(8,128)(2,1)S(1)} collective-permute-done((bf16[272,128]{1,0:T(8,128)(2,1)S(1)}, bf16[272,128]{1,0:T(8,128)(2,1)S(1)}, u32[]{:S(2)}, u32[]{:S(2)}) %collective-permute-start.10) | collective-permute-done | bytes 69664 | tf_op jit(solution)/shard_map/ppermute | solution.py:444
  21.4 0.0 collective-permute-start.7
  21.4 0.5 %collective-permute-start.11 = (bf16[272,128]{1,0:T(8,128)(2,1)S(1)}, bf16[272,128]{1,0:T(8,128)(2,1)S(1)}, u32[]{:S(2)}, u32[]{:S(2)}) collective-permute-start(bf16[272,128]{1,0:T(8,128)(2,1)S(1)} %collective-permute-done.10.refs_6_), channel_id=1, source_target_pairs={{0,4},{4,0},{8,12},{12,8},{1,5},{5,1},{9,13},{13,9},{2,6},{6,2},{1... | collective-permute-start | bytes 208904 | tf_op jit(solution)/shard_map/ppermute | solution.py:444
  21.9 0.9 %sum_early_tilts.1.total_ref = f32[256,2048]{1,0:T(8,128)S(1)} custom-call(bf16[256,256]{1,0:T(8,128)(2,1)S(1)} %get-tuple-element.11.rows_ref.refs_1_, bf16[4,160,2048]{2,1,0:T(8,128)(2,1)S(1)} %get-tuple-element.12.weights_ref, bf16[544,128]{1,0:T(8,128)(2,1)S(1)} %constant_dynamic-update-slice_fusion.refs_0_, ...), custom_call_target="tpu_custom_call" | custom-call | tf_op jit(solution)/shard_map/sum_early_tilts/pallas_call | solution.py:403
  22.8 0.0 collective-permute-done.9.refs_5_
  22.8 0.0 collective-permute-done.7.refs_3_
  22.9 1.7 %finish_volume.1 = bf16[16,64,512]{2,1,0:T(8,128)(2,1)} custom-call(bf16[256,256]{1,0:T(8,128)(2,1)S(1)} %get-tuple-element.11.rows_ref.refs_1_, bf16[4,160,2048]{2,1,0:T(8,128)(2,1)S(1)} %get-tuple-element.12.weights_ref, f32[256,2048]{1,0:T(8,128)S(1)} %sum_early_tilts.1.total_ref, bf16[272,128]{1,0:T(8,128)(2,1)S(1)} %collective-permute-done.4.refs_0_, ...), custom_call_target="tpu_custom_call" | custom-call | tf_op jit(solution)/shard_map/finish_volume/pallas_call | solution.py:403
  (13 shorter events, 0.0 us)
Async XLA Ops:
  0.0 12.7 %copy-start.2 = (bf16[2,256,256]{2,1,0:T(8,128)(2,1)S(1)}, bf16[2,256,256]{2,1,0:T(8,128)(2,1)}, u32[]{:S(2)}) copy-start(bf16[2,256,256]{2,1,0:T(8,128)(2,1)} %constant.5.clone.waves) | copy-start | bytes 786436
  0.0 12.7 %copy-start = (s32[4,4]{1,0:T(4,128)S(1)}, s32[4,4]{1,0:T(4,128)}, u32[]{:S(2)}) copy-start(s32[4,4]{1,0:T(4,128)} %defocus_ref.1) | copy-start | bytes 196
  0.0 12.7 %copy-start.1 = (f32[4]{0:T(128)S(1)}, f32[4]{0:T(128)}, u32[]{:S(2)}) copy-start(f32[4]{0:T(128)} %angle_ref.1) | copy-start | bytes 52
  4.5 6.6 %collective-permute-start = (bf16[272,128]{1,0:T(8,128)(2,1)}, bf16[272,128]{1,0:T(8,128)(2,1)S(1)}, u32[]{:S(2)}, u32[]{:S(2)}) collective-permute-start(bf16[272,128]{1,0:T(8,128)(2,1)} %get-tuple-element.14), channel_id=1, source_target_pairs={{0,1},{1,0},{2,3},{3,2},{4,5},{5,4},{6,7},{7,6},{8,9},{9,8},{10,11... | collective-permute-start | bytes 208904 | tf_op jit(solution)/shard_map/ppermute | solution.py:444
  7.6 7.4 %collective-permute-start.4 = (bf16[272,128]{1,0:T(8,128)(2,1)}, bf16[272,128]{1,0:T(8,128)(2,1)S(1)}, u32[]{:S(2)}, u32[]{:S(2)}) collective-permute-start(bf16[272,128]{1,0:T(8,128)(2,1)} %get-tuple-element.15), channel_id=1, source_target_pairs={{0,3},{1,2},{2,1},{3,0},{4,7},{5,6},{6,5},{7,4},{8,11},{9,10},{10,... | collective-permute-start | bytes 208904 | tf_op jit(solution)/shard_map/ppermute | solution.py:444
  10.1 7.0 %collective-permute-start.8 = (bf16[272,128]{1,0:T(8,128)(2,1)}, bf16[272,128]{1,0:T(8,128)(2,1)S(1)}, u32[]{:S(2)}, u32[]{:S(2)}) collective-permute-start(bf16[272,128]{1,0:T(8,128)(2,1)} %get-tuple-element.16), channel_id=1, source_target_pairs={{0,2},{1,3},{2,0},{3,1},{4,6},{5,7},{6,4},{7,5},{8,10},{9,11},{10,... | collective-permute-start | bytes 208904 | tf_op jit(solution)/shard_map/ppermute | solution.py:444
  11.1 5.3 %collective-permute-start.2 = (bf16[544,128]{1,0:T(8,128)(2,1)S(1)}, bf16[544,128]{1,0:T(8,128)(2,1)S(1)}, u32[]{:S(2)}, u32[]{:S(2)}) collective-permute-start(bf16[544,128]{1,0:T(8,128)(2,1)S(1)} %constant_dynamic-update-slice_fusion.refs_0_), channel_id=1, source_target_pairs={{0,8},{4,12},{8,0},{12,4},{1,9},{5,13},{9,1},{13,5},{2,10},{6,14},... | collective-permute-start | bytes 417800 | tf_op jit(solution)/shard_map/ppermute | solution.py:444
  12.7 8.7 %collective-permute-start.1 = (bf16[544,128]{1,0:T(8,128)(2,1)S(1)}, bf16[544,128]{1,0:T(8,128)(2,1)S(1)}, u32[]{:S(2)}, u32[]{:S(2)}) collective-permute-start(bf16[544,128]{1,0:T(8,128)(2,1)S(1)} %constant_dynamic-update-slice_fusion.refs_0_), channel_id=1, source_target_pairs={{0,4},{4,0},{8,12},{12,8},{1,5},{5,1},{9,13},{13,9},{2,6},{6,2},{1... | collective-permute-start | bytes 417800 | tf_op jit(solution)/shard_map/ppermute | solution.py:444
  15.0 4.7 %collective-permute-start.6 = (bf16[272,128]{1,0:T(8,128)(2,1)S(1)}, bf16[272,128]{1,0:T(8,128)(2,1)S(1)}, u32[]{:S(2)}, u32[]{:S(2)}) collective-permute-start(bf16[272,128]{1,0:T(8,128)(2,1)S(1)} %collective-permute-done.4.refs_0_), channel_id=1, source_target_pairs={{0,8},{4,12},{8,0},{12,4},{1,9},{5,13},{9,1},{13,5},{2,10},{6,14},... | collective-permute-start | bytes 208904 | tf_op jit(solution)/shard_map/ppermute | solution.py:444
  16.4 5.5 %collective-permute-start.3 = (bf16[544,128]{1,0:T(8,128)(2,1)S(1)}, bf16[544,128]{1,0:T(8,128)(2,1)S(1)}, u32[]{:S(2)}, u32[]{:S(2)}) collective-permute-start(bf16[544,128]{1,0:T(8,128)(2,1)S(1)} %collective-permute-done.2.refs_2_), channel_id=1, source_target_pairs={{0,4},{4,0},{8,12},{12,8},{1,5},{5,1},{9,13},{13,9},{2,6},{6,2},{1... | collective-permute-start | bytes 417800 | tf_op jit(solution)/shard_map/ppermute | solution.py:444
  17.1 4.3 %collective-permute-start.10 = (bf16[272,128]{1,0:T(8,128)(2,1)S(1)}, bf16[272,128]{1,0:T(8,128)(2,1)S(1)}, u32[]{:S(2)}, u32[]{:S(2)}) collective-permute-start(bf16[272,128]{1,0:T(8,128)(2,1)S(1)} %after.1.refs_4_), channel_id=1, source_target_pairs={{0,8},{4,12},{8,0},{12,4},{1,9},{5,13},{9,1},{13,5},{2,10},{6,14},... | collective-permute-start | bytes 208904 | tf_op jit(solution)/shard_map/ppermute | solution.py:444
  18.6 4.2 %collective-permute-start.9 = (bf16[272,128]{1,0:T(8,128)(2,1)S(1)}, bf16[272,128]{1,0:T(8,128)(2,1)S(1)}, u32[]{:S(2)}, u32[]{:S(2)}) collective-permute-start(bf16[272,128]{1,0:T(8,128)(2,1)S(1)} %after.1.refs_4_), channel_id=1, source_target_pairs={{0,4},{4,0},{8,12},{12,8},{1,5},{5,1},{9,13},{13,9},{2,6},{6,2},{1... | collective-permute-start | bytes 208904 | tf_op jit(solution)/shard_map/ppermute | solution.py:444
  19.7 3.1 %collective-permute-start.5 = (bf16[272,128]{1,0:T(8,128)(2,1)S(1)}, bf16[272,128]{1,0:T(8,128)(2,1)S(1)}, u32[]{:S(2)}, u32[]{:S(2)}) collective-permute-start(bf16[272,128]{1,0:T(8,128)(2,1)S(1)} %collective-permute-done.4.refs_0_), channel_id=1, source_target_pairs={{0,4},{4,0},{8,12},{12,8},{1,5},{5,1},{9,13},{13,9},{2,6},{6,2},{1... | collective-permute-start | bytes 208904 | tf_op jit(solution)/shard_map/ppermute | solution.py:444
  21.4 1.5 %collective-permute-start.7 = (bf16[272,128]{1,0:T(8,128)(2,1)S(1)}, bf16[272,128]{1,0:T(8,128)(2,1)S(1)}, u32[]{:S(2)}, u32[]{:S(2)}) collective-permute-start(bf16[272,128]{1,0:T(8,128)(2,1)S(1)} %collective-permute-done.6.refs_2_), channel_id=1, source_target_pairs={{0,4},{4,0},{8,12},{12,8},{1,5},{5,1},{9,13},{13,9},{2,6},{6,2},{1... | collective-permute-start | bytes 208904 | tf_op jit(solution)/shard_map/ppermute | solution.py:444
  21.4 1.5 %collective-permute-start.11 = (bf16[272,128]{1,0:T(8,128)(2,1)S(1)}, bf16[272,128]{1,0:T(8,128)(2,1)S(1)}, u32[]{:S(2)}, u32[]{:S(2)}) collective-permute-start(bf16[272,128]{1,0:T(8,128)(2,1)S(1)} %collective-permute-done.10.refs_6_), channel_id=1, source_target_pairs={{0,4},{4,0},{8,12},{12,8},{1,5},{5,1},{9,13},{13,9},{2,6},{6,2},{1... | collective-permute-start | bytes 208904 | tf_op jit(solution)/shard_map/ppermute | solution.py:444
